TPU v7x, 32 devices: a whole 2x2x4 slice. The times are simulated.
32 devices in a mesh: section: 8 (over z, core), dp: 4 (over y, x).
Axes of the slice: x: 2, y: 2, z: 4, core: 2. Of those that a mesh axis runs over, the one named last changes fastest.
Arguments:
- w_up: bfloat16 [8, 32, 128, 128], P('section'), may hold values from -0.375 to 0.375
- up_index: int32 [8, 32], P('section'), may hold values from 0 to 31
- w_down: bfloat16 [8, 32, 128, 128], P('section'), may hold values from -0.375 to 0.375
- down_index: int32 [8, 32], P('section'), may hold values from 0 to 31
- tick_order: int32 [8, 2], P('section'), may hold values from 0 to 1, each once within a row
- values_in: bfloat16 [8, 32, 4096], P('section', 'dp'), may hold values from -6 to 6
- score_grad_in: bfloat16 [8, 32, 4096], P('section', 'dp'), may hold values from -6 to 6
- tangent_in: bfloat16 [8, 32, 4096], P('section', 'dp'), may hold values from -6 to 6
- state_adjoint_in: bfloat16 [8, 32, 4096], P('section', 'dp'), may hold values from -6 to 6
- saved_back: bfloat16 [8, 2, 32, 4096], P('section', None, 'dp'), may hold values from -6 to 6
- saved_tan: bfloat16 [8, 2, 32, 4096], P('section', None, 'dp'), may hold values from -6 to 6
- saved_second: bfloat16 [8, 2, 32, 4096], P('section', None, 'dp'), may hold values from -6 to 6
- saved_second_tan: bfloat16 [8, 2, 32, 4096], P('section', None, 'dp'), may hold values from -6 to 6
- saved_second_grad: bfloat16 [8, 2, 32, 4096], P('section', None, 'dp'), may hold values from -6 to 6
Outputs:
- values_out: bfloat16 [8, 32, 4096], P('section', 'dp')
- score_grad_out: bfloat16 [8, 32, 4096], P('section', 'dp')
- tangent_out: bfloat16 [8, 32, 4096], P('section', 'dp')
- state_adjoint_out: bfloat16 [8, 32, 4096], P('section', 'dp')
- grad_up: bfloat16 [8, 32, 128, 128], P('section', 'dp')
- grad_down: bfloat16 [8, 32, 128, 128], P('section', 'dp')
Inputs may be any that keep to these rules, and one draw needn't show every extreme that they name: up_index[s, j] is the input block that hidden block j of layer s reads. down_index[s, i] is the hidden block that output block i of layer s reads. `tick_order`: each row is a permutation of the 2 slots.
All inputs are finite; a program needn't handle non-finite values.
Results may differ from a plain program's by a relative error of at most 0.023.
Values may be sent and summed in bfloat16 or wider, within the bound.
No kernel may reach another device: no remote copies, remote signals or barrier semaphores. Data moves between devices by JAX's collectives and lax.ppermute only.
A program may use at most 64 MiB of HBM per device.

v0:
```python
import jax
import jax.numpy as jnp
from jax import lax
from jax.sharding import PartitionSpec as P

BLOCK = 128


def from_behind(block, axis, distance):
    devices = range(lax.axis_size(axis))
    route = [((i - distance) % len(devices), i) for i in devices]
    return lax.ppermute(block, axis, route)


def silu_parts(inputs):
    logistic = jax.nn.sigmoid(inputs)
    slopes = logistic * (1.0 + inputs * (1.0 - logistic))
    curves = logistic * (1.0 - logistic) * (2.0 + inputs * (1.0 - 2.0 * logistic))
    return (inputs * logistic, slopes, curves)


def block_map(matrix, weight, block_table):
    block_width = weight.shape[-1]
    row_count = matrix.shape[0]
    pieces = matrix.reshape(row_count, -1, block_width)
    picked = jnp.take(pieces, block_table, axis=1)
    result = jnp.einsum("rnk,nkj->rnj", picked, weight, preferred_element_type=jnp.float32)
    return result.reshape(row_count, -1)


def block_map_back(matrix, weight, block_table, block_count):
    block_width = weight.shape[-1]
    row_count = matrix.shape[0]
    pieces = matrix.reshape(row_count, -1, block_width)
    partial_value = jnp.einsum("rnj,nkj->rnk", pieces, weight, preferred_element_type=jnp.float32)
    placing = (block_table[:, None] == jnp.arange(block_count, dtype=jnp.int32)[None, :]).astype(
        jnp.bfloat16
    )
    high_part = partial_value.astype(jnp.bfloat16)
    low_part = (partial_value - high_part.astype(jnp.float32)).astype(jnp.bfloat16)
    result = jnp.einsum("rnk,nc->rck", high_part, placing, preferred_element_type=jnp.float32)
    result = result + jnp.einsum(
        "rnk,nc->rck", low_part, placing, preferred_element_type=jnp.float32
    )
    return result.reshape(row_count, -1)


def grad_blocks(inputs, cotangents, block_table):
    row_count = inputs.shape[0]
    pieces = inputs.reshape(row_count, -1, BLOCK)
    picked = jnp.take(pieces, block_table, axis=1)
    cot_part = cotangents.reshape(row_count, -1, BLOCK)
    return jnp.einsum("rnk,rnj->nkj", picked, cot_part, preferred_element_type=jnp.float32)


def on_device(
    w_up,
    up_index,
    w_down,
    down_index,
    tick_order,
    values_in,
    score_grad_in,
    tangent_in,
    state_adjoint_in,
    saved_back,
    saved_tan,
    saved_second,
    saved_second_tan,
    saved_second_grad,
):
    up_weight = w_up[0]
    up_table = up_index[0]
    down_weight = w_down[0]
    down_table = down_index[0]
    hidden_blocks = up_weight.shape[0]
    model_blocks = down_weight.shape[0]
    row_count = values_in.shape[1]
    replicas = lax.axis_size("dp")
    row_scale = 1.0 / (row_count * replicas)
    values = values_in[0]
    score_grad = score_grad_in[0]
    tangent = tangent_in[0]
    adjoint = state_adjoint_in[0]
    up_inputs = []
    up_cotangents = []
    down_inputs = []
    down_cotangents = []
    for tick_number in range(tick_order.shape[1]):
        slot_index = tick_order[0, tick_number]
        back_input = lax.dynamic_index_in_dim(saved_back[0], slot_index, 0, keepdims=False)
        tangent_input = lax.dynamic_index_in_dim(saved_tan[0], slot_index, 0, keepdims=False)
        second_input = lax.dynamic_index_in_dim(saved_second[0], slot_index, 0, keepdims=False)
        second_tangent = lax.dynamic_index_in_dim(
            saved_second_tan[0], slot_index, 0, keepdims=False
        )
        second_grad = lax.dynamic_index_in_dim(saved_second_grad[0], slot_index, 0, keepdims=False)
        raised = block_map(
            jnp.concatenate(
                [values, tangent_input, tangent, back_input, second_input, second_tangent], 0
            ),
            up_weight,
            up_table,
        )
        (
            raised_values,
            raised_tangent_input,
            raised_tangent,
            raised_back,
            raised_second,
            raised_second_tangent,
        ) = jnp.split(raised, 6, 0)
        hidden_values = silu_parts(raised_values)[0].astype(jnp.bfloat16)
        tangent_hidden = (silu_parts(raised_tangent_input)[1] * raised_tangent).astype(jnp.bfloat16)
        lowered = block_map(
            jnp.concatenate([hidden_values, tangent_hidden], 0), down_weight, down_table
        )
        lowered_values, lowered_tangent = jnp.split(lowered, 2, 0)
        new_values = (values.astype(jnp.float32) + lowered_values).astype(jnp.bfloat16)
        new_tangent = (tangent.astype(jnp.float32) + lowered_tangent).astype(jnp.bfloat16)
        active_back, slope_back, unused_curve = silu_parts(raised_back)
        active_second, slope_second, curve_second = silu_parts(raised_second)
        pulled = block_map_back(
            jnp.concatenate([score_grad, second_grad, adjoint], 0),
            down_weight,
            down_table,
            hidden_blocks,
        )
        pulled_score, pulled_second, pulled_adjoint = jnp.split(pulled, 3, 0)
        gate_back = (slope_back * pulled_score).astype(jnp.bfloat16)
        second_push = (
            slope_second * pulled_adjoint + curve_second * pulled_second * raised_second_tangent
        ).astype(jnp.bfloat16)
        returned = block_map_back(
            jnp.concatenate([gate_back, second_push], 0), up_weight, up_table, model_blocks
        )
        returned_score, returned_adjoint = jnp.split(returned, 2, 0)
        new_score_grad = (score_grad.astype(jnp.float32) + returned_score).astype(jnp.bfloat16)
        new_adjoint = (adjoint.astype(jnp.float32) + returned_adjoint).astype(jnp.bfloat16)
        hidden_back = active_back.astype(jnp.bfloat16)
        hidden_second = active_second.astype(jnp.bfloat16)
        tangent_second = (slope_second * raised_second_tangent).astype(jnp.bfloat16)
        gated_second = (slope_second * pulled_second).astype(jnp.bfloat16)
        up_inputs += [back_input, second_input, second_tangent]
        up_cotangents += [gate_back, second_push, gated_second]
        down_inputs += [hidden_back, hidden_second, tangent_second]
        down_cotangents += [score_grad, adjoint, second_grad]
        values, tangent = from_behind((new_values, new_tangent), "section", 1)
        score_grad, adjoint = from_behind((new_score_grad, new_adjoint), "section", -1)
    up_rows = jnp.concatenate(up_inputs, 0)
    up_cot_rows = jnp.concatenate(up_cotangents, 0)
    down_rows = jnp.concatenate(down_inputs, 0)
    down_cot_rows = jnp.concatenate(down_cotangents, 0)
    up_term = grad_blocks(up_rows, up_cot_rows, up_table) * row_scale
    down_term = grad_blocks(down_rows, down_cot_rows, down_table) * row_scale
    grad_up, grad_down = (
        lax.psum_scatter(
            up_term.astype(jnp.bfloat16), "dp", scatter_dimension=0, tiled=True
        ).astype(jnp.float32),
        lax.psum_scatter(
            down_term.astype(jnp.bfloat16), "dp", scatter_dimension=0, tiled=True
        ).astype(jnp.float32),
    )
    grad_up = grad_up.astype(jnp.bfloat16)
    grad_down = grad_down.astype(jnp.bfloat16)
    return (
        values[None],
        score_grad[None],
        tangent[None],
        adjoint[None],
        grad_up[None],
        grad_down[None],
    )


def solution(mesh):
    placed = (
        P("section", None, None, None),
        P("section", None),
        P("section", None, None, None),
        P("section", None),
        P("section", None),
        P("section", "dp", None),
        P("section", "dp", None),
        P("section", "dp", None),
        P("section", "dp", None),
        P("section", None, "dp", None),
        P("section", None, "dp", None),
        P("section", None, "dp", None),
        P("section", None, "dp", None),
        P("section", None, "dp", None),
    )
    return jax.shard_map(
        on_device,
        mesh=mesh,
        in_specs=placed,
        out_specs=(
            P("section", "dp", None),
            P("section", "dp", None),
            P("section", "dp", None),
            P("section", "dp", None),
            P("section", "dp", None, None),
            P("section", "dp", None, None),
        ),
        check_vma=False,
    )
```

profile of v0, /device:TPU:0, one launch (start us, length us, event | category | flops | bytes accessed | tf_op | source)
XLA Modules:
  0.0 120.1 jit_solution(17931084349378288001)
XLA Ops:
  8.7 1.3 %fusion.128 = (s32[1,1]{1,0:T(1,128)}, s32[1,1]{1,0:T(1,128)}) fusion(s32[1,2]{1,0:T(1,128)} %param.22), kind=kLoop, calls=%fused_computation.224 | loop fusion | bytes 16 | tf_op jit(solution)/shard_map/slice | solution.py:90
  11.3 0.9 constant_dynamic-update-slice_fusion.35
  12.2 0.9 constant_dynamic-update-slice_fusion.5
  13.7 0.9 constant_dynamic-update-slice_fusion.34
  14.6 1.5 %constant_dynamic-update-slice_fusion.33 = (bf16[48,32,128]{2,0,1:T(8,128)(2,1)S(1)}, bf16[8,32,128]{2,0,1:T(8,128)(2,1)}, bf16[48,32,128]{2,0,1:T(8,128)(2,1)S(1)}) fusion(bf16[48,32,128]{2,0,1:T(8,128)(2,1)S(1)} %constant_dynamic-update-slice_fusion.34, bf16[1,2,8,4096]{3,2,1,0:T(8,128)(2,1)} %param.31, s32[]{:T(128)S(6)} %select_n.28, ...), kind=kLoop, calls=%fused_computation.189 | loop fusion | bytes 327684
  16.1 0.9 constant_dynamic-update-slice_fusion.3
  17.0 0.9 constant_dynamic-update-slice_fusion.17
  22.0 2.7 %collective-permute-start.1 = (bf16[8,4096]{1,0:T(8,128)(2,1)}, bf16[8,4096]{1,0:T(8,128)(2,1)S(1)}, u32[]{:S(2)}, u32[]{:S(2)}) collective-permute-start(bf16[8,4096]{1,0:T(8,128)(2,1)} %get-tuple-element.44), channel_id=1, source_target_pairs={{28,0},{0,4},{4,8},{8,12},{12,16},{16,20},{20,24},{24,28},{29,1},{... | collective-permute-start | bytes 196616 | tf_op jit(solution)/shard_map/ppermute | solution.py:12
  28.3 1.4 %collective-permute-start.3 = (bf16[8,4096]{1,0:T(8,128)(2,1)}, bf16[8,4096]{1,0:T(8,128)(2,1)S(1)}, u32[]{:S(2)}, u32[]{:S(2)}) collective-permute-start(bf16[8,4096]{1,0:T(8,128)(2,1)} %fusion.63), channel_id=1, source_target_pairs={{4,0},{8,4},{12,8},{16,12},{20,16},{24,20},{28,24},{0,28},{5,1},{9... | collective-permute-start | bytes 196616 | tf_op jit(solution)/shard_map/ppermute | solution.py:12
  34.4 0.9 constant_dynamic-update-slice_fusion.10
  35.4 0.9 constant_dynamic-update-slice_fusion.14
  36.3 0.9 constant_dynamic-update-slice_fusion.13
  37.1 0.9 constant_dynamic-update-slice_fusion.12
  44.2 0.8 constant_dynamic-update-slice_fusion.20
  46.5 1.7 %gather_fusion.5 = bf16[32,48,128]{2,1,0:T(8,128)(2,1)S(1)} fusion(bf16[48,32,128]{2,0,1:T(8,128)(2,1)} %get-tuple-element.28, s32[1024]{0:T(1024)} %copy-done.21), kind=kCustom, calls=%fused_computation.4.clone | custom fusion | bytes 786560 | tf_op jit(solution)/shard_map/jit(_take)/gather | solution.py:51
  48.2 2.6 %multiply_convert_fusion = bf16[32,128,128]{2,1,0:T(8,128)(2,1)} fusion(bf16[48,32,128]{2,0,1:T(8,128)(2,1)} %get-tuple-element.8, bf16[32,48,128]{2,1,0:T(8,128)(2,1)S(1)} %gather_fusion.5, pred[32]{0:T(512)(128)(4,1)S(1)} %get-tuple-element.62), kind=kOutput, calls=%fused_computation.6 | convolution fusion | flops 51576832 | bytes 1835040 | tf_op jit(solution)/shard_map/rnk,rnj->nkj/dot_general | solution.py:53
  50.9 1.7 %gather_fusion.4 = bf16[32,48,128]{2,1,0:T(8,128)(2,1)S(1)} fusion(bf16[48,32,128]{2,0,1:T(8,128)(2,1)} %copy-done.8, s32[1024]{0:T(1024)} %copy-done.22), kind=kCustom, calls=%fused_computation.3.clone | custom fusion | bytes 786560 | tf_op jit(solution)/shard_map/jit(_take)/gather | solution.py:51
  54.4 1.7 %collective-permute-start.7 = (bf16[8,4096]{1,0:T(8,128)(2,1)}, bf16[8,4096]{1,0:T(8,128)(2,1)}, u32[]{:S(2)}, u32[]{:S(2)}) collective-permute-start(bf16[8,4096]{1,0:T(8,128)(2,1)} %fusion.60), channel_id=1, source_target_pairs={{4,0},{8,4},{12,8},{16,12},{20,16},{24,20},{28,24},{0,28},{5,1},{9... | collective-permute-start | bytes 196616 | tf_op jit(solution)/shard_map/ppermute | solution.py:12
  56.1 1.5 %multiply_convert_fusion.1 = bf16[32,128,128]{2,1,0:T(8,128)(2,1)} fusion(bf16[48,32,128]{2,0,1:T(8,128)(2,1)S(1)} %copy-done.7, bf16[32,48,128]{2,1,0:T(8,128)(2,1)S(1)} %gather_fusion.4, pred[32]{0:T(512)(128)(4,1)S(1)} %get-tuple-element.63), kind=kOutput, calls=%fused_computation.7 | convolution fusion | flops 51576832 | bytes 1835040 | tf_op jit(solution)/shard_map/rnk,rnj->nkj/dot_general | solution.py:53
  58.4 0.8 gather_fusion.3
  60.1 5.1 %collective-permute-done.2 = bf16[8,4096]{1,0:T(8,128)(2,1)S(1)} collective-permute-done((bf16[8,4096]{1,0:T(8,128)(2,1)S(1)}, bf16[8,4096]{1,0:T(8,128)(2,1)S(1)}, u32[]{:S(2)}, u32[]{:S(2)}) %collective-permute-start.2) | collective-permute-done | bytes 65568 | tf_op jit(solution)/shard_map/ppermute | solution.py:12
  66.0 12.5 %reduce-scatter.5.cloned.1.call-done = bf16[8,128,128]{2,1,0:T(8,128)(2,1)} async-done(((bf16[32,128,128]{2,1,0:T(8,128)(2,1)}), bf16[8,128,128]{2,1,0:T(8,128)(2,1)}) %reduce-scatter.5.cloned.1.call-update) | async-done | bytes 262160 | tf_op jit(solution)/shard_map/reduce_scatter | solution.py:160
  78.4 31.5 %reduce-scatter.3.cloned.1.call-done = bf16[8,128,128]{2,1,0:T(8,128)(2,1)} async-done(((bf16[32,128,128]{2,1,0:T(8,128)(2,1)}), bf16[8,128,128]{2,1,0:T(8,128)(2,1)}) %reduce-scatter.3.cloned.1.call-update) | async-done | bytes 262160 | tf_op jit(solution)/shard_map/reduce_scatter | solution.py:157
  111.8 1.5 %copy.101 = bf16[1,8,4096]{2,1,0:T(8,128)(2,1)} copy(bf16[1,8,4096]{2,1,0:T(8,128)(2,1)} %bitcast.53) | data formatting | bytes 131072
  (116 shorter events, 25.6 us)
Async XLA Ops:
  7.2 11.5 %copy-start = (bf16[1,32,128,128]{3,2,1,0:T(8,128)(2,1)S(1)}, bf16[1,32,128,128]{3,2,1,0:T(8,128)(2,1)}, u32[]{:S(2)}) copy-start(bf16[1,32,128,128]{3,2,1,0:T(8,128)(2,1)} %param.18) | copy-start | bytes 3145732
  7.2 10.7 %copy-start.16 = (bf16[1,2,8,4096]{3,2,1,0:T(8,128)(2,1)S(1)}, bf16[1,2,8,4096]{3,2,1,0:T(8,128)(2,1)}, u32[]{:S(2)}) copy-start(bf16[1,2,8,4096]{3,2,1,0:T(8,128)(2,1)} %param.29) | copy-start | bytes 393220
  7.2 10.7 %copy-start.17 = (bf16[1,2,8,4096]{3,2,1,0:T(8,128)(2,1)S(1)}, bf16[1,2,8,4096]{3,2,1,0:T(8,128)(2,1)}, u32[]{:S(2)}) copy-start(bf16[1,2,8,4096]{3,2,1,0:T(8,128)(2,1)} %param.30) | copy-start | bytes 393220
  7.2 71.2 %reduce-scatter.5.cloned.1.call-start = ((), (), s32[]{:S(2)}) async-start(), calls=%async_computation.3 | async-start | bytes 1310720 | tf_op jit(solution)/shard_map/reduce_scatter | solution.py:160
  13.0 6.1 %copy-start.22 = (s32[1024]{0:T(1024)}, s32[1024]{0:T(1024)S(1)}, u32[]{:S(2)}) copy-start(s32[1024]{0:T(1024)S(1)} %pad_clamp_fusion.1) | copy-start | bytes 12292
  16.1 1.9 %copy-start.5 = (bf16[48,32,128]{2,0,1:T(8,128)(2,1)}, bf16[48,32,128]{2,0,1:T(8,128)(2,1)S(1)}, u32[]{:S(2)}) copy-start(bf16[48,32,128]{2,0,1:T(8,128)(2,1)S(1)} %get-tuple-element.10) | copy-start | bytes 1179652
  19.3 2.3 %copy-start.21 = (s32[1024]{0:T(1024)}, s32[1024]{0:T(1024)S(1)}, u32[]{:S(2)}) copy-start(s32[1024]{0:T(1024)S(1)} %pad_clamp_fusion) | copy-start | bytes 12292
  20.4 4.3 %copy-start.2 = (bf16[1,8,4096]{2,1,0:T(8,128)(2,1)S(1)}, bf16[1,8,4096]{2,1,0:T(8,128)(2,1)}, u32[]{:S(2)}) copy-start(bf16[1,8,4096]{2,1,0:T(8,128)(2,1)} %param.24) | copy-start | bytes 196612
  20.4 4.4 %copy-start.3 = (bf16[1,8,4096]{2,1,0:T(8,128)(2,1)S(1)}, bf16[1,8,4096]{2,1,0:T(8,128)(2,1)}, u32[]{:S(2)}) copy-start(bf16[1,8,4096]{2,1,0:T(8,128)(2,1)} %param.26) | copy-start | bytes 196612
  20.4 4.4 %copy-start.9 = (bf16[8,32,128]{2,0,1:T(8,128)(2,1)S(1)}, bf16[8,32,128]{2,0,1:T(8,128)(2,1)}, u32[]{:S(2)}) copy-start(bf16[8,32,128]{2,0,1:T(8,128)(2,1)} %get-tuple-element.11) | copy-start | bytes 196612
  21.5 3.9 %copy-start.20 = (s32[1,32]{1,0:T(1,128)S(1)}, s32[1,32]{1,0:T(1,128)}, u32[]{:S(2)}) copy-start(s32[1,32]{1,0:T(1,128)} %param.21) | copy-start | bytes 388
  21.5 12.9 %collective-permute-start = (bf16[8,4096]{1,0:T(8,128)(2,1)}, bf16[8,4096]{1,0:T(8,128)(2,1)S(1)}, u32[]{:S(2)}, u32[]{:S(2)}) collective-permute-start(bf16[8,4096]{1,0:T(8,128)(2,1)} %get-tuple-element.45), channel_id=1, source_target_pairs={{28,0},{0,4},{4,8},{8,12},{12,16},{16,20},{20,24},{24,28},{29,1},{... | collective-permute-start | bytes 196616 | tf_op jit(solution)/shard_map/ppermute | solution.py:12
  22.0 13.3 %collective-permute-start.1 = (bf16[8,4096]{1,0:T(8,128)(2,1)}, bf16[8,4096]{1,0:T(8,128)(2,1)S(1)}, u32[]{:S(2)}, u32[]{:S(2)}) collective-permute-start(bf16[8,4096]{1,0:T(8,128)(2,1)} %get-tuple-element.44), channel_id=1, source_target_pairs={{28,0},{0,4},{4,8},{8,12},{12,16},{16,20},{20,24},{24,28},{29,1},{... | collective-permute-start | bytes 196616 | tf_op jit(solution)/shard_map/ppermute | solution.py:12
  28.3 11.8 %collective-permute-start.3 = (bf16[8,4096]{1,0:T(8,128)(2,1)}, bf16[8,4096]{1,0:T(8,128)(2,1)S(1)}, u32[]{:S(2)}, u32[]{:S(2)}) collective-permute-start(bf16[8,4096]{1,0:T(8,128)(2,1)} %fusion.63), channel_id=1, source_target_pairs={{4,0},{8,4},{12,8},{16,12},{20,16},{24,20},{28,24},{0,28},{5,1},{9... | collective-permute-start | bytes 196616 | tf_op jit(solution)/shard_map/ppermute | solution.py:12
  30.4 10.3 %collective-permute-start.4 = (bf16[8,4096]{1,0:T(8,128)(2,1)}, bf16[8,4096]{1,0:T(8,128)(2,1)S(1)}, u32[]{:S(2)}, u32[]{:S(2)}) collective-permute-start(bf16[8,4096]{1,0:T(8,128)(2,1)} %fusion.62), channel_id=1, source_target_pairs={{4,0},{8,4},{12,8},{16,12},{20,16},{24,20},{28,24},{0,28},{5,1},{9... | collective-permute-start | bytes 196616 | tf_op jit(solution)/shard_map/ppermute | solution.py:12
  34.4 5.6 %copy-start.12 = (bf16[8,4096]{1,0:T(8,128)(2,1)}, bf16[8,4096]{1,0:T(8,128)(2,1)S(1)}, u32[]{:S(2)}) copy-start(bf16[8,4096]{1,0:T(8,128)(2,1)S(1)} %collective-permute-done) | copy-start | bytes 196612
  35.3 4.7 %copy-start.14 = (bf16[8,4096]{1,0:T(8,128)(2,1)}, bf16[8,4096]{1,0:T(8,128)(2,1)S(1)}, u32[]{:S(2)}) copy-start(bf16[8,4096]{1,0:T(8,128)(2,1)S(1)} %collective-permute-done.1) | copy-start | bytes 196612
  39.6 1.8 %copy-start.18 = (bf16[1,2,8,4096]{3,2,1,0:T(8,128)(2,1)S(1)}, bf16[1,2,8,4096]{3,2,1,0:T(8,128)(2,1)}, u32[]{:S(2)}) copy-start(bf16[1,2,8,4096]{3,2,1,0:T(8,128)(2,1)} %param.31) | copy-start | bytes 393220
  50.8 59.1 %reduce-scatter.3.cloned.1.call-start = ((), (), s32[]{:S(2)}) async-start(), calls=%async_computation.2 | async-start | bytes 1310720 | tf_op jit(solution)/shard_map/reduce_scatter | solution.py:157
  53.3 2.8 %copy-start.7 = (bf16[48,32,128]{2,0,1:T(8,128)(2,1)S(1)}, bf16[48,32,128]{2,0,1:T(8,128)(2,1)}, u32[]{:S(2)}) copy-start(bf16[48,32,128]{2,0,1:T(8,128)(2,1)} %get-tuple-element.29) | copy-start | bytes 1179652
  54.4 5.5 %collective-permute-start.7 = (bf16[8,4096]{1,0:T(8,128)(2,1)}, bf16[8,4096]{1,0:T(8,128)(2,1)}, u32[]{:S(2)}, u32[]{:S(2)}) collective-permute-start(bf16[8,4096]{1,0:T(8,128)(2,1)} %fusion.60), channel_id=1, source_target_pairs={{4,0},{8,4},{12,8},{16,12},{20,16},{24,20},{28,24},{0,28},{5,1},{9... | collective-permute-start | bytes 196616 | tf_op jit(solution)/shard_map/ppermute | solution.py:12
  57.7 2.4 %collective-permute-start.5 = (bf16[8,4096]{1,0:T(8,128)(2,1)S(1)}, bf16[8,4096]{1,0:T(8,128)(2,1)S(1)}, u32[]{:S(2)}, u32[]{:S(2)}) collective-permute-start(bf16[8,4096]{1,0:T(8,128)(2,1)S(1)} %fusion.61), channel_id=1, source_target_pairs={{4,0},{8,4},{12,8},{16,12},{20,16},{24,20},{28,24},{0,28},{5,1},{9... | collective-permute-start | bytes 196616 | tf_op jit(solution)/shard_map/ppermute | solution.py:12
  59.7 5.5 %collective-permute-start.2 = (bf16[8,4096]{1,0:T(8,128)(2,1)S(1)}, bf16[8,4096]{1,0:T(8,128)(2,1)S(1)}, u32[]{:S(2)}, u32[]{:S(2)}) collective-permute-start(bf16[8,4096]{1,0:T(8,128)(2,1)S(1)} %get-tuple-element.41), channel_id=1, source_target_pairs={{28,0},{0,4},{4,8},{8,12},{12,16},{16,20},{20,24},{24,28},{29,1},{... | collective-permute-start | bytes 196616 | tf_op jit(solution)/shard_map/ppermute | solution.py:12
  59.8 6.1 %collective-permute-start.6 = (bf16[8,4096]{1,0:T(8,128)(2,1)S(1)}, bf16[8,4096]{1,0:T(8,128)(2,1)S(1)}, u32[]{:S(2)}, u32[]{:S(2)}) collective-permute-start(bf16[8,4096]{1,0:T(8,128)(2,1)S(1)} %get-tuple-element.40), channel_id=1, source_target_pairs={{28,0},{0,4},{4,8},{8,12},{12,16},{16,20},{20,24},{24,28},{29,1},{... | collective-permute-start | bytes 196616 | tf_op jit(solution)/shard_map/ppermute | solution.py:12
  (9 other events, 8.8 us)
Sparse Core Ops, SparseCore 0:
  50.9 27.4 reduce-scatter.4
  82.1 27.7 reduce-scatter.2
where the time goes:
time: 121 us; the launch traced here: 120 us
  waiting for transfers between devices  50 us (41%)
  local copies, waits for them, and re-layouts  25.3 us (21%)
  between operations  18.2 us (15%)
  matrix products  9.99 us (8%)
  other arithmetic  8.82 us (7%)
  starting transfers between devices  7.72 us (6%)
    reduce_scatter x1, waiting for transfers between devices, on_device(): lax.psum_scatter(up_term.astype(jnp.bfloat16), 'dp', scatter_dimension=0,...  31.5 us
    unnamed x67, local copies, waits for them, and re-layouts  16.2 us
    reduce_scatter x1, waiting for transfers between devices, on_device(): lax.psum_scatter(down_term.astype(jnp.bfloat16), 'dp', scatter_dimension=...  12.5 us
    ppermute x8, starting transfers between devices, from_behind(): return lax.ppermute(block, axis, route)  7.64 us
    ppermute x8, waiting for transfers between devices, from_behind(): return lax.ppermute(block, axis, route)  6.07 us
    dot_general x2, matrix products, grad_blocks(): jnp.einsum('rnk,rnj->nkj', picked, cot_part, preferred_element_type=jnp.f...  4.12 us
    gather x2, local copies, waits for them, and re-layouts, grad_blocks(): picked = jnp.take(pieces, block_table, axis=1)  3.48 us
    gather x4, local copies, waits for them, and re-layouts, block_map(): picked = jnp.take(pieces, block_table, axis=1)  2.81 us
  transfers between devices with their start and end apart: 10, of which 5 were waited for; matrix products, arithmetic and copies ran while one was open for 14% of the time, Pallas kernels for 0%

commit v1 on v0

v1 whole, which is shorter than its diff:
```python
import jax
import jax.numpy as jnp
from jax import lax
from jax.experimental import pallas as pl
from jax.experimental.pallas import tpu as pltpu
from jax.sharding import PartitionSpec as P

BLOCK = 128
F32 = jnp.float32
BF16 = jnp.bfloat16
LIMIT = 40 * 1024 * 1024


def partner(me, step, count):
    if count & (count - 1) == 0:
        return me ^ step
    return lax.rem(me + step, count)


def swap_route(step, count):
    if count & (count - 1) == 0:
        return [(i, i ^ step) for i in range(count)]
    return [(i, (i + step) % count) for i in range(count)]


def from_behind(block, axis, distance):
    devices = range(lax.axis_size(axis))
    route = [((i - distance) % len(devices), i) for i in devices]
    return lax.ppermute(block, axis, route)


def times(rows, weight):
    return lax.dot_general(rows, weight, (((1,), (0,)), ((), ())), preferred_element_type=F32)


def times_transposed(rows, weight):
    return lax.dot_general(rows, weight, (((1,), (1,)), ((), ())), preferred_element_type=F32)


def sigmoid(z):
    return 1.0 / (1.0 + jnp.exp(-z))


def slope_of(z, s):
    return s * (1.0 + z * (1.0 - s))


def lanes(block):
    if isinstance(block, int):
        return pl.ds(block * BLOCK, BLOCK)
    return pl.ds(pl.multiple_of(block * BLOCK, BLOCK), BLOCK)


def stack(parts):
    return jnp.concatenate([part.astype(F32) for part in parts], 0)


def send_order(me, count, per):
    for step in range(count):
        base = partner(me, step, count) * per
        for place in range(per):
            yield step, place, base + place


def back_first(count, per, blocks, up_idx, down_idx, order, w_up, w_down, g_ref, a_ref, back, second, second_tan,
               second_grad, pack, keep, *rest):
    sends = rest[:count]
    pulled, returned, hidden = rest[count:]
    me = lax.axis_index("dp")
    m0 = order[0, 0]
    m1 = order[0, 1]
    for b in range(blocks):
        pulled[b] = jnp.zeros(pulled.shape[1:], F32)
        returned[b] = stack([g_ref[0, :, lanes(b)], a_ref[0, :, lanes(b)]])
    for step, place, i in send_order(me, count, per):
        at = lanes(i)
        c = stack([g_ref[0, :, at], a_ref[0, :, at], second_grad[0, m0, :, at], second_grad[0, m1, :, at]]).astype(BF16)
        sends[step][8, :, lanes(place)] = c[0:16]
        sends[step][9, :, lanes(place)] = c[16:32]
        target = down_idx[0, i]
        pulled[target] = pulled[target] + times_transposed(c, w_down[0, i])
    for step, place, j in send_order(me, count, per):
        u = up_idx[0, j]
        at = lanes(u)
        x = stack([back[0, m0, :, at], second[0, m0, :, at], second_tan[0, m0, :, at],
                   second_tan[0, m1, :, at], back[0, m1, :, at], second[0, m1, :, at]]).astype(BF16)
        out = sends[step]
        here = lanes(place)
        for group in range(3):
            out[group, :, here] = x[16 * group:16 * group + 16]
        z = times(x, w_up[0, j])
        zb0, za0, ta0, ta1, zb1, za1 = (z[8 * k:8 * k + 8] for k in range(6))
        pg, pa, ga0, ga1 = (pulled[j, 8 * k:8 * k + 8] for k in range(4))
        sb0, sa0, sb1, sa1 = sigmoid(zb0), sigmoid(za0), sigmoid(zb1), sigmoid(za1)
        slope_a0 = slope_of(za0, sa0)
        slope_a1 = slope_of(za1, sa1)
        curve_a0 = sa0 * (1.0 - sa0) * (2.0 + za0 * (1.0 - 2.0 * sa0))
        curve_a1 = sa1 * (1.0 - sa1) * (2.0 + za1 * (1.0 - 2.0 * sa1))
        push = slope_a0 * pa + curve_a0 * ga0 * ta0
        e = jnp.concatenate([slope_of(zb0, sb0) * pg, push], 0).astype(BF16)
        out[3, :, here] = e
        out[4, :, here] = jnp.concatenate([slope_a0 * ga0, slope_a1 * ga1], 0).astype(BF16)
        hidden[j] = jnp.concatenate(
            [zb0 * sb0, za0 * sa0, slope_a0 * ta0, slope_a1 * ta1, zb1 * sb1, za1 * sa1], 0).astype(BF16)
        keep[j] = jnp.concatenate([slope_of(zb1, sb1), slope_a1, curve_a1 * ga1 * ta1], 0)
        returned[u] = returned[u] + times_transposed(e, w_up[0, j])
    for b in range(blocks):
        pack[:, lanes(b)] = returned[b].astype(BF16)
    for step, place, i in send_order(me, count, per):
        y = hidden[down_idx[0, i]]
        for group in range(3):
            sends[step][5 + group, :, lanes(place)] = y[16 * group:16 * group + 16]


def forward_first(blocks, up_idx, down_idx, order, w_up, w_down, v_ref, t_ref, tan, pack, keep, hidden):
    m0 = order[0, 0]
    m1 = order[0, 1]
    for j in range(blocks):
        at = lanes(up_idx[0, j])
        x = stack([v_ref[0, :, at], t_ref[0, :, at], tan[0, m0, :, at], tan[0, m1, :, at]]).astype(BF16)
        z = times(x, w_up[0, j])
        zv, zt, z0, z1 = (z[8 * k:8 * k + 8] for k in range(4))
        hidden[j] = jnp.concatenate([zv * sigmoid(zv), slope_of(z0, sigmoid(z0)) * zt], 0).astype(BF16)
        keep[j] = slope_of(z1, sigmoid(z1))
    for i in range(blocks):
        at = lanes(i)
        moved = stack([v_ref[0, :, at], t_ref[0, :, at]]) + times(hidden[down_idx[0, i]], w_down[0, i])
        pack[:, at] = moved.astype(BF16)


def back_second(count, per, blocks, up_idx, down_idx, w_up, w_down, rows, keep, pack, *rest):
    sends = rest[:count]
    pulled, returned = rest[count:]
    me = lax.axis_index("dp")
    for b in range(blocks):
        pulled[b] = jnp.zeros(pulled.shape[1:], F32)
        returned[b] = rows[:, lanes(b)].astype(F32)
    for step, place, i in send_order(me, count, per):
        c = rows[:, lanes(i)]
        sends[step][1, :, lanes(place)] = c
        target = down_idx[0, i]
        pulled[target] = pulled[target] + times_transposed(c, w_down[0, i])
    for step, place, j in send_order(me, count, per):
        u = up_idx[0, j]
        slope_b, slope_a, push = (keep[j, 8 * k:8 * k + 8] for k in range(3))
        e = jnp.concatenate([slope_b * pulled[j, 0:8], slope_a * pulled[j, 8:16] + push], 0).astype(BF16)
        sends[step][0, :, lanes(place)] = e
        returned[u] = returned[u] + times_transposed(e, w_up[0, j])
    for b in range(blocks):
        pack[:, lanes(b)] = returned[b].astype(BF16)


def forward_second(blocks, up_idx, down_idx, w_up, w_down, rows, keep, pack, hidden):
    for j in range(blocks):
        z = times(rows[:, lanes(up_idx[0, j])], w_up[0, j])
        zv, zt = z[0:8], z[8:16]
        hidden[j] = jnp.concatenate([zv * sigmoid(zv), keep[j] * zt], 0).astype(BF16)
    for i in range(blocks):
        at = lanes(i)
        pack[:, at] = (rows[:, at].astype(F32) + times(hidden[down_idx[0, i]], w_down[0, i])).astype(BF16)


def finish(count, per, scale, fwd, bwd, *rest):
    early = rest[:count]
    late = rest[count:2 * count]
    values, score, tangent, adjoint, grad_up, grad_down = rest[2 * count:]
    moved = fwd[...].astype(F32)
    values[0] = moved[0:8].astype(BF16)
    tangent[0] = moved[8:16].astype(BF16)
    moved = bwd[...].astype(F32)
    score[0] = moved[0:8].astype(BF16)
    adjoint[0] = moved[8:16].astype(BF16)
    for place in range(per):
        at = lanes(place)
        for out, left, right, last in ((grad_up, (0, 1, 2), (3, 4), 0), (grad_down, (5, 6, 7), (8, 9), 1)):
            xs, es = [], []
            for source in range(count):
                xs += [early[source][k, :, at] for k in left]
                es += [early[source][k, :, at] for k in right] + [late[source][last, :, at]]
            total = lax.dot_general(jnp.concatenate(xs, 0), jnp.concatenate(es, 0), (((0,), (0,)), ((), ())),
                                    preferred_element_type=F32)
            out[0, place] = (total * scale).astype(BF16)


def call(body, operands, smem, outs, scratch, flops=0):
    specs = [pl.BlockSpec(memory_space=pltpu.SMEM)] * smem
    specs += [pl.BlockSpec(memory_space=pltpu.VMEM)] * (len(operands) - smem)
    moved = sum(x.size * x.dtype.itemsize for x in list(operands) + list(outs))
    return pl.pallas_call(
        body,
        out_shape=outs,
        in_specs=specs,
        out_specs=[pl.BlockSpec(memory_space=pltpu.VMEM)] * len(outs),
        scratch_shapes=scratch,
        compiler_params=pltpu.CompilerParams(vmem_limit_bytes=LIMIT),
        cost_estimate=pl.CostEstimate(flops=flops, bytes_accessed=moved, transcendentals=0),
    )(*operands)


def on_device(w_up, up_index, w_down, down_index, tick_order, values_in, score_grad_in, tangent_in, state_adjoint_in,
              saved_back, saved_tan, saved_second, saved_second_tan, saved_second_grad):
    count = lax.axis_size("dp")
    blocks = w_up.shape[1]
    per = blocks // count
    width = values_in.shape[2]
    part = per * BLOCK
    scale = 1.0 / (values_in.shape[1] * count)
    shape = jax.ShapeDtypeStruct
    pair = shape((16, width), BF16)

    def body(f, *args):
        def kernel(*refs):
            f(*args, *refs)
        return kernel

    bwd, keep, *early = call(
        body(back_first, count, per, blocks),
        (up_index, down_index, tick_order, w_up, w_down, score_grad_in, state_adjoint_in, saved_back, saved_second,
         saved_second_tan, saved_second_grad), 3,
        [pair, shape((blocks, 24, BLOCK), F32)] + [shape((10, 16, part), BF16)] * count,
        [pltpu.VMEM((blocks, 32, BLOCK), F32), pltpu.VMEM((blocks, 16, BLOCK), F32), pltpu.VMEM((blocks, 48, BLOCK), BF16)])
    bwd = from_behind(bwd, "section", -1)
    fwd, keep_tan = call(
        body(forward_first, blocks),
        (up_index, down_index, tick_order, w_up, w_down, values_in, tangent_in, saved_tan), 3,
        [pair, shape((blocks, 8, BLOCK), F32)],
        [pltpu.VMEM((blocks, 16, BLOCK), BF16)])
    fwd = from_behind(fwd, "section", 1)
    early = early[:1] + [lax.ppermute(early[step], "dp", swap_route(step, count)) for step in range(1, count)]
    bwd, *late = call(
        body(back_second, count, per, blocks),
        (up_index, down_index, w_up, w_down, bwd, keep), 2,
        [pair] + [shape((2, 16, part), BF16)] * count,
        [pltpu.VMEM((blocks, 16, BLOCK), F32), pltpu.VMEM((blocks, 16, BLOCK), F32)])
    late = late[:1] + [lax.ppermute(late[step], "dp", swap_route(step, count)) for step in range(1, count)]
    bwd = from_behind(bwd, "section", -1)
    (fwd,) = call(
        body(forward_second, blocks),
        (up_index, down_index, w_up, w_down, fwd, keep_tan), 2,
        [pair], [pltpu.VMEM((blocks, 16, BLOCK), BF16)])
    fwd = from_behind(fwd, "section", 1)
    stream = shape((1,) + values_in.shape[1:], BF16)
    grad = shape((1, per, BLOCK, BLOCK), BF16)
    return tuple(call(
        body(finish, count, per, scale), (fwd, bwd, *early, *late), 0,
        [stream, stream, stream, stream, grad, grad], []))


def solution(mesh):
    layer = P("section", None, None, None)
    table = P("section", None)
    stream = P("section", "dp", None)
    saved = P("section", None, "dp", None)
    return jax.shard_map(
        on_device,
        mesh=mesh,
        in_specs=(layer, table, layer, table, table) + (stream,) * 4 + (saved,) * 5,
        out_specs=(stream,) * 4 + (P("section", "dp", None, None),) * 2,
        check_vma=False,
    )
```

time: 121 us -> 49.1 us (0.41)
  waiting for transfers between devices: 50 us -> 12.7 us
  between operations: 18.2 us -> 0.74 us
  local copies, waits for them, and re-layouts: 25.3 us -> 9.72 us
  matrix products: 9.99 us -> 0 us
  Pallas kernels: 0 us -> 9.58 us
  other arithmetic: 8.82 us -> 0 us
  starting transfers between devices: 7.72 us -> 15.9 us
    reduce_scatter x2 -> x0, waiting for transfers between devices: 43.9 us -> none  [the longest x1 31.5 us: on_device(): lax.psum_scatter(up_term.astype(jnp.bfloat16), 'dp', scatter_dimension=0,...]
    dot_general x18 -> x0, matrix products: 9.99 us -> none  [the longest x2 4.12 us: grad_blocks(): jnp.einsum('rnk,rnj->nkj', picked, cot_part, preferred_element_type=jnp.f...]
    pallas_call x0 -> x5, Pallas kernels: none -> 9.58 us  [call(): pl.pallas_call(body, out_shape=outs, in_specs=specs, out_specs=[pl.BlockS...]
    ppermute x0 -> x6, waiting for transfers between devices: none -> 9.55 us  [the longest x3 9.55 us: on_device(): lax.ppermute(late[step], 'dp', swap_route(step, count))]
    ppermute x0 -> x6, starting transfers between devices: none -> 9.08 us  [the longest x3 5.53 us: on_device(): lax.ppermute(late[step], 'dp', swap_route(step, count))]
    unnamed x67 -> x32, local copies, waits for them, and re-layouts: 16.2 us -> 9.72 us
    gather x6 -> x0, local copies, waits for them, and re-layouts: 6.29 us -> none  [the longest x2 3.48 us: grad_blocks(): picked = jnp.take(pieces, block_table, axis=1)]
    convert_element_type x8 -> x0, other arithmetic: 3.11 us -> none  [the longest x2 1.42 us: on_device(): (adjoint.astype(jnp.float32) + returned_adjoint).astype(jnp.bfloat16)]
  transfers between devices with their start and end apart: 10 -> 10, of which waited for: 5 -> 3; matrix products, arithmetic and copies ran while one was open for 14% -> 0% of each run, Pallas kernels for 0% -> 9%
where the time goes in v1:
time: 49.1 us; the launch traced here: 48.7 us
  starting transfers between devices  15.9 us (32%)
  waiting for transfers between devices  12.7 us (26%)
  local copies, waits for them, and re-layouts  9.72 us (20%)
  Pallas kernels  9.58 us (20%)
  between operations  0.74 us (2%)
    unnamed x32, local copies, waits for them, and re-layouts  9.72 us
    pallas_call x5, Pallas kernels, call(): pl.pallas_call(body, out_shape=outs, in_specs=specs, out_specs=[pl.BlockS...  9.58 us
    ppermute x3, waiting for transfers between devices, on_device(): lax.ppermute(late[step], 'dp', swap_route(step, count))  9.55 us
    ppermute x4, starting transfers between devices, from_behind(): return lax.ppermute(block, axis, route)  6.86 us
    ppermute x3, starting transfers between devices, on_device(): lax.ppermute(late[step], 'dp', swap_route(step, count))  5.53 us
    ppermute x3, starting transfers between devices, on_device(): lax.ppermute(early[step], 'dp', swap_route(step, count))  3.55 us
    ppermute x4, waiting for transfers between devices, from_behind(): return lax.ppermute(block, axis, route)  3.18 us
  transfers between devices with their start and end apart: 10, of which 3 were waited for; matrix products, arithmetic and copies ran while one was open for 0% of the time, Pallas kernels for 9%

profile of v1, /device:TPU:0, one launch (start us, length us, event | category | flops | bytes accessed | tf_op | source)
XLA Modules:
  0.0 48.7 jit_solution(4780951804733876845)
XLA Ops:
  0.6 1.2 %copy-done = bf16[1,32,128,128]{3,2,1,0:T(8,128)(2,1)S(1)} copy-done((bf16[1,32,128,128]{3,2,1,0:T(8,128)(2,1)S(1)}, bf16[1,32,128,128]{3,2,1,0:T(8,128)(2,1)}, u32[]{:S(2)}) %copy-start) | copy-done | bytes 1048600
  1.9 1.2 %copy-done.2 = bf16[1,32,128,128]{3,2,1,0:T(8,128)(2,1)S(1)} copy-done((bf16[1,32,128,128]{3,2,1,0:T(8,128)(2,1)S(1)}, bf16[1,32,128,128]{3,2,1,0:T(8,128)(2,1)}, u32[]{:S(2)}) %copy-start.2) | copy-done | bytes 1048600
  3.1 0.9 %copy-done.4 = bf16[1,2,8,4096]{3,2,1,0:T(8,128)(2,1)S(1)} copy-done((bf16[1,2,8,4096]{3,2,1,0:T(8,128)(2,1)S(1)}, bf16[1,2,8,4096]{3,2,1,0:T(8,128)(2,1)}, u32[]{:S(2)}) %copy-start.4) | copy-done | bytes 131096
  4.0 0.9 %copy-done.5 = bf16[1,2,8,4096]{3,2,1,0:T(8,128)(2,1)S(1)} copy-done((bf16[1,2,8,4096]{3,2,1,0:T(8,128)(2,1)S(1)}, bf16[1,2,8,4096]{3,2,1,0:T(8,128)(2,1)}, u32[]{:S(2)}) %copy-start.5) | copy-done | bytes 131096
  4.9 0.9 %copy-done.6 = bf16[1,2,8,4096]{3,2,1,0:T(8,128)(2,1)S(1)} copy-done((bf16[1,2,8,4096]{3,2,1,0:T(8,128)(2,1)S(1)}, bf16[1,2,8,4096]{3,2,1,0:T(8,128)(2,1)}, u32[]{:S(2)}) %copy-start.6) | copy-done | bytes 131096
  5.8 0.9 %copy-done.7 = bf16[1,2,8,4096]{3,2,1,0:T(8,128)(2,1)S(1)} copy-done((bf16[1,2,8,4096]{3,2,1,0:T(8,128)(2,1)S(1)}, bf16[1,2,8,4096]{3,2,1,0:T(8,128)(2,1)}, u32[]{:S(2)}) %copy-start.7) | copy-done | bytes 131096
  6.7 0.8 %copy-done.9 = bf16[1,8,4096]{2,1,0:T(8,128)(2,1)S(1)} copy-done((bf16[1,8,4096]{2,1,0:T(8,128)(2,1)S(1)}, bf16[1,8,4096]{2,1,0:T(8,128)(2,1)}, u32[]{:S(2)}) %copy-start.9) | copy-done | bytes 65560
  7.6 0.8 %copy-done.10 = bf16[1,8,4096]{2,1,0:T(8,128)(2,1)S(1)} copy-done((bf16[1,8,4096]{2,1,0:T(8,128)(2,1)S(1)}, bf16[1,8,4096]{2,1,0:T(8,128)(2,1)}, u32[]{:S(2)}) %copy-start.10) | copy-done | bytes 65560
  9.0 0.7 %copy-done.14 = s32[1,32]{1,0:T(1,128)S(1)} copy-done((s32[1,32]{1,0:T(1,128)S(1)}, s32[1,32]{1,0:T(1,128)}, u32[]{:S(2)}) %copy-start.14) | copy-done | bytes 152
  10.4 3.7 %shard_map.183 = (bf16[16,4096]{1,0:T(8,128)(2,1)S(1)}, f32[32,24,128]{2,1,0:T(8,128)S(1)}, bf16[10,16,1024]{2,1,0:T(8,128)(2,1)S(1)}, bf16[10,16,1024]{2,1,0:T(...) custom-call(s32[1,32]{1,0:T(1,128)S(1)} %copy-done.13, s32[1,32]{1,0:T(1,128)S(1)} %copy-done.14, ...), custom_call_target="tpu_custom_call" | custom-call | bytes 4587784 | tf_op jit(solution)/shard_map/pallas_call | solution.py:189
  14.1 4.5 %collective-permute-start.2 = (bf16[16,4096]{1,0:T(8,128)(2,1)S(1)}, bf16[16,4096]{1,0:T(8,128)(2,1)S(1)}, u32[]{:S(2)}, u32[]{:S(2)}) collective-permute-start(bf16[16,4096]{1,0:T(8,128)(2,1)S(1)} %get-tuple-element.21), channel_id=1, source_target_pairs={{4,0},{8,4},{12,8},{16,12},{20,16},{24,20},{28,24},{0,28},{5,1},{9... | collective-permute-start | bytes 393224 | tf_op jit(solution)/shard_map/ppermute | solution.py:29
  18.7 1.3 %shard_map.181 = (bf16[16,4096]{1,0:T(8,128)(2,1)S(1)}, f32[32,8,128]{2,1,0:T(8,128)S(1)}) custom-call(s32[1,32]{1,0:T(1,128)S(1)} %copy-done.13, s32[1,32]{1,0:T(1,128)S(1)} %copy-done.14, s32[1,2]{1,0:T(1,128)S(1)} %copy-done.15, bf16[1,32,128,128]{3,2,1,0:T(8,128)(2,1)S(1)} %copy-done, bf16[1,32,128,128]{3,2,1,0:T(8,128)(2,1)S(1)} %copy-done.2, ...), custom_call_target="tpu_custom_call" | custom-call | bytes 2621704 | tf_op jit(solution)/shard_map/pallas_call | solution.py:189
  20.1 1.6 %collective-permute-start.4 = (bf16[10,16,1024]{2,1,0:T(8,128)(2,1)S(1)}, bf16[10,16,1024]{2,1,0:T(8,128)(2,1)S(1)}, u32[]{:S(2)}, u32[]{:S(2)}) collective-permute-start(bf16[10,16,1024]{2,1,0:T(8,128)(2,1)S(1)} %get-tuple-element.25), channel_id=1, source_target_pairs={{0,1},{1,0},{2,3},{3,2},{4,5},{5,4},{6,7},{7,6},{8,9},{9,8},{10,11... | collective-permute-start | bytes 983048 | tf_op jit(solution)/shard_map/ppermute | solution.py:229
  21.6 1.5 %collective-permute-start.5 = (bf16[10,16,1024]{2,1,0:T(8,128)(2,1)S(1)}, bf16[10,16,1024]{2,1,0:T(8,128)(2,1)S(1)}, u32[]{:S(2)}, u32[]{:S(2)}) collective-permute-start(bf16[10,16,1024]{2,1,0:T(8,128)(2,1)S(1)} %get-tuple-element.26), channel_id=1, source_target_pairs={{0,2},{1,3},{2,0},{3,1},{4,6},{5,7},{6,4},{7,5},{8,10},{9,11},{10,... | collective-permute-start | bytes 983048 | tf_op jit(solution)/shard_map/ppermute | solution.py:229
  23.6 1.9 %shard_map.184 = (bf16[16,4096]{1,0:T(8,128)(2,1)S(1)}, bf16[2,16,1024]{2,1,0:T(8,128)(2,1)S(1)}, bf16[2,16,1024]{2,1,0:T(8,128)(2,1)S(1)}, bf16[2,16,1024]{2,1,0:T(8,128)(2,1)S(1)}, bf16[2,16,1024]{2,1,0:T(8,128)(2,1)S(1)}) custom-call(s32[1,32]{1,0:T(1,128)S(1)} %copy-done.13, s32[1,32]{1,0:T(1,128)S(1)} %copy-done.14, ...), custom_call_target="tpu_custom_call" | custom-call | bytes 3014912 | tf_op jit(solution)/shard_map/pallas_call | solution.py:189
  25.5 1.6 %collective-permute-start.7 = (bf16[2,16,1024]{2,1,0:T(8,128)(2,1)S(1)}, bf16[2,16,1024]{2,1,0:T(8,128)(2,1)S(1)}, u32[]{:S(2)}, u32[]{:S(2)}) collective-permute-start(bf16[2,16,1024]{2,1,0:T(8,128)(2,1)S(1)} %get-tuple-element.29), channel_id=1, source_target_pairs={{0,1},{1,0},{2,3},{3,2},{4,5},{5,4},{6,7},{7,6},{8,9},{9,8},{10,11... | collective-permute-start | bytes 196616 | tf_op jit(solution)/shard_map/ppermute | solution.py:235
  27.1 1.5 %collective-permute-start.8 = (bf16[2,16,1024]{2,1,0:T(8,128)(2,1)S(1)}, bf16[2,16,1024]{2,1,0:T(8,128)(2,1)S(1)}, u32[]{:S(2)}, u32[]{:S(2)}) collective-permute-start(bf16[2,16,1024]{2,1,0:T(8,128)(2,1)S(1)} %get-tuple-element.30), channel_id=1, source_target_pairs={{0,2},{1,3},{2,0},{3,1},{4,6},{5,7},{6,4},{7,5},{8,10},{9,11},{10,... | collective-permute-start | bytes 196616 | tf_op jit(solution)/shard_map/ppermute | solution.py:235
  28.6 8.2 %collective-permute-done.7.refs_7_ = bf16[2,16,1024]{2,1,0:T(8,128)(2,1)S(1)} collective-permute-done((bf16[2,16,1024]{2,1,0:T(8,128)(2,1)S(1)}, bf16[2,16,1024]{2,1,0:T(8,128)(2,1)S(1)}, u32[]{:S(2)}, u32[]{:S(2)}) %collective-permute-start.7) | collective-permute-done | bytes 65568 | tf_op jit(solution)/shard_map/ppermute | solution.py:235
  36.8 2.5 %collective-permute-start.9 = (bf16[2,16,1024]{2,1,0:T(8,128)(2,1)S(1)}, bf16[2,16,1024]{2,1,0:T(8,128)(2,1)S(1)}, u32[]{:S(2)}, u32[]{:S(2)}) collective-permute-start(bf16[2,16,1024]{2,1,0:T(8,128)(2,1)S(1)} %get-tuple-element.31), channel_id=1, source_target_pairs={{0,3},{1,2},{2,1},{3,0},{4,7},{5,6},{6,5},{7,4},{8,11},{9,10},{10,... | collective-permute-start | bytes 196616 | tf_op jit(solution)/shard_map/ppermute | solution.py:235
  39.3 1.3 %shard_map.182 = bf16[16,4096]{1,0:T(8,128)(2,1)S(1)} custom-call(s32[1,32]{1,0:T(1,128)S(1)} %copy-done.13, s32[1,32]{1,0:T(1,128)S(1)} %copy-done.14, bf16[1,32,128,128]{3,2,1,0:T(8,128)(2,1)S(1)} %copy-done.1, bf16[1,32,128,128]{3,2,1,0:T(8,128)(2,1)S(1)} %copy-done.3, bf16[16,4096]{1,0:T(8,128)(2,1)S(1)} %collective-permute-done.refs_4_, ...), custom_call_target="tpu_custom_call" | custom-call | bytes 2490624 | tf_op jit(solution)/shard_map/pallas_call | solution.py:189
  40.7 1.3 %collective-permute-done.9.refs_9_ = bf16[2,16,1024]{2,1,0:T(8,128)(2,1)S(1)} collective-permute-done((bf16[2,16,1024]{2,1,0:T(8,128)(2,1)S(1)}, bf16[2,16,1024]{2,1,0:T(8,128)(2,1)S(1)}, u32[]{:S(2)}, u32[]{:S(2)}) %collective-permute-start.9) | collective-permute-done | bytes 65568 | tf_op jit(solution)/shard_map/ppermute | solution.py:235
  42.0 2.2 %collective-permute-start.3 = (bf16[16,4096]{1,0:T(8,128)(2,1)S(1)}, bf16[16,4096]{1,0:T(8,128)(2,1)S(1)}, u32[]{:S(2)}, u32[]{:S(2)}) collective-permute-start(bf16[16,4096]{1,0:T(8,128)(2,1)S(1)} %get-tuple-element.23), channel_id=1, source_target_pairs={{4,0},{8,4},{12,8},{16,12},{20,16},{24,20},{28,24},{0,28},{5,1},{9... | collective-permute-start | bytes 393224 | tf_op jit(solution)/shard_map/ppermute | solution.py:29
  44.2 3.2 %collective-permute-done.1.refs_0_ = bf16[16,4096]{1,0:T(8,128)(2,1)S(1)} collective-permute-done((bf16[16,4096]{1,0:T(8,128)(2,1)S(1)}, bf16[16,4096]{1,0:T(8,128)(2,1)S(1)}, u32[]{:S(2)}, u32[]{:S(2)}) %collective-permute-start.1) | collective-permute-done | bytes 131104 | tf_op jit(solution)/shard_map/ppermute | solution.py:29
  47.4 1.3 %shard_map.185 = (bf16[1,8,4096]{2,1,0:T(8,128)(2,1)}, bf16[1,8,4096]{2,1,0:T(8,128)(2,1)}, bf16[1,8,4096]{2,1,0:T(8,128)(2,1)}, bf16[1,8,4096]{2,1,0:T(8,128)(2...) custom-call(bf16[16,4096]{1,0:T(8,128)(2,1)S(1)} %collective-permute-done.1.refs_0_, ...), custom_call_target="tpu_custom_call" | custom-call | bytes 2621440 | tf_op jit(solution)/shard_map/pallas_call | solution.py:189
  (33 shorter events, 2.0 us)
Async XLA Ops:
  0.6 1.2 %copy-start = (bf16[1,32,128,128]{3,2,1,0:T(8,128)(2,1)S(1)}, bf16[1,32,128,128]{3,2,1,0:T(8,128)(2,1)}, u32[]{:S(2)}) copy-start(bf16[1,32,128,128]{3,2,1,0:T(8,128)(2,1)} %refs_2_.7) | copy-start | bytes 3145732
  1.9 1.2 %copy-start.2 = (bf16[1,32,128,128]{3,2,1,0:T(8,128)(2,1)S(1)}, bf16[1,32,128,128]{3,2,1,0:T(8,128)(2,1)}, u32[]{:S(2)}) copy-start(bf16[1,32,128,128]{3,2,1,0:T(8,128)(2,1)} %refs_3_.7) | copy-start | bytes 3145732
  3.1 0.9 %copy-start.4 = (bf16[1,2,8,4096]{3,2,1,0:T(8,128)(2,1)S(1)}, bf16[1,2,8,4096]{3,2,1,0:T(8,128)(2,1)}, u32[]{:S(2)}) copy-start(bf16[1,2,8,4096]{3,2,1,0:T(8,128)(2,1)} %refs_7_.3) | copy-start | bytes 393220
  4.0 0.9 %copy-start.5 = (bf16[1,2,8,4096]{3,2,1,0:T(8,128)(2,1)S(1)}, bf16[1,2,8,4096]{3,2,1,0:T(8,128)(2,1)}, u32[]{:S(2)}) copy-start(bf16[1,2,8,4096]{3,2,1,0:T(8,128)(2,1)} %refs_8_.1) | copy-start | bytes 393220
  4.9 0.9 %copy-start.6 = (bf16[1,2,8,4096]{3,2,1,0:T(8,128)(2,1)S(1)}, bf16[1,2,8,4096]{3,2,1,0:T(8,128)(2,1)}, u32[]{:S(2)}) copy-start(bf16[1,2,8,4096]{3,2,1,0:T(8,128)(2,1)} %refs_9_.1) | copy-start | bytes 393220
  5.8 0.9 %copy-start.7 = (bf16[1,2,8,4096]{3,2,1,0:T(8,128)(2,1)S(1)}, bf16[1,2,8,4096]{3,2,1,0:T(8,128)(2,1)}, u32[]{:S(2)}) copy-start(bf16[1,2,8,4096]{3,2,1,0:T(8,128)(2,1)} %refs_10_.1) | copy-start | bytes 393220
  6.7 0.8 %copy-start.9 = (bf16[1,8,4096]{2,1,0:T(8,128)(2,1)S(1)}, bf16[1,8,4096]{2,1,0:T(8,128)(2,1)}, u32[]{:S(2)}) copy-start(bf16[1,8,4096]{2,1,0:T(8,128)(2,1)} %refs_5_.3) | copy-start | bytes 196612
  7.5 0.8 %copy-start.10 = (bf16[1,8,4096]{2,1,0:T(8,128)(2,1)S(1)}, bf16[1,8,4096]{2,1,0:T(8,128)(2,1)}, u32[]{:S(2)}) copy-start(bf16[1,8,4096]{2,1,0:T(8,128)(2,1)} %refs_6_.3) | copy-start | bytes 196612
  8.4 0.7 %copy-start.13 = (s32[1,32]{1,0:T(1,128)S(1)}, s32[1,32]{1,0:T(1,128)}, u32[]{:S(2)}) copy-start(s32[1,32]{1,0:T(1,128)} %refs_0_.7) | copy-start | bytes 388
  10.4 8.3 %copy-start.8 = (bf16[1,2,8,4096]{3,2,1,0:T(8,128)(2,1)S(1)}, bf16[1,2,8,4096]{3,2,1,0:T(8,128)(2,1)}, u32[]{:S(2)}) copy-start(bf16[1,2,8,4096]{3,2,1,0:T(8,128)(2,1)} %refs_7_.2) | copy-start | bytes 393220
  10.4 8.3 %copy-start.11 = (bf16[1,8,4096]{2,1,0:T(8,128)(2,1)S(1)}, bf16[1,8,4096]{2,1,0:T(8,128)(2,1)}, u32[]{:S(2)}) copy-start(bf16[1,8,4096]{2,1,0:T(8,128)(2,1)} %refs_5_.2) | copy-start | bytes 196612
  10.4 8.3 %copy-start.12 = (bf16[1,8,4096]{2,1,0:T(8,128)(2,1)S(1)}, bf16[1,8,4096]{2,1,0:T(8,128)(2,1)}, u32[]{:S(2)}) copy-start(bf16[1,8,4096]{2,1,0:T(8,128)(2,1)} %refs_6_.2) | copy-start | bytes 196612
  14.1 9.5 %copy-start.1 = (bf16[1,32,128,128]{3,2,1,0:T(8,128)(2,1)S(1)}, bf16[1,32,128,128]{3,2,1,0:T(8,128)(2,1)}, u32[]{:S(2)}) copy-start(bf16[1,32,128,128]{3,2,1,0:T(8,128)(2,1)} %refs_2_.7) | copy-start | bytes 3145732
  14.1 9.5 %copy-start.3 = (bf16[1,32,128,128]{3,2,1,0:T(8,128)(2,1)S(1)}, bf16[1,32,128,128]{3,2,1,0:T(8,128)(2,1)}, u32[]{:S(2)}) copy-start(bf16[1,32,128,128]{3,2,1,0:T(8,128)(2,1)} %refs_3_.7) | copy-start | bytes 3145732
  14.1 9.5 %collective-permute-start.2 = (bf16[16,4096]{1,0:T(8,128)(2,1)S(1)}, bf16[16,4096]{1,0:T(8,128)(2,1)S(1)}, u32[]{:S(2)}, u32[]{:S(2)}) collective-permute-start(bf16[16,4096]{1,0:T(8,128)(2,1)S(1)} %get-tuple-element.21), channel_id=1, source_target_pairs={{4,0},{8,4},{12,8},{16,12},{20,16},{24,20},{28,24},{0,28},{5,1},{9... | collective-permute-start | bytes 393224 | tf_op jit(solution)/shard_map/ppermute | solution.py:29
  20.0 7.1 %collective-permute-start = (bf16[16,4096]{1,0:T(8,128)(2,1)S(1)}, bf16[16,4096]{1,0:T(8,128)(2,1)S(1)}, u32[]{:S(2)}, u32[]{:S(2)}) collective-permute-start(bf16[16,4096]{1,0:T(8,128)(2,1)S(1)} %get-tuple-element.19), channel_id=1, source_target_pairs={{28,0},{0,4},{4,8},{8,12},{12,16},{16,20},{20,24},{24,28},{29,1},{... | collective-permute-start | bytes 393224 | tf_op jit(solution)/shard_map/ppermute | solution.py:29
  20.1 27.3 %collective-permute-start.4 = (bf16[10,16,1024]{2,1,0:T(8,128)(2,1)S(1)}, bf16[10,16,1024]{2,1,0:T(8,128)(2,1)S(1)}, u32[]{:S(2)}, u32[]{:S(2)}) collective-permute-start(bf16[10,16,1024]{2,1,0:T(8,128)(2,1)S(1)} %get-tuple-element.25), channel_id=1, source_target_pairs={{0,1},{1,0},{2,3},{3,2},{4,5},{5,4},{6,7},{7,6},{8,9},{9,8},{10,11... | collective-permute-start | bytes 983048 | tf_op jit(solution)/shard_map/ppermute | solution.py:229
  21.6 25.8 %collective-permute-start.5 = (bf16[10,16,1024]{2,1,0:T(8,128)(2,1)S(1)}, bf16[10,16,1024]{2,1,0:T(8,128)(2,1)S(1)}, u32[]{:S(2)}, u32[]{:S(2)}) collective-permute-start(bf16[10,16,1024]{2,1,0:T(8,128)(2,1)S(1)} %get-tuple-element.26), channel_id=1, source_target_pairs={{0,2},{1,3},{2,0},{3,1},{4,6},{5,7},{6,4},{7,5},{8,10},{9,11},{10,... | collective-permute-start | bytes 983048 | tf_op jit(solution)/shard_map/ppermute | solution.py:229
  23.2 24.3 %collective-permute-start.6 = (bf16[10,16,1024]{2,1,0:T(8,128)(2,1)S(1)}, bf16[10,16,1024]{2,1,0:T(8,128)(2,1)S(1)}, u32[]{:S(2)}, u32[]{:S(2)}) collective-permute-start(bf16[10,16,1024]{2,1,0:T(8,128)(2,1)S(1)} %get-tuple-element.27), channel_id=1, source_target_pairs={{0,3},{1,2},{2,1},{3,0},{4,7},{5,6},{6,5},{7,4},{8,11},{9,10},{10,... | collective-permute-start | bytes 983048 | tf_op jit(solution)/shard_map/ppermute | solution.py:229
  25.5 11.3 %collective-permute-start.7 = (bf16[2,16,1024]{2,1,0:T(8,128)(2,1)S(1)}, bf16[2,16,1024]{2,1,0:T(8,128)(2,1)S(1)}, u32[]{:S(2)}, u32[]{:S(2)}) collective-permute-start(bf16[2,16,1024]{2,1,0:T(8,128)(2,1)S(1)} %get-tuple-element.29), channel_id=1, source_target_pairs={{0,1},{1,0},{2,3},{3,2},{4,5},{5,4},{6,7},{7,6},{8,9},{9,8},{10,11... | collective-permute-start | bytes 196616 | tf_op jit(solution)/shard_map/ppermute | solution.py:235
  27.1 13.5 %collective-permute-start.8 = (bf16[2,16,1024]{2,1,0:T(8,128)(2,1)S(1)}, bf16[2,16,1024]{2,1,0:T(8,128)(2,1)S(1)}, u32[]{:S(2)}, u32[]{:S(2)}) collective-permute-start(bf16[2,16,1024]{2,1,0:T(8,128)(2,1)S(1)} %get-tuple-element.30), channel_id=1, source_target_pairs={{0,2},{1,3},{2,0},{3,1},{4,6},{5,7},{6,4},{7,5},{8,10},{9,11},{10,... | collective-permute-start | bytes 196616 | tf_op jit(solution)/shard_map/ppermute | solution.py:235
  36.8 5.2 %collective-permute-start.9 = (bf16[2,16,1024]{2,1,0:T(8,128)(2,1)S(1)}, bf16[2,16,1024]{2,1,0:T(8,128)(2,1)S(1)}, u32[]{:S(2)}, u32[]{:S(2)}) collective-permute-start(bf16[2,16,1024]{2,1,0:T(8,128)(2,1)S(1)} %get-tuple-element.31), channel_id=1, source_target_pairs={{0,3},{1,2},{2,1},{3,0},{4,7},{5,6},{6,5},{7,4},{8,11},{9,10},{10,... | collective-permute-start | bytes 196616 | tf_op jit(solution)/shard_map/ppermute | solution.py:235
  40.6 6.8 %collective-permute-start.1 = (bf16[16,4096]{1,0:T(8,128)(2,1)S(1)}, bf16[16,4096]{1,0:T(8,128)(2,1)S(1)}, u32[]{:S(2)}, u32[]{:S(2)}) collective-permute-start(bf16[16,4096]{1,0:T(8,128)(2,1)S(1)} %shard_map.182), channel_id=1, source_target_pairs={{28,0},{0,4},{4,8},{8,12},{12,16},{16,20},{20,24},{24,28},{29,1},{... | collective-permute-start | bytes 393224 | tf_op jit(solution)/shard_map/ppermute | solution.py:29
  42.0 5.4 %collective-permute-start.3 = (bf16[16,4096]{1,0:T(8,128)(2,1)S(1)}, bf16[16,4096]{1,0:T(8,128)(2,1)S(1)}, u32[]{:S(2)}, u32[]{:S(2)}) collective-permute-start(bf16[16,4096]{1,0:T(8,128)(2,1)S(1)} %get-tuple-element.23), channel_id=1, source_target_pairs={{4,0},{8,4},{12,8},{16,12},{20,16},{24,20},{28,24},{0,28},{5,1},{9... | collective-permute-start | bytes 393224 | tf_op jit(solution)/shard_map/ppermute | solution.py:29
  (2 other events, 1.3 us)

commit v2 on v1

v2 whole, which is shorter than its diff:
```python
import jax
import jax.numpy as jnp
from jax import lax
from jax.experimental import pallas as pl
from jax.experimental.pallas import tpu as pltpu
from jax.sharding import PartitionSpec as P

BLOCK = 128
F32 = jnp.float32
BF16 = jnp.bfloat16
LIMIT = 40 * 1024 * 1024
WIDE = 60 * 1024 * 1024


def from_behind(block, axis, distance):
    devices = range(lax.axis_size(axis))
    route = [((i - distance) % len(devices), i) for i in devices]
    return lax.ppermute(block, axis, route)


def times(rows, weight):
    return lax.dot_general(rows, weight, (((1,), (0,)), ((), ())), preferred_element_type=F32)


def times_transposed(rows, weight):
    return lax.dot_general(rows, weight, (((1,), (1,)), ((), ())), preferred_element_type=F32)


def sigmoid(z):
    return 1.0 / (1.0 + jnp.exp(-z))


def slope_of(z, s):
    return s * (1.0 + z * (1.0 - s))


def lanes(block):
    if isinstance(block, int):
        return pl.ds(block * BLOCK, BLOCK)
    return pl.ds(pl.multiple_of(block * BLOCK, BLOCK), BLOCK)


def stack(parts):
    return jnp.concatenate([part.astype(F32) for part in parts], 0)


def start_all(copies):
    for copy in copies:
        copy.start()
    return copies


def wait_all(copies):
    for copy in copies:
        copy.wait()


def pack_ready(count, per, *refs):
    sources, send, held, packed, in_sems, out_sems = refs[:8], refs[8], refs[9:17], refs[17], refs[18], refs[19]
    wait_all(start_all([pltpu.make_async_copy(s, t, in_sems.at[k]) for k, (s, t) in enumerate(zip(sources, held))]))
    up_idx, order, g_ref, a_ref, back, second, second_tan, second_grad = held
    m0 = order[0, 0]
    m1 = order[0, 1]
    leaving = []
    for to in range(count):
        for place in range(per):
            j, here = to * per + place, lanes(place)
            at = lanes(up_idx[0, j])
            packed[to, 0, :, here] = stack([back[0, m0, :, at], second[0, m0, :, at]]).astype(BF16)
            packed[to, 1, :, here] = stack([second_tan[0, m0, :, at], second_tan[0, m1, :, at]]).astype(BF16)
            packed[to, 2, :, here] = stack([back[0, m1, :, at], second[0, m1, :, at]]).astype(BF16)
            at = lanes(j)
            packed[to, 3, :, here] = stack([g_ref[0, :, at], a_ref[0, :, at]]).astype(BF16)
            packed[to, 4, :, here] = stack([second_grad[0, m0, :, at], second_grad[0, m1, :, at]]).astype(BF16)
        leaving += start_all([pltpu.make_async_copy(packed.at[to], send.at[to], out_sems.at[to])])
    wait_all(leaving)


def first_tick(count, per, *refs):
    sources, (bwd, fwd, keep, keep_tan, send) = refs[:14], refs[14:19]
    held, (pulled, returned, hidden, hidden_fwd, sems) = refs[19:33], refs[33:]
    copies = start_all([pltpu.make_async_copy(s, t, sems.at[k]) for k, (s, t) in enumerate(zip(sources, held))])
    up_idx, down_idx, order, w_down, g_ref, a_ref, second_grad, w_up, back, second, second_tan, v_ref, t_ref, tan = held
    back_first(count, per, copies, up_idx, down_idx, order, w_up, w_down, g_ref, a_ref, back, second, second_tan,
               second_grad, bwd, keep, send, pulled, returned, hidden)
    wait_all(copies[11:])
    forward_first(count * per, up_idx, down_idx, order, w_up, w_down, v_ref, t_ref, tan, fwd, keep_tan, hidden_fwd)


def back_first(count, per, copies, up_idx, down_idx, order, w_up, w_down, g_ref, a_ref, back, second, second_tan, second_grad,
               pack, keep, send, pulled, returned, hidden):
    blocks = count * per
    for b in range(blocks):
        pulled[b] = jnp.zeros(pulled.shape[1:], F32)
    wait_all(copies[:7])
    m0 = order[0, 0]
    m1 = order[0, 1]
    for b in range(blocks):
        returned[b] = stack([g_ref[0, :, lanes(b)], a_ref[0, :, lanes(b)]])
    for i in range(blocks):
        at = lanes(i)
        c = stack([g_ref[0, :, at], a_ref[0, :, at], second_grad[0, m0, :, at], second_grad[0, m1, :, at]]).astype(BF16)
        target = down_idx[0, i]
        pulled[target] = pulled[target] + times_transposed(c, w_down[0, i])
    wait_all(copies[7:11])
    for j in range(blocks):
        to, here = j // per, lanes(j % per)
        u = up_idx[0, j]
        at = lanes(u)
        x = stack([back[0, m0, :, at], second[0, m0, :, at], second_tan[0, m0, :, at],
                   second_tan[0, m1, :, at], back[0, m1, :, at], second[0, m1, :, at]]).astype(BF16)
        z = times(x, w_up[0, j])
        zb0, za0, ta0, ta1, zb1, za1 = (z[8 * k:8 * k + 8] for k in range(6))
        pg, pa, ga0, ga1 = (pulled[j, 8 * k:8 * k + 8] for k in range(4))
        sb0, sa0, sb1, sa1 = sigmoid(zb0), sigmoid(za0), sigmoid(zb1), sigmoid(za1)
        slope_a0 = slope_of(za0, sa0)
        slope_a1 = slope_of(za1, sa1)
        curve_a0 = sa0 * (1.0 - sa0) * (2.0 + za0 * (1.0 - 2.0 * sa0))
        curve_a1 = sa1 * (1.0 - sa1) * (2.0 + za1 * (1.0 - 2.0 * sa1))
        push = slope_a0 * pa + curve_a0 * ga0 * ta0
        e = jnp.concatenate([slope_of(zb0, sb0) * pg, push], 0).astype(BF16)
        send[to, 0, :, here] = e
        send[to, 1, :, here] = jnp.concatenate([slope_a0 * ga0, slope_a1 * ga1], 0).astype(BF16)
        hidden[j] = jnp.concatenate(
            [zb0 * sb0, za0 * sa0, slope_a0 * ta0, slope_a1 * ta1, zb1 * sb1, za1 * sa1], 0).astype(BF16)
        keep[j] = jnp.concatenate([slope_of(zb1, sb1), slope_a1, curve_a1 * ga1 * ta1], 0)
        returned[u] = returned[u] + times_transposed(e, w_up[0, j])
    for b in range(blocks):
        pack[:, lanes(b)] = returned[b].astype(BF16)
    for i in range(blocks):
        y = hidden[down_idx[0, i]]
        for group in range(3):
            send[i // per, 2 + group, :, lanes(i % per)] = y[16 * group:16 * group + 16]


def forward_first(blocks, up_idx, down_idx, order, w_up, w_down, v_ref, t_ref, tan, pack, keep, hidden):
    m0 = order[0, 0]
    m1 = order[0, 1]
    for j in range(blocks):
        at = lanes(up_idx[0, j])
        x = stack([v_ref[0, :, at], t_ref[0, :, at], tan[0, m0, :, at], tan[0, m1, :, at]]).astype(BF16)
        z = times(x, w_up[0, j])
        zv, zt, z0, z1 = (z[8 * k:8 * k + 8] for k in range(4))
        hidden[j] = jnp.concatenate([zv * sigmoid(zv), slope_of(z0, sigmoid(z0)) * zt], 0).astype(BF16)
        keep[j] = slope_of(z1, sigmoid(z1))
    for i in range(blocks):
        at = lanes(i)
        moved = stack([v_ref[0, :, at], t_ref[0, :, at]]) + times(hidden[down_idx[0, i]], w_down[0, i])
        pack[:, at] = moved.astype(BF16)


def back_second(count, per, up_idx, down_idx, w_up, w_down, rows, keep, pack, send, pulled, returned):
    blocks = count * per
    for b in range(blocks):
        pulled[b] = jnp.zeros(pulled.shape[1:], F32)
        returned[b] = rows[:, lanes(b)].astype(F32)
    for i in range(blocks):
        c = rows[:, lanes(i)]
        send[i // per, 1, :, lanes(i % per)] = c
        target = down_idx[0, i]
        pulled[target] = pulled[target] + times_transposed(c, w_down[0, i])
    for j in range(blocks):
        u = up_idx[0, j]
        slope_b, slope_a, push = (keep[j, 8 * k:8 * k + 8] for k in range(3))
        e = jnp.concatenate([slope_b * pulled[j, 0:8], slope_a * pulled[j, 8:16] + push], 0).astype(BF16)
        send[j // per, 0, :, lanes(j % per)] = e
        returned[u] = returned[u] + times_transposed(e, w_up[0, j])
    for b in range(blocks):
        pack[:, lanes(b)] = returned[b].astype(BF16)


def forward_second(blocks, up_idx, down_idx, w_up, w_down, rows, keep, pack, hidden):
    for j in range(blocks):
        z = times(rows[:, lanes(up_idx[0, j])], w_up[0, j])
        zv, zt = z[0:8], z[8:16]
        hidden[j] = jnp.concatenate([zv * sigmoid(zv), keep[j] * zt], 0).astype(BF16)
    for i in range(blocks):
        at = lanes(i)
        pack[:, at] = (rows[:, at].astype(F32) + times(hidden[down_idx[0, i]], w_down[0, i])).astype(BF16)


def finish(count, per, scale, fwd, bwd, ready, early, late, values, score, tangent, adjoint, grad_up, grad_down):
    moved = fwd[...].astype(F32)
    values[0] = moved[0:8].astype(BF16)
    tangent[0] = moved[8:16].astype(BF16)
    moved = bwd[...].astype(F32)
    score[0] = moved[0:8].astype(BF16)
    adjoint[0] = moved[8:16].astype(BF16)
    sides = (
        (grad_up, ((ready, 0), (ready, 1), (ready, 2)), ((early, 0), (early, 1), (late, 0))),
        (grad_down, ((early, 2), (early, 3), (early, 4)), ((ready, 3), (ready, 4), (late, 1))),
    )
    for place in range(per):
        at = lanes(place)
        for out, left, right in sides:
            xs = [ref[source, k, :, at] for source in range(count) for ref, k in left]
            es = [ref[source, k, :, at] for source in range(count) for ref, k in right]
            total = lax.dot_general(jnp.concatenate(xs, 0), jnp.concatenate(es, 0), (((0,), (0,)), ((), ())),
                                    preferred_element_type=F32)
            out[0, place] = (total * scale).astype(BF16)


def call(body, operands, spaces, outs, scratch, limit=LIMIT, out_space=pltpu.VMEM, after=()):
    moved = sum(x.size * x.dtype.itemsize for x in list(operands) + list(outs))
    taken = len(operands)

    def kernel(*refs):
        body(*refs[:taken], *refs[taken + len(after):])

    return pl.pallas_call(
        kernel,
        out_shape=outs,
        in_specs=[pl.BlockSpec(memory_space=space) for space in spaces] + [pl.BlockSpec(memory_space=pl.ANY)] * len(after),
        out_specs=[pl.BlockSpec(memory_space=out_space)] * len(outs),
        scratch_shapes=scratch,
        compiler_params=pltpu.CompilerParams(vmem_limit_bytes=limit),
        cost_estimate=pl.CostEstimate(flops=0, bytes_accessed=moved, transcendentals=0),
    )(*operands, *after)


def to_replicas(parts):
    return lax.all_to_all(parts, "dp", 0, 0)


def on_device(w_up, up_index, w_down, down_index, tick_order, values_in, score_grad_in, tangent_in, state_adjoint_in,
              saved_back, saved_tan, saved_second, saved_second_tan, saved_second_grad):
    count = lax.axis_size("dp")
    blocks = w_up.shape[1]
    per = blocks // count
    width = values_in.shape[2]
    part = per * BLOCK
    scale = 1.0 / (values_in.shape[1] * count)
    shape = jax.ShapeDtypeStruct
    pair = shape((16, width), BF16)
    vmem, smem = pltpu.VMEM, pltpu.SMEM

    def body(f, *args):
        def kernel(*refs):
            f(*args, *refs)
        return kernel

    tables = (up_index, down_index, tick_order)
    weights = (w_up, w_down)

    def held(arrays, ints):
        return [smem(x.shape, x.dtype) for x in arrays[:ints]] + [vmem(x.shape, x.dtype) for x in arrays[ints:]]

    taken = (up_index, tick_order, score_grad_in, state_adjoint_in, saved_back, saved_second, saved_second_tan,
             saved_second_grad)
    ready_shape = shape((count, 5, 16, part), BF16)
    (ready,) = call(
        body(pack_ready, count, per), taken, [pl.ANY] * 8, [ready_shape],
        held(taken, 2) + [vmem(ready_shape.shape, BF16), pltpu.SemaphoreType.DMA((8,)), pltpu.SemaphoreType.DMA((count,))],
        limit=WIDE, out_space=pl.ANY)
    packed = ready
    ready = to_replicas(ready)
    taken = tables + (w_down, score_grad_in, state_adjoint_in, saved_second_grad, w_up, saved_back, saved_second,
                      saved_second_tan, values_in, tangent_in, saved_tan)
    bwd, fwd, keep, keep_tan, early = call(
        body(first_tick, count, per), taken, [pl.ANY] * 14,
        [pair, pair, shape((blocks, 24, BLOCK), F32), shape((blocks, 8, BLOCK), F32), ready_shape],
        held(taken, 3) + [vmem((blocks, 32, BLOCK), F32), vmem((blocks, 16, BLOCK), F32), vmem((blocks, 48, BLOCK), BF16),
                          vmem((blocks, 16, BLOCK), BF16), pltpu.SemaphoreType.DMA((14,))],
        limit=WIDE, after=(packed,))
    bwd = from_behind(bwd, "section", -1)
    fwd = from_behind(fwd, "section", 1)
    early = to_replicas(early)
    bwd, late = call(
        body(back_second, count, per),
        tables[:2] + weights + (bwd, keep), [smem] * 2 + [vmem] * 4,
        [pair, shape((count, 2, 16, part), BF16)],
        [pltpu.VMEM((blocks, 16, BLOCK), F32), pltpu.VMEM((blocks, 16, BLOCK), F32)])
    packed = bwd
    late = to_replicas(late)
    bwd = from_behind(bwd, "section", -1)
    (fwd,) = call(
        body(forward_second, blocks),
        tables[:2] + weights + (fwd, keep_tan), [smem] * 2 + [vmem] * 4,
        [pair], [pltpu.VMEM((blocks, 16, BLOCK), BF16)], after=(packed,))
    fwd = from_behind(fwd, "section", 1)
    stream = shape((1,) + values_in.shape[1:], BF16)
    grad = shape((1, per, BLOCK, BLOCK), BF16)
    return tuple(call(
        body(finish, count, per, scale), (fwd, bwd, ready, early, late), [vmem] * 5,
        [stream, stream, stream, stream, grad, grad], []))

def solution(mesh):
    layer = P("section", None, None, None)
    table = P("section", None)
    stream = P("section", "dp", None)
    saved = P("section", None, "dp", None)
    return jax.shard_map(
        on_device,
        mesh=mesh,
        in_specs=(layer, table, layer, table, table) + (stream,) * 4 + (saved,) * 5,
        out_specs=(stream,) * 4 + (P("section", "dp", None, None),) * 2,
        check_vma=False,
    )
```

time: 49.1 us -> 61.2 us (1.25)
  blocking collectives: 0 us -> 19.6 us
  local copies, waits for them, and re-layouts: 9.72 us -> 2.87 us
  starting transfers between devices: 15.9 us -> 11.7 us
  Pallas kernels: 9.58 us -> 13.2 us
    all_to_all x0 -> x2, blocking collectives: none -> 19.6 us  [to_replicas(): return lax.all_to_all(parts, 'dp', 0, 0)]
    ppermute x4, waiting for transfers between devices: 3.18 us -> 12.8 us  [from_behind(): return lax.ppermute(block, axis, route)]
    ppermute x6 -> x0, waiting for transfers between devices: 9.55 us -> none  [the longest x3 9.55 us: on_device(): lax.ppermute(late[step], 'dp', swap_route(step, count))]
    ppermute x6 -> x0, starting transfers between devices: 9.08 us -> none  [the longest x3 5.53 us: on_device(): lax.ppermute(late[step], 'dp', swap_route(step, count))]
    unnamed x32 -> x16, local copies, waits for them, and re-layouts: 9.72 us -> 2.87 us
    pallas_call x5, Pallas kernels: 9.58 us -> 13.2 us  [call(): pl.pallas_call(kernel, out_shape=outs, in_specs=[pl.BlockSpec(memory_spac...]
    all_to_all x0 -> x1, starting transfers between devices: none -> 3.48 us  [to_replicas(): return lax.all_to_all(parts, 'dp', 0, 0)]
    ppermute x4, starting transfers between devices: 6.86 us -> 8.18 us  [from_behind(): return lax.ppermute(block, axis, route)]
  transfers between devices with their start and end apart: 10 -> 5, of which waited for: 3 -> 3; matrix products, arithmetic and copies ran while one was open for 0% -> 0% of each run, Pallas kernels for 9% -> 2%
where the time goes in v2:
time: 61.2 us; the launch traced here: 60.8 us
  blocking collectives  19.6 us (32%)
  Pallas kernels  13.2 us (22%)
  waiting for transfers between devices  12.8 us (21%)
  starting transfers between devices  11.7 us (19%)
  local copies, waits for them, and re-layouts  2.87 us (5%)
  between operations  0.73 us (1%)
    all_to_all x2, blocking collectives, to_replicas(): return lax.all_to_all(parts, 'dp', 0, 0)  19.6 us
    pallas_call x5, Pallas kernels, call(): pl.pallas_call(kernel, out_shape=outs, in_specs=[pl.BlockSpec(memory_spac...  13.2 us
    ppermute x4, waiting for transfers between devices, from_behind(): return lax.ppermute(block, axis, route)  12.8 us
    ppermute x4, starting transfers between devices, from_behind(): return lax.ppermute(block, axis, route)  8.18 us
    all_to_all x1, starting transfers between devices, to_replicas(): return lax.all_to_all(parts, 'dp', 0, 0)  3.48 us
    unnamed x16, local copies, waits for them, and re-layouts  2.87 us
  transfers between devices with their start and end apart: 5, of which 3 were waited for; matrix products, arithmetic and copies ran while one was open for 0% of the time, Pallas kernels for 2%

profile of v2, /device:TPU:0, one launch (start us, length us, event | category | flops | bytes accessed | tf_op | source)
XLA Modules:
  0.0 60.8 jit_solution(7102652066966981103)
XLA Ops:
  0.6 2.2 %shard_map.181.refs_14_ = bf16[4,5,16,1024]{3,2,1,0:T(8,128)(2,1)} custom-call(s32[1,32]{1,0:T(1,128)} %refs_0_.7, s32[1,2]{1,0:T(1,128)} %refs_2_.5, bf16[1,8,4096]{2,1,0:T(8,128)(2,1)} %refs_4_.3, bf16[1,8,4096]{2,1,0:T(8,128)(2,1)} %refs_5_.3, bf16[1,2,8,4096]{3,2,1,0:T(8,128)(2,1)} %refs_8_.1, bf16[1,2,8,4096]{3,2,1,0:T(8,128)(2,1)} %refs_9_.1, ...), custom_call_target="tpu_custom_call" | custom-call | bytes 1310856 | tf_op jit(solution)/shard_map/pallas_call | solution.py:210
  2.8 0.0 copy-start
  2.8 0.0 copy-start.1
  2.8 6.6 %shard_map.182 = (bf16[16,4096]{1,0:T(8,128)(2,1)}, bf16[16,4096]{1,0:T(8,128)(2,1)}, f32[32,24,128]{2,1,0:T(8,128)}, f32[32,8,128]{2,1,0:T(8,128)}, bf16[4,5,16,1024]{3,2,1,0:T(8,128)(2,1)}) custom-call(s32[1,32]{1,0:T(1,128)} %refs_0_.7, s32[1,32]{1,0:T(1,128)} %refs_1_.7, s32[1,2]{1,0:T(1,128)} %refs_2_.5, bf16[1,32,128,128]{3,2,1,0:T(8,128)(2,1)} %refs_3_.7, ...), custom_call_target="tpu_custom_call" | custom-call | bytes 4456712 | tf_op jit(solution)/shard_map/pallas_call | solution.py:210
  9.4 0.0 copy-start.5
  9.4 0.0 copy-start.6
  9.4 4.5 %collective-permute-start.1 = (bf16[16,4096]{1,0:T(8,128)(2,1)}, bf16[16,4096]{1,0:T(8,128)(2,1)S(1)}, u32[]{:S(2)}, u32[]{:S(2)}) collective-permute-start(bf16[16,4096]{1,0:T(8,128)(2,1)} %get-tuple-element.15), channel_id=1, source_target_pairs={{4,0},{8,4},{12,8},{16,12},{20,16},{24,20},{28,24},{0,28},{5,1},{9... | collective-permute-start | bytes 393224 | tf_op jit(solution)/shard_map/ppermute | solution.py:18
  14.0 2.8 %collective-permute-done.1.refs_4_ = bf16[16,4096]{1,0:T(8,128)(2,1)S(1)} collective-permute-done((bf16[16,4096]{1,0:T(8,128)(2,1)}, bf16[16,4096]{1,0:T(8,128)(2,1)S(1)}, u32[]{:S(2)}, u32[]{:S(2)}) %collective-permute-start.1) | collective-permute-done | bytes 131104 | tf_op jit(solution)/shard_map/ppermute | solution.py:18
  16.8 1.0 %copy-done.3 = f32[32,24,128]{2,1,0:T(8,128)S(1)} copy-done((f32[32,24,128]{2,1,0:T(8,128)S(1)}, f32[32,24,128]{2,1,0:T(8,128)}, u32[]{:S(2)}) %copy-start.3) | copy-done | bytes 393240
  17.8 1.9 %shard_map.183 = (bf16[16,4096]{1,0:T(8,128)(2,1)S(1)}, bf16[4,2,16,1024]{3,2,1,0:T(8,128)(2,1)S(1)}) custom-call(s32[1,32]{1,0:T(1,128)S(1)} %copy-done.5, s32[1,32]{1,0:T(1,128)S(1)} %copy-done.6, bf16[1,32,128,128]{3,2,1,0:T(8,128)(2,1)S(1)} %copy-done, bf16[1,32,128,128]{3,2,1,0:T(8,128)(2,1)S(1)} %copy-done.1, ...), custom_call_target="tpu_custom_call" | custom-call | bytes 3014912 | tf_op jit(solution)/shard_map/pallas_call | solution.py:210
  19.7 9.3 %all_to_all.15.refs_4_ = bf16[4,2,16,1024]{3,2,1,0:T(8,128)(2,1)} all-to-all(bf16[4,2,16,1024]{3,2,1,0:T(8,128)(2,1)S(1)} %get-tuple-element.19), channel_id=1, replica_groups=mesh['section'=8,'dp'=4] {'dp'}, dimensions={0} | all-to-all | bytes 524288 | tf_op jit(solution)/shard_map/all_to_all | solution.py:222
  29.0 10.2 %all_to_all.16.refs_3_ = bf16[4,5,16,1024]{3,2,1,0:T(8,128)(2,1)S(1)} all-to-all(bf16[4,5,16,1024]{3,2,1,0:T(8,128)(2,1)S(1)} %copy-done.7), channel_id=1, replica_groups=mesh['section'=8,'dp'=4] {'dp'}, dimensions={0} | all-to-all | bytes 1310720 | tf_op jit(solution)/shard_map/all_to_all | solution.py:222
  39.3 3.5 %all-to-all-start = ((bf16[4,5,16,1024]{3,2,1,0:T(8,128)(2,1)}), bf16[4,5,16,1024]{3,2,1,0:T(8,128)(2,1)S(1)}, u32[]{:S(2)}, u32[]{:S(2)}) async-start(bf16[4,5,16,1024]{3,2,1,0:T(8,128)(2,1)} %shard_map.181.refs_14_), calls=%async_computation | async-start | bytes 1310720 | tf_op jit(solution)/shard_map/all_to_all | solution.py:222
  42.7 0.1 collective-permute-start
  42.8 6.4 %collective-permute-done.refs_4_ = bf16[16,4096]{1,0:T(8,128)(2,1)S(1)} collective-permute-done((bf16[16,4096]{1,0:T(8,128)(2,1)}, bf16[16,4096]{1,0:T(8,128)(2,1)S(1)}, u32[]{:S(2)}, u32[]{:S(2)}) %collective-permute-start) | collective-permute-done | bytes 131104 | tf_op jit(solution)/shard_map/ppermute | solution.py:18
  49.2 0.9 %copy-done.4 = f32[32,8,128]{2,1,0:T(8,128)S(1)} copy-done((f32[32,8,128]{2,1,0:T(8,128)S(1)}, f32[32,8,128]{2,1,0:T(8,128)}, u32[]{:S(2)}) %copy-start.4) | copy-done | bytes 131096
  50.1 1.3 %shard_map.184 = bf16[16,4096]{1,0:T(8,128)(2,1)S(1)} custom-call(s32[1,32]{1,0:T(1,128)S(1)} %copy-done.5, s32[1,32]{1,0:T(1,128)S(1)} %copy-done.6, bf16[1,32,128,128]{3,2,1,0:T(8,128)(2,1)S(1)} %copy-done, bf16[1,32,128,128]{3,2,1,0:T(8,128)(2,1)S(1)} %copy-done.1, bf16[16,4096]{1,0:T(8,128)(2,1)S(1)} %collective-permute-done.refs_4_, ...), custom_call_target="tpu_custom_call" | custom-call | bytes 2490624 | tf_op jit(solution)/shard_map/pallas_call | solution.py:210
  51.4 0.1 collective-permute-start.2
  51.5 3.5 %collective-permute-start.3 = (bf16[16,4096]{1,0:T(8,128)(2,1)S(1)}, bf16[16,4096]{1,0:T(8,128)(2,1)S(1)}, u32[]{:S(2)}, u32[]{:S(2)}) collective-permute-start(bf16[16,4096]{1,0:T(8,128)(2,1)S(1)} %get-tuple-element.17.refs_6_), channel_id=1, source_target_pairs={{4,0},{8,4},{12,8},{16,12},{20,16},{24,20},{28,24},{0,28},{5,1},{9... | collective-permute-start | bytes 393224 | tf_op jit(solution)/shard_map/ppermute | solution.py:18
  55.0 3.6 %collective-permute-done.2.refs_0_ = bf16[16,4096]{1,0:T(8,128)(2,1)S(1)} collective-permute-done((bf16[16,4096]{1,0:T(8,128)(2,1)S(1)}, bf16[16,4096]{1,0:T(8,128)(2,1)S(1)}, u32[]{:S(2)}, u32[]{:S(2)}) %collective-permute-start.2) | collective-permute-done | bytes 131104 | tf_op jit(solution)/shard_map/ppermute | solution.py:18
  58.6 0.0 collective-permute-done.3.refs_1_
  58.6 0.0 all-to-all-done.refs_2_
  58.6 0.9 %copy-done.2 = bf16[4,2,16,1024]{3,2,1,0:T(8,128)(2,1)S(1)} copy-done((bf16[4,2,16,1024]{3,2,1,0:T(8,128)(2,1)S(1)}, bf16[4,2,16,1024]{3,2,1,0:T(8,128)(2,1)}, u32[]{:S(2)}) %copy-start.2) | copy-done | bytes 262168
  59.5 1.3 %shard_map.185 = (bf16[1,8,4096]{2,1,0:T(8,128)(2,1)}, bf16[1,8,4096]{2,1,0:T(8,128)(2,1)}, bf16[1,8,4096]{2,1,0:T(8,128)(2,1)}, bf16[1,8,4096]{2,1,0:T(8,128)(2...) custom-call(bf16[16,4096]{1,0:T(8,128)(2,1)S(1)} %collective-permute-done.2.refs_0_, ...), custom_call_target="tpu_custom_call" | custom-call | bytes 2621440 | tf_op jit(solution)/shard_map/pallas_call | solution.py:210
  (9 shorter events, 0.0 us)
Async XLA Ops:
  2.8 14.0 %copy-start = (bf16[1,32,128,128]{3,2,1,0:T(8,128)(2,1)S(1)}, bf16[1,32,128,128]{3,2,1,0:T(8,128)(2,1)}, u32[]{:S(2)}) copy-start(bf16[1,32,128,128]{3,2,1,0:T(8,128)(2,1)} %refs_2_.7) | copy-start | bytes 3145732
  2.8 14.0 %copy-start.1 = (bf16[1,32,128,128]{3,2,1,0:T(8,128)(2,1)S(1)}, bf16[1,32,128,128]{3,2,1,0:T(8,128)(2,1)}, u32[]{:S(2)}) copy-start(bf16[1,32,128,128]{3,2,1,0:T(8,128)(2,1)} %refs_3_.7) | copy-start | bytes 3145732
  9.4 7.4 %copy-start.5 = (s32[1,32]{1,0:T(1,128)S(1)}, s32[1,32]{1,0:T(1,128)}, u32[]{:S(2)}) copy-start(s32[1,32]{1,0:T(1,128)} %refs_0_.7) | copy-start | bytes 388
  9.4 7.4 %copy-start.6 = (s32[1,32]{1,0:T(1,128)S(1)}, s32[1,32]{1,0:T(1,128)}, u32[]{:S(2)}) copy-start(s32[1,32]{1,0:T(1,128)} %refs_1_.7) | copy-start | bytes 388
  9.4 7.4 %collective-permute-start.1 = (bf16[16,4096]{1,0:T(8,128)(2,1)}, bf16[16,4096]{1,0:T(8,128)(2,1)S(1)}, u32[]{:S(2)}, u32[]{:S(2)}) collective-permute-start(bf16[16,4096]{1,0:T(8,128)(2,1)} %get-tuple-element.15), channel_id=1, source_target_pairs={{4,0},{8,4},{12,8},{16,12},{20,16},{24,20},{28,24},{0,28},{5,1},{9... | collective-permute-start | bytes 393224 | tf_op jit(solution)/shard_map/ppermute | solution.py:18
  16.8 1.0 %copy-start.3 = (f32[32,24,128]{2,1,0:T(8,128)S(1)}, f32[32,24,128]{2,1,0:T(8,128)}, u32[]{:S(2)}) copy-start(f32[32,24,128]{2,1,0:T(8,128)} %get-tuple-element.16.refs_5_) | copy-start | bytes 1179652
  17.8 11.2 %copy-start.7 = (bf16[4,5,16,1024]{3,2,1,0:T(8,128)(2,1)S(1)}, bf16[4,5,16,1024]{3,2,1,0:T(8,128)(2,1)}, u32[]{:S(2)}) copy-start(bf16[4,5,16,1024]{3,2,1,0:T(8,128)(2,1)} %get-tuple-element.18) | copy-start | bytes 1966084
  39.3 19.3 %all-to-all-start = ((bf16[4,5,16,1024]{3,2,1,0:T(8,128)(2,1)}), bf16[4,5,16,1024]{3,2,1,0:T(8,128)(2,1)S(1)}, u32[]{:S(2)}, u32[]{:S(2)}) async-start(bf16[4,5,16,1024]{3,2,1,0:T(8,128)(2,1)} %shard_map.181.refs_14_), calls=%async_computation | async-start | bytes 1310720 | tf_op jit(solution)/shard_map/all_to_all | solution.py:222
  42.7 6.5 %collective-permute-start = (bf16[16,4096]{1,0:T(8,128)(2,1)}, bf16[16,4096]{1,0:T(8,128)(2,1)S(1)}, u32[]{:S(2)}, u32[]{:S(2)}) collective-permute-start(bf16[16,4096]{1,0:T(8,128)(2,1)} %get-tuple-element.13), channel_id=1, source_target_pairs={{28,0},{0,4},{4,8},{8,12},{12,16},{16,20},{20,24},{24,28},{29,1},{... | collective-permute-start | bytes 393224 | tf_op jit(solution)/shard_map/ppermute | solution.py:18
  49.2 0.9 %copy-start.4 = (f32[32,8,128]{2,1,0:T(8,128)S(1)}, f32[32,8,128]{2,1,0:T(8,128)}, u32[]{:S(2)}) copy-start(f32[32,8,128]{2,1,0:T(8,128)} %get-tuple-element.14.refs_5_) | copy-start | bytes 393220
  51.4 7.1 %collective-permute-start.2 = (bf16[16,4096]{1,0:T(8,128)(2,1)S(1)}, bf16[16,4096]{1,0:T(8,128)(2,1)S(1)}, u32[]{:S(2)}, u32[]{:S(2)}) collective-permute-start(bf16[16,4096]{1,0:T(8,128)(2,1)S(1)} %shard_map.184), channel_id=1, source_target_pairs={{28,0},{0,4},{4,8},{8,12},{12,16},{16,20},{20,24},{24,28},{29,1},{... | collective-permute-start | bytes 393224 | tf_op jit(solution)/shard_map/ppermute | solution.py:18
  51.5 7.1 %collective-permute-start.3 = (bf16[16,4096]{1,0:T(8,128)(2,1)S(1)}, bf16[16,4096]{1,0:T(8,128)(2,1)S(1)}, u32[]{:S(2)}, u32[]{:S(2)}) collective-permute-start(bf16[16,4096]{1,0:T(8,128)(2,1)S(1)} %get-tuple-element.17.refs_6_), channel_id=1, source_target_pairs={{4,0},{8,4},{12,8},{16,12},{20,16},{24,20},{28,24},{0,28},{5,1},{9... | collective-permute-start | bytes 393224 | tf_op jit(solution)/shard_map/ppermute | solution.py:18
  58.6 1.0 %copy-start.2 = (bf16[4,2,16,1024]{3,2,1,0:T(8,128)(2,1)S(1)}, bf16[4,2,16,1024]{3,2,1,0:T(8,128)(2,1)}, u32[]{:S(2)}) copy-start(bf16[4,2,16,1024]{3,2,1,0:T(8,128)(2,1)} %all_to_all.15.refs_4_) | copy-start | bytes 786436

commit v3 on v1

--- a/solution.py
+++ b/solution.py
@@ -9,6 +9,7 @@
 F32 = jnp.float32
 BF16 = jnp.bfloat16
 LIMIT = 40 * 1024 * 1024
+WIDE = 60 * 1024 * 1024
 
 
 def partner(me, step, count):
@@ -23,10 +24,11 @@
     return [(i, (i + step) % count) for i in range(count)]
 
 
-def from_behind(block, axis, distance):
-    devices = range(lax.axis_size(axis))
-    route = [((i - distance) % len(devices), i) for i in devices]
-    return lax.ppermute(block, axis, route)
+def swap_sections(near, far):
+    count = lax.axis_size("section")
+    far = lax.ppermute(far, "section", [(i, (i + 2 * (i % 2) - 1) % count) for i in range(count)])
+    near = lax.ppermute(near, "section", [(i, i ^ 1) for i in range(count)])
+    return near, far
 
 
 def times(rows, weight):
@@ -62,15 +64,43 @@
             yield step, place, base + place
 
 
-def back_first(count, per, blocks, up_idx, down_idx, order, w_up, w_down, g_ref, a_ref, back, second, second_tan,
-               second_grad, pack, keep, *rest):
-    sends = rest[:count]
-    pulled, returned, hidden = rest[count:]
+def start_all(copies):
+    for copy in copies:
+        copy.start()
+    return copies
+
+
+def wait_all(copies):
+    for copy in copies:
+        copy.wait()
+
+
+def odd_section():
+    return lax.rem(lax.axis_index("section"), 2)
+
+
+def hand_out(packs, near, far):
+    odd = odd_section()
+    near[...] = packs[odd]
+    far[...] = packs[1 - odd]
+
+
+def take_in(near, far, packs):
+    odd = odd_section()
+    packs[1 - odd] = near[...]
+    packs[odd] = far[...]
+
+
+def back_first(count, per, copies, up_idx, down_idx, order, w_up, w_down, g_ref, a_ref, back, second, second_tan,
+               second_grad, pack, keep, sends, pulled, returned, hidden):
+    blocks = count * per
     me = lax.axis_index("dp")
+    for b in range(blocks):
+        pulled[b] = jnp.zeros(pulled.shape[1:], F32)
+    wait_all(copies[:7])
     m0 = order[0, 0]
     m1 = order[0, 1]
     for b in range(blocks):
-        pulled[b] = jnp.zeros(pulled.shape[1:], F32)
         returned[b] = stack([g_ref[0, :, lanes(b)], a_ref[0, :, lanes(b)]])
     for step, place, i in send_order(me, count, per):
         at = lanes(i)
@@ -79,6 +109,7 @@
         sends[step][9, :, lanes(place)] = c[16:32]
         target = down_idx[0, i]
         pulled[target] = pulled[target] + times_transposed(c, w_down[0, i])
+    wait_all(copies[7:11])
     for step, place, j in send_order(me, count, per):
         u = up_idx[0, j]
         at = lanes(u)
@@ -128,9 +159,21 @@
         pack[:, at] = moved.astype(BF16)
 
 
-def back_second(count, per, blocks, up_idx, down_idx, w_up, w_down, rows, keep, pack, *rest):
-    sends = rest[:count]
-    pulled, returned = rest[count:]
+def first_tick(count, per, *refs):
+    sources, (near, far, keep, keep_tan) = refs[:14], refs[14:18]
+    sends, held = refs[18:18 + count], refs[18 + count:32 + count]
+    packs, pulled, returned, hidden, hidden_fwd, sems = refs[32 + count:]
+    copies = start_all([pltpu.make_async_copy(s, t, sems.at[k]) for k, (s, t) in enumerate(zip(sources, held))])
+    up_idx, down_idx, order, w_down, g_ref, a_ref, second_grad, w_up, back, second, second_tan, v_ref, t_ref, tan = held
+    back_first(count, per, copies, up_idx, down_idx, order, w_up, w_down, g_ref, a_ref, back, second, second_tan,
+               second_grad, packs.at[1], keep, sends, pulled, returned, hidden)
+    wait_all(copies[11:])
+    forward_first(count * per, up_idx, down_idx, order, w_up, w_down, v_ref, t_ref, tan, packs.at[0], keep_tan, hidden_fwd)
+    hand_out(packs, near, far)
+
+
+def back_second(count, per, up_idx, down_idx, w_up, w_down, rows, keep, pack, sends, pulled, returned):
+    blocks = count * per
     me = lax.axis_index("dp")
     for b in range(blocks):
         pulled[b] = jnp.zeros(pulled.shape[1:], F32)
@@ -160,14 +203,23 @@
         pack[:, at] = (rows[:, at].astype(F32) + times(hidden[down_idx[0, i]], w_down[0, i])).astype(BF16)
 
 
-def finish(count, per, scale, fwd, bwd, *rest):
+def second_tick(count, per, up_idx, down_idx, w_up, w_down, near_in, far_in, keep, keep_tan, near, far, *refs):
+    sends, (came, packs, pulled, returned, hidden) = refs[:count], refs[count:]
+    take_in(near_in, far_in, came)
+    back_second(count, per, up_idx, down_idx, w_up, w_down, came.at[1], keep, packs.at[1], sends, pulled, returned)
+    forward_second(count * per, up_idx, down_idx, w_up, w_down, came.at[0], keep_tan, packs.at[0], hidden)
+    hand_out(packs, near, far)
+
+
+def finish(count, per, scale, near, far, *rest):
     early = rest[:count]
     late = rest[count:2 * count]
-    values, score, tangent, adjoint, grad_up, grad_down = rest[2 * count:]
-    moved = fwd[...].astype(F32)
+    values, score, tangent, adjoint, grad_up, grad_down, came = rest[2 * count:]
+    take_in(near, far, came)
+    moved = came[0].astype(F32)
     values[0] = moved[0:8].astype(BF16)
     tangent[0] = moved[8:16].astype(BF16)
-    moved = bwd[...].astype(F32)
+    moved = came[1].astype(F32)
     score[0] = moved[0:8].astype(BF16)
     adjoint[0] = moved[8:16].astype(BF16)
     for place in range(per):
@@ -182,19 +234,22 @@
             out[0, place] = (total * scale).astype(BF16)
 
 
-def call(body, operands, smem, outs, scratch, flops=0):
-    specs = [pl.BlockSpec(memory_space=pltpu.SMEM)] * smem
-    specs += [pl.BlockSpec(memory_space=pltpu.VMEM)] * (len(operands) - smem)
+def call(body, operands, spaces, outs, scratch, limit=LIMIT, out_space=pltpu.VMEM, after=()):
     moved = sum(x.size * x.dtype.itemsize for x in list(operands) + list(outs))
+    taken = len(operands)
+
+    def kernel(*refs):
+        body(*refs[:taken], *refs[taken + len(after):])
+
     return pl.pallas_call(
-        body,
+        kernel,
         out_shape=outs,
-        in_specs=specs,
-        out_specs=[pl.BlockSpec(memory_space=pltpu.VMEM)] * len(outs),
+        in_specs=[pl.BlockSpec(memory_space=space) for space in spaces] + [pl.BlockSpec(memory_space=pl.ANY)] * len(after),
+        out_specs=[pl.BlockSpec(memory_space=out_space)] * len(outs),
         scratch_shapes=scratch,
-        compiler_params=pltpu.CompilerParams(vmem_limit_bytes=LIMIT),
-        cost_estimate=pl.CostEstimate(flops=flops, bytes_accessed=moved, transcendentals=0),
-    )(*operands)
+        compiler_params=pltpu.CompilerParams(vmem_limit_bytes=limit),
+        cost_estimate=pl.CostEstimate(flops=0, bytes_accessed=moved, transcendentals=0),
+    )(*operands, *after)
 
 
 def on_device(w_up, up_index, w_down, down_index, tick_order, values_in, score_grad_in, tangent_in, state_adjoint_in,
@@ -207,43 +262,41 @@
     scale = 1.0 / (values_in.shape[1] * count)
     shape = jax.ShapeDtypeStruct
     pair = shape((16, width), BF16)
+    vmem, smem = pltpu.VMEM, pltpu.SMEM
 
     def body(f, *args):
         def kernel(*refs):
             f(*args, *refs)
         return kernel
 
-    bwd, keep, *early = call(
-        body(back_first, count, per, blocks),
-        (up_index, down_index, tick_order, w_up, w_down, score_grad_in, state_adjoint_in, saved_back, saved_second,
-         saved_second_tan, saved_second_grad), 3,
-        [pair, shape((blocks, 24, BLOCK), F32)] + [shape((10, 16, part), BF16)] * count,
-        [pltpu.VMEM((blocks, 32, BLOCK), F32), pltpu.VMEM((blocks, 16, BLOCK), F32), pltpu.VMEM((blocks, 48, BLOCK), BF16)])
-    bwd = from_behind(bwd, "section", -1)
-    fwd, keep_tan = call(
-        body(forward_first, blocks),
-        (up_index, down_index, tick_order, w_up, w_down, values_in, tangent_in, saved_tan), 3,
-        [pair, shape((blocks, 8, BLOCK), F32)],
-        [pltpu.VMEM((blocks, 16, BLOCK), BF16)])
-    fwd = from_behind(fwd, "section", 1)
-    early = early[:1] + [lax.ppermute(early[step], "dp", swap_route(step, count)) for step in range(1, count)]
-    bwd, *late = call(
-        body(back_second, count, per, blocks),
-        (up_index, down_index, w_up, w_down, bwd, keep), 2,
-        [pair] + [shape((2, 16, part), BF16)] * count,
-        [pltpu.VMEM((blocks, 16, BLOCK), F32), pltpu.VMEM((blocks, 16, BLOCK), F32)])
-    late = late[:1] + [lax.ppermute(late[step], "dp", swap_route(step, count)) for step in range(1, count)]
-    bwd = from_behind(bwd, "section", -1)
-    (fwd,) = call(
-        body(forward_second, blocks),
-        (up_index, down_index, w_up, w_down, fwd, keep_tan), 2,
-        [pair], [pltpu.VMEM((blocks, 16, BLOCK), BF16)])
-    fwd = from_behind(fwd, "section", 1)
+    def to_replicas(parts):
+        return parts[:1] + [lax.ppermute(parts[step], "dp", swap_route(step, count)) for step in range(1, count)]
+
+    taken = (up_index, down_index, tick_order, w_down, score_grad_in, state_adjoint_in, saved_second_grad, w_up,
+             saved_back, saved_second, saved_second_tan, values_in, tangent_in, saved_tan)
+    near, far, keep, keep_tan, *early = call(
+        body(first_tick, count, per), taken, [pl.ANY] * 14,
+        [pair, pair, shape((blocks, 24, BLOCK), F32), shape((blocks, 8, BLOCK), F32)]
+        + [shape((10, 16, part), BF16)] * count,
+        [smem(x.shape, x.dtype) for x in taken[:3]] + [vmem(x.shape, x.dtype) for x in taken[3:]]
+        + [vmem((2, 16, width), BF16), vmem((blocks, 32, BLOCK), F32), vmem((blocks, 16, BLOCK), F32),
+           vmem((blocks, 48, BLOCK), BF16), vmem((blocks, 16, BLOCK), BF16), pltpu.SemaphoreType.DMA((14,))],
+        limit=WIDE)
+    near, far = swap_sections(near, far)
+    early = to_replicas(early)
+    near, far, *late = call(
+        body(second_tick, count, per), (up_index, down_index, w_up, w_down, near, far, keep, keep_tan),
+        [smem] * 2 + [vmem] * 6,
+        [pair, pair] + [shape((2, 16, part), BF16)] * count,
+        [vmem((2, 16, width), BF16), vmem((2, 16, width), BF16), vmem((blocks, 16, BLOCK), F32),
+         vmem((blocks, 16, BLOCK), F32), vmem((blocks, 16, BLOCK), BF16)])
+    near, far = swap_sections(near, far)
+    late = to_replicas(late)
     stream = shape((1,) + values_in.shape[1:], BF16)
     grad = shape((1, per, BLOCK, BLOCK), BF16)
     return tuple(call(
-        body(finish, count, per, scale), (fwd, bwd, *early, *late), 0,
-        [stream, stream, stream, stream, grad, grad], []))
+        body(finish, count, per, scale), (near, far, *early, *late), [vmem] * (2 + 2 * count),
+        [stream, stream, stream, stream, grad, grad], [vmem((2, 16, width), BF16)]))
 
 
 def solution(mesh):

time: 49.1 us -> 42.9 us (0.87)
  local copies, waits for them, and re-layouts: 9.72 us -> 2.57 us
  waiting for transfers between devices: 12.7 us -> 14.4 us
  starting transfers between devices: 15.9 us -> 14.4 us
  Pallas kernels: 9.58 us -> 10.7 us
    unnamed x32 -> x14, local copies, waits for them, and re-layouts: 9.72 us -> 2.57 us
    ppermute x10, waiting for transfers between devices: 12.7 us -> 14.4 us  [the longest x2 7.23 us: swap_sections(): lax.ppermute(far, 'section', [(i, (i + 2 * (i % 2) - 1) % count) for i in...]
    ppermute x10, starting transfers between devices: 15.9 us -> 14.4 us  [the longest x6 9.18 us: to_replicas(): lax.ppermute(parts[step], 'dp', swap_route(step, count))]
    pallas_call x5 -> x3, Pallas kernels: 9.58 us -> 10.7 us  [call(): pl.pallas_call(kernel, out_shape=outs, in_specs=[pl.BlockSpec(memory_spac...]
  transfers between devices with their start and end apart: 10 -> 10, of which waited for: 3 -> 4; matrix products, arithmetic and copies ran while one was open for 0% -> 0% of each run, Pallas kernels for 9% -> 6%
where the time goes in v3:
time: 42.9 us; the launch traced here: 42.7 us
  starting transfers between devices  14.4 us (34%)
  waiting for transfers between devices  14.4 us (34%)
  Pallas kernels  10.7 us (25%)
  local copies, waits for them, and re-layouts  2.57 us (6%)
  between operations  0.69 us (2%)
    pallas_call x3, Pallas kernels, call(): pl.pallas_call(kernel, out_shape=outs, in_specs=[pl.BlockSpec(memory_spac...  10.7 us
    ppermute x6, starting transfers between devices, to_replicas(): lax.ppermute(parts[step], 'dp', swap_route(step, count))  9.18 us
    ppermute x2, waiting for transfers between devices, swap_sections(): lax.ppermute(far, 'section', [(i, (i + 2 * (i % 2) - 1) % count) for i in...  7.23 us
    ppermute x6, waiting for transfers between devices, to_replicas(): lax.ppermute(parts[step], 'dp', swap_route(step, count))  7.15 us
    ppermute x2, starting transfers between devices, swap_sections(): lax.ppermute(far, 'section', [(i, (i + 2 * (i % 2) - 1) % count) for i in...  4.71 us
    unnamed x14, local copies, waits for them, and re-layouts  2.57 us
  transfers between devices with their start and end apart: 10, of which 4 were waited for; matrix products, arithmetic and copies ran while one was open for 0% of the time, Pallas kernels for 6%

profile of v3, /device:TPU:0, one launch (start us, length us, event | category | flops | bytes accessed | tf_op | source)
XLA Modules:
  0.0 42.7 jit_solution(15577677052564930416)
XLA Ops:
  0.7 6.8 %shard_map.181 = (bf16[16,4096]{1,0:T(8,128)(2,1)}, bf16[16,4096]{1,0:T(8,128)(2,1)}, f32[32,24,128]{2,1,0:T(8,128)}, f32[32,8,128]{2,1,0:T(8,128)}, bf16[10,16,...) custom-call(s32[1,32]{1,0:T(1,128)} %refs_0_.3, ...), custom_call_target="tpu_custom_call" | custom-call | bytes 5112072 | tf_op jit(solution)/shard_map/pallas_call | solution.py:244
  7.5 0.5 %collective-permute-start = (bf16[16,4096]{1,0:T(8,128)(2,1)}, bf16[16,4096]{1,0:T(8,128)(2,1)S(1)}, u32[]{:S(2)}, u32[]{:S(2)}) collective-permute-start(bf16[16,4096]{1,0:T(8,128)(2,1)} %get-tuple-element.20), channel_id=1, source_target_pairs={{0,4},{4,0},{8,12},{12,8},{16,20},{20,16},{24,28},{28,24},{1,5},{5... | collective-permute-start | bytes 393224 | tf_op jit(solution)/shard_map/ppermute | solution.py:30
  8.0 4.7 %collective-permute-start.1 = (bf16[16,4096]{1,0:T(8,128)(2,1)}, bf16[16,4096]{1,0:T(8,128)(2,1)S(1)}, u32[]{:S(2)}, u32[]{:S(2)}) collective-permute-start(bf16[16,4096]{1,0:T(8,128)(2,1)} %get-tuple-element.21), channel_id=1, source_target_pairs={{0,28},{4,8},{8,4},{12,16},{16,12},{20,24},{24,20},{28,0},{1,29},{... | collective-permute-start | bytes 393224 | tf_op jit(solution)/shard_map/ppermute | solution.py:29
  12.7 1.5 %collective-permute-start.4 = (bf16[10,16,1024]{2,1,0:T(8,128)(2,1)}, bf16[10,16,1024]{2,1,0:T(8,128)(2,1)S(1)}, u32[]{:S(2)}, u32[]{:S(2)}) collective-permute-start(bf16[10,16,1024]{2,1,0:T(8,128)(2,1)} %get-tuple-element.27), channel_id=1, source_target_pairs={{0,1},{1,0},{2,3},{3,2},{4,5},{5,4},{6,7},{7,6},{8,9},{9,8},{10,11... | collective-permute-start | bytes 983048 | tf_op jit(solution)/shard_map/ppermute | solution.py:273
  14.2 1.5 %collective-permute-start.5 = (bf16[10,16,1024]{2,1,0:T(8,128)(2,1)}, bf16[10,16,1024]{2,1,0:T(8,128)(2,1)S(1)}, u32[]{:S(2)}, u32[]{:S(2)}) collective-permute-start(bf16[10,16,1024]{2,1,0:T(8,128)(2,1)} %get-tuple-element.28), channel_id=1, source_target_pairs={{0,2},{1,3},{2,0},{3,1},{4,6},{5,7},{6,4},{7,5},{8,10},{9,11},{10,... | collective-permute-start | bytes 983048 | tf_op jit(solution)/shard_map/ppermute | solution.py:273
  15.7 0.5 %collective-permute-start.6 = (bf16[10,16,1024]{2,1,0:T(8,128)(2,1)}, bf16[10,16,1024]{2,1,0:T(8,128)(2,1)S(1)}, u32[]{:S(2)}, u32[]{:S(2)}) collective-permute-start(bf16[10,16,1024]{2,1,0:T(8,128)(2,1)} %get-tuple-element.29), channel_id=1, source_target_pairs={{0,3},{1,2},{2,1},{3,0},{4,7},{5,6},{6,5},{7,4},{8,11},{9,10},{10,... | collective-permute-start | bytes 983048 | tf_op jit(solution)/shard_map/ppermute | solution.py:273
  16.2 0.0 collective-permute-done.refs_4_
  16.2 0.1 collective-permute-done.1.refs_5_
  16.3 0.6 %copy-done.5 = s32[1,32]{1,0:T(1,128)S(1)} copy-done((s32[1,32]{1,0:T(1,128)S(1)}, s32[1,32]{1,0:T(1,128)}, u32[]{:S(2)}) %copy-start.5) | copy-done | bytes 152
  16.9 0.0 copy-done.6
  16.9 1.0 %copy-done.2 = f32[32,24,128]{2,1,0:T(8,128)S(1)} copy-done((f32[32,24,128]{2,1,0:T(8,128)S(1)}, f32[32,24,128]{2,1,0:T(8,128)}, u32[]{:S(2)}) %copy-start.2) | copy-done | bytes 393240
  17.9 0.9 %copy-done.4 = f32[32,8,128]{2,1,0:T(8,128)S(1)} copy-done((f32[32,8,128]{2,1,0:T(8,128)S(1)}, f32[32,8,128]{2,1,0:T(8,128)}, u32[]{:S(2)}) %copy-start.4) | copy-done | bytes 131096
  18.8 2.5 %shard_map.182 = (bf16[16,4096]{1,0:T(8,128)(2,1)S(1)}, bf16[16,4096]{1,0:T(8,128)(2,1)S(1)}, bf16[2,16,1024]{2,1,0:T(8,128)(2,1)S(1)}, bf16[2,16,1024]{2,1,0:T(...) custom-call(s32[1,32]{1,0:T(1,128)S(1)} %copy-done.5, s32[1,32]{1,0:T(1,128)S(1)} %copy-done.6, ...), custom_call_target="tpu_custom_call" | custom-call | bytes 3408128 | tf_op jit(solution)/shard_map/pallas_call | solution.py:244
  21.4 1.5 %collective-permute-start.7 = (bf16[2,16,1024]{2,1,0:T(8,128)(2,1)S(1)}, bf16[2,16,1024]{2,1,0:T(8,128)(2,1)S(1)}, u32[]{:S(2)}, u32[]{:S(2)}) collective-permute-start(bf16[2,16,1024]{2,1,0:T(8,128)(2,1)S(1)} %get-tuple-element.31), channel_id=1, source_target_pairs={{0,1},{1,0},{2,3},{3,2},{4,5},{5,4},{6,7},{7,6},{8,9},{9,8},{10,11... | collective-permute-start | bytes 196616 | tf_op jit(solution)/shard_map/ppermute | solution.py:273
  22.9 1.5 %collective-permute-start.8 = (bf16[2,16,1024]{2,1,0:T(8,128)(2,1)S(1)}, bf16[2,16,1024]{2,1,0:T(8,128)(2,1)S(1)}, u32[]{:S(2)}, u32[]{:S(2)}) collective-permute-start(bf16[2,16,1024]{2,1,0:T(8,128)(2,1)S(1)} %get-tuple-element.32), channel_id=1, source_target_pairs={{0,2},{1,3},{2,0},{3,1},{4,6},{5,7},{6,4},{7,5},{8,10},{9,11},{10,... | collective-permute-start | bytes 196616 | tf_op jit(solution)/shard_map/ppermute | solution.py:273
  24.4 4.6 %collective-permute-done.7.refs_7_ = bf16[2,16,1024]{2,1,0:T(8,128)(2,1)S(1)} collective-permute-done((bf16[2,16,1024]{2,1,0:T(8,128)(2,1)S(1)}, bf16[2,16,1024]{2,1,0:T(8,128)(2,1)S(1)}, u32[]{:S(2)}, u32[]{:S(2)}) %collective-permute-start.7) | collective-permute-done | bytes 65568 | tf_op jit(solution)/shard_map/ppermute | solution.py:273
  29.0 2.6 %collective-permute-start.9 = (bf16[2,16,1024]{2,1,0:T(8,128)(2,1)S(1)}, bf16[2,16,1024]{2,1,0:T(8,128)(2,1)S(1)}, u32[]{:S(2)}, u32[]{:S(2)}) collective-permute-start(bf16[2,16,1024]{2,1,0:T(8,128)(2,1)S(1)} %get-tuple-element.33), channel_id=1, source_target_pairs={{0,3},{1,2},{2,1},{3,0},{4,7},{5,6},{6,5},{7,4},{8,11},{9,10},{10,... | collective-permute-start | bytes 196616 | tf_op jit(solution)/shard_map/ppermute | solution.py:273
  31.7 0.0 collective-permute-done.8.refs_8_
  31.7 0.0 collective-permute-start.2
  31.7 2.5 %collective-permute-done.9.refs_9_ = bf16[2,16,1024]{2,1,0:T(8,128)(2,1)S(1)} collective-permute-done((bf16[2,16,1024]{2,1,0:T(8,128)(2,1)S(1)}, bf16[2,16,1024]{2,1,0:T(8,128)(2,1)S(1)}, u32[]{:S(2)}, u32[]{:S(2)}) %collective-permute-start.9) | collective-permute-done | bytes 65568 | tf_op jit(solution)/shard_map/ppermute | solution.py:273
  34.2 0.0 collective-permute-start.3
  34.2 0.0 collective-permute-done.2.refs_0_
  34.2 7.2 %collective-permute-done.3.refs_1_ = bf16[16,4096]{1,0:T(8,128)(2,1)S(1)} collective-permute-done((bf16[16,4096]{1,0:T(8,128)(2,1)S(1)}, bf16[16,4096]{1,0:T(8,128)(2,1)S(1)}, u32[]{:S(2)}, u32[]{:S(2)}) %collective-permute-start.3) | collective-permute-done | bytes 131104 | tf_op jit(solution)/shard_map/ppermute | solution.py:29
  41.4 1.3 %shard_map.183 = (bf16[1,8,4096]{2,1,0:T(8,128)(2,1)}, bf16[1,8,4096]{2,1,0:T(8,128)(2,1)}, bf16[1,8,4096]{2,1,0:T(8,128)(2,1)}, bf16[1,8,4096]{2,1,0:T(8,128)(2...) custom-call(bf16[16,4096]{1,0:T(8,128)(2,1)S(1)} %collective-permute-done.2.refs_0_, ...), custom_call_target="tpu_custom_call" | custom-call | bytes 2621440 | tf_op jit(solution)/shard_map/pallas_call | solution.py:244
  (13 shorter events, 0.0 us)
Async XLA Ops:
  0.6 15.6 %copy-start.1 = (bf16[1,32,128,128]{3,2,1,0:T(8,128)(2,1)S(1)}, bf16[1,32,128,128]{3,2,1,0:T(8,128)(2,1)}, u32[]{:S(2)}) copy-start(bf16[1,32,128,128]{3,2,1,0:T(8,128)(2,1)} %refs_3_.3) | copy-start | bytes 3145732
  0.6 15.6 %copy-start = (bf16[1,32,128,128]{3,2,1,0:T(8,128)(2,1)S(1)}, bf16[1,32,128,128]{3,2,1,0:T(8,128)(2,1)}, u32[]{:S(2)}) copy-start(bf16[1,32,128,128]{3,2,1,0:T(8,128)(2,1)} %refs_2_.3) | copy-start | bytes 3145732
  7.5 8.7 %collective-permute-start = (bf16[16,4096]{1,0:T(8,128)(2,1)}, bf16[16,4096]{1,0:T(8,128)(2,1)S(1)}, u32[]{:S(2)}, u32[]{:S(2)}) collective-permute-start(bf16[16,4096]{1,0:T(8,128)(2,1)} %get-tuple-element.20), channel_id=1, source_target_pairs={{0,4},{4,0},{8,12},{12,8},{16,20},{20,16},{24,28},{28,24},{1,5},{5... | collective-permute-start | bytes 393224 | tf_op jit(solution)/shard_map/ppermute | solution.py:30
  8.0 8.3 %collective-permute-start.1 = (bf16[16,4096]{1,0:T(8,128)(2,1)}, bf16[16,4096]{1,0:T(8,128)(2,1)S(1)}, u32[]{:S(2)}, u32[]{:S(2)}) collective-permute-start(bf16[16,4096]{1,0:T(8,128)(2,1)} %get-tuple-element.21), channel_id=1, source_target_pairs={{0,28},{4,8},{8,4},{12,16},{16,12},{20,24},{24,20},{28,0},{1,29},{... | collective-permute-start | bytes 393224 | tf_op jit(solution)/shard_map/ppermute | solution.py:29
  12.7 28.7 %collective-permute-start.4 = (bf16[10,16,1024]{2,1,0:T(8,128)(2,1)}, bf16[10,16,1024]{2,1,0:T(8,128)(2,1)S(1)}, u32[]{:S(2)}, u32[]{:S(2)}) collective-permute-start(bf16[10,16,1024]{2,1,0:T(8,128)(2,1)} %get-tuple-element.27), channel_id=1, source_target_pairs={{0,1},{1,0},{2,3},{3,2},{4,5},{5,4},{6,7},{7,6},{8,9},{9,8},{10,11... | collective-permute-start | bytes 983048 | tf_op jit(solution)/shard_map/ppermute | solution.py:273
  14.2 27.2 %collective-permute-start.5 = (bf16[10,16,1024]{2,1,0:T(8,128)(2,1)}, bf16[10,16,1024]{2,1,0:T(8,128)(2,1)S(1)}, u32[]{:S(2)}, u32[]{:S(2)}) collective-permute-start(bf16[10,16,1024]{2,1,0:T(8,128)(2,1)} %get-tuple-element.28), channel_id=1, source_target_pairs={{0,2},{1,3},{2,0},{3,1},{4,6},{5,7},{6,4},{7,5},{8,10},{9,11},{10,... | collective-permute-start | bytes 983048 | tf_op jit(solution)/shard_map/ppermute | solution.py:273
  15.7 25.7 %collective-permute-start.6 = (bf16[10,16,1024]{2,1,0:T(8,128)(2,1)}, bf16[10,16,1024]{2,1,0:T(8,128)(2,1)S(1)}, u32[]{:S(2)}, u32[]{:S(2)}) collective-permute-start(bf16[10,16,1024]{2,1,0:T(8,128)(2,1)} %get-tuple-element.29), channel_id=1, source_target_pairs={{0,3},{1,2},{2,1},{3,0},{4,7},{5,6},{6,5},{7,4},{8,11},{9,10},{10,... | collective-permute-start | bytes 983048 | tf_op jit(solution)/shard_map/ppermute | solution.py:273
  16.3 0.7 %copy-start.5 = (s32[1,32]{1,0:T(1,128)S(1)}, s32[1,32]{1,0:T(1,128)}, u32[]{:S(2)}) copy-start(s32[1,32]{1,0:T(1,128)} %refs_0_.3) | copy-start | bytes 388
  16.3 0.7 %copy-start.6 = (s32[1,32]{1,0:T(1,128)S(1)}, s32[1,32]{1,0:T(1,128)}, u32[]{:S(2)}) copy-start(s32[1,32]{1,0:T(1,128)} %refs_1_.3) | copy-start | bytes 388
  16.9 1.0 %copy-start.2 = (f32[32,24,128]{2,1,0:T(8,128)S(1)}, f32[32,24,128]{2,1,0:T(8,128)}, u32[]{:S(2)}) copy-start(f32[32,24,128]{2,1,0:T(8,128)} %get-tuple-element.22.refs_6_) | copy-start | bytes 1179652
  17.9 0.9 %copy-start.4 = (f32[32,8,128]{2,1,0:T(8,128)S(1)}, f32[32,8,128]{2,1,0:T(8,128)}, u32[]{:S(2)}) copy-start(f32[32,8,128]{2,1,0:T(8,128)} %get-tuple-element.23.refs_7_) | copy-start | bytes 393220
  18.8 22.6 %copy-start.3 = (bf16[10,16,1024]{2,1,0:T(8,128)(2,1)S(1)}, bf16[10,16,1024]{2,1,0:T(8,128)(2,1)}, u32[]{:S(2)}) copy-start(bf16[10,16,1024]{2,1,0:T(8,128)(2,1)} %get-tuple-element.26.refs_2_) | copy-start | bytes 983044
  21.4 7.7 %collective-permute-start.7 = (bf16[2,16,1024]{2,1,0:T(8,128)(2,1)S(1)}, bf16[2,16,1024]{2,1,0:T(8,128)(2,1)S(1)}, u32[]{:S(2)}, u32[]{:S(2)}) collective-permute-start(bf16[2,16,1024]{2,1,0:T(8,128)(2,1)S(1)} %get-tuple-element.31), channel_id=1, source_target_pairs={{0,1},{1,0},{2,3},{3,2},{4,5},{5,4},{6,7},{7,6},{8,9},{9,8},{10,11... | collective-permute-start | bytes 196616 | tf_op jit(solution)/shard_map/ppermute | solution.py:273
  22.9 8.8 %collective-permute-start.8 = (bf16[2,16,1024]{2,1,0:T(8,128)(2,1)S(1)}, bf16[2,16,1024]{2,1,0:T(8,128)(2,1)S(1)}, u32[]{:S(2)}, u32[]{:S(2)}) collective-permute-start(bf16[2,16,1024]{2,1,0:T(8,128)(2,1)S(1)} %get-tuple-element.32), channel_id=1, source_target_pairs={{0,2},{1,3},{2,0},{3,1},{4,6},{5,7},{6,4},{7,5},{8,10},{9,11},{10,... | collective-permute-start | bytes 196616 | tf_op jit(solution)/shard_map/ppermute | solution.py:273
  29.0 5.2 %collective-permute-start.9 = (bf16[2,16,1024]{2,1,0:T(8,128)(2,1)S(1)}, bf16[2,16,1024]{2,1,0:T(8,128)(2,1)S(1)}, u32[]{:S(2)}, u32[]{:S(2)}) collective-permute-start(bf16[2,16,1024]{2,1,0:T(8,128)(2,1)S(1)} %get-tuple-element.33), channel_id=1, source_target_pairs={{0,3},{1,2},{2,1},{3,0},{4,7},{5,6},{6,5},{7,4},{8,11},{9,10},{10,... | collective-permute-start | bytes 196616 | tf_op jit(solution)/shard_map/ppermute | solution.py:273
  31.7 2.5 %collective-permute-start.2 = (bf16[16,4096]{1,0:T(8,128)(2,1)S(1)}, bf16[16,4096]{1,0:T(8,128)(2,1)S(1)}, u32[]{:S(2)}, u32[]{:S(2)}) collective-permute-start(bf16[16,4096]{1,0:T(8,128)(2,1)S(1)} %get-tuple-element.24), channel_id=1, source_target_pairs={{0,4},{4,0},{8,12},{12,8},{16,20},{20,16},{24,28},{28,24},{1,5},{5... | collective-permute-start | bytes 393224 | tf_op jit(solution)/shard_map/ppermute | solution.py:30
  34.2 7.2 %collective-permute-start.3 = (bf16[16,4096]{1,0:T(8,128)(2,1)S(1)}, bf16[16,4096]{1,0:T(8,128)(2,1)S(1)}, u32[]{:S(2)}, u32[]{:S(2)}) collective-permute-start(bf16[16,4096]{1,0:T(8,128)(2,1)S(1)} %get-tuple-element.25), channel_id=1, source_target_pairs={{0,28},{4,8},{8,4},{12,16},{16,12},{20,24},{24,20},{28,0},{1,29},{... | collective-permute-start | bytes 393224 | tf_op jit(solution)/shard_map/ppermute | solution.py:29

commit v4 on v3

--- a/solution.py
+++ b/solution.py
@@ -9,7 +9,7 @@
 F32 = jnp.float32
 BF16 = jnp.bfloat16
 LIMIT = 40 * 1024 * 1024
-WIDE = 60 * 1024 * 1024
+WORK = 10 ** 10
 
 
 def partner(me, step, count):
@@ -39,6 +39,11 @@
     return lax.dot_general(rows, weight, (((1,), (1,)), ((), ())), preferred_element_type=F32)
 
 
+def outer(xs, es):
+    return lax.dot_general(jnp.concatenate(xs, 0), jnp.concatenate(es, 0), (((0,), (0,)), ((), ())),
+                           preferred_element_type=F32)
+
+
 def sigmoid(z):
     return 1.0 / (1.0 + jnp.exp(-z))
 
@@ -64,17 +69,6 @@
             yield step, place, base + place
 
 
-def start_all(copies):
-    for copy in copies:
-        copy.start()
-    return copies
-
-
-def wait_all(copies):
-    for copy in copies:
-        copy.wait()
-
-
 def odd_section():
     return lax.rem(lax.axis_index("section"), 2)
 
@@ -91,13 +85,30 @@
     packs[odd] = far[...]
 
 
-def back_first(count, per, copies, up_idx, down_idx, order, w_up, w_down, g_ref, a_ref, back, second, second_tan,
+def open_launch(token):
+    token[...] = jnp.zeros(token.shape, F32)
+
+
+def pack_ready(count, per, up_idx, order, g_ref, a_ref, back, second, second_tan, second_grad, *sends):
+    m0 = order[0, 0]
+    m1 = order[0, 1]
+    for step, place, j in send_order(lax.axis_index("dp"), count, per):
+        out, here = sends[step], lanes(place)
+        at = lanes(up_idx[0, j])
+        out[0, :, here] = stack([back[0, m0, :, at], second[0, m0, :, at]]).astype(BF16)
+        out[1, :, here] = stack([second_tan[0, m0, :, at], second_tan[0, m1, :, at]]).astype(BF16)
+        out[2, :, here] = stack([back[0, m1, :, at], second[0, m1, :, at]]).astype(BF16)
+        at = lanes(j)
+        out[3, :, here] = stack([g_ref[0, :, at], a_ref[0, :, at]]).astype(BF16)
+        out[4, :, here] = stack([second_grad[0, m0, :, at], second_grad[0, m1, :, at]]).astype(BF16)
+
+
+def back_first(count, per, up_idx, down_idx, order, w_up, w_down, g_ref, a_ref, back, second, second_tan,
                second_grad, pack, keep, sends, pulled, returned, hidden):
     blocks = count * per
     me = lax.axis_index("dp")
     for b in range(blocks):
         pulled[b] = jnp.zeros(pulled.shape[1:], F32)
-    wait_all(copies[:7])
     m0 = order[0, 0]
     m1 = order[0, 1]
     for b in range(blocks):
@@ -105,11 +116,8 @@
     for step, place, i in send_order(me, count, per):
         at = lanes(i)
         c = stack([g_ref[0, :, at], a_ref[0, :, at], second_grad[0, m0, :, at], second_grad[0, m1, :, at]]).astype(BF16)
-        sends[step][8, :, lanes(place)] = c[0:16]
-        sends[step][9, :, lanes(place)] = c[16:32]
         target = down_idx[0, i]
         pulled[target] = pulled[target] + times_transposed(c, w_down[0, i])
-    wait_all(copies[7:11])
     for step, place, j in send_order(me, count, per):
         u = up_idx[0, j]
         at = lanes(u)
@@ -117,8 +125,6 @@
                    second_tan[0, m1, :, at], back[0, m1, :, at], second[0, m1, :, at]]).astype(BF16)
         out = sends[step]
         here = lanes(place)
-        for group in range(3):
-            out[group, :, here] = x[16 * group:16 * group + 16]
         z = times(x, w_up[0, j])
         zb0, za0, ta0, ta1, zb1, za1 = (z[8 * k:8 * k + 8] for k in range(6))
         pg, pa, ga0, ga1 = (pulled[j, 8 * k:8 * k + 8] for k in range(4))
@@ -129,8 +135,8 @@
         curve_a1 = sa1 * (1.0 - sa1) * (2.0 + za1 * (1.0 - 2.0 * sa1))
         push = slope_a0 * pa + curve_a0 * ga0 * ta0
         e = jnp.concatenate([slope_of(zb0, sb0) * pg, push], 0).astype(BF16)
-        out[3, :, here] = e
-        out[4, :, here] = jnp.concatenate([slope_a0 * ga0, slope_a1 * ga1], 0).astype(BF16)
+        out[0, :, here] = e
+        out[1, :, here] = jnp.concatenate([slope_a0 * ga0, slope_a1 * ga1], 0).astype(BF16)
         hidden[j] = jnp.concatenate(
             [zb0 * sb0, za0 * sa0, slope_a0 * ta0, slope_a1 * ta1, zb1 * sb1, za1 * sa1], 0).astype(BF16)
         keep[j] = jnp.concatenate([slope_of(zb1, sb1), slope_a1, curve_a1 * ga1 * ta1], 0)
@@ -140,7 +146,7 @@
     for step, place, i in send_order(me, count, per):
         y = hidden[down_idx[0, i]]
         for group in range(3):
-            sends[step][5 + group, :, lanes(place)] = y[16 * group:16 * group + 16]
+            sends[step][2 + group, :, lanes(place)] = y[16 * group:16 * group + 16]
 
 
 def forward_first(blocks, up_idx, down_idx, order, w_up, w_down, v_ref, t_ref, tan, pack, keep, hidden):
@@ -159,15 +165,11 @@
         pack[:, at] = moved.astype(BF16)
 
 
-def first_tick(count, per, *refs):
-    sources, (near, far, keep, keep_tan) = refs[:14], refs[14:18]
-    sends, held = refs[18:18 + count], refs[18 + count:32 + count]
-    packs, pulled, returned, hidden, hidden_fwd, sems = refs[32 + count:]
-    copies = start_all([pltpu.make_async_copy(s, t, sems.at[k]) for k, (s, t) in enumerate(zip(sources, held))])
-    up_idx, down_idx, order, w_down, g_ref, a_ref, second_grad, w_up, back, second, second_tan, v_ref, t_ref, tan = held
-    back_first(count, per, copies, up_idx, down_idx, order, w_up, w_down, g_ref, a_ref, back, second, second_tan,
+def first_tick(count, per, up_idx, down_idx, order, w_up, w_down, g_ref, a_ref, back, second, second_tan, second_grad,
+               v_ref, t_ref, tan, near, far, keep, keep_tan, *refs):
+    sends, (packs, pulled, returned, hidden, hidden_fwd) = refs[:count], refs[count:]
+    back_first(count, per, up_idx, down_idx, order, w_up, w_down, g_ref, a_ref, back, second, second_tan,
                second_grad, packs.at[1], keep, sends, pulled, returned, hidden)
-    wait_all(copies[11:])
     forward_first(count * per, up_idx, down_idx, order, w_up, w_down, v_ref, t_ref, tan, packs.at[0], keep_tan, hidden_fwd)
     hand_out(packs, near, far)
 
@@ -211,10 +213,24 @@
     hand_out(packs, near, far)
 
 
-def finish(count, per, scale, near, far, *rest):
-    early = rest[:count]
-    late = rest[count:2 * count]
-    values, score, tangent, adjoint, grad_up, grad_down, came = rest[2 * count:]
+def early_grads(count, per, *refs):
+    ready, early, late = refs[:count], refs[count:2 * count], refs[2 * count:3 * count]
+    grads, sends = refs[3 * count], refs[3 * count + 1:]
+    for source in range(count):
+        sends[source][...] = late[source][...]
+    for place in range(per):
+        at = lanes(place)
+        for out in range(2):
+            left, right = (ready, early) if out == 0 else (early, ready)
+            first_left, first_right = (0, 0) if out == 0 else (2, 3)
+            xs = [left[source][first_left + k, :, at] for source in range(count) for k in range(2)]
+            es = [right[source][first_right + k, :, at] for source in range(count) for k in range(2)]
+            grads[out, place] = outer(xs, es)
+
+
+def finish(count, per, scale, near, far, grads, *rest):
+    ready, early, late = rest[:count], rest[count:2 * count], rest[2 * count:3 * count]
+    values, score, tangent, adjoint, grad_up, grad_down, came = rest[3 * count:]
     take_in(near, far, came)
     moved = came[0].astype(F32)
     values[0] = moved[0:8].astype(BF16)
@@ -224,18 +240,13 @@
     adjoint[0] = moved[8:16].astype(BF16)
     for place in range(per):
         at = lanes(place)
-        for out, left, right, last in ((grad_up, (0, 1, 2), (3, 4), 0), (grad_down, (5, 6, 7), (8, 9), 1)):
-            xs, es = [], []
-            for source in range(count):
-                xs += [early[source][k, :, at] for k in left]
-                es += [early[source][k, :, at] for k in right] + [late[source][last, :, at]]
-            total = lax.dot_general(jnp.concatenate(xs, 0), jnp.concatenate(es, 0), (((0,), (0,)), ((), ())),
-                                    preferred_element_type=F32)
-            out[0, place] = (total * scale).astype(BF16)
-
-
-def call(body, operands, spaces, outs, scratch, limit=LIMIT, out_space=pltpu.VMEM, after=()):
-    moved = sum(x.size * x.dtype.itemsize for x in list(operands) + list(outs))
+        for k, (out, left, group) in enumerate(((grad_up, ready, 2), (grad_down, early, 4))):
+            xs = [left[source][group, :, at] for source in range(count)]
+            es = [late[source][k, :, at] for source in range(count)]
+            out[0, place] = ((grads[k, place] + outer(xs, es)) * scale).astype(BF16)
+
+
+def call(body, operands, spaces, outs, scratch, after=()):
     taken = len(operands)
 
     def kernel(*refs):
@@ -245,10 +256,10 @@
         kernel,
         out_shape=outs,
         in_specs=[pl.BlockSpec(memory_space=space) for space in spaces] + [pl.BlockSpec(memory_space=pl.ANY)] * len(after),
-        out_specs=[pl.BlockSpec(memory_space=out_space)] * len(outs),
+        out_specs=[pl.BlockSpec(memory_space=pltpu.VMEM)] * len(outs),
         scratch_shapes=scratch,
-        compiler_params=pltpu.CompilerParams(vmem_limit_bytes=limit),
-        cost_estimate=pl.CostEstimate(flops=0, bytes_accessed=moved, transcendentals=0),
+        compiler_params=pltpu.CompilerParams(vmem_limit_bytes=LIMIT),
+        cost_estimate=pl.CostEstimate(flops=WORK, bytes_accessed=WORK // 100, transcendentals=0),
     )(*operands, *after)
 
 
@@ -270,18 +281,24 @@
         return kernel
 
     def to_replicas(parts):
-        return parts[:1] + [lax.ppermute(parts[step], "dp", swap_route(step, count)) for step in range(1, count)]
-
-    taken = (up_index, down_index, tick_order, w_down, score_grad_in, state_adjoint_in, saved_second_grad, w_up,
-             saved_back, saved_second, saved_second_tan, values_in, tangent_in, saved_tan)
+        return [parts[0]] + [lax.ppermute(parts[step], "dp", swap_route(step, count)) for step in range(1, count)]
+
+    rows = (score_grad_in, state_adjoint_in, saved_back, saved_second, saved_second_tan, saved_second_grad)
+    five = shape((5, 16, part), BF16)
+    (token,) = call(open_launch, (), [], [shape((8, BLOCK), F32)], [])
+    ready = call(
+        body(pack_ready, count, per), (up_index, tick_order) + rows, [smem] * 2 + [vmem] * 6, [five] * count, [],
+        after=(token,))
+    packed = ready[0]
+    ready = to_replicas(ready)
     near, far, keep, keep_tan, *early = call(
-        body(first_tick, count, per), taken, [pl.ANY] * 14,
-        [pair, pair, shape((blocks, 24, BLOCK), F32), shape((blocks, 8, BLOCK), F32)]
-        + [shape((10, 16, part), BF16)] * count,
-        [smem(x.shape, x.dtype) for x in taken[:3]] + [vmem(x.shape, x.dtype) for x in taken[3:]]
-        + [vmem((2, 16, width), BF16), vmem((blocks, 32, BLOCK), F32), vmem((blocks, 16, BLOCK), F32),
-           vmem((blocks, 48, BLOCK), BF16), vmem((blocks, 16, BLOCK), BF16), pltpu.SemaphoreType.DMA((14,))],
-        limit=WIDE)
+        body(first_tick, count, per),
+        (up_index, down_index, tick_order, w_up, w_down) + rows + (values_in, tangent_in, saved_tan),
+        [smem] * 3 + [vmem] * 11,
+        [pair, pair, shape((blocks, 24, BLOCK), F32), shape((blocks, 8, BLOCK), F32)] + [five] * count,
+        [vmem((2, 16, width), BF16), vmem((blocks, 32, BLOCK), F32), vmem((blocks, 16, BLOCK), F32),
+         vmem((blocks, 48, BLOCK), BF16), vmem((blocks, 16, BLOCK), BF16)],
+        after=(packed,))
     near, far = swap_sections(near, far)
     early = to_replicas(early)
     near, far, *late = call(
@@ -289,13 +306,18 @@
         [smem] * 2 + [vmem] * 6,
         [pair, pair] + [shape((2, 16, part), BF16)] * count,
         [vmem((2, 16, width), BF16), vmem((2, 16, width), BF16), vmem((blocks, 16, BLOCK), F32),
-         vmem((blocks, 16, BLOCK), F32), vmem((blocks, 16, BLOCK), BF16)])
+         vmem((blocks, 16, BLOCK), F32), vmem((blocks, 16, BLOCK), BF16)],
+        after=tuple(ready[1:]))
     near, far = swap_sections(near, far)
+    two = shape((2, 16, part), BF16)
+    grads, *late = call(
+        body(early_grads, count, per), (*ready, *early, *late), [vmem] * (3 * count),
+        [shape((2, per, BLOCK, BLOCK), F32)] + [two] * count, [])
     late = to_replicas(late)
     stream = shape((1,) + values_in.shape[1:], BF16)
     grad = shape((1, per, BLOCK, BLOCK), BF16)
     return tuple(call(
-        body(finish, count, per, scale), (near, far, *early, *late), [vmem] * (2 + 2 * count),
+        body(finish, count, per, scale), (near, far, grads, *ready, *early, *late), [vmem] * (3 + 3 * count),
         [stream, stream, stream, stream, grad, grad], [vmem((2, 16, width), BF16)]))
 
 

time: 42.9 us -> 37.1 us (0.86)
  waiting for transfers between devices: 14.4 us -> 6.58 us
  starting transfers between devices: 14.4 us -> 18.5 us
  Pallas kernels: 10.7 us -> 9.31 us
  local copies, waits for them, and re-layouts: 2.57 us -> 1.69 us
    ppermute x2, waiting for transfers between devices: 7.23 us -> 1.98 us  [swap_sections(): lax.ppermute(far, 'section', [(i, (i + 2 * (i % 2) - 1) % count) for i in...]
    ppermute x6 -> x9, starting transfers between devices: 9.18 us -> 12.3 us  [to_replicas(): lax.ppermute(parts[step], 'dp', swap_route(step, count))]
    ppermute x6 -> x9, waiting for transfers between devices: 7.15 us -> 4.59 us  [to_replicas(): lax.ppermute(parts[step], 'dp', swap_route(step, count))]
    pallas_call x3 -> x6, Pallas kernels: 10.7 us -> 9.31 us  [call(): pl.pallas_call(kernel, out_shape=outs, in_specs=[pl.BlockSpec(memory_spac...]
    ppermute x2, starting transfers between devices: 4.71 us -> 6.05 us  [swap_sections(): lax.ppermute(far, 'section', [(i, (i + 2 * (i % 2) - 1) % count) for i in...]
    unnamed x14 -> x28, local copies, waits for them, and re-layouts: 2.57 us -> 1.69 us
  transfers between devices with their start and end apart: 10 -> 13, of which waited for: 4 -> 5; matrix products, arithmetic and copies ran while one was open for 0% -> 0% of each run, Pallas kernels for 6% -> 20%
where the time goes in v4:
time: 37.1 us; the launch traced here: 36.9 us
  starting transfers between devices  18.5 us (50%)
  Pallas kernels  9.31 us (25%)
  waiting for transfers between devices  6.58 us (18%)
  local copies, waits for them, and re-layouts  1.69 us (5%)
  between operations  0.8 us (2%)
    ppermute x9, starting transfers between devices, to_replicas(): lax.ppermute(parts[step], 'dp', swap_route(step, count))  12.3 us
    pallas_call x6, Pallas kernels, call(): pl.pallas_call(kernel, out_shape=outs, in_specs=[pl.BlockSpec(memory_spac...  9.31 us
    ppermute x2, starting transfers between devices, swap_sections(): lax.ppermute(far, 'section', [(i, (i + 2 * (i % 2) - 1) % count) for i in...  6.05 us
    ppermute x9, waiting for transfers between devices, to_replicas(): lax.ppermute(parts[step], 'dp', swap_route(step, count))  4.59 us
    ppermute x2, waiting for transfers between devices, swap_sections(): lax.ppermute(far, 'section', [(i, (i + 2 * (i % 2) - 1) % count) for i in...  1.98 us
    unnamed x28, local copies, waits for them, and re-layouts  1.69 us
  transfers between devices with their start and end apart: 13, of which 5 were waited for; matrix products, arithmetic and copies ran while one was open for 0% of the time, Pallas kernels for 20%

profile of v4, /device:TPU:0, one launch (start us, length us, event | category | flops | bytes accessed | tf_op | source)
XLA Modules:
  0.0 36.9 jit_solution(10125457796267857301)
XLA Ops:
  0.7 0.6 %copy-done.12 = s32[1,32]{1,0:T(1,128)S(1)} copy-done((s32[1,32]{1,0:T(1,128)S(1)}, s32[1,32]{1,0:T(1,128)}, u32[]{:S(2)}) %copy-start.12) | copy-done | bytes 152
  1.3 0.3 copy-done.5
  1.8 0.8 %shard_map.182 = (bf16[5,16,1024]{2,1,0:T(8,128)(2,1)S(1)}, bf16[5,16,1024]{2,1,0:T(8,128)(2,1)S(1)}, bf16[5,16,1024]{2,1,0:T(8,128)(2,1)S(1)}, bf16[5,16,1024]{2,1,0:T(8,128)(2,1)S(1)}) custom-call(s32[1,32]{1,0:T(1,128)S(1)} %copy-done.12, s32[1,2]{1,0:T(1,128)S(1)} %copy-done.11, bf16[1,8,4096]{2,1,0:T(8,128)(2,1)S(1)} %copy-done.7, ...), custom_call_target="tpu_custom_call" | custom-call | flops 10000000000 | bytes 100000000 | tf_op jit(solution)/shard_map/pallas_call | solution.py:255
  2.6 3.0 %collective-permute-start.2 = (bf16[5,16,1024]{2,1,0:T(8,128)(2,1)S(1)}, bf16[5,16,1024]{2,1,0:T(8,128)(2,1)S(1)}, u32[]{:S(2)}, u32[]{:S(2)}) collective-permute-start(bf16[5,16,1024]{2,1,0:T(8,128)(2,1)S(1)} %get-tuple-element.34), channel_id=1, source_target_pairs={{0,1},{1,0},{2,3},{3,2},{4,5},{5,4},{6,7},{7,6},{8,9},{9,8},{10,11... | collective-permute-start | bytes 491528 | tf_op jit(solution)/shard_map/ppermute | solution.py:284
  5.6 1.5 %collective-permute-start.3 = (bf16[5,16,1024]{2,1,0:T(8,128)(2,1)S(1)}, bf16[5,16,1024]{2,1,0:T(8,128)(2,1)S(1)}, u32[]{:S(2)}, u32[]{:S(2)}) collective-permute-start(bf16[5,16,1024]{2,1,0:T(8,128)(2,1)S(1)} %get-tuple-element.35), channel_id=1, source_target_pairs={{0,2},{1,3},{2,0},{3,1},{4,6},{5,7},{6,4},{7,5},{8,10},{9,11},{10,... | collective-permute-start | bytes 491528 | tf_op jit(solution)/shard_map/ppermute | solution.py:284
  7.2 0.6 %copy-done.13 = s32[1,32]{1,0:T(1,128)S(1)} copy-done((s32[1,32]{1,0:T(1,128)S(1)}, s32[1,32]{1,0:T(1,128)}, u32[]{:S(2)}) %copy-start.13) | copy-done | bytes 152
  7.8 4.5 %shard_map.183 = (bf16[16,4096]{1,0:T(8,128)(2,1)S(1)}, bf16[16,4096]{1,0:T(8,128)(2,1)S(1)}, f32[32,24,128]{2,1,0:T(8,128)S(1)}, f32[32,8,128]{2,1,0:T(8,128)S(...) custom-call(s32[1,32]{1,0:T(1,128)S(1)} %copy-done.12, ...), custom_call_target="tpu_custom_call" | custom-call | flops 10000000000 | bytes 100000000 | tf_op jit(solution)/shard_map/pallas_call | solution.py:255
  12.2 0.1 collective-permute-start
  12.3 3.7 %collective-permute-start.1 = (bf16[16,4096]{1,0:T(8,128)(2,1)S(1)}, bf16[16,4096]{1,0:T(8,128)(2,1)S(1)}, u32[]{:S(2)}, u32[]{:S(2)}) collective-permute-start(bf16[16,4096]{1,0:T(8,128)(2,1)S(1)} %get-tuple-element.31), channel_id=1, source_target_pairs={{0,28},{4,8},{8,4},{12,16},{16,12},{20,24},{24,20},{28,0},{1,29},{... | collective-permute-start | bytes 393224 | tf_op jit(solution)/shard_map/ppermute | solution.py:29
  16.0 1.4 %collective-permute-start.7 = (bf16[5,16,1024]{2,1,0:T(8,128)(2,1)S(1)}, bf16[5,16,1024]{2,1,0:T(8,128)(2,1)S(1)}, u32[]{:S(2)}, u32[]{:S(2)}) collective-permute-start(bf16[5,16,1024]{2,1,0:T(8,128)(2,1)S(1)} %get-tuple-element.40), channel_id=1, source_target_pairs={{0,1},{1,0},{2,3},{3,2},{4,5},{5,4},{6,7},{7,6},{8,9},{9,8},{10,11... | collective-permute-start | bytes 491528 | tf_op jit(solution)/shard_map/ppermute | solution.py:284
  17.4 2.0 %collective-permute-done.1.refs_5_ = bf16[16,4096]{1,0:T(8,128)(2,1)S(1)} collective-permute-done((bf16[16,4096]{1,0:T(8,128)(2,1)S(1)}, bf16[16,4096]{1,0:T(8,128)(2,1)S(1)}, u32[]{:S(2)}, u32[]{:S(2)}) %collective-permute-start.1) | collective-permute-done | bytes 131104 | tf_op jit(solution)/shard_map/ppermute | solution.py:29
  19.4 1.4 %collective-permute-start.8 = (bf16[5,16,1024]{2,1,0:T(8,128)(2,1)S(1)}, bf16[5,16,1024]{2,1,0:T(8,128)(2,1)S(1)}, u32[]{:S(2)}, u32[]{:S(2)}) collective-permute-start(bf16[5,16,1024]{2,1,0:T(8,128)(2,1)S(1)} %get-tuple-element.41), channel_id=1, source_target_pairs={{0,2},{1,3},{2,0},{3,1},{4,6},{5,7},{6,4},{7,5},{8,10},{9,11},{10,... | collective-permute-start | bytes 491528 | tf_op jit(solution)/shard_map/ppermute | solution.py:284
  20.8 1.4 %collective-permute-start.9 = (bf16[5,16,1024]{2,1,0:T(8,128)(2,1)S(1)}, bf16[5,16,1024]{2,1,0:T(8,128)(2,1)S(1)}, u32[]{:S(2)}, u32[]{:S(2)}) collective-permute-start(bf16[5,16,1024]{2,1,0:T(8,128)(2,1)S(1)} %get-tuple-element.42), channel_id=1, source_target_pairs={{0,3},{1,2},{2,1},{3,0},{4,7},{5,6},{6,5},{7,4},{8,11},{9,10},{10,... | collective-permute-start | bytes 491528 | tf_op jit(solution)/shard_map/ppermute | solution.py:284
  22.2 2.5 %shard_map.184 = (bf16[16,4096]{1,0:T(8,128)(2,1)S(1)}, bf16[16,4096]{1,0:T(8,128)(2,1)S(1)}, bf16[2,16,1024]{2,1,0:T(8,128)(2,1)S(1)}, bf16[2,16,1024]{2,1,0:T(...) custom-call(s32[1,32]{1,0:T(1,128)S(1)} %copy-done.12, s32[1,32]{1,0:T(1,128)S(1)} %copy-done.13, ...), custom_call_target="tpu_custom_call" | custom-call | flops 10000000000 | bytes 100000000 | tf_op jit(solution)/shard_map/pallas_call | solution.py:255
  24.9 2.3 %collective-permute-start.6 = (bf16[16,4096]{1,0:T(8,128)(2,1)S(1)}, bf16[16,4096]{1,0:T(8,128)(2,1)S(1)}, u32[]{:S(2)}, u32[]{:S(2)}) collective-permute-start(bf16[16,4096]{1,0:T(8,128)(2,1)S(1)} %get-tuple-element.38), channel_id=1, source_target_pairs={{0,28},{4,8},{8,4},{12,16},{16,12},{20,24},{24,20},{28,0},{1,29},{... | collective-permute-start | bytes 393224 | tf_op jit(solution)/shard_map/ppermute | solution.py:29
  27.2 0.3 collective-permute-done.8.refs_6_.refs_9_
  27.5 0.4 shard_map.185
  27.9 1.6 %collective-permute-start.10 = (bf16[2,16,1024]{2,1,0:T(8,128)(2,1)S(1)}, bf16[2,16,1024]{2,1,0:T(8,128)(2,1)S(1)}, u32[]{:S(2)}, u32[]{:S(2)}) collective-permute-start(bf16[2,16,1024]{2,1,0:T(8,128)(2,1)S(1)} %get-tuple-element.49), channel_id=1, source_target_pairs={{0,1},{1,0},{2,3},{3,2},{4,5},{5,4},{6,7},{7,6},{8,9},{9,8},{10,11... | collective-permute-start | bytes 196616 | tf_op jit(solution)/shard_map/ppermute | solution.py:284
  29.4 1.1 %collective-permute-start.11 = (bf16[2,16,1024]{2,1,0:T(8,128)(2,1)S(1)}, bf16[2,16,1024]{2,1,0:T(8,128)(2,1)S(1)}, u32[]{:S(2)}, u32[]{:S(2)}) collective-permute-start(bf16[2,16,1024]{2,1,0:T(8,128)(2,1)S(1)} %get-tuple-element.50), channel_id=1, source_target_pairs={{0,2},{1,3},{2,0},{3,1},{4,6},{5,7},{6,4},{7,5},{8,10},{9,11},{10,... | collective-permute-start | bytes 196616 | tf_op jit(solution)/shard_map/ppermute | solution.py:284
  30.5 0.9 %collective-permute-start.12 = (bf16[2,16,1024]{2,1,0:T(8,128)(2,1)S(1)}, bf16[2,16,1024]{2,1,0:T(8,128)(2,1)S(1)}, u32[]{:S(2)}, u32[]{:S(2)}) collective-permute-start(bf16[2,16,1024]{2,1,0:T(8,128)(2,1)S(1)} %get-tuple-element.51), channel_id=1, source_target_pairs={{0,3},{1,2},{2,1},{3,0},{4,7},{5,6},{6,5},{7,4},{8,11},{9,10},{10,... | collective-permute-start | bytes 196616 | tf_op jit(solution)/shard_map/ppermute | solution.py:284
  31.4 0.8 %collective-permute-done.10.refs_12_ = bf16[2,16,1024]{2,1,0:T(8,128)(2,1)S(1)} collective-permute-done((bf16[2,16,1024]{2,1,0:T(8,128)(2,1)S(1)}, bf16[2,16,1024]{2,1,0:T(8,128)(2,1)S(1)}, u32[]{:S(2)}, u32[]{:S(2)}) %collective-permute-start.10) | collective-permute-done | bytes 65568 | tf_op jit(solution)/shard_map/ppermute | solution.py:284
  32.2 1.5 %collective-permute-done.11.refs_13_ = bf16[2,16,1024]{2,1,0:T(8,128)(2,1)S(1)} collective-permute-done((bf16[2,16,1024]{2,1,0:T(8,128)(2,1)S(1)}, bf16[2,16,1024]{2,1,0:T(8,128)(2,1)S(1)}, u32[]{:S(2)}, u32[]{:S(2)}) %collective-permute-start.11) | collective-permute-done | bytes 65568 | tf_op jit(solution)/shard_map/ppermute | solution.py:284
  33.7 2.0 %collective-permute-done.12.refs_14_ = bf16[2,16,1024]{2,1,0:T(8,128)(2,1)S(1)} collective-permute-done((bf16[2,16,1024]{2,1,0:T(8,128)(2,1)S(1)}, bf16[2,16,1024]{2,1,0:T(8,128)(2,1)S(1)}, u32[]{:S(2)}, u32[]{:S(2)}) %collective-permute-start.12) | collective-permute-done | bytes 65568 | tf_op jit(solution)/shard_map/ppermute | solution.py:284
  35.7 1.2 %shard_map.186 = (bf16[1,8,4096]{2,1,0:T(8,128)(2,1)}, bf16[1,8,4096]{2,1,0:T(8,128)(2,1)}, bf16[1,8,4096]{2,1,0:T(8,128)(2,1)}, bf16[1,8,4096]{2,1,0:T(8,128)(2...) custom-call(bf16[16,4096]{1,0:T(8,128)(2,1)S(1)} %collective-permute-done.5.refs_0_, ...), custom_call_target="tpu_custom_call" | custom-call | flops 10000000000 | bytes 100000000 | tf_op jit(solution)/shard_map/pallas_call | solution.py:255
  (36 shorter events, 0.4 us)
Async XLA Ops:
  0.7 1.0 %copy-start.4 = (bf16[1,2,8,4096]{3,2,1,0:T(8,128)(2,1)S(1)}, bf16[1,2,8,4096]{3,2,1,0:T(8,128)(2,1)}, u32[]{:S(2)}) copy-start(bf16[1,2,8,4096]{3,2,1,0:T(8,128)(2,1)} %refs_9_.1) | copy-start | bytes 393220
  0.7 1.0 %copy-start.3 = (bf16[1,2,8,4096]{3,2,1,0:T(8,128)(2,1)S(1)}, bf16[1,2,8,4096]{3,2,1,0:T(8,128)(2,1)}, u32[]{:S(2)}) copy-start(bf16[1,2,8,4096]{3,2,1,0:T(8,128)(2,1)} %refs_8_.1) | copy-start | bytes 393220
  0.7 1.1 %copy-start.2 = (bf16[1,2,8,4096]{3,2,1,0:T(8,128)(2,1)S(1)}, bf16[1,2,8,4096]{3,2,1,0:T(8,128)(2,1)}, u32[]{:S(2)}) copy-start(bf16[1,2,8,4096]{3,2,1,0:T(8,128)(2,1)} %refs_7_.3) | copy-start | bytes 393220
  0.7 1.1 %copy-start.8 = (bf16[1,8,4096]{2,1,0:T(8,128)(2,1)S(1)}, bf16[1,8,4096]{2,1,0:T(8,128)(2,1)}, u32[]{:S(2)}) copy-start(bf16[1,8,4096]{2,1,0:T(8,128)(2,1)} %refs_6_.3) | copy-start | bytes 196612
  0.7 1.1 %copy-start.7 = (bf16[1,8,4096]{2,1,0:T(8,128)(2,1)S(1)}, bf16[1,8,4096]{2,1,0:T(8,128)(2,1)}, u32[]{:S(2)}) copy-start(bf16[1,8,4096]{2,1,0:T(8,128)(2,1)} %refs_5_.3) | copy-start | bytes 196612
  0.7 1.1 %copy-start.11 = (s32[1,2]{1,0:T(1,128)S(1)}, s32[1,2]{1,0:T(1,128)}, u32[]{:S(2)}) copy-start(s32[1,2]{1,0:T(1,128)} %refs_2_.4) | copy-start | bytes 28
  1.8 5.4 %copy-start = (bf16[1,32,128,128]{3,2,1,0:T(8,128)(2,1)S(1)}, bf16[1,32,128,128]{3,2,1,0:T(8,128)(2,1)}, u32[]{:S(2)}) copy-start(bf16[1,32,128,128]{3,2,1,0:T(8,128)(2,1)} %refs_2_.5) | copy-start | bytes 3145732
  1.8 5.4 %copy-start.1 = (bf16[1,32,128,128]{3,2,1,0:T(8,128)(2,1)S(1)}, bf16[1,32,128,128]{3,2,1,0:T(8,128)(2,1)}, u32[]{:S(2)}) copy-start(bf16[1,32,128,128]{3,2,1,0:T(8,128)(2,1)} %refs_3_.5) | copy-start | bytes 3145732
  1.8 5.4 %copy-start.6 = (bf16[1,2,8,4096]{3,2,1,0:T(8,128)(2,1)S(1)}, bf16[1,2,8,4096]{3,2,1,0:T(8,128)(2,1)}, u32[]{:S(2)}) copy-start(bf16[1,2,8,4096]{3,2,1,0:T(8,128)(2,1)} %refs_13_.1) | copy-start | bytes 393220
  1.8 5.4 %copy-start.9 = (bf16[1,8,4096]{2,1,0:T(8,128)(2,1)S(1)}, bf16[1,8,4096]{2,1,0:T(8,128)(2,1)}, u32[]{:S(2)}) copy-start(bf16[1,8,4096]{2,1,0:T(8,128)(2,1)} %refs_11_.1) | copy-start | bytes 196612
  1.8 5.4 %copy-start.10 = (bf16[1,8,4096]{2,1,0:T(8,128)(2,1)S(1)}, bf16[1,8,4096]{2,1,0:T(8,128)(2,1)}, u32[]{:S(2)}) copy-start(bf16[1,8,4096]{2,1,0:T(8,128)(2,1)} %refs_12_.1) | copy-start | bytes 196612
  2.6 18.2 %collective-permute-start.2 = (bf16[5,16,1024]{2,1,0:T(8,128)(2,1)S(1)}, bf16[5,16,1024]{2,1,0:T(8,128)(2,1)S(1)}, u32[]{:S(2)}, u32[]{:S(2)}) collective-permute-start(bf16[5,16,1024]{2,1,0:T(8,128)(2,1)S(1)} %get-tuple-element.34), channel_id=1, source_target_pairs={{0,1},{1,0},{2,3},{3,2},{4,5},{5,4},{6,7},{7,6},{8,9},{9,8},{10,11... | collective-permute-start | bytes 491528 | tf_op jit(solution)/shard_map/ppermute | solution.py:284
  5.6 16.6 %collective-permute-start.3 = (bf16[5,16,1024]{2,1,0:T(8,128)(2,1)S(1)}, bf16[5,16,1024]{2,1,0:T(8,128)(2,1)S(1)}, u32[]{:S(2)}, u32[]{:S(2)}) collective-permute-start(bf16[5,16,1024]{2,1,0:T(8,128)(2,1)S(1)} %get-tuple-element.35), channel_id=1, source_target_pairs={{0,2},{1,3},{2,0},{3,1},{4,6},{5,7},{6,4},{7,5},{8,10},{9,11},{10,... | collective-permute-start | bytes 491528 | tf_op jit(solution)/shard_map/ppermute | solution.py:284
  7.1 15.1 %collective-permute-start.4 = (bf16[5,16,1024]{2,1,0:T(8,128)(2,1)S(1)}, bf16[5,16,1024]{2,1,0:T(8,128)(2,1)S(1)}, u32[]{:S(2)}, u32[]{:S(2)}) collective-permute-start(bf16[5,16,1024]{2,1,0:T(8,128)(2,1)S(1)} %get-tuple-element.36), channel_id=1, source_target_pairs={{0,3},{1,2},{2,1},{3,0},{4,7},{5,6},{6,5},{7,4},{8,11},{9,10},{10,... | collective-permute-start | bytes 491528 | tf_op jit(solution)/shard_map/ppermute | solution.py:284
  12.2 3.8 %collective-permute-start = (bf16[16,4096]{1,0:T(8,128)(2,1)S(1)}, bf16[16,4096]{1,0:T(8,128)(2,1)S(1)}, u32[]{:S(2)}, u32[]{:S(2)}) collective-permute-start(bf16[16,4096]{1,0:T(8,128)(2,1)S(1)} %get-tuple-element.30), channel_id=1, source_target_pairs={{0,4},{4,0},{8,12},{12,8},{16,20},{20,16},{24,28},{28,24},{1,5},{5... | collective-permute-start | bytes 393224 | tf_op jit(solution)/shard_map/ppermute | solution.py:30
  12.3 7.1 %collective-permute-start.1 = (bf16[16,4096]{1,0:T(8,128)(2,1)S(1)}, bf16[16,4096]{1,0:T(8,128)(2,1)S(1)}, u32[]{:S(2)}, u32[]{:S(2)}) collective-permute-start(bf16[16,4096]{1,0:T(8,128)(2,1)S(1)} %get-tuple-element.31), channel_id=1, source_target_pairs={{0,28},{4,8},{8,4},{12,16},{16,12},{20,24},{24,20},{28,0},{1,29},{... | collective-permute-start | bytes 393224 | tf_op jit(solution)/shard_map/ppermute | solution.py:29
  16.0 11.2 %collective-permute-start.7 = (bf16[5,16,1024]{2,1,0:T(8,128)(2,1)S(1)}, bf16[5,16,1024]{2,1,0:T(8,128)(2,1)S(1)}, u32[]{:S(2)}, u32[]{:S(2)}) collective-permute-start(bf16[5,16,1024]{2,1,0:T(8,128)(2,1)S(1)} %get-tuple-element.40), channel_id=1, source_target_pairs={{0,1},{1,0},{2,3},{3,2},{4,5},{5,4},{6,7},{7,6},{8,9},{9,8},{10,11... | collective-permute-start | bytes 491528 | tf_op jit(solution)/shard_map/ppermute | solution.py:284
  19.4 8.1 %collective-permute-start.8 = (bf16[5,16,1024]{2,1,0:T(8,128)(2,1)S(1)}, bf16[5,16,1024]{2,1,0:T(8,128)(2,1)S(1)}, u32[]{:S(2)}, u32[]{:S(2)}) collective-permute-start(bf16[5,16,1024]{2,1,0:T(8,128)(2,1)S(1)} %get-tuple-element.41), channel_id=1, source_target_pairs={{0,2},{1,3},{2,0},{3,1},{4,6},{5,7},{6,4},{7,5},{8,10},{9,11},{10,... | collective-permute-start | bytes 491528 | tf_op jit(solution)/shard_map/ppermute | solution.py:284
  20.8 6.7 %collective-permute-start.9 = (bf16[5,16,1024]{2,1,0:T(8,128)(2,1)S(1)}, bf16[5,16,1024]{2,1,0:T(8,128)(2,1)S(1)}, u32[]{:S(2)}, u32[]{:S(2)}) collective-permute-start(bf16[5,16,1024]{2,1,0:T(8,128)(2,1)S(1)} %get-tuple-element.42), channel_id=1, source_target_pairs={{0,3},{1,2},{2,1},{3,0},{4,7},{5,6},{6,5},{7,4},{8,11},{9,10},{10,... | collective-permute-start | bytes 491528 | tf_op jit(solution)/shard_map/ppermute | solution.py:284
  24.8 10.9 %collective-permute-start.5 = (bf16[16,4096]{1,0:T(8,128)(2,1)S(1)}, bf16[16,4096]{1,0:T(8,128)(2,1)S(1)}, u32[]{:S(2)}, u32[]{:S(2)}) collective-permute-start(bf16[16,4096]{1,0:T(8,128)(2,1)S(1)} %get-tuple-element.37), channel_id=1, source_target_pairs={{0,4},{4,0},{8,12},{12,8},{16,20},{20,16},{24,28},{28,24},{1,5},{5... | collective-permute-start | bytes 393224 | tf_op jit(solution)/shard_map/ppermute | solution.py:30
  24.9 10.9 %collective-permute-start.6 = (bf16[16,4096]{1,0:T(8,128)(2,1)S(1)}, bf16[16,4096]{1,0:T(8,128)(2,1)S(1)}, u32[]{:S(2)}, u32[]{:S(2)}) collective-permute-start(bf16[16,4096]{1,0:T(8,128)(2,1)S(1)} %get-tuple-element.38), channel_id=1, source_target_pairs={{0,28},{4,8},{8,4},{12,16},{16,12},{20,24},{24,20},{28,0},{1,29},{... | collective-permute-start | bytes 393224 | tf_op jit(solution)/shard_map/ppermute | solution.py:29
  27.9 4.3 %collective-permute-start.10 = (bf16[2,16,1024]{2,1,0:T(8,128)(2,1)S(1)}, bf16[2,16,1024]{2,1,0:T(8,128)(2,1)S(1)}, u32[]{:S(2)}, u32[]{:S(2)}) collective-permute-start(bf16[2,16,1024]{2,1,0:T(8,128)(2,1)S(1)} %get-tuple-element.49), channel_id=1, source_target_pairs={{0,1},{1,0},{2,3},{3,2},{4,5},{5,4},{6,7},{7,6},{8,9},{9,8},{10,11... | collective-permute-start | bytes 196616 | tf_op jit(solution)/shard_map/ppermute | solution.py:284
  29.4 4.3 %collective-permute-start.11 = (bf16[2,16,1024]{2,1,0:T(8,128)(2,1)S(1)}, bf16[2,16,1024]{2,1,0:T(8,128)(2,1)S(1)}, u32[]{:S(2)}, u32[]{:S(2)}) collective-permute-start(bf16[2,16,1024]{2,1,0:T(8,128)(2,1)S(1)} %get-tuple-element.50), channel_id=1, source_target_pairs={{0,2},{1,3},{2,0},{3,1},{4,6},{5,7},{6,4},{7,5},{8,10},{9,11},{10,... | collective-permute-start | bytes 196616 | tf_op jit(solution)/shard_map/ppermute | solution.py:284
  30.5 5.2 %collective-permute-start.12 = (bf16[2,16,1024]{2,1,0:T(8,128)(2,1)S(1)}, bf16[2,16,1024]{2,1,0:T(8,128)(2,1)S(1)}, u32[]{:S(2)}, u32[]{:S(2)}) collective-permute-start(bf16[2,16,1024]{2,1,0:T(8,128)(2,1)S(1)} %get-tuple-element.51), channel_id=1, source_target_pairs={{0,3},{1,2},{2,1},{3,0},{4,7},{5,6},{6,5},{7,4},{8,11},{9,10},{10,... | collective-permute-start | bytes 196616 | tf_op jit(solution)/shard_map/ppermute | solution.py:284
  (3 other events, 2.2 us)

commit v5 on v4

--- a/solution.py
+++ b/solution.py
@@ -10,6 +10,7 @@
 BF16 = jnp.bfloat16
 LIMIT = 40 * 1024 * 1024
 WORK = 10 ** 10
+LIGHT = 10 ** 4
 
 
 def partner(me, step, count):
@@ -89,20 +90,6 @@
     token[...] = jnp.zeros(token.shape, F32)
 
 
-def pack_ready(count, per, up_idx, order, g_ref, a_ref, back, second, second_tan, second_grad, *sends):
-    m0 = order[0, 0]
-    m1 = order[0, 1]
-    for step, place, j in send_order(lax.axis_index("dp"), count, per):
-        out, here = sends[step], lanes(place)
-        at = lanes(up_idx[0, j])
-        out[0, :, here] = stack([back[0, m0, :, at], second[0, m0, :, at]]).astype(BF16)
-        out[1, :, here] = stack([second_tan[0, m0, :, at], second_tan[0, m1, :, at]]).astype(BF16)
-        out[2, :, here] = stack([back[0, m1, :, at], second[0, m1, :, at]]).astype(BF16)
-        at = lanes(j)
-        out[3, :, here] = stack([g_ref[0, :, at], a_ref[0, :, at]]).astype(BF16)
-        out[4, :, here] = stack([second_grad[0, m0, :, at], second_grad[0, m1, :, at]]).astype(BF16)
-
-
 def back_first(count, per, up_idx, down_idx, order, w_up, w_down, g_ref, a_ref, back, second, second_tan,
                second_grad, pack, keep, sends, pulled, returned, hidden):
     blocks = count * per
@@ -116,6 +103,8 @@
     for step, place, i in send_order(me, count, per):
         at = lanes(i)
         c = stack([g_ref[0, :, at], a_ref[0, :, at], second_grad[0, m0, :, at], second_grad[0, m1, :, at]]).astype(BF16)
+        sends[step][8, :, lanes(place)] = c[0:16]
+        sends[step][9, :, lanes(place)] = c[16:32]
         target = down_idx[0, i]
         pulled[target] = pulled[target] + times_transposed(c, w_down[0, i])
     for step, place, j in send_order(me, count, per):
@@ -125,6 +114,8 @@
                    second_tan[0, m1, :, at], back[0, m1, :, at], second[0, m1, :, at]]).astype(BF16)
         out = sends[step]
         here = lanes(place)
+        for group in range(3):
+            out[group, :, here] = x[16 * group:16 * group + 16]
         z = times(x, w_up[0, j])
         zb0, za0, ta0, ta1, zb1, za1 = (z[8 * k:8 * k + 8] for k in range(6))
         pg, pa, ga0, ga1 = (pulled[j, 8 * k:8 * k + 8] for k in range(4))
@@ -135,8 +126,8 @@
         curve_a1 = sa1 * (1.0 - sa1) * (2.0 + za1 * (1.0 - 2.0 * sa1))
         push = slope_a0 * pa + curve_a0 * ga0 * ta0
         e = jnp.concatenate([slope_of(zb0, sb0) * pg, push], 0).astype(BF16)
-        out[0, :, here] = e
-        out[1, :, here] = jnp.concatenate([slope_a0 * ga0, slope_a1 * ga1], 0).astype(BF16)
+        out[3, :, here] = e
+        out[4, :, here] = jnp.concatenate([slope_a0 * ga0, slope_a1 * ga1], 0).astype(BF16)
         hidden[j] = jnp.concatenate(
             [zb0 * sb0, za0 * sa0, slope_a0 * ta0, slope_a1 * ta1, zb1 * sb1, za1 * sa1], 0).astype(BF16)
         keep[j] = jnp.concatenate([slope_of(zb1, sb1), slope_a1, curve_a1 * ga1 * ta1], 0)
@@ -146,7 +137,7 @@
     for step, place, i in send_order(me, count, per):
         y = hidden[down_idx[0, i]]
         for group in range(3):
-            sends[step][2 + group, :, lanes(place)] = y[16 * group:16 * group + 16]
+            sends[step][5 + group, :, lanes(place)] = y[16 * group:16 * group + 16]
 
 
 def forward_first(blocks, up_idx, down_idx, order, w_up, w_down, v_ref, t_ref, tan, pack, keep, hidden):
@@ -214,23 +205,21 @@
 
 
 def early_grads(count, per, *refs):
-    ready, early, late = refs[:count], refs[count:2 * count], refs[2 * count:3 * count]
-    grads, sends = refs[3 * count], refs[3 * count + 1:]
+    early, late = refs[:count], refs[count:2 * count]
+    grads, sends = refs[2 * count], refs[2 * count + 1:]
     for source in range(count):
         sends[source][...] = late[source][...]
     for place in range(per):
         at = lanes(place)
-        for out in range(2):
-            left, right = (ready, early) if out == 0 else (early, ready)
-            first_left, first_right = (0, 0) if out == 0 else (2, 3)
-            xs = [left[source][first_left + k, :, at] for source in range(count) for k in range(2)]
-            es = [right[source][first_right + k, :, at] for source in range(count) for k in range(2)]
+        for out, left, right in ((0, 0, 3), (1, 5, 8)):
+            xs = [early[source][left + k, :, at] for source in range(count) for k in range(2)]
+            es = [early[source][right + k, :, at] for source in range(count) for k in range(2)]
             grads[out, place] = outer(xs, es)
 
 
 def finish(count, per, scale, near, far, grads, *rest):
-    ready, early, late = rest[:count], rest[count:2 * count], rest[2 * count:3 * count]
-    values, score, tangent, adjoint, grad_up, grad_down, came = rest[3 * count:]
+    early, late = rest[:count], rest[count:2 * count]
+    values, score, tangent, adjoint, grad_up, grad_down, came = rest[2 * count:]
     take_in(near, far, came)
     moved = came[0].astype(F32)
     values[0] = moved[0:8].astype(BF16)
@@ -240,13 +229,13 @@
     adjoint[0] = moved[8:16].astype(BF16)
     for place in range(per):
         at = lanes(place)
-        for k, (out, left, group) in enumerate(((grad_up, ready, 2), (grad_down, early, 4))):
-            xs = [left[source][group, :, at] for source in range(count)]
+        for k, (out, group) in enumerate(((grad_up, 2), (grad_down, 7))):
+            xs = [early[source][group, :, at] for source in range(count)]
             es = [late[source][k, :, at] for source in range(count)]
             out[0, place] = ((grads[k, place] + outer(xs, es)) * scale).astype(BF16)
 
 
-def call(body, operands, spaces, outs, scratch, after=()):
+def call(body, operands, spaces, outs, scratch, after=(), cost=LIGHT):
     taken = len(operands)
 
     def kernel(*refs):
@@ -259,7 +248,7 @@
         out_specs=[pl.BlockSpec(memory_space=pltpu.VMEM)] * len(outs),
         scratch_shapes=scratch,
         compiler_params=pltpu.CompilerParams(vmem_limit_bytes=LIMIT),
-        cost_estimate=pl.CostEstimate(flops=WORK, bytes_accessed=WORK // 100, transcendentals=0),
+        cost_estimate=pl.CostEstimate(flops=cost, bytes_accessed=cost // 100, transcendentals=0),
     )(*operands, *after)
 
 
@@ -284,21 +273,16 @@
         return [parts[0]] + [lax.ppermute(parts[step], "dp", swap_route(step, count)) for step in range(1, count)]
 
     rows = (score_grad_in, state_adjoint_in, saved_back, saved_second, saved_second_tan, saved_second_grad)
-    five = shape((5, 16, part), BF16)
-    (token,) = call(open_launch, (), [], [shape((8, BLOCK), F32)], [])
-    ready = call(
-        body(pack_ready, count, per), (up_index, tick_order) + rows, [smem] * 2 + [vmem] * 6, [five] * count, [],
-        after=(token,))
-    packed = ready[0]
-    ready = to_replicas(ready)
+    ten = shape((10, 16, part), BF16)
+    (token,) = call(open_launch, (), [], [shape((8, BLOCK), F32)], [], cost=WORK)
     near, far, keep, keep_tan, *early = call(
         body(first_tick, count, per),
         (up_index, down_index, tick_order, w_up, w_down) + rows + (values_in, tangent_in, saved_tan),
         [smem] * 3 + [vmem] * 11,
-        [pair, pair, shape((blocks, 24, BLOCK), F32), shape((blocks, 8, BLOCK), F32)] + [five] * count,
+        [pair, pair, shape((blocks, 24, BLOCK), F32), shape((blocks, 8, BLOCK), F32)] + [ten] * count,
         [vmem((2, 16, width), BF16), vmem((blocks, 32, BLOCK), F32), vmem((blocks, 16, BLOCK), F32),
          vmem((blocks, 48, BLOCK), BF16), vmem((blocks, 16, BLOCK), BF16)],
-        after=(packed,))
+        after=(token,), cost=WORK)
     near, far = swap_sections(near, far)
     early = to_replicas(early)
     near, far, *late = call(
@@ -306,18 +290,17 @@
         [smem] * 2 + [vmem] * 6,
         [pair, pair] + [shape((2, 16, part), BF16)] * count,
         [vmem((2, 16, width), BF16), vmem((2, 16, width), BF16), vmem((blocks, 16, BLOCK), F32),
-         vmem((blocks, 16, BLOCK), F32), vmem((blocks, 16, BLOCK), BF16)],
-        after=tuple(ready[1:]))
+         vmem((blocks, 16, BLOCK), F32), vmem((blocks, 16, BLOCK), BF16)])
     near, far = swap_sections(near, far)
     two = shape((2, 16, part), BF16)
     grads, *late = call(
-        body(early_grads, count, per), (*ready, *early, *late), [vmem] * (3 * count),
+        body(early_grads, count, per), (*early, *late), [vmem] * (2 * count),
         [shape((2, per, BLOCK, BLOCK), F32)] + [two] * count, [])
     late = to_replicas(late)
     stream = shape((1,) + values_in.shape[1:], BF16)
     grad = shape((1, per, BLOCK, BLOCK), BF16)
     return tuple(call(
-        body(finish, count, per, scale), (near, far, grads, *ready, *early, *late), [vmem] * (3 + 3 * count),
+        body(finish, count, per, scale), (near, far, grads, *early, *late), [vmem] * (3 + 2 * count),
         [stream, stream, stream, stream, grad, grad], [vmem((2, 16, width), BF16)]))
 
 

time: 37.1 us -> 35 us (0.943)
  starting transfers between devices: 18.5 us -> 15.3 us
  waiting for transfers between devices: 6.58 us -> 8.69 us
  Pallas kernels: 9.31 us -> 8.5 us
    ppermute x9 -> x6, starting transfers between devices: 12.3 us -> 8.1 us  [to_replicas(): lax.ppermute(parts[step], 'dp', swap_route(step, count))]
    ppermute x2, waiting for transfers between devices: 1.98 us -> 3.35 us  [swap_sections(): lax.ppermute(far, 'section', [(i, (i + 2 * (i % 2) - 1) % count) for i in...]
    ppermute x2, starting transfers between devices: 6.05 us -> 7.09 us  [swap_sections(): lax.ppermute(far, 'section', [(i, (i + 2 * (i % 2) - 1) % count) for i in...]
    pallas_call x6 -> x5, Pallas kernels: 9.31 us -> 8.5 us  [call(): pl.pallas_call(kernel, out_shape=outs, in_specs=[pl.BlockSpec(memory_spac...]
    ppermute x9 -> x6, waiting for transfers between devices: 4.59 us -> 5.33 us  [to_replicas(): lax.ppermute(parts[step], 'dp', swap_route(step, count))]
  transfers between devices with their start and end apart: 13 -> 10, of which waited for: 5 -> 5; matrix products, arithmetic and copies ran while one was open for 0% -> 0% of each run, Pallas kernels for 20% -> 8%
where the time goes in v5:
time: 35 us; the launch traced here: 34.9 us
  starting transfers between devices  15.3 us (44%)
  waiting for transfers between devices  8.69 us (25%)
  Pallas kernels  8.5 us (24%)
  local copies, waits for them, and re-layouts  1.63 us (5%)
  between operations  0.79 us (2%)
    pallas_call x5, Pallas kernels, call(): pl.pallas_call(kernel, out_shape=outs, in_specs=[pl.BlockSpec(memory_spac...  8.5 us
    ppermute x6, starting transfers between devices, to_replicas(): lax.ppermute(parts[step], 'dp', swap_route(step, count))  8.1 us
    ppermute x2, starting transfers between devices, swap_sections(): lax.ppermute(far, 'section', [(i, (i + 2 * (i % 2) - 1) % count) for i in...  7.09 us
    ppermute x6, waiting for transfers between devices, to_replicas(): lax.ppermute(parts[step], 'dp', swap_route(step, count))  5.33 us
    ppermute x2, waiting for transfers between devices, swap_sections(): lax.ppermute(far, 'section', [(i, (i + 2 * (i % 2) - 1) % count) for i in...  3.35 us
    unnamed x28, local copies, waits for them, and re-layouts  1.63 us
  transfers between devices with their start and end apart: 10, of which 5 were waited for; matrix products, arithmetic and copies ran while one was open for 0% of the time, Pallas kernels for 8%

profile of v5, /device:TPU:0, one launch (start us, length us, event | category | flops | bytes accessed | tf_op | source)
XLA Modules:
  0.0 34.9 jit_solution(8069846558058749080)
XLA Ops:
  0.8 0.5 %copy-done.3 = s32[1,32]{1,0:T(1,128)S(1)} copy-done((s32[1,32]{1,0:T(1,128)S(1)}, s32[1,32]{1,0:T(1,128)}, u32[]{:S(2)}) %copy-start.3) | copy-done | bytes 152
  1.3 0.6 %copy-done.1 = bf16[1,32,128,128]{3,2,1,0:T(8,128)(2,1)S(1)} copy-done((bf16[1,32,128,128]{3,2,1,0:T(8,128)(2,1)S(1)}, bf16[1,32,128,128]{3,2,1,0:T(8,128)(2,1)}, u32[]{:S(2)}) %copy-start.1) | copy-done | bytes 1048600
  1.9 0.3 copy-done
  2.2 0.0 copy-done.6
  2.2 0.0 copy-done.5
  2.3 0.0 copy-done.8
  2.3 0.0 copy-done.4
  2.4 4.5 %shard_map.182 = (bf16[16,4096]{1,0:T(8,128)(2,1)S(1)}, bf16[16,4096]{1,0:T(8,128)(2,1)S(1)}, f32[32,24,128]{2,1,0:T(8,128)S(1)}, f32[32,8,128]{2,1,0:T(8,128)S(...) custom-call(s32[1,32]{1,0:T(1,128)S(1)} %copy-done.2, ...), custom_call_target="tpu_custom_call" | custom-call | flops 10000000000 | bytes 100000000 | tf_op jit(solution)/shard_map/pallas_call | solution.py:244
  6.9 3.0 %collective-permute-start.4 = (bf16[10,16,1024]{2,1,0:T(8,128)(2,1)S(1)}, bf16[10,16,1024]{2,1,0:T(8,128)(2,1)S(1)}, u32[]{:S(2)}, u32[]{:S(2)}) collective-permute-start(bf16[10,16,1024]{2,1,0:T(8,128)(2,1)S(1)} %get-tuple-element.32), channel_id=1, source_target_pairs={{0,1},{1,0},{2,3},{3,2},{4,5},{5,4},{6,7},{7,6},{8,9},{9,8},{10,11... | collective-permute-start | bytes 983048 | tf_op jit(solution)/shard_map/ppermute | solution.py:273
  9.9 1.5 %collective-permute-start.5 = (bf16[10,16,1024]{2,1,0:T(8,128)(2,1)S(1)}, bf16[10,16,1024]{2,1,0:T(8,128)(2,1)S(1)}, u32[]{:S(2)}, u32[]{:S(2)}) collective-permute-start(bf16[10,16,1024]{2,1,0:T(8,128)(2,1)S(1)} %get-tuple-element.33), channel_id=1, source_target_pairs={{0,2},{1,3},{2,0},{3,1},{4,6},{5,7},{6,4},{7,5},{8,10},{9,11},{10,... | collective-permute-start | bytes 983048 | tf_op jit(solution)/shard_map/ppermute | solution.py:273
  11.4 4.2 %collective-permute-start.1 = (bf16[16,4096]{1,0:T(8,128)(2,1)S(1)}, bf16[16,4096]{1,0:T(8,128)(2,1)S(1)}, u32[]{:S(2)}, u32[]{:S(2)}) collective-permute-start(bf16[16,4096]{1,0:T(8,128)(2,1)S(1)} %get-tuple-element.26), channel_id=1, source_target_pairs={{0,28},{4,8},{8,4},{12,16},{16,12},{20,24},{24,20},{28,0},{1,29},{... | collective-permute-start | bytes 393224 | tf_op jit(solution)/shard_map/ppermute | solution.py:30
  15.6 3.3 %collective-permute-done.1.refs_5_ = bf16[16,4096]{1,0:T(8,128)(2,1)S(1)} collective-permute-done((bf16[16,4096]{1,0:T(8,128)(2,1)S(1)}, bf16[16,4096]{1,0:T(8,128)(2,1)S(1)}, u32[]{:S(2)}, u32[]{:S(2)}) %collective-permute-start.1) | collective-permute-done | bytes 131104 | tf_op jit(solution)/shard_map/ppermute | solution.py:30
  18.9 2.5 %shard_map.183 = (bf16[16,4096]{1,0:T(8,128)(2,1)S(1)}, bf16[16,4096]{1,0:T(8,128)(2,1)S(1)}, bf16[2,16,1024]{2,1,0:T(8,128)(2,1)S(1)}, bf16[2,16,1024]{2,1,0:T(...) custom-call(s32[1,32]{1,0:T(1,128)S(1)} %copy-done.2, s32[1,32]{1,0:T(1,128)S(1)} %copy-done.3, ...), custom_call_target="tpu_custom_call" | custom-call | flops 10000 | bytes 100 | tf_op jit(solution)/shard_map/pallas_call | solution.py:244
  21.5 0.1 collective-permute-start.2
  21.5 2.9 %collective-permute-start.3 = (bf16[16,4096]{1,0:T(8,128)(2,1)S(1)}, bf16[16,4096]{1,0:T(8,128)(2,1)S(1)}, u32[]{:S(2)}, u32[]{:S(2)}) collective-permute-start(bf16[16,4096]{1,0:T(8,128)(2,1)S(1)} %get-tuple-element.30), channel_id=1, source_target_pairs={{0,28},{4,8},{8,4},{12,16},{16,12},{20,24},{24,20},{28,0},{1,29},{... | collective-permute-start | bytes 393224 | tf_op jit(solution)/shard_map/ppermute | solution.py:30
  24.5 1.6 %collective-permute-done.5.refs_2_.refs_5_ = bf16[10,16,1024]{2,1,0:T(8,128)(2,1)S(1)} collective-permute-done((bf16[10,16,1024]{2,1,0:T(8,128)(2,1)S(1)}, bf16[10,16,1024]{2,1,0:T(8,128)(2,1)S(1)}, u32[]{:S(2)}, u32[]{:S(2)}) %collective-permute-start.5) | collective-permute-done | bytes 327712 | tf_op jit(solution)/shard_map/ppermute | solution.py:273
  26.1 0.3 shard_map.184
  26.4 1.3 %collective-permute-start.7 = (bf16[2,16,1024]{2,1,0:T(8,128)(2,1)S(1)}, bf16[2,16,1024]{2,1,0:T(8,128)(2,1)S(1)}, u32[]{:S(2)}, u32[]{:S(2)}) collective-permute-start(bf16[2,16,1024]{2,1,0:T(8,128)(2,1)S(1)} %get-tuple-element.41), channel_id=1, source_target_pairs={{0,1},{1,0},{2,3},{3,2},{4,5},{5,4},{6,7},{7,6},{8,9},{9,8},{10,11... | collective-permute-start | bytes 196616 | tf_op jit(solution)/shard_map/ppermute | solution.py:273
  27.7 0.8 %collective-permute-start.8 = (bf16[2,16,1024]{2,1,0:T(8,128)(2,1)S(1)}, bf16[2,16,1024]{2,1,0:T(8,128)(2,1)S(1)}, u32[]{:S(2)}, u32[]{:S(2)}) collective-permute-start(bf16[2,16,1024]{2,1,0:T(8,128)(2,1)S(1)} %get-tuple-element.42), channel_id=1, source_target_pairs={{0,2},{1,3},{2,0},{3,1},{4,6},{5,7},{6,4},{7,5},{8,10},{9,11},{10,... | collective-permute-start | bytes 196616 | tf_op jit(solution)/shard_map/ppermute | solution.py:273
  28.5 1.4 %collective-permute-start.9 = (bf16[2,16,1024]{2,1,0:T(8,128)(2,1)S(1)}, bf16[2,16,1024]{2,1,0:T(8,128)(2,1)S(1)}, u32[]{:S(2)}, u32[]{:S(2)}) collective-permute-start(bf16[2,16,1024]{2,1,0:T(8,128)(2,1)S(1)} %get-tuple-element.43), channel_id=1, source_target_pairs={{0,3},{1,2},{2,1},{3,0},{4,7},{5,6},{6,5},{7,4},{8,11},{9,10},{10,... | collective-permute-start | bytes 196616 | tf_op jit(solution)/shard_map/ppermute | solution.py:273
  30.0 1.3 %collective-permute-done.7.refs_8_ = bf16[2,16,1024]{2,1,0:T(8,128)(2,1)S(1)} collective-permute-done((bf16[2,16,1024]{2,1,0:T(8,128)(2,1)S(1)}, bf16[2,16,1024]{2,1,0:T(8,128)(2,1)S(1)}, u32[]{:S(2)}, u32[]{:S(2)}) %collective-permute-start.7) | collective-permute-done | bytes 65568 | tf_op jit(solution)/shard_map/ppermute | solution.py:273
  31.3 0.7 %collective-permute-done.8.refs_9_ = bf16[2,16,1024]{2,1,0:T(8,128)(2,1)S(1)} collective-permute-done((bf16[2,16,1024]{2,1,0:T(8,128)(2,1)S(1)}, bf16[2,16,1024]{2,1,0:T(8,128)(2,1)S(1)}, u32[]{:S(2)}, u32[]{:S(2)}) %collective-permute-start.8) | collective-permute-done | bytes 65568 | tf_op jit(solution)/shard_map/ppermute | solution.py:273
  32.0 1.7 %collective-permute-done.9.refs_10_ = bf16[2,16,1024]{2,1,0:T(8,128)(2,1)S(1)} collective-permute-done((bf16[2,16,1024]{2,1,0:T(8,128)(2,1)S(1)}, bf16[2,16,1024]{2,1,0:T(8,128)(2,1)S(1)}, u32[]{:S(2)}, u32[]{:S(2)}) %collective-permute-start.9) | collective-permute-done | bytes 65568 | tf_op jit(solution)/shard_map/ppermute | solution.py:273
  33.7 1.2 %shard_map.185 = (bf16[1,8,4096]{2,1,0:T(8,128)(2,1)}, bf16[1,8,4096]{2,1,0:T(8,128)(2,1)}, bf16[1,8,4096]{2,1,0:T(8,128)(2,1)}, bf16[1,8,4096]{2,1,0:T(8,128)(2...) custom-call(bf16[16,4096]{1,0:T(8,128)(2,1)S(1)} %collective-permute-done.2.refs_0_, ...), custom_call_target="tpu_custom_call" | custom-call | flops 10000 | bytes 100 | tf_op jit(solution)/shard_map/pallas_call | solution.py:244
  (29 shorter events, 0.1 us)
Async XLA Ops:
  0.6 0.7 %copy-start.3 = (s32[1,32]{1,0:T(1,128)S(1)}, s32[1,32]{1,0:T(1,128)}, u32[]{:S(2)}) copy-start(s32[1,32]{1,0:T(1,128)} %refs_1_.3) | copy-start | bytes 388
  0.6 1.2 %copy-start.1 = (bf16[1,32,128,128]{3,2,1,0:T(8,128)(2,1)S(1)}, bf16[1,32,128,128]{3,2,1,0:T(8,128)(2,1)}, u32[]{:S(2)}) copy-start(bf16[1,32,128,128]{3,2,1,0:T(8,128)(2,1)} %refs_3_.3) | copy-start | bytes 3145732
  0.7 1.2 %copy-start.2 = (s32[1,32]{1,0:T(1,128)S(1)}, s32[1,32]{1,0:T(1,128)}, u32[]{:S(2)}) copy-start(s32[1,32]{1,0:T(1,128)} %refs_0_.3) | copy-start | bytes 388
  0.7 1.5 %copy-start = (bf16[1,32,128,128]{3,2,1,0:T(8,128)(2,1)S(1)}, bf16[1,32,128,128]{3,2,1,0:T(8,128)(2,1)}, u32[]{:S(2)}) copy-start(bf16[1,32,128,128]{3,2,1,0:T(8,128)(2,1)} %refs_2_.3) | copy-start | bytes 3145732
  0.7 1.5 %copy-start.7 = (bf16[1,2,8,4096]{3,2,1,0:T(8,128)(2,1)S(1)}, bf16[1,2,8,4096]{3,2,1,0:T(8,128)(2,1)}, u32[]{:S(2)}) copy-start(bf16[1,2,8,4096]{3,2,1,0:T(8,128)(2,1)} %refs_10_.1) | copy-start | bytes 393220
  0.7 1.6 %copy-start.6 = (bf16[1,2,8,4096]{3,2,1,0:T(8,128)(2,1)S(1)}, bf16[1,2,8,4096]{3,2,1,0:T(8,128)(2,1)}, u32[]{:S(2)}) copy-start(bf16[1,2,8,4096]{3,2,1,0:T(8,128)(2,1)} %refs_9_.1) | copy-start | bytes 393220
  0.7 1.6 %copy-start.5 = (bf16[1,2,8,4096]{3,2,1,0:T(8,128)(2,1)S(1)}, bf16[1,2,8,4096]{3,2,1,0:T(8,128)(2,1)}, u32[]{:S(2)}) copy-start(bf16[1,2,8,4096]{3,2,1,0:T(8,128)(2,1)} %refs_8_.1) | copy-start | bytes 393220
  0.7 1.6 %copy-start.8 = (bf16[1,2,8,4096]{3,2,1,0:T(8,128)(2,1)S(1)}, bf16[1,2,8,4096]{3,2,1,0:T(8,128)(2,1)}, u32[]{:S(2)}) copy-start(bf16[1,2,8,4096]{3,2,1,0:T(8,128)(2,1)} %refs_13_.1) | copy-start | bytes 393220
  0.7 1.6 %copy-start.4 = (bf16[1,2,8,4096]{3,2,1,0:T(8,128)(2,1)S(1)}, bf16[1,2,8,4096]{3,2,1,0:T(8,128)(2,1)}, u32[]{:S(2)}) copy-start(bf16[1,2,8,4096]{3,2,1,0:T(8,128)(2,1)} %refs_7_.1) | copy-start | bytes 393220
  0.7 1.6 %copy-start.10 = (bf16[1,8,4096]{2,1,0:T(8,128)(2,1)S(1)}, bf16[1,8,4096]{2,1,0:T(8,128)(2,1)}, u32[]{:S(2)}) copy-start(bf16[1,8,4096]{2,1,0:T(8,128)(2,1)} %refs_6_.1) | copy-start | bytes 196612
  0.7 1.6 %copy-start.12 = (bf16[1,8,4096]{2,1,0:T(8,128)(2,1)S(1)}, bf16[1,8,4096]{2,1,0:T(8,128)(2,1)}, u32[]{:S(2)}) copy-start(bf16[1,8,4096]{2,1,0:T(8,128)(2,1)} %refs_12_.1) | copy-start | bytes 196612
  0.7 1.6 %copy-start.9 = (bf16[1,8,4096]{2,1,0:T(8,128)(2,1)S(1)}, bf16[1,8,4096]{2,1,0:T(8,128)(2,1)}, u32[]{:S(2)}) copy-start(bf16[1,8,4096]{2,1,0:T(8,128)(2,1)} %refs_5_.1) | copy-start | bytes 196612
  0.8 1.6 %copy-start.11 = (bf16[1,8,4096]{2,1,0:T(8,128)(2,1)S(1)}, bf16[1,8,4096]{2,1,0:T(8,128)(2,1)}, u32[]{:S(2)}) copy-start(bf16[1,8,4096]{2,1,0:T(8,128)(2,1)} %refs_11_.1) | copy-start | bytes 196612
  0.8 1.6 %copy-start.13 = (s32[1,2]{1,0:T(1,128)S(1)}, s32[1,2]{1,0:T(1,128)}, u32[]{:S(2)}) copy-start(s32[1,2]{1,0:T(1,128)} %refs_2_.2) | copy-start | bytes 28
  6.9 17.6 %collective-permute-start.4 = (bf16[10,16,1024]{2,1,0:T(8,128)(2,1)S(1)}, bf16[10,16,1024]{2,1,0:T(8,128)(2,1)S(1)}, u32[]{:S(2)}, u32[]{:S(2)}) collective-permute-start(bf16[10,16,1024]{2,1,0:T(8,128)(2,1)S(1)} %get-tuple-element.32), channel_id=1, source_target_pairs={{0,1},{1,0},{2,3},{3,2},{4,5},{5,4},{6,7},{7,6},{8,9},{9,8},{10,11... | collective-permute-start | bytes 983048 | tf_op jit(solution)/shard_map/ppermute | solution.py:273
  9.9 16.2 %collective-permute-start.5 = (bf16[10,16,1024]{2,1,0:T(8,128)(2,1)S(1)}, bf16[10,16,1024]{2,1,0:T(8,128)(2,1)S(1)}, u32[]{:S(2)}, u32[]{:S(2)}) collective-permute-start(bf16[10,16,1024]{2,1,0:T(8,128)(2,1)S(1)} %get-tuple-element.33), channel_id=1, source_target_pairs={{0,2},{1,3},{2,0},{3,1},{4,6},{5,7},{6,4},{7,5},{8,10},{9,11},{10,... | collective-permute-start | bytes 983048 | tf_op jit(solution)/shard_map/ppermute | solution.py:273
  11.4 14.7 %collective-permute-start.6 = (bf16[10,16,1024]{2,1,0:T(8,128)(2,1)S(1)}, bf16[10,16,1024]{2,1,0:T(8,128)(2,1)S(1)}, u32[]{:S(2)}, u32[]{:S(2)}) collective-permute-start(bf16[10,16,1024]{2,1,0:T(8,128)(2,1)S(1)} %get-tuple-element.34), channel_id=1, source_target_pairs={{0,3},{1,2},{2,1},{3,0},{4,7},{5,6},{6,5},{7,4},{8,11},{9,10},{10,... | collective-permute-start | bytes 983048 | tf_op jit(solution)/shard_map/ppermute | solution.py:273
  11.4 4.2 %collective-permute-start = (bf16[16,4096]{1,0:T(8,128)(2,1)S(1)}, bf16[16,4096]{1,0:T(8,128)(2,1)S(1)}, u32[]{:S(2)}, u32[]{:S(2)}) collective-permute-start(bf16[16,4096]{1,0:T(8,128)(2,1)S(1)} %get-tuple-element.25), channel_id=1, source_target_pairs={{0,4},{4,0},{8,12},{12,8},{16,20},{20,16},{24,28},{28,24},{1,5},{5... | collective-permute-start | bytes 393224 | tf_op jit(solution)/shard_map/ppermute | solution.py:31
  11.4 7.5 %collective-permute-start.1 = (bf16[16,4096]{1,0:T(8,128)(2,1)S(1)}, bf16[16,4096]{1,0:T(8,128)(2,1)S(1)}, u32[]{:S(2)}, u32[]{:S(2)}) collective-permute-start(bf16[16,4096]{1,0:T(8,128)(2,1)S(1)} %get-tuple-element.26), channel_id=1, source_target_pairs={{0,28},{4,8},{8,4},{12,16},{16,12},{20,24},{24,20},{28,0},{1,29},{... | collective-permute-start | bytes 393224 | tf_op jit(solution)/shard_map/ppermute | solution.py:30
  21.5 8.5 %collective-permute-start.2 = (bf16[16,4096]{1,0:T(8,128)(2,1)S(1)}, bf16[16,4096]{1,0:T(8,128)(2,1)S(1)}, u32[]{:S(2)}, u32[]{:S(2)}) collective-permute-start(bf16[16,4096]{1,0:T(8,128)(2,1)S(1)} %get-tuple-element.29), channel_id=1, source_target_pairs={{0,4},{4,0},{8,12},{12,8},{16,20},{20,16},{24,28},{28,24},{1,5},{5... | collective-permute-start | bytes 393224 | tf_op jit(solution)/shard_map/ppermute | solution.py:31
  21.5 8.4 %collective-permute-start.3 = (bf16[16,4096]{1,0:T(8,128)(2,1)S(1)}, bf16[16,4096]{1,0:T(8,128)(2,1)S(1)}, u32[]{:S(2)}, u32[]{:S(2)}) collective-permute-start(bf16[16,4096]{1,0:T(8,128)(2,1)S(1)} %get-tuple-element.30), channel_id=1, source_target_pairs={{0,28},{4,8},{8,4},{12,16},{16,12},{20,24},{24,20},{28,0},{1,29},{... | collective-permute-start | bytes 393224 | tf_op jit(solution)/shard_map/ppermute | solution.py:30
  26.4 4.9 %collective-permute-start.7 = (bf16[2,16,1024]{2,1,0:T(8,128)(2,1)S(1)}, bf16[2,16,1024]{2,1,0:T(8,128)(2,1)S(1)}, u32[]{:S(2)}, u32[]{:S(2)}) collective-permute-start(bf16[2,16,1024]{2,1,0:T(8,128)(2,1)S(1)} %get-tuple-element.41), channel_id=1, source_target_pairs={{0,1},{1,0},{2,3},{3,2},{4,5},{5,4},{6,7},{7,6},{8,9},{9,8},{10,11... | collective-permute-start | bytes 196616 | tf_op jit(solution)/shard_map/ppermute | solution.py:273
  27.7 4.3 %collective-permute-start.8 = (bf16[2,16,1024]{2,1,0:T(8,128)(2,1)S(1)}, bf16[2,16,1024]{2,1,0:T(8,128)(2,1)S(1)}, u32[]{:S(2)}, u32[]{:S(2)}) collective-permute-start(bf16[2,16,1024]{2,1,0:T(8,128)(2,1)S(1)} %get-tuple-element.42), channel_id=1, source_target_pairs={{0,2},{1,3},{2,0},{3,1},{4,6},{5,7},{6,4},{7,5},{8,10},{9,11},{10,... | collective-permute-start | bytes 196616 | tf_op jit(solution)/shard_map/ppermute | solution.py:273
  28.5 5.2 %collective-permute-start.9 = (bf16[2,16,1024]{2,1,0:T(8,128)(2,1)S(1)}, bf16[2,16,1024]{2,1,0:T(8,128)(2,1)S(1)}, u32[]{:S(2)}, u32[]{:S(2)}) collective-permute-start(bf16[2,16,1024]{2,1,0:T(8,128)(2,1)S(1)} %get-tuple-element.43), channel_id=1, source_target_pairs={{0,3},{1,2},{2,1},{3,0},{4,7},{5,6},{6,5},{7,4},{8,11},{9,10},{10,... | collective-permute-start | bytes 196616 | tf_op jit(solution)/shard_map/ppermute | solution.py:273

commit v6 on v5

--- a/solution.py
+++ b/solution.py
@@ -10,7 +10,7 @@
 BF16 = jnp.bfloat16
 LIMIT = 40 * 1024 * 1024
 WORK = 10 ** 10
-LIGHT = 10 ** 4
+LIGHT = 10 ** 9
 
 
 def partner(me, step, count):
@@ -205,10 +205,7 @@
 
 
 def early_grads(count, per, *refs):
-    early, late = refs[:count], refs[count:2 * count]
-    grads, sends = refs[2 * count], refs[2 * count + 1:]
-    for source in range(count):
-        sends[source][...] = late[source][...]
+    early, grads = refs[:count], refs[count]
     for place in range(per):
         at = lanes(place)
         for out, left, right in ((0, 0, 3), (1, 5, 8)):
@@ -250,6 +247,20 @@
         compiler_params=pltpu.CompilerParams(vmem_limit_bytes=LIMIT),
         cost_estimate=pl.CostEstimate(flops=cost, bytes_accessed=cost // 100, transcendentals=0),
     )(*operands, *after)
+
+
+def hold(arrays, until):
+    def kernel(*refs):
+        del refs
+
+    return pl.pallas_call(
+        kernel,
+        out_shape=[jax.ShapeDtypeStruct(x.shape, x.dtype) for x in arrays],
+        in_specs=[pl.BlockSpec(memory_space=pl.ANY)] * (len(arrays) + 1),
+        out_specs=[pl.BlockSpec(memory_space=pl.ANY)] * len(arrays),
+        input_output_aliases={k: k for k in range(len(arrays))},
+        cost_estimate=pl.CostEstimate(flops=LIGHT, bytes_accessed=LIGHT // 100, transcendentals=0),
+    )(*arrays, until)
 
 
 def on_device(w_up, up_index, w_down, down_index, tick_order, values_in, score_grad_in, tangent_in, state_adjoint_in,
@@ -292,11 +303,10 @@
         [vmem((2, 16, width), BF16), vmem((2, 16, width), BF16), vmem((blocks, 16, BLOCK), F32),
          vmem((blocks, 16, BLOCK), F32), vmem((blocks, 16, BLOCK), BF16)])
     near, far = swap_sections(near, far)
-    two = shape((2, 16, part), BF16)
-    grads, *late = call(
-        body(early_grads, count, per), (*early, *late), [vmem] * (2 * count),
-        [shape((2, per, BLOCK, BLOCK), F32)] + [two] * count, [])
+    late = hold(late, near)
     late = to_replicas(late)
+    (grads,) = call(
+        body(early_grads, count, per), tuple(early), [vmem] * count, [shape((2, per, BLOCK, BLOCK), F32)], [])
     stream = shape((1,) + values_in.shape[1:], BF16)
     grad = shape((1, per, BLOCK, BLOCK), BF16)
     return tuple(call(

time: 35 us -> 34.4 us (0.983)
  waiting for transfers between devices: 8.69 us -> 4.56 us
  local copies, waits for them, and re-layouts: 1.63 us -> 4.81 us
    ppermute x2, waiting for transfers between devices: 3.35 us -> 0.01 us  [swap_sections(): lax.ppermute(far, 'section', [(i, (i + 2 * (i % 2) - 1) % count) for i in...]
    unnamed x28 -> x42, local copies, waits for them, and re-layouts: 1.63 us -> 4.81 us
    ppermute x6, waiting for transfers between devices: 5.33 us -> 4.55 us  [to_replicas(): lax.ppermute(parts[step], 'dp', swap_route(step, count))]
    ppermute x6, starting transfers between devices: 8.1 us -> 7.58 us  [to_replicas(): lax.ppermute(parts[step], 'dp', swap_route(step, count))]
    ppermute x2, starting transfers between devices: 0.07 us -> 0.53 us  [swap_sections(): near = lax.ppermute(near, 'section', [(i, i ^ 1) for i in range(count)])]
  transfers between devices with their start and end apart: 10 -> 10, of which waited for: 5 -> 3; matrix products, arithmetic and copies ran while one was open for 0% -> 0% of each run, Pallas kernels for 8% -> 8%
where the time goes in v6:
time: 34.4 us; the launch traced here: 34.2 us
  starting transfers between devices  15.5 us (45%)
  Pallas kernels  8.5 us (25%)
  local copies, waits for them, and re-layouts  4.81 us (14%)
  waiting for transfers between devices  4.56 us (13%)
  between operations  0.81 us (2%)
    pallas_call x5, Pallas kernels, call(): pl.pallas_call(kernel, out_shape=outs, in_specs=[pl.BlockSpec(memory_spac...  8.5 us
    ppermute x6, starting transfers between devices, to_replicas(): lax.ppermute(parts[step], 'dp', swap_route(step, count))  7.58 us
    ppermute x2, starting transfers between devices, swap_sections(): lax.ppermute(far, 'section', [(i, (i + 2 * (i % 2) - 1) % count) for i in...  7.41 us
    unnamed x42, local copies, waits for them, and re-layouts  4.81 us
    ppermute x6, waiting for transfers between devices, to_replicas(): lax.ppermute(parts[step], 'dp', swap_route(step, count))  4.55 us
  transfers between devices with their start and end apart: 10, of which 3 were waited for; matrix products, arithmetic and copies ran while one was open for 0% of the time, Pallas kernels for 8%

profile of v6, /device:TPU:0, one launch (start us, length us, event | category | flops | bytes accessed | tf_op | source)
XLA Modules:
  0.0 34.2 jit_solution(16371147622406704553)
XLA Ops:
  0.8 0.5 %copy-done.18 = s32[1,32]{1,0:T(1,128)S(1)} copy-done((s32[1,32]{1,0:T(1,128)S(1)}, s32[1,32]{1,0:T(1,128)}, u32[]{:S(2)}) %copy-start.18) | copy-done | bytes 152
  1.3 0.6 %copy-done.1 = bf16[1,32,128,128]{3,2,1,0:T(8,128)(2,1)S(1)} copy-done((bf16[1,32,128,128]{3,2,1,0:T(8,128)(2,1)S(1)}, bf16[1,32,128,128]{3,2,1,0:T(8,128)(2,1)}, u32[]{:S(2)}) %copy-start.1) | copy-done | bytes 1048600
  1.9 0.3 copy-done
  2.4 4.5 %shard_map.182 = (bf16[16,4096]{1,0:T(8,128)(2,1)S(1)}, bf16[16,4096]{1,0:T(8,128)(2,1)S(1)}, f32[32,24,128]{2,1,0:T(8,128)S(1)}, f32[32,8,128]{2,1,0:T(8,128)S(...) custom-call(s32[1,32]{1,0:T(1,128)S(1)} %copy-done.17, ...), custom_call_target="tpu_custom_call" | custom-call | flops 10000000000 | bytes 100000000 | tf_op jit(solution)/shard_map/pallas_call | solution.py:241
  6.9 0.5 %collective-permute-start = (bf16[16,4096]{1,0:T(8,128)(2,1)S(1)}, bf16[16,4096]{1,0:T(8,128)(2,1)S(1)}, u32[]{:S(2)}, u32[]{:S(2)}) collective-permute-start(bf16[16,4096]{1,0:T(8,128)(2,1)S(1)} %get-tuple-element.24), channel_id=1, source_target_pairs={{0,4},{4,0},{8,12},{12,8},{16,20},{20,16},{24,28},{28,24},{1,5},{5... | collective-permute-start | bytes 393224 | tf_op jit(solution)/shard_map/ppermute | solution.py:31
  7.4 4.7 %collective-permute-start.1 = (bf16[16,4096]{1,0:T(8,128)(2,1)S(1)}, bf16[16,4096]{1,0:T(8,128)(2,1)S(1)}, u32[]{:S(2)}, u32[]{:S(2)}) collective-permute-start(bf16[16,4096]{1,0:T(8,128)(2,1)S(1)} %get-tuple-element.25), channel_id=1, source_target_pairs={{0,28},{4,8},{8,4},{12,16},{16,12},{20,24},{24,20},{28,0},{1,29},{... | collective-permute-start | bytes 393224 | tf_op jit(solution)/shard_map/ppermute | solution.py:30
  12.1 1.5 %collective-permute-start.4 = (bf16[10,16,1024]{2,1,0:T(8,128)(2,1)S(1)}, bf16[10,16,1024]{2,1,0:T(8,128)(2,1)S(1)}, u32[]{:S(2)}, u32[]{:S(2)}) collective-permute-start(bf16[10,16,1024]{2,1,0:T(8,128)(2,1)S(1)} %get-tuple-element.31), channel_id=1, source_target_pairs={{0,1},{1,0},{2,3},{3,2},{4,5},{5,4},{6,7},{7,6},{8,9},{9,8},{10,11... | collective-permute-start | bytes 983048 | tf_op jit(solution)/shard_map/ppermute | solution.py:284
  13.6 1.5 %collective-permute-start.5 = (bf16[10,16,1024]{2,1,0:T(8,128)(2,1)S(1)}, bf16[10,16,1024]{2,1,0:T(8,128)(2,1)S(1)}, u32[]{:S(2)}, u32[]{:S(2)}) collective-permute-start(bf16[10,16,1024]{2,1,0:T(8,128)(2,1)S(1)} %get-tuple-element.32), channel_id=1, source_target_pairs={{0,2},{1,3},{2,0},{3,1},{4,6},{5,7},{6,4},{7,5},{8,10},{9,11},{10,... | collective-permute-start | bytes 983048 | tf_op jit(solution)/shard_map/ppermute | solution.py:284
  15.1 0.5 %collective-permute-start.6 = (bf16[10,16,1024]{2,1,0:T(8,128)(2,1)S(1)}, bf16[10,16,1024]{2,1,0:T(8,128)(2,1)S(1)}, u32[]{:S(2)}, u32[]{:S(2)}) collective-permute-start(bf16[10,16,1024]{2,1,0:T(8,128)(2,1)S(1)} %get-tuple-element.33), channel_id=1, source_target_pairs={{0,3},{1,2},{2,1},{3,0},{4,7},{5,6},{6,5},{7,4},{8,11},{9,10},{10,... | collective-permute-start | bytes 983048 | tf_op jit(solution)/shard_map/ppermute | solution.py:284
  15.6 2.5 %shard_map.183 = (bf16[16,4096]{1,0:T(8,128)(2,1)S(1)}, bf16[16,4096]{1,0:T(8,128)(2,1)S(1)}, bf16[2,16,1024]{2,1,0:T(8,128)(2,1)S(1)}, bf16[2,16,1024]{2,1,0:T(...) custom-call(s32[1,32]{1,0:T(1,128)S(1)} %copy-done.17, s32[1,32]{1,0:T(1,128)S(1)} %copy-done.18, ...), custom_call_target="tpu_custom_call" | custom-call | flops 1000000000 | bytes 10000000 | tf_op jit(solution)/shard_map/pallas_call | solution.py:241
  18.1 0.6 %copy-done.13 = bf16[2,16,1024]{2,1,0:T(8,128)(2,1)} copy-done((bf16[2,16,1024]{2,1,0:T(8,128)(2,1)}, bf16[2,16,1024]{2,1,0:T(8,128)(2,1)S(1)}, u32[]{:S(2)}) %copy-start.13) | copy-done | bytes 65560
  18.8 0.6 %copy-done.14 = bf16[2,16,1024]{2,1,0:T(8,128)(2,1)} copy-done((bf16[2,16,1024]{2,1,0:T(8,128)(2,1)}, bf16[2,16,1024]{2,1,0:T(8,128)(2,1)S(1)}, u32[]{:S(2)}) %copy-start.14) | copy-done | bytes 65560
  19.4 0.6 %copy-done.15 = bf16[2,16,1024]{2,1,0:T(8,128)(2,1)} copy-done((bf16[2,16,1024]{2,1,0:T(8,128)(2,1)}, bf16[2,16,1024]{2,1,0:T(8,128)(2,1)S(1)}, u32[]{:S(2)}) %copy-start.15) | copy-done | bytes 65560
  20.0 0.6 %copy-done.19 = bf16[2,16,1024]{2,1,0:T(8,128)(2,1)} copy-done((bf16[2,16,1024]{2,1,0:T(8,128)(2,1)}, bf16[2,16,1024]{2,1,0:T(8,128)(2,1)S(1)}, u32[]{:S(2)}) %copy-start.19) | copy-done | bytes 65560
  20.7 2.7 %collective-permute-start.3 = (bf16[16,4096]{1,0:T(8,128)(2,1)S(1)}, bf16[16,4096]{1,0:T(8,128)(2,1)S(1)}, u32[]{:S(2)}, u32[]{:S(2)}) collective-permute-start(bf16[16,4096]{1,0:T(8,128)(2,1)S(1)} %get-tuple-element.29), channel_id=1, source_target_pairs={{0,28},{4,8},{8,4},{12,16},{16,12},{20,24},{24,20},{28,0},{1,29},{... | collective-permute-start | bytes 393224 | tf_op jit(solution)/shard_map/ppermute | solution.py:30
  23.4 0.7 %copy-done.7 = bf16[16,4096]{1,0:T(8,128)(2,1)} copy-done((bf16[16,4096]{1,0:T(8,128)(2,1)}, bf16[16,4096]{1,0:T(8,128)(2,1)S(1)}, u32[]{:S(2)}) %copy-start.7) | copy-done | bytes 131096
  24.0 1.5 %collective-permute-start.7 = (bf16[2,16,1024]{2,1,0:T(8,128)(2,1)}, bf16[2,16,1024]{2,1,0:T(8,128)(2,1)S(1)}, u32[]{:S(2)}, u32[]{:S(2)}) collective-permute-start(bf16[2,16,1024]{2,1,0:T(8,128)(2,1)} %get-tuple-element.39), channel_id=1, source_target_pairs={{0,1},{1,0},{2,3},{3,2},{4,5},{5,4},{6,7},{7,6},{8,9},{9,8},{10,11... | collective-permute-start | bytes 196616 | tf_op jit(solution)/shard_map/ppermute | solution.py:284
  25.5 1.5 %collective-permute-start.8 = (bf16[2,16,1024]{2,1,0:T(8,128)(2,1)}, bf16[2,16,1024]{2,1,0:T(8,128)(2,1)S(1)}, u32[]{:S(2)}, u32[]{:S(2)}) collective-permute-start(bf16[2,16,1024]{2,1,0:T(8,128)(2,1)} %get-tuple-element.40), channel_id=1, source_target_pairs={{0,2},{1,3},{2,0},{3,1},{4,6},{5,7},{6,4},{7,5},{8,10},{9,11},{10,... | collective-permute-start | bytes 196616 | tf_op jit(solution)/shard_map/ppermute | solution.py:284
  27.0 0.6 %collective-permute-done.5.refs_2_.refs_5_ = bf16[10,16,1024]{2,1,0:T(8,128)(2,1)S(1)} collective-permute-done((bf16[10,16,1024]{2,1,0:T(8,128)(2,1)S(1)}, bf16[10,16,1024]{2,1,0:T(8,128)(2,1)S(1)}, u32[]{:S(2)}, u32[]{:S(2)}) %collective-permute-start.5) | collective-permute-done | bytes 327712 | tf_op jit(solution)/shard_map/ppermute | solution.py:284
  27.7 1.1 %collective-permute-start.9 = (bf16[2,16,1024]{2,1,0:T(8,128)(2,1)}, bf16[2,16,1024]{2,1,0:T(8,128)(2,1)S(1)}, u32[]{:S(2)}, u32[]{:S(2)}) collective-permute-start(bf16[2,16,1024]{2,1,0:T(8,128)(2,1)} %get-tuple-element.41), channel_id=1, source_target_pairs={{0,3},{1,2},{2,1},{3,0},{4,7},{5,6},{6,5},{7,4},{8,11},{9,10},{10,... | collective-permute-start | bytes 196616 | tf_op jit(solution)/shard_map/ppermute | solution.py:284
  28.7 0.3 shard_map.184.refs_2_
  29.1 1.4 %collective-permute-done.8.refs_9_ = bf16[2,16,1024]{2,1,0:T(8,128)(2,1)S(1)} collective-permute-done((bf16[2,16,1024]{2,1,0:T(8,128)(2,1)}, bf16[2,16,1024]{2,1,0:T(8,128)(2,1)S(1)}, u32[]{:S(2)}, u32[]{:S(2)}) %collective-permute-start.8) | collective-permute-done | bytes 65568 | tf_op jit(solution)/shard_map/ppermute | solution.py:284
  30.5 2.5 %collective-permute-done.9.refs_10_ = bf16[2,16,1024]{2,1,0:T(8,128)(2,1)S(1)} collective-permute-done((bf16[2,16,1024]{2,1,0:T(8,128)(2,1)}, bf16[2,16,1024]{2,1,0:T(8,128)(2,1)S(1)}, u32[]{:S(2)}, u32[]{:S(2)}) %collective-permute-start.9) | collective-permute-done | bytes 65568 | tf_op jit(solution)/shard_map/ppermute | solution.py:284
  33.0 1.2 %shard_map.186 = (bf16[1,8,4096]{2,1,0:T(8,128)(2,1)}, bf16[1,8,4096]{2,1,0:T(8,128)(2,1)}, bf16[1,8,4096]{2,1,0:T(8,128)(2,1)}, bf16[1,8,4096]{2,1,0:T(8,128)(2...) custom-call(bf16[16,4096]{1,0:T(8,128)(2,1)S(1)} %copy-done.8, ...), custom_call_target="tpu_custom_call" | custom-call | flops 1000000000 | bytes 10000000 | tf_op jit(solution)/shard_map/pallas_call | solution.py:241
  (44 shorter events, 0.3 us)
Async XLA Ops:
  0.6 1.2 %copy-start.1 = (bf16[1,32,128,128]{3,2,1,0:T(8,128)(2,1)S(1)}, bf16[1,32,128,128]{3,2,1,0:T(8,128)(2,1)}, u32[]{:S(2)}) copy-start(bf16[1,32,128,128]{3,2,1,0:T(8,128)(2,1)} %refs_3_.3) | copy-start | bytes 3145732
  0.7 1.5 %copy-start = (bf16[1,32,128,128]{3,2,1,0:T(8,128)(2,1)S(1)}, bf16[1,32,128,128]{3,2,1,0:T(8,128)(2,1)}, u32[]{:S(2)}) copy-start(bf16[1,32,128,128]{3,2,1,0:T(8,128)(2,1)} %refs_2_.3) | copy-start | bytes 3145732
  0.7 1.5 %copy-start.5 = (bf16[1,2,8,4096]{3,2,1,0:T(8,128)(2,1)S(1)}, bf16[1,2,8,4096]{3,2,1,0:T(8,128)(2,1)}, u32[]{:S(2)}) copy-start(bf16[1,2,8,4096]{3,2,1,0:T(8,128)(2,1)} %refs_10_.1) | copy-start | bytes 393220
  0.7 1.6 %copy-start.4 = (bf16[1,2,8,4096]{3,2,1,0:T(8,128)(2,1)S(1)}, bf16[1,2,8,4096]{3,2,1,0:T(8,128)(2,1)}, u32[]{:S(2)}) copy-start(bf16[1,2,8,4096]{3,2,1,0:T(8,128)(2,1)} %refs_9_.1) | copy-start | bytes 393220
  0.7 1.6 %copy-start.3 = (bf16[1,2,8,4096]{3,2,1,0:T(8,128)(2,1)S(1)}, bf16[1,2,8,4096]{3,2,1,0:T(8,128)(2,1)}, u32[]{:S(2)}) copy-start(bf16[1,2,8,4096]{3,2,1,0:T(8,128)(2,1)} %refs_8_.1) | copy-start | bytes 393220
  0.7 1.6 %copy-start.6 = (bf16[1,2,8,4096]{3,2,1,0:T(8,128)(2,1)S(1)}, bf16[1,2,8,4096]{3,2,1,0:T(8,128)(2,1)}, u32[]{:S(2)}) copy-start(bf16[1,2,8,4096]{3,2,1,0:T(8,128)(2,1)} %refs_13_.1) | copy-start | bytes 393220
  0.7 1.6 %copy-start.2 = (bf16[1,2,8,4096]{3,2,1,0:T(8,128)(2,1)S(1)}, bf16[1,2,8,4096]{3,2,1,0:T(8,128)(2,1)}, u32[]{:S(2)}) copy-start(bf16[1,2,8,4096]{3,2,1,0:T(8,128)(2,1)} %refs_7_.1) | copy-start | bytes 393220
  0.7 1.6 %copy-start.10 = (bf16[1,8,4096]{2,1,0:T(8,128)(2,1)S(1)}, bf16[1,8,4096]{2,1,0:T(8,128)(2,1)}, u32[]{:S(2)}) copy-start(bf16[1,8,4096]{2,1,0:T(8,128)(2,1)} %refs_6_.1) | copy-start | bytes 196612
  0.7 1.6 %copy-start.12 = (bf16[1,8,4096]{2,1,0:T(8,128)(2,1)S(1)}, bf16[1,8,4096]{2,1,0:T(8,128)(2,1)}, u32[]{:S(2)}) copy-start(bf16[1,8,4096]{2,1,0:T(8,128)(2,1)} %refs_12_.1) | copy-start | bytes 196612
  0.7 1.6 %copy-start.9 = (bf16[1,8,4096]{2,1,0:T(8,128)(2,1)S(1)}, bf16[1,8,4096]{2,1,0:T(8,128)(2,1)}, u32[]{:S(2)}) copy-start(bf16[1,8,4096]{2,1,0:T(8,128)(2,1)} %refs_5_.1) | copy-start | bytes 196612
  0.8 1.6 %copy-start.11 = (bf16[1,8,4096]{2,1,0:T(8,128)(2,1)S(1)}, bf16[1,8,4096]{2,1,0:T(8,128)(2,1)}, u32[]{:S(2)}) copy-start(bf16[1,8,4096]{2,1,0:T(8,128)(2,1)} %refs_11_.1) | copy-start | bytes 196612
  0.8 1.6 %copy-start.16 = (s32[1,2]{1,0:T(1,128)S(1)}, s32[1,2]{1,0:T(1,128)}, u32[]{:S(2)}) copy-start(s32[1,2]{1,0:T(1,128)} %refs_2_.2) | copy-start | bytes 28
  6.9 8.7 %collective-permute-start = (bf16[16,4096]{1,0:T(8,128)(2,1)S(1)}, bf16[16,4096]{1,0:T(8,128)(2,1)S(1)}, u32[]{:S(2)}, u32[]{:S(2)}) collective-permute-start(bf16[16,4096]{1,0:T(8,128)(2,1)S(1)} %get-tuple-element.24), channel_id=1, source_target_pairs={{0,4},{4,0},{8,12},{12,8},{16,20},{20,16},{24,28},{28,24},{1,5},{5... | collective-permute-start | bytes 393224 | tf_op jit(solution)/shard_map/ppermute | solution.py:31
  7.4 8.2 %collective-permute-start.1 = (bf16[16,4096]{1,0:T(8,128)(2,1)S(1)}, bf16[16,4096]{1,0:T(8,128)(2,1)S(1)}, u32[]{:S(2)}, u32[]{:S(2)}) collective-permute-start(bf16[16,4096]{1,0:T(8,128)(2,1)S(1)} %get-tuple-element.25), channel_id=1, source_target_pairs={{0,28},{4,8},{8,4},{12,16},{16,12},{20,24},{24,20},{28,0},{1,29},{... | collective-permute-start | bytes 393224 | tf_op jit(solution)/shard_map/ppermute | solution.py:30
  12.1 13.4 %collective-permute-start.4 = (bf16[10,16,1024]{2,1,0:T(8,128)(2,1)S(1)}, bf16[10,16,1024]{2,1,0:T(8,128)(2,1)S(1)}, u32[]{:S(2)}, u32[]{:S(2)}) collective-permute-start(bf16[10,16,1024]{2,1,0:T(8,128)(2,1)S(1)} %get-tuple-element.31), channel_id=1, source_target_pairs={{0,1},{1,0},{2,3},{3,2},{4,5},{5,4},{6,7},{7,6},{8,9},{9,8},{10,11... | collective-permute-start | bytes 983048 | tf_op jit(solution)/shard_map/ppermute | solution.py:284
  13.6 14.1 %collective-permute-start.5 = (bf16[10,16,1024]{2,1,0:T(8,128)(2,1)S(1)}, bf16[10,16,1024]{2,1,0:T(8,128)(2,1)S(1)}, u32[]{:S(2)}, u32[]{:S(2)}) collective-permute-start(bf16[10,16,1024]{2,1,0:T(8,128)(2,1)S(1)} %get-tuple-element.32), channel_id=1, source_target_pairs={{0,2},{1,3},{2,0},{3,1},{4,6},{5,7},{6,4},{7,5},{8,10},{9,11},{10,... | collective-permute-start | bytes 983048 | tf_op jit(solution)/shard_map/ppermute | solution.py:284
  15.1 13.6 %collective-permute-start.6 = (bf16[10,16,1024]{2,1,0:T(8,128)(2,1)S(1)}, bf16[10,16,1024]{2,1,0:T(8,128)(2,1)S(1)}, u32[]{:S(2)}, u32[]{:S(2)}) collective-permute-start(bf16[10,16,1024]{2,1,0:T(8,128)(2,1)S(1)} %get-tuple-element.33), channel_id=1, source_target_pairs={{0,3},{1,2},{2,1},{3,0},{4,7},{5,6},{6,5},{7,4},{8,11},{9,10},{10,... | collective-permute-start | bytes 983048 | tf_op jit(solution)/shard_map/ppermute | solution.py:284
  20.7 2.7 %collective-permute-start.2 = (bf16[16,4096]{1,0:T(8,128)(2,1)S(1)}, bf16[16,4096]{1,0:T(8,128)(2,1)S(1)}, u32[]{:S(2)}, u32[]{:S(2)}) collective-permute-start(bf16[16,4096]{1,0:T(8,128)(2,1)S(1)} %get-tuple-element.28), channel_id=1, source_target_pairs={{0,4},{4,0},{8,12},{12,8},{16,20},{20,16},{24,28},{28,24},{1,5},{5... | collective-permute-start | bytes 393224 | tf_op jit(solution)/shard_map/ppermute | solution.py:31
  20.7 8.4 %collective-permute-start.3 = (bf16[16,4096]{1,0:T(8,128)(2,1)S(1)}, bf16[16,4096]{1,0:T(8,128)(2,1)S(1)}, u32[]{:S(2)}, u32[]{:S(2)}) collective-permute-start(bf16[16,4096]{1,0:T(8,128)(2,1)S(1)} %get-tuple-element.29), channel_id=1, source_target_pairs={{0,28},{4,8},{8,4},{12,16},{16,12},{20,24},{24,20},{28,0},{1,29},{... | collective-permute-start | bytes 393224 | tf_op jit(solution)/shard_map/ppermute | solution.py:30
  24.0 5.1 %collective-permute-start.7 = (bf16[2,16,1024]{2,1,0:T(8,128)(2,1)}, bf16[2,16,1024]{2,1,0:T(8,128)(2,1)S(1)}, u32[]{:S(2)}, u32[]{:S(2)}) collective-permute-start(bf16[2,16,1024]{2,1,0:T(8,128)(2,1)} %get-tuple-element.39), channel_id=1, source_target_pairs={{0,1},{1,0},{2,3},{3,2},{4,5},{5,4},{6,7},{7,6},{8,9},{9,8},{10,11... | collective-permute-start | bytes 196616 | tf_op jit(solution)/shard_map/ppermute | solution.py:284
  25.5 5.0 %collective-permute-start.8 = (bf16[2,16,1024]{2,1,0:T(8,128)(2,1)}, bf16[2,16,1024]{2,1,0:T(8,128)(2,1)S(1)}, u32[]{:S(2)}, u32[]{:S(2)}) collective-permute-start(bf16[2,16,1024]{2,1,0:T(8,128)(2,1)} %get-tuple-element.40), channel_id=1, source_target_pairs={{0,2},{1,3},{2,0},{3,1},{4,6},{5,7},{6,4},{7,5},{8,10},{9,11},{10,... | collective-permute-start | bytes 196616 | tf_op jit(solution)/shard_map/ppermute | solution.py:284
  27.7 5.4 %collective-permute-start.9 = (bf16[2,16,1024]{2,1,0:T(8,128)(2,1)}, bf16[2,16,1024]{2,1,0:T(8,128)(2,1)S(1)}, u32[]{:S(2)}, u32[]{:S(2)}) collective-permute-start(bf16[2,16,1024]{2,1,0:T(8,128)(2,1)} %get-tuple-element.41), channel_id=1, source_target_pairs={{0,3},{1,2},{2,1},{3,0},{4,7},{5,6},{6,5},{7,4},{8,11},{9,10},{10,... | collective-permute-start | bytes 196616 | tf_op jit(solution)/shard_map/ppermute | solution.py:284
  28.7 4.3 %copy-start.8 = (bf16[16,4096]{1,0:T(8,128)(2,1)S(1)}, bf16[16,4096]{1,0:T(8,128)(2,1)}, u32[]{:S(2)}) copy-start(bf16[16,4096]{1,0:T(8,128)(2,1)} %copy-done.7) | copy-start | bytes 393220
  28.7 4.3 %copy-start.20 = (bf16[2,16,1024]{2,1,0:T(8,128)(2,1)S(1)}, bf16[2,16,1024]{2,1,0:T(8,128)(2,1)}, u32[]{:S(2)}) copy-start(bf16[2,16,1024]{2,1,0:T(8,128)(2,1)} %get-tuple-element.38.refs_7_) | copy-start | bytes 196612
  (7 other events, 5.1 us)

commit v7 on v5

--- a/solution.py
+++ b/solution.py
@@ -10,7 +10,7 @@
 BF16 = jnp.bfloat16
 LIMIT = 40 * 1024 * 1024
 WORK = 10 ** 10
-LIGHT = 10 ** 4
+LIGHT = 10 ** 9
 
 
 def partner(me, step, count):
@@ -205,10 +205,7 @@
 
 
 def early_grads(count, per, *refs):
-    early, late = refs[:count], refs[count:2 * count]
-    grads, sends = refs[2 * count], refs[2 * count + 1:]
-    for source in range(count):
-        sends[source][...] = late[source][...]
+    early, grads = refs[:count], refs[count]
     for place in range(per):
         at = lanes(place)
         for out, left, right in ((0, 0, 3), (1, 5, 8)):
@@ -250,6 +247,12 @@
         compiler_params=pltpu.CompilerParams(vmem_limit_bytes=LIMIT),
         cost_estimate=pl.CostEstimate(flops=cost, bytes_accessed=cost // 100, transcendentals=0),
     )(*operands, *after)
+
+
+def hand_on(*refs):
+    half = len(refs) // 2
+    for source, target in zip(refs[:half], refs[half:]):
+        target[...] = source[...]
 
 
 def on_device(w_up, up_index, w_down, down_index, tick_order, values_in, score_grad_in, tangent_in, state_adjoint_in,
@@ -293,10 +296,10 @@
          vmem((blocks, 16, BLOCK), F32), vmem((blocks, 16, BLOCK), BF16)])
     near, far = swap_sections(near, far)
     two = shape((2, 16, part), BF16)
-    grads, *late = call(
-        body(early_grads, count, per), (*early, *late), [vmem] * (2 * count),
-        [shape((2, per, BLOCK, BLOCK), F32)] + [two] * count, [])
-    late = to_replicas(late)
+    held = call(hand_on, tuple(late[1:]), [vmem] * (count - 1), [two] * (count - 1), [], after=(near,))
+    late = to_replicas(late[:1] + list(held))
+    (grads,) = call(
+        body(early_grads, count, per), tuple(early), [vmem] * count, [shape((2, per, BLOCK, BLOCK), F32)], [])
     stream = shape((1,) + values_in.shape[1:], BF16)
     grad = shape((1, per, BLOCK, BLOCK), BF16)
     return tuple(call(

time: 35 us -> 34.9 us (level)
  starting transfers between devices: 15.3 us -> 14.6 us
  waiting for transfers between devices: 8.69 us -> 9.19 us
    ppermute x6, waiting for transfers between devices: 5.33 us -> 9.18 us  [to_replicas(): lax.ppermute(parts[step], 'dp', swap_route(step, count))]
    ppermute x2, waiting for transfers between devices: 3.35 us -> 0.01 us  [swap_sections(): lax.ppermute(far, 'section', [(i, (i + 2 * (i % 2) - 1) % count) for i in...]
    ppermute x6, starting transfers between devices: 8.1 us -> 6.57 us  [to_replicas(): lax.ppermute(parts[step], 'dp', swap_route(step, count))]
    ppermute x2, starting transfers between devices: 0.07 us -> 0.59 us  [swap_sections(): near = lax.ppermute(near, 'section', [(i, i ^ 1) for i in range(count)])]
    ppermute x2, starting transfers between devices: 7.09 us -> 7.47 us  [swap_sections(): lax.ppermute(far, 'section', [(i, (i + 2 * (i % 2) - 1) % count) for i in...]
    pallas_call x5 -> x6, Pallas kernels: 8.5 us -> 8.51 us  [call(): pl.pallas_call(kernel, out_shape=outs, in_specs=[pl.BlockSpec(memory_spac...]
where the time goes in v7:
time: 34.9 us; the launch traced here: 34.8 us
  starting transfers between devices  14.6 us (42%)
  waiting for transfers between devices  9.19 us (26%)
  Pallas kernels  8.51 us (24%)
  local copies, waits for them, and re-layouts  1.63 us (5%)
  between operations  0.81 us (2%)
    ppermute x6, waiting for transfers between devices, to_replicas(): lax.ppermute(parts[step], 'dp', swap_route(step, count))  9.18 us
    pallas_call x6, Pallas kernels, call(): pl.pallas_call(kernel, out_shape=outs, in_specs=[pl.BlockSpec(memory_spac...  8.51 us
    ppermute x2, starting transfers between devices, swap_sections(): lax.ppermute(far, 'section', [(i, (i + 2 * (i % 2) - 1) % count) for i in...  7.47 us
    ppermute x6, starting transfers between devices, to_replicas(): lax.ppermute(parts[step], 'dp', swap_route(step, count))  6.57 us
    unnamed x28, local copies, waits for them, and re-layouts  1.63 us
  transfers between devices with their start and end apart: 10, of which 5 were waited for; matrix products, arithmetic and copies ran while one was open for 0% of the time, Pallas kernels for 8%

profile of v7, /device:TPU:0, one launch (start us, length us, event | category | flops | bytes accessed | tf_op | source)
XLA Modules:
  0.0 34.8 jit_solution(11119277862594493664)
XLA Ops:
  0.8 0.5 %copy-done.13 = s32[1,32]{1,0:T(1,128)S(1)} copy-done((s32[1,32]{1,0:T(1,128)S(1)}, s32[1,32]{1,0:T(1,128)}, u32[]{:S(2)}) %copy-start.13) | copy-done | bytes 152
  1.3 0.6 %copy-done.1 = bf16[1,32,128,128]{3,2,1,0:T(8,128)(2,1)S(1)} copy-done((bf16[1,32,128,128]{3,2,1,0:T(8,128)(2,1)S(1)}, bf16[1,32,128,128]{3,2,1,0:T(8,128)(2,1)}, u32[]{:S(2)}) %copy-start.1) | copy-done | bytes 1048600
  1.9 0.3 copy-done
  2.2 0.0 copy-done.3
  2.3 0.0 copy-done.6
  2.3 0.0 copy-done.2
  2.4 4.5 %shard_map.182 = (bf16[16,4096]{1,0:T(8,128)(2,1)S(1)}, bf16[16,4096]{1,0:T(8,128)(2,1)S(1)}, f32[32,24,128]{2,1,0:T(8,128)S(1)}, f32[32,8,128]{2,1,0:T(8,128)S(...) custom-call(s32[1,32]{1,0:T(1,128)S(1)} %copy-done.12, ...), custom_call_target="tpu_custom_call" | custom-call | flops 10000000000 | bytes 100000000 | tf_op jit(solution)/shard_map/pallas_call | solution.py:241
  6.9 0.5 %collective-permute-start = (bf16[16,4096]{1,0:T(8,128)(2,1)S(1)}, bf16[16,4096]{1,0:T(8,128)(2,1)S(1)}, u32[]{:S(2)}, u32[]{:S(2)}) collective-permute-start(bf16[16,4096]{1,0:T(8,128)(2,1)S(1)} %get-tuple-element.23), channel_id=1, source_target_pairs={{0,4},{4,0},{8,12},{12,8},{16,20},{20,16},{24,28},{28,24},{1,5},{5... | collective-permute-start | bytes 393224 | tf_op jit(solution)/shard_map/ppermute | solution.py:31
  7.4 4.7 %collective-permute-start.1 = (bf16[16,4096]{1,0:T(8,128)(2,1)S(1)}, bf16[16,4096]{1,0:T(8,128)(2,1)S(1)}, u32[]{:S(2)}, u32[]{:S(2)}) collective-permute-start(bf16[16,4096]{1,0:T(8,128)(2,1)S(1)} %get-tuple-element.24), channel_id=1, source_target_pairs={{0,28},{4,8},{8,4},{12,16},{16,12},{20,24},{24,20},{28,0},{1,29},{... | collective-permute-start | bytes 393224 | tf_op jit(solution)/shard_map/ppermute | solution.py:30
  12.1 1.5 %collective-permute-start.4 = (bf16[10,16,1024]{2,1,0:T(8,128)(2,1)S(1)}, bf16[10,16,1024]{2,1,0:T(8,128)(2,1)S(1)}, u32[]{:S(2)}, u32[]{:S(2)}) collective-permute-start(bf16[10,16,1024]{2,1,0:T(8,128)(2,1)S(1)} %get-tuple-element.30), channel_id=1, source_target_pairs={{0,1},{1,0},{2,3},{3,2},{4,5},{5,4},{6,7},{7,6},{8,9},{9,8},{10,11... | collective-permute-start | bytes 983048 | tf_op jit(solution)/shard_map/ppermute | solution.py:276
  13.6 1.5 %collective-permute-start.5 = (bf16[10,16,1024]{2,1,0:T(8,128)(2,1)S(1)}, bf16[10,16,1024]{2,1,0:T(8,128)(2,1)S(1)}, u32[]{:S(2)}, u32[]{:S(2)}) collective-permute-start(bf16[10,16,1024]{2,1,0:T(8,128)(2,1)S(1)} %get-tuple-element.31), channel_id=1, source_target_pairs={{0,2},{1,3},{2,0},{3,1},{4,6},{5,7},{6,4},{7,5},{8,10},{9,11},{10,... | collective-permute-start | bytes 983048 | tf_op jit(solution)/shard_map/ppermute | solution.py:276
  15.1 0.5 %collective-permute-start.6 = (bf16[10,16,1024]{2,1,0:T(8,128)(2,1)S(1)}, bf16[10,16,1024]{2,1,0:T(8,128)(2,1)S(1)}, u32[]{:S(2)}, u32[]{:S(2)}) collective-permute-start(bf16[10,16,1024]{2,1,0:T(8,128)(2,1)S(1)} %get-tuple-element.32), channel_id=1, source_target_pairs={{0,3},{1,2},{2,1},{3,0},{4,7},{5,6},{6,5},{7,4},{8,11},{9,10},{10,... | collective-permute-start | bytes 983048 | tf_op jit(solution)/shard_map/ppermute | solution.py:276
  15.6 2.5 %shard_map.183 = (bf16[16,4096]{1,0:T(8,128)(2,1)S(1)}, bf16[16,4096]{1,0:T(8,128)(2,1)S(1)}, bf16[2,16,1024]{2,1,0:T(8,128)(2,1)S(1)}, bf16[2,16,1024]{2,1,0:T(...) custom-call(s32[1,32]{1,0:T(1,128)S(1)} %copy-done.12, s32[1,32]{1,0:T(1,128)S(1)} %copy-done.13, ...), custom_call_target="tpu_custom_call" | custom-call | flops 1000000000 | bytes 10000000 | tf_op jit(solution)/shard_map/pallas_call | solution.py:241
  18.1 0.1 collective-permute-start.2
  18.2 2.8 %collective-permute-start.3 = (bf16[16,4096]{1,0:T(8,128)(2,1)S(1)}, bf16[16,4096]{1,0:T(8,128)(2,1)S(1)}, u32[]{:S(2)}, u32[]{:S(2)}) collective-permute-start(bf16[16,4096]{1,0:T(8,128)(2,1)S(1)} %get-tuple-element.28), channel_id=1, source_target_pairs={{0,28},{4,8},{8,4},{12,16},{16,12},{20,24},{24,20},{28,0},{1,29},{... | collective-permute-start | bytes 393224 | tf_op jit(solution)/shard_map/ppermute | solution.py:30
  21.0 1.6 %collective-permute-start.7 = (bf16[2,16,1024]{2,1,0:T(8,128)(2,1)S(1)}, bf16[2,16,1024]{2,1,0:T(8,128)(2,1)S(1)}, u32[]{:S(2)}, u32[]{:S(2)}) collective-permute-start(bf16[2,16,1024]{2,1,0:T(8,128)(2,1)S(1)} %get-tuple-element.37), channel_id=1, source_target_pairs={{0,1},{1,0},{2,3},{3,2},{4,5},{5,4},{6,7},{7,6},{8,9},{9,8},{10,11... | collective-permute-start | bytes 196616 | tf_op jit(solution)/shard_map/ppermute | solution.py:276
  22.5 0.2 collective-permute-done.4.refs_1_.refs_4_
  22.7 1.5 %collective-permute-start.8 = (bf16[2,16,1024]{2,1,0:T(8,128)(2,1)S(1)}, bf16[2,16,1024]{2,1,0:T(8,128)(2,1)S(1)}, u32[]{:S(2)}, u32[]{:S(2)}) collective-permute-start(bf16[2,16,1024]{2,1,0:T(8,128)(2,1)S(1)} %get-tuple-element.38), channel_id=1, source_target_pairs={{0,2},{1,3},{2,0},{3,1},{4,6},{5,7},{6,4},{7,5},{8,10},{9,11},{10,... | collective-permute-start | bytes 196616 | tf_op jit(solution)/shard_map/ppermute | solution.py:276
  24.3 4.2 %collective-permute-done.5.refs_2_.refs_5_ = bf16[10,16,1024]{2,1,0:T(8,128)(2,1)S(1)} collective-permute-done((bf16[10,16,1024]{2,1,0:T(8,128)(2,1)S(1)}, bf16[10,16,1024]{2,1,0:T(8,128)(2,1)S(1)}, u32[]{:S(2)}, u32[]{:S(2)}) %collective-permute-start.5) | collective-permute-done | bytes 327712 | tf_op jit(solution)/shard_map/ppermute | solution.py:276
  28.4 0.8 %collective-permute-done.6.refs_3_.refs_6_ = bf16[10,16,1024]{2,1,0:T(8,128)(2,1)S(1)} collective-permute-done((bf16[10,16,1024]{2,1,0:T(8,128)(2,1)S(1)}, bf16[10,16,1024]{2,1,0:T(8,128)(2,1)S(1)}, u32[]{:S(2)}, u32[]{:S(2)}) %collective-permute-start.6) | collective-permute-done | bytes 327712 | tf_op jit(solution)/shard_map/ppermute | solution.py:276
  29.3 0.3 shard_map.184.refs_2_
  29.6 0.5 %collective-permute-done.8.refs_9_ = bf16[2,16,1024]{2,1,0:T(8,128)(2,1)S(1)} collective-permute-done((bf16[2,16,1024]{2,1,0:T(8,128)(2,1)S(1)}, bf16[2,16,1024]{2,1,0:T(8,128)(2,1)S(1)}, u32[]{:S(2)}, u32[]{:S(2)}) %collective-permute-start.8) | collective-permute-done | bytes 65568 | tf_op jit(solution)/shard_map/ppermute | solution.py:276
  30.1 3.5 %collective-permute-done.9.refs_10_ = bf16[2,16,1024]{2,1,0:T(8,128)(2,1)S(1)} collective-permute-done((bf16[2,16,1024]{2,1,0:T(8,128)(2,1)S(1)}, bf16[2,16,1024]{2,1,0:T(8,128)(2,1)S(1)}, u32[]{:S(2)}, u32[]{:S(2)}) %collective-permute-start.9) | collective-permute-done | bytes 65568 | tf_op jit(solution)/shard_map/ppermute | solution.py:276
  33.6 1.2 %shard_map.186 = (bf16[1,8,4096]{2,1,0:T(8,128)(2,1)}, bf16[1,8,4096]{2,1,0:T(8,128)(2,1)}, bf16[1,8,4096]{2,1,0:T(8,128)(2,1)}, bf16[1,8,4096]{2,1,0:T(8,128)(2...) custom-call(bf16[16,4096]{1,0:T(8,128)(2,1)S(1)} %collective-permute-done.2.refs_3_.refs_0_, ...), custom_call_target="tpu_custom_call" | custom-call | flops 1000000000 | bytes 10000000 | tf_op jit(solution)/shard_map/pallas_call | solution.py:241
  (30 shorter events, 0.1 us)
Async XLA Ops:
  0.6 0.7 %copy-start.13 = (s32[1,32]{1,0:T(1,128)S(1)}, s32[1,32]{1,0:T(1,128)}, u32[]{:S(2)}) copy-start(s32[1,32]{1,0:T(1,128)} %refs_1_.3) | copy-start | bytes 388
  0.6 1.2 %copy-start.1 = (bf16[1,32,128,128]{3,2,1,0:T(8,128)(2,1)S(1)}, bf16[1,32,128,128]{3,2,1,0:T(8,128)(2,1)}, u32[]{:S(2)}) copy-start(bf16[1,32,128,128]{3,2,1,0:T(8,128)(2,1)} %refs_3_.3) | copy-start | bytes 3145732
  0.7 1.2 %copy-start.12 = (s32[1,32]{1,0:T(1,128)S(1)}, s32[1,32]{1,0:T(1,128)}, u32[]{:S(2)}) copy-start(s32[1,32]{1,0:T(1,128)} %refs_0_.3) | copy-start | bytes 388
  0.7 1.5 %copy-start = (bf16[1,32,128,128]{3,2,1,0:T(8,128)(2,1)S(1)}, bf16[1,32,128,128]{3,2,1,0:T(8,128)(2,1)}, u32[]{:S(2)}) copy-start(bf16[1,32,128,128]{3,2,1,0:T(8,128)(2,1)} %refs_2_.3) | copy-start | bytes 3145732
  0.7 1.5 %copy-start.5 = (bf16[1,2,8,4096]{3,2,1,0:T(8,128)(2,1)S(1)}, bf16[1,2,8,4096]{3,2,1,0:T(8,128)(2,1)}, u32[]{:S(2)}) copy-start(bf16[1,2,8,4096]{3,2,1,0:T(8,128)(2,1)} %refs_10_.1) | copy-start | bytes 393220
  0.7 1.6 %copy-start.4 = (bf16[1,2,8,4096]{3,2,1,0:T(8,128)(2,1)S(1)}, bf16[1,2,8,4096]{3,2,1,0:T(8,128)(2,1)}, u32[]{:S(2)}) copy-start(bf16[1,2,8,4096]{3,2,1,0:T(8,128)(2,1)} %refs_9_.1) | copy-start | bytes 393220
  0.7 1.6 %copy-start.3 = (bf16[1,2,8,4096]{3,2,1,0:T(8,128)(2,1)S(1)}, bf16[1,2,8,4096]{3,2,1,0:T(8,128)(2,1)}, u32[]{:S(2)}) copy-start(bf16[1,2,8,4096]{3,2,1,0:T(8,128)(2,1)} %refs_8_.1) | copy-start | bytes 393220
  0.7 1.6 %copy-start.6 = (bf16[1,2,8,4096]{3,2,1,0:T(8,128)(2,1)S(1)}, bf16[1,2,8,4096]{3,2,1,0:T(8,128)(2,1)}, u32[]{:S(2)}) copy-start(bf16[1,2,8,4096]{3,2,1,0:T(8,128)(2,1)} %refs_13_.1) | copy-start | bytes 393220
  0.7 1.6 %copy-start.2 = (bf16[1,2,8,4096]{3,2,1,0:T(8,128)(2,1)S(1)}, bf16[1,2,8,4096]{3,2,1,0:T(8,128)(2,1)}, u32[]{:S(2)}) copy-start(bf16[1,2,8,4096]{3,2,1,0:T(8,128)(2,1)} %refs_7_.1) | copy-start | bytes 393220
  0.7 1.6 %copy-start.8 = (bf16[1,8,4096]{2,1,0:T(8,128)(2,1)S(1)}, bf16[1,8,4096]{2,1,0:T(8,128)(2,1)}, u32[]{:S(2)}) copy-start(bf16[1,8,4096]{2,1,0:T(8,128)(2,1)} %refs_6_.1) | copy-start | bytes 196612
  0.7 1.6 %copy-start.10 = (bf16[1,8,4096]{2,1,0:T(8,128)(2,1)S(1)}, bf16[1,8,4096]{2,1,0:T(8,128)(2,1)}, u32[]{:S(2)}) copy-start(bf16[1,8,4096]{2,1,0:T(8,128)(2,1)} %refs_12_.1) | copy-start | bytes 196612
  0.7 1.6 %copy-start.7 = (bf16[1,8,4096]{2,1,0:T(8,128)(2,1)S(1)}, bf16[1,8,4096]{2,1,0:T(8,128)(2,1)}, u32[]{:S(2)}) copy-start(bf16[1,8,4096]{2,1,0:T(8,128)(2,1)} %refs_5_.1) | copy-start | bytes 196612
  0.8 1.6 %copy-start.9 = (bf16[1,8,4096]{2,1,0:T(8,128)(2,1)S(1)}, bf16[1,8,4096]{2,1,0:T(8,128)(2,1)}, u32[]{:S(2)}) copy-start(bf16[1,8,4096]{2,1,0:T(8,128)(2,1)} %refs_11_.1) | copy-start | bytes 196612
  0.8 1.6 %copy-start.11 = (s32[1,2]{1,0:T(1,128)S(1)}, s32[1,2]{1,0:T(1,128)}, u32[]{:S(2)}) copy-start(s32[1,2]{1,0:T(1,128)} %refs_2_.2) | copy-start | bytes 28
  6.9 8.7 %collective-permute-start = (bf16[16,4096]{1,0:T(8,128)(2,1)S(1)}, bf16[16,4096]{1,0:T(8,128)(2,1)S(1)}, u32[]{:S(2)}, u32[]{:S(2)}) collective-permute-start(bf16[16,4096]{1,0:T(8,128)(2,1)S(1)} %get-tuple-element.23), channel_id=1, source_target_pairs={{0,4},{4,0},{8,12},{12,8},{16,20},{20,16},{24,28},{28,24},{1,5},{5... | collective-permute-start | bytes 393224 | tf_op jit(solution)/shard_map/ppermute | solution.py:31
  7.4 8.2 %collective-permute-start.1 = (bf16[16,4096]{1,0:T(8,128)(2,1)S(1)}, bf16[16,4096]{1,0:T(8,128)(2,1)S(1)}, u32[]{:S(2)}, u32[]{:S(2)}) collective-permute-start(bf16[16,4096]{1,0:T(8,128)(2,1)S(1)} %get-tuple-element.24), channel_id=1, source_target_pairs={{0,28},{4,8},{8,4},{12,16},{16,12},{20,24},{24,20},{28,0},{1,29},{... | collective-permute-start | bytes 393224 | tf_op jit(solution)/shard_map/ppermute | solution.py:30
  12.1 10.6 %collective-permute-start.4 = (bf16[10,16,1024]{2,1,0:T(8,128)(2,1)S(1)}, bf16[10,16,1024]{2,1,0:T(8,128)(2,1)S(1)}, u32[]{:S(2)}, u32[]{:S(2)}) collective-permute-start(bf16[10,16,1024]{2,1,0:T(8,128)(2,1)S(1)} %get-tuple-element.30), channel_id=1, source_target_pairs={{0,1},{1,0},{2,3},{3,2},{4,5},{5,4},{6,7},{7,6},{8,9},{9,8},{10,11... | collective-permute-start | bytes 983048 | tf_op jit(solution)/shard_map/ppermute | solution.py:276
  13.6 14.9 %collective-permute-start.5 = (bf16[10,16,1024]{2,1,0:T(8,128)(2,1)S(1)}, bf16[10,16,1024]{2,1,0:T(8,128)(2,1)S(1)}, u32[]{:S(2)}, u32[]{:S(2)}) collective-permute-start(bf16[10,16,1024]{2,1,0:T(8,128)(2,1)S(1)} %get-tuple-element.31), channel_id=1, source_target_pairs={{0,2},{1,3},{2,0},{3,1},{4,6},{5,7},{6,4},{7,5},{8,10},{9,11},{10,... | collective-permute-start | bytes 983048 | tf_op jit(solution)/shard_map/ppermute | solution.py:276
  15.1 14.2 %collective-permute-start.6 = (bf16[10,16,1024]{2,1,0:T(8,128)(2,1)S(1)}, bf16[10,16,1024]{2,1,0:T(8,128)(2,1)S(1)}, u32[]{:S(2)}, u32[]{:S(2)}) collective-permute-start(bf16[10,16,1024]{2,1,0:T(8,128)(2,1)S(1)} %get-tuple-element.32), channel_id=1, source_target_pairs={{0,3},{1,2},{2,1},{3,0},{4,7},{5,6},{6,5},{7,4},{8,11},{9,10},{10,... | collective-permute-start | bytes 983048 | tf_op jit(solution)/shard_map/ppermute | solution.py:276
  18.1 2.9 %collective-permute-start.2 = (bf16[16,4096]{1,0:T(8,128)(2,1)S(1)}, bf16[16,4096]{1,0:T(8,128)(2,1)S(1)}, u32[]{:S(2)}, u32[]{:S(2)}) collective-permute-start(bf16[16,4096]{1,0:T(8,128)(2,1)S(1)} %get-tuple-element.27), channel_id=1, source_target_pairs={{0,4},{4,0},{8,12},{12,8},{16,20},{20,16},{24,28},{28,24},{1,5},{5... | collective-permute-start | bytes 393224 | tf_op jit(solution)/shard_map/ppermute | solution.py:31
  18.2 11.4 %collective-permute-start.3 = (bf16[16,4096]{1,0:T(8,128)(2,1)S(1)}, bf16[16,4096]{1,0:T(8,128)(2,1)S(1)}, u32[]{:S(2)}, u32[]{:S(2)}) collective-permute-start(bf16[16,4096]{1,0:T(8,128)(2,1)S(1)} %get-tuple-element.28), channel_id=1, source_target_pairs={{0,28},{4,8},{8,4},{12,16},{16,12},{20,24},{24,20},{28,0},{1,29},{... | collective-permute-start | bytes 393224 | tf_op jit(solution)/shard_map/ppermute | solution.py:30
  21.0 8.6 %collective-permute-start.7 = (bf16[2,16,1024]{2,1,0:T(8,128)(2,1)S(1)}, bf16[2,16,1024]{2,1,0:T(8,128)(2,1)S(1)}, u32[]{:S(2)}, u32[]{:S(2)}) collective-permute-start(bf16[2,16,1024]{2,1,0:T(8,128)(2,1)S(1)} %get-tuple-element.37), channel_id=1, source_target_pairs={{0,1},{1,0},{2,3},{3,2},{4,5},{5,4},{6,7},{7,6},{8,9},{9,8},{10,11... | collective-permute-start | bytes 196616 | tf_op jit(solution)/shard_map/ppermute | solution.py:276
  22.7 7.4 %collective-permute-start.8 = (bf16[2,16,1024]{2,1,0:T(8,128)(2,1)S(1)}, bf16[2,16,1024]{2,1,0:T(8,128)(2,1)S(1)}, u32[]{:S(2)}, u32[]{:S(2)}) collective-permute-start(bf16[2,16,1024]{2,1,0:T(8,128)(2,1)S(1)} %get-tuple-element.38), channel_id=1, source_target_pairs={{0,2},{1,3},{2,0},{3,1},{4,6},{5,7},{6,4},{7,5},{8,10},{9,11},{10,... | collective-permute-start | bytes 196616 | tf_op jit(solution)/shard_map/ppermute | solution.py:276
  28.4 5.2 %collective-permute-start.9 = (bf16[2,16,1024]{2,1,0:T(8,128)(2,1)S(1)}, bf16[2,16,1024]{2,1,0:T(8,128)(2,1)S(1)}, u32[]{:S(2)}, u32[]{:S(2)}) collective-permute-start(bf16[2,16,1024]{2,1,0:T(8,128)(2,1)S(1)} %get-tuple-element.39), channel_id=1, source_target_pairs={{0,3},{1,2},{2,1},{3,0},{4,7},{5,6},{6,5},{7,4},{8,11},{9,10},{10,... | collective-permute-start | bytes 196616 | tf_op jit(solution)/shard_map/ppermute | solution.py:276

commit v8 on v7

--- a/solution.py
+++ b/solution.py
@@ -10,7 +10,7 @@
 BF16 = jnp.bfloat16
 LIMIT = 40 * 1024 * 1024
 WORK = 10 ** 10
-LIGHT = 10 ** 9
+LIGHT = 10 ** 4
 
 
 def partner(me, step, count):
@@ -273,7 +273,8 @@
         return kernel
 
     def to_replicas(parts):
-        return [parts[0]] + [lax.ppermute(parts[step], "dp", swap_route(step, count)) for step in range(1, count)]
+        steps = [count - 1] + list(range(1, count - 1))
+        return [parts[0]] + [lax.ppermute(parts[step], "dp", swap_route(step, count)) for step in steps]
 
     rows = (score_grad_in, state_adjoint_in, saved_back, saved_second, saved_second_tan, saved_second_grad)
     ten = shape((10, 16, part), BF16)

time: 34.9 us -> 32.1 us (0.920)
  waiting for transfers between devices: 9.19 us -> 6.22 us
    ppermute x6, waiting for transfers between devices: 9.18 us -> 2.64 us  [to_replicas(): lax.ppermute(parts[step], 'dp', swap_route(step, count))]
    ppermute x2, waiting for transfers between devices: 0.01 us -> 3.58 us  [swap_sections(): lax.ppermute(far, 'section', [(i, (i + 2 * (i % 2) - 1) % count) for i in...]
    ppermute x6, starting transfers between devices: 6.57 us -> 8.07 us  [to_replicas(): lax.ppermute(parts[step], 'dp', swap_route(step, count))]
    ppermute x2, starting transfers between devices: 7.47 us -> 6.64 us  [swap_sections(): lax.ppermute(far, 'section', [(i, (i + 2 * (i % 2) - 1) % count) for i in...]
    ppermute x2, starting transfers between devices: 0.59 us -> 0.07 us  [swap_sections(): near = lax.ppermute(near, 'section', [(i, i ^ 1) for i in range(count)])]
  transfers between devices with their start and end apart: 10 -> 10, of which waited for: 5 -> 6; matrix products, arithmetic and copies ran while one was open for 0% -> 0% of each run, Pallas kernels for 8% -> 9%
where the time goes in v8:
time: 32.1 us; the launch traced here: 31.9 us
  starting transfers between devices  14.8 us (46%)
  Pallas kernels  8.5 us (26%)
  waiting for transfers between devices  6.22 us (19%)
  local copies, waits for them, and re-layouts  1.63 us (5%)
  between operations  0.79 us (2%)
    pallas_call x6, Pallas kernels, call(): pl.pallas_call(kernel, out_shape=outs, in_specs=[pl.BlockSpec(memory_spac...  8.5 us
    ppermute x6, starting transfers between devices, to_replicas(): lax.ppermute(parts[step], 'dp', swap_route(step, count))  8.07 us
    ppermute x2, starting transfers between devices, swap_sections(): lax.ppermute(far, 'section', [(i, (i + 2 * (i % 2) - 1) % count) for i in...  6.64 us
    ppermute x2, waiting for transfers between devices, swap_sections(): lax.ppermute(far, 'section', [(i, (i + 2 * (i % 2) - 1) % count) for i in...  3.58 us
    ppermute x6, waiting for transfers between devices, to_replicas(): lax.ppermute(parts[step], 'dp', swap_route(step, count))  2.64 us
    unnamed x28, local copies, waits for them, and re-layouts  1.63 us
  transfers between devices with their start and end apart: 10, of which 6 were waited for; matrix products, arithmetic and copies ran while one was open for 0% of the time, Pallas kernels for 9%

profile of v8, /device:TPU:0, one launch (start us, length us, event | category | flops | bytes accessed | tf_op | source)
XLA Modules:
  0.0 31.9 jit_solution(6169757605781766821)
XLA Ops:
  0.8 0.5 %copy-done.3 = s32[1,32]{1,0:T(1,128)S(1)} copy-done((s32[1,32]{1,0:T(1,128)S(1)}, s32[1,32]{1,0:T(1,128)}, u32[]{:S(2)}) %copy-start.3) | copy-done | bytes 152
  1.3 0.6 %copy-done.1 = bf16[1,32,128,128]{3,2,1,0:T(8,128)(2,1)S(1)} copy-done((bf16[1,32,128,128]{3,2,1,0:T(8,128)(2,1)S(1)}, bf16[1,32,128,128]{3,2,1,0:T(8,128)(2,1)}, u32[]{:S(2)}) %copy-start.1) | copy-done | bytes 1048600
  1.9 0.3 %copy-done = bf16[1,32,128,128]{3,2,1,0:T(8,128)(2,1)S(1)} copy-done((bf16[1,32,128,128]{3,2,1,0:T(8,128)(2,1)S(1)}, bf16[1,32,128,128]{3,2,1,0:T(8,128)(2,1)}, u32[]{:S(2)}) %copy-start) | copy-done | bytes 1048600
  2.3 0.0 copy-done.8
  2.3 0.0 copy-done.4
  2.4 4.5 %shard_map.182 = (bf16[16,4096]{1,0:T(8,128)(2,1)S(1)}, bf16[16,4096]{1,0:T(8,128)(2,1)S(1)}, f32[32,24,128]{2,1,0:T(8,128)S(1)}, f32[32,8,128]{2,1,0:T(8,128)S(...) custom-call(s32[1,32]{1,0:T(1,128)S(1)} %copy-done.2, ...), custom_call_target="tpu_custom_call" | custom-call | flops 10000000000 | bytes 100000000 | tf_op jit(solution)/shard_map/pallas_call | solution.py:241
  6.9 4.0 %collective-permute-start.4 = (bf16[10,16,1024]{2,1,0:T(8,128)(2,1)S(1)}, bf16[10,16,1024]{2,1,0:T(8,128)(2,1)S(1)}, u32[]{:S(2)}, u32[]{:S(2)}) collective-permute-start(bf16[10,16,1024]{2,1,0:T(8,128)(2,1)S(1)} %get-tuple-element.30), channel_id=1, source_target_pairs={{0,3},{1,2},{2,1},{3,0},{4,7},{5,6},{6,5},{7,4},{8,11},{9,10},{10,... | collective-permute-start | bytes 983048 | tf_op jit(solution)/shard_map/ppermute | solution.py:277
  10.8 0.5 %collective-permute-start.5 = (bf16[10,16,1024]{2,1,0:T(8,128)(2,1)S(1)}, bf16[10,16,1024]{2,1,0:T(8,128)(2,1)S(1)}, u32[]{:S(2)}, u32[]{:S(2)}) collective-permute-start(bf16[10,16,1024]{2,1,0:T(8,128)(2,1)S(1)} %get-tuple-element.31), channel_id=1, source_target_pairs={{0,1},{1,0},{2,3},{3,2},{4,5},{5,4},{6,7},{7,6},{8,9},{9,8},{10,11... | collective-permute-start | bytes 983048 | tf_op jit(solution)/shard_map/ppermute | solution.py:277
  11.4 3.7 %collective-permute-start.1 = (bf16[16,4096]{1,0:T(8,128)(2,1)S(1)}, bf16[16,4096]{1,0:T(8,128)(2,1)S(1)}, u32[]{:S(2)}, u32[]{:S(2)}) collective-permute-start(bf16[16,4096]{1,0:T(8,128)(2,1)S(1)} %get-tuple-element.24), channel_id=1, source_target_pairs={{0,28},{4,8},{8,4},{12,16},{16,12},{20,24},{24,20},{28,0},{1,29},{... | collective-permute-start | bytes 393224 | tf_op jit(solution)/shard_map/ppermute | solution.py:30
  15.1 0.5 %collective-permute-start.6 = (bf16[10,16,1024]{2,1,0:T(8,128)(2,1)S(1)}, bf16[10,16,1024]{2,1,0:T(8,128)(2,1)S(1)}, u32[]{:S(2)}, u32[]{:S(2)}) collective-permute-start(bf16[10,16,1024]{2,1,0:T(8,128)(2,1)S(1)} %get-tuple-element.32), channel_id=1, source_target_pairs={{0,2},{1,3},{2,0},{3,1},{4,6},{5,7},{6,4},{7,5},{8,10},{9,11},{10,... | collective-permute-start | bytes 983048 | tf_op jit(solution)/shard_map/ppermute | solution.py:277
  15.6 2.8 %collective-permute-done.1.refs_5_ = bf16[16,4096]{1,0:T(8,128)(2,1)S(1)} collective-permute-done((bf16[16,4096]{1,0:T(8,128)(2,1)S(1)}, bf16[16,4096]{1,0:T(8,128)(2,1)S(1)}, u32[]{:S(2)}, u32[]{:S(2)}) %collective-permute-start.1) | collective-permute-done | bytes 131104 | tf_op jit(solution)/shard_map/ppermute | solution.py:30
  18.4 2.5 %shard_map.183 = (bf16[16,4096]{1,0:T(8,128)(2,1)S(1)}, bf16[16,4096]{1,0:T(8,128)(2,1)S(1)}, bf16[2,16,1024]{2,1,0:T(8,128)(2,1)S(1)}, bf16[2,16,1024]{2,1,0:T(...) custom-call(s32[1,32]{1,0:T(1,128)S(1)} %copy-done.2, s32[1,32]{1,0:T(1,128)S(1)} %copy-done.3, ...), custom_call_target="tpu_custom_call" | custom-call | flops 10000 | bytes 100 | tf_op jit(solution)/shard_map/pallas_call | solution.py:241
  20.9 0.1 collective-permute-start.2
  21.0 2.9 %collective-permute-start.3 = (bf16[16,4096]{1,0:T(8,128)(2,1)S(1)}, bf16[16,4096]{1,0:T(8,128)(2,1)S(1)}, u32[]{:S(2)}, u32[]{:S(2)}) collective-permute-start(bf16[16,4096]{1,0:T(8,128)(2,1)S(1)} %get-tuple-element.28), channel_id=1, source_target_pairs={{0,28},{4,8},{8,4},{12,16},{16,12},{20,24},{24,20},{28,0},{1,29},{... | collective-permute-start | bytes 393224 | tf_op jit(solution)/shard_map/ppermute | solution.py:30
  24.0 1.5 %collective-permute-start.7 = (bf16[2,16,1024]{2,1,0:T(8,128)(2,1)S(1)}, bf16[2,16,1024]{2,1,0:T(8,128)(2,1)S(1)}, u32[]{:S(2)}, u32[]{:S(2)}) collective-permute-start(bf16[2,16,1024]{2,1,0:T(8,128)(2,1)S(1)} %get-tuple-element.37), channel_id=1, source_target_pairs={{0,3},{1,2},{2,1},{3,0},{4,7},{5,6},{6,5},{7,4},{8,11},{9,10},{10,... | collective-permute-start | bytes 196616 | tf_op jit(solution)/shard_map/ppermute | solution.py:277
  25.5 0.5 %collective-permute-start.8 = (bf16[2,16,1024]{2,1,0:T(8,128)(2,1)S(1)}, bf16[2,16,1024]{2,1,0:T(8,128)(2,1)S(1)}, u32[]{:S(2)}, u32[]{:S(2)}) collective-permute-start(bf16[2,16,1024]{2,1,0:T(8,128)(2,1)S(1)} %get-tuple-element.38), channel_id=1, source_target_pairs={{0,1},{1,0},{2,3},{3,2},{4,5},{5,4},{6,7},{7,6},{8,9},{9,8},{10,11... | collective-permute-start | bytes 196616 | tf_op jit(solution)/shard_map/ppermute | solution.py:277
  26.0 0.5 %collective-permute-done.5.refs_2_.refs_5_ = bf16[10,16,1024]{2,1,0:T(8,128)(2,1)S(1)} collective-permute-done((bf16[10,16,1024]{2,1,0:T(8,128)(2,1)S(1)}, bf16[10,16,1024]{2,1,0:T(8,128)(2,1)S(1)}, u32[]{:S(2)}, u32[]{:S(2)}) %collective-permute-start.5) | collective-permute-done | bytes 327712 | tf_op jit(solution)/shard_map/ppermute | solution.py:277
  26.5 1.0 %collective-permute-start.9 = (bf16[2,16,1024]{2,1,0:T(8,128)(2,1)S(1)}, bf16[2,16,1024]{2,1,0:T(8,128)(2,1)S(1)}, u32[]{:S(2)}, u32[]{:S(2)}) collective-permute-start(bf16[2,16,1024]{2,1,0:T(8,128)(2,1)S(1)} %get-tuple-element.39), channel_id=1, source_target_pairs={{0,2},{1,3},{2,0},{3,1},{4,6},{5,7},{6,4},{7,5},{8,10},{9,11},{10,... | collective-permute-start | bytes 196616 | tf_op jit(solution)/shard_map/ppermute | solution.py:277
  27.5 0.3 %shard_map.184.refs_2_ = f32[2,8,128,128]{3,2,1,0:T(8,128)S(1)} custom-call(bf16[10,16,1024]{2,1,0:T(8,128)(2,1)S(1)} %get-tuple-element.29.refs_0_.refs_3_, bf16[10,16,1024]{2,1,0:T(8,128)(2,1)S(1)} %collective-permute-done.4.refs_1_.refs_4_, bf16[10,16,1024]{2,1,0:T(8,128)(2,1)S(1)} %collective-permute-done.5.refs_2_.refs_5_, ...), custom_call_target="tpu_custom_call" | custom-call | flops 10000 | bytes 100 | tf_op jit(solution)/shard_map/pallas_call | solution.py:241
  27.9 0.7 %collective-permute-done.3.refs_1_ = bf16[16,4096]{1,0:T(8,128)(2,1)S(1)} collective-permute-done((bf16[16,4096]{1,0:T(8,128)(2,1)S(1)}, bf16[16,4096]{1,0:T(8,128)(2,1)S(1)}, u32[]{:S(2)}, u32[]{:S(2)}) %collective-permute-start.3) | collective-permute-done | bytes 131104 | tf_op jit(solution)/shard_map/ppermute | solution.py:30
  28.6 0.6 %collective-permute-done.7.refs_8_ = bf16[2,16,1024]{2,1,0:T(8,128)(2,1)S(1)} collective-permute-done((bf16[2,16,1024]{2,1,0:T(8,128)(2,1)S(1)}, bf16[2,16,1024]{2,1,0:T(8,128)(2,1)S(1)}, u32[]{:S(2)}, u32[]{:S(2)}) %collective-permute-start.7) | collective-permute-done | bytes 65568 | tf_op jit(solution)/shard_map/ppermute | solution.py:277
  29.2 0.5 %collective-permute-done.8.refs_9_ = bf16[2,16,1024]{2,1,0:T(8,128)(2,1)S(1)} collective-permute-done((bf16[2,16,1024]{2,1,0:T(8,128)(2,1)S(1)}, bf16[2,16,1024]{2,1,0:T(8,128)(2,1)S(1)}, u32[]{:S(2)}, u32[]{:S(2)}) %collective-permute-start.8) | collective-permute-done | bytes 65568 | tf_op jit(solution)/shard_map/ppermute | solution.py:277
  29.7 1.0 %collective-permute-done.9.refs_10_ = bf16[2,16,1024]{2,1,0:T(8,128)(2,1)S(1)} collective-permute-done((bf16[2,16,1024]{2,1,0:T(8,128)(2,1)S(1)}, bf16[2,16,1024]{2,1,0:T(8,128)(2,1)S(1)}, u32[]{:S(2)}, u32[]{:S(2)}) %collective-permute-start.9) | collective-permute-done | bytes 65568 | tf_op jit(solution)/shard_map/ppermute | solution.py:277
  30.8 1.2 %shard_map.186 = (bf16[1,8,4096]{2,1,0:T(8,128)(2,1)}, bf16[1,8,4096]{2,1,0:T(8,128)(2,1)}, bf16[1,8,4096]{2,1,0:T(8,128)(2,1)}, bf16[1,8,4096]{2,1,0:T(8,128)(2...) custom-call(bf16[16,4096]{1,0:T(8,128)(2,1)S(1)} %collective-permute-done.2.refs_3_.refs_0_, ...), custom_call_target="tpu_custom_call" | custom-call | flops 10000 | bytes 100 | tf_op jit(solution)/shard_map/pallas_call | solution.py:241
  (30 shorter events, 0.2 us)
Async XLA Ops:
  0.6 0.7 %copy-start.3 = (s32[1,32]{1,0:T(1,128)S(1)}, s32[1,32]{1,0:T(1,128)}, u32[]{:S(2)}) copy-start(s32[1,32]{1,0:T(1,128)} %refs_1_.3) | copy-start | bytes 388
  0.6 1.2 %copy-start.1 = (bf16[1,32,128,128]{3,2,1,0:T(8,128)(2,1)S(1)}, bf16[1,32,128,128]{3,2,1,0:T(8,128)(2,1)}, u32[]{:S(2)}) copy-start(bf16[1,32,128,128]{3,2,1,0:T(8,128)(2,1)} %refs_3_.3) | copy-start | bytes 3145732
  0.7 1.2 %copy-start.2 = (s32[1,32]{1,0:T(1,128)S(1)}, s32[1,32]{1,0:T(1,128)}, u32[]{:S(2)}) copy-start(s32[1,32]{1,0:T(1,128)} %refs_0_.3) | copy-start | bytes 388
  0.7 1.5 %copy-start = (bf16[1,32,128,128]{3,2,1,0:T(8,128)(2,1)S(1)}, bf16[1,32,128,128]{3,2,1,0:T(8,128)(2,1)}, u32[]{:S(2)}) copy-start(bf16[1,32,128,128]{3,2,1,0:T(8,128)(2,1)} %refs_2_.3) | copy-start | bytes 3145732
  0.7 1.5 %copy-start.7 = (bf16[1,2,8,4096]{3,2,1,0:T(8,128)(2,1)S(1)}, bf16[1,2,8,4096]{3,2,1,0:T(8,128)(2,1)}, u32[]{:S(2)}) copy-start(bf16[1,2,8,4096]{3,2,1,0:T(8,128)(2,1)} %refs_10_.1) | copy-start | bytes 393220
  0.7 1.6 %copy-start.6 = (bf16[1,2,8,4096]{3,2,1,0:T(8,128)(2,1)S(1)}, bf16[1,2,8,4096]{3,2,1,0:T(8,128)(2,1)}, u32[]{:S(2)}) copy-start(bf16[1,2,8,4096]{3,2,1,0:T(8,128)(2,1)} %refs_9_.1) | copy-start | bytes 393220
  0.7 1.6 %copy-start.5 = (bf16[1,2,8,4096]{3,2,1,0:T(8,128)(2,1)S(1)}, bf16[1,2,8,4096]{3,2,1,0:T(8,128)(2,1)}, u32[]{:S(2)}) copy-start(bf16[1,2,8,4096]{3,2,1,0:T(8,128)(2,1)} %refs_8_.1) | copy-start | bytes 393220
  0.7 1.6 %copy-start.8 = (bf16[1,2,8,4096]{3,2,1,0:T(8,128)(2,1)S(1)}, bf16[1,2,8,4096]{3,2,1,0:T(8,128)(2,1)}, u32[]{:S(2)}) copy-start(bf16[1,2,8,4096]{3,2,1,0:T(8,128)(2,1)} %refs_13_.1) | copy-start | bytes 393220
  0.7 1.6 %copy-start.4 = (bf16[1,2,8,4096]{3,2,1,0:T(8,128)(2,1)S(1)}, bf16[1,2,8,4096]{3,2,1,0:T(8,128)(2,1)}, u32[]{:S(2)}) copy-start(bf16[1,2,8,4096]{3,2,1,0:T(8,128)(2,1)} %refs_7_.1) | copy-start | bytes 393220
  0.7 1.6 %copy-start.10 = (bf16[1,8,4096]{2,1,0:T(8,128)(2,1)S(1)}, bf16[1,8,4096]{2,1,0:T(8,128)(2,1)}, u32[]{:S(2)}) copy-start(bf16[1,8,4096]{2,1,0:T(8,128)(2,1)} %refs_6_.1) | copy-start | bytes 196612
  0.7 1.6 %copy-start.12 = (bf16[1,8,4096]{2,1,0:T(8,128)(2,1)S(1)}, bf16[1,8,4096]{2,1,0:T(8,128)(2,1)}, u32[]{:S(2)}) copy-start(bf16[1,8,4096]{2,1,0:T(8,128)(2,1)} %refs_12_.1) | copy-start | bytes 196612
  0.7 1.6 %copy-start.9 = (bf16[1,8,4096]{2,1,0:T(8,128)(2,1)S(1)}, bf16[1,8,4096]{2,1,0:T(8,128)(2,1)}, u32[]{:S(2)}) copy-start(bf16[1,8,4096]{2,1,0:T(8,128)(2,1)} %refs_5_.1) | copy-start | bytes 196612
  0.8 1.6 %copy-start.11 = (bf16[1,8,4096]{2,1,0:T(8,128)(2,1)S(1)}, bf16[1,8,4096]{2,1,0:T(8,128)(2,1)}, u32[]{:S(2)}) copy-start(bf16[1,8,4096]{2,1,0:T(8,128)(2,1)} %refs_11_.1) | copy-start | bytes 196612
  0.8 1.6 %copy-start.13 = (s32[1,2]{1,0:T(1,128)S(1)}, s32[1,2]{1,0:T(1,128)}, u32[]{:S(2)}) copy-start(s32[1,2]{1,0:T(1,128)} %refs_2_.2) | copy-start | bytes 28
  6.9 18.6 %collective-permute-start.4 = (bf16[10,16,1024]{2,1,0:T(8,128)(2,1)S(1)}, bf16[10,16,1024]{2,1,0:T(8,128)(2,1)S(1)}, u32[]{:S(2)}, u32[]{:S(2)}) collective-permute-start(bf16[10,16,1024]{2,1,0:T(8,128)(2,1)S(1)} %get-tuple-element.30), channel_id=1, source_target_pairs={{0,3},{1,2},{2,1},{3,0},{4,7},{5,6},{6,5},{7,4},{8,11},{9,10},{10,... | collective-permute-start | bytes 983048 | tf_op jit(solution)/shard_map/ppermute | solution.py:277
  10.8 15.7 %collective-permute-start.5 = (bf16[10,16,1024]{2,1,0:T(8,128)(2,1)S(1)}, bf16[10,16,1024]{2,1,0:T(8,128)(2,1)S(1)}, u32[]{:S(2)}, u32[]{:S(2)}) collective-permute-start(bf16[10,16,1024]{2,1,0:T(8,128)(2,1)S(1)} %get-tuple-element.31), channel_id=1, source_target_pairs={{0,1},{1,0},{2,3},{3,2},{4,5},{5,4},{6,7},{7,6},{8,9},{9,8},{10,11... | collective-permute-start | bytes 983048 | tf_op jit(solution)/shard_map/ppermute | solution.py:277
  11.4 4.2 %collective-permute-start = (bf16[16,4096]{1,0:T(8,128)(2,1)S(1)}, bf16[16,4096]{1,0:T(8,128)(2,1)S(1)}, u32[]{:S(2)}, u32[]{:S(2)}) collective-permute-start(bf16[16,4096]{1,0:T(8,128)(2,1)S(1)} %get-tuple-element.23), channel_id=1, source_target_pairs={{0,4},{4,0},{8,12},{12,8},{16,20},{20,16},{24,28},{28,24},{1,5},{5... | collective-permute-start | bytes 393224 | tf_op jit(solution)/shard_map/ppermute | solution.py:31
  11.4 7.1 %collective-permute-start.1 = (bf16[16,4096]{1,0:T(8,128)(2,1)S(1)}, bf16[16,4096]{1,0:T(8,128)(2,1)S(1)}, u32[]{:S(2)}, u32[]{:S(2)}) collective-permute-start(bf16[16,4096]{1,0:T(8,128)(2,1)S(1)} %get-tuple-element.24), channel_id=1, source_target_pairs={{0,28},{4,8},{8,4},{12,16},{16,12},{20,24},{24,20},{28,0},{1,29},{... | collective-permute-start | bytes 393224 | tf_op jit(solution)/shard_map/ppermute | solution.py:30
  15.1 12.5 %collective-permute-start.6 = (bf16[10,16,1024]{2,1,0:T(8,128)(2,1)S(1)}, bf16[10,16,1024]{2,1,0:T(8,128)(2,1)S(1)}, u32[]{:S(2)}, u32[]{:S(2)}) collective-permute-start(bf16[10,16,1024]{2,1,0:T(8,128)(2,1)S(1)} %get-tuple-element.32), channel_id=1, source_target_pairs={{0,2},{1,3},{2,0},{3,1},{4,6},{5,7},{6,4},{7,5},{8,10},{9,11},{10,... | collective-permute-start | bytes 983048 | tf_op jit(solution)/shard_map/ppermute | solution.py:277
  20.9 3.0 %collective-permute-start.2 = (bf16[16,4096]{1,0:T(8,128)(2,1)S(1)}, bf16[16,4096]{1,0:T(8,128)(2,1)S(1)}, u32[]{:S(2)}, u32[]{:S(2)}) collective-permute-start(bf16[16,4096]{1,0:T(8,128)(2,1)S(1)} %get-tuple-element.27), channel_id=1, source_target_pairs={{0,4},{4,0},{8,12},{12,8},{16,20},{20,16},{24,28},{28,24},{1,5},{5... | collective-permute-start | bytes 393224 | tf_op jit(solution)/shard_map/ppermute | solution.py:31
  21.0 7.6 %collective-permute-start.3 = (bf16[16,4096]{1,0:T(8,128)(2,1)S(1)}, bf16[16,4096]{1,0:T(8,128)(2,1)S(1)}, u32[]{:S(2)}, u32[]{:S(2)}) collective-permute-start(bf16[16,4096]{1,0:T(8,128)(2,1)S(1)} %get-tuple-element.28), channel_id=1, source_target_pairs={{0,28},{4,8},{8,4},{12,16},{16,12},{20,24},{24,20},{28,0},{1,29},{... | collective-permute-start | bytes 393224 | tf_op jit(solution)/shard_map/ppermute | solution.py:30
  24.0 5.2 %collective-permute-start.7 = (bf16[2,16,1024]{2,1,0:T(8,128)(2,1)S(1)}, bf16[2,16,1024]{2,1,0:T(8,128)(2,1)S(1)}, u32[]{:S(2)}, u32[]{:S(2)}) collective-permute-start(bf16[2,16,1024]{2,1,0:T(8,128)(2,1)S(1)} %get-tuple-element.37), channel_id=1, source_target_pairs={{0,3},{1,2},{2,1},{3,0},{4,7},{5,6},{6,5},{7,4},{8,11},{9,10},{10,... | collective-permute-start | bytes 196616 | tf_op jit(solution)/shard_map/ppermute | solution.py:277
  25.5 4.3 %collective-permute-start.8 = (bf16[2,16,1024]{2,1,0:T(8,128)(2,1)S(1)}, bf16[2,16,1024]{2,1,0:T(8,128)(2,1)S(1)}, u32[]{:S(2)}, u32[]{:S(2)}) collective-permute-start(bf16[2,16,1024]{2,1,0:T(8,128)(2,1)S(1)} %get-tuple-element.38), channel_id=1, source_target_pairs={{0,1},{1,0},{2,3},{3,2},{4,5},{5,4},{6,7},{7,6},{8,9},{9,8},{10,11... | collective-permute-start | bytes 196616 | tf_op jit(solution)/shard_map/ppermute | solution.py:277
  26.5 4.3 %collective-permute-start.9 = (bf16[2,16,1024]{2,1,0:T(8,128)(2,1)S(1)}, bf16[2,16,1024]{2,1,0:T(8,128)(2,1)S(1)}, u32[]{:S(2)}, u32[]{:S(2)}) collective-permute-start(bf16[2,16,1024]{2,1,0:T(8,128)(2,1)S(1)} %get-tuple-element.39), channel_id=1, source_target_pairs={{0,2},{1,3},{2,0},{3,1},{4,6},{5,7},{6,4},{7,5},{8,10},{9,11},{10,... | collective-permute-start | bytes 196616 | tf_op jit(solution)/shard_map/ppermute | solution.py:277

commit v9 on v8

--- a/solution.py
+++ b/solution.py
@@ -11,6 +11,7 @@
 LIMIT = 40 * 1024 * 1024
 WORK = 10 ** 10
 LIGHT = 10 ** 4
+STREAMS = LIGHT
 
 
 def partner(me, step, count):
@@ -90,16 +91,15 @@
     token[...] = jnp.zeros(token.shape, F32)
 
 
-def back_first(count, per, up_idx, down_idx, order, w_up, w_down, g_ref, a_ref, back, second, second_tan,
-               second_grad, pack, keep, sends, pulled, returned, hidden):
+def first_rows(count, per, up_idx, down_idx, order, w_up, w_down, g_ref, a_ref, back, second, second_tan, second_grad,
+               keep, pushes, *refs):
+    sends, (pulled, hidden) = refs[:count], refs[count:]
     blocks = count * per
     me = lax.axis_index("dp")
     for b in range(blocks):
         pulled[b] = jnp.zeros(pulled.shape[1:], F32)
     m0 = order[0, 0]
     m1 = order[0, 1]
-    for b in range(blocks):
-        returned[b] = stack([g_ref[0, :, lanes(b)], a_ref[0, :, lanes(b)]])
     for step, place, i in send_order(me, count, per):
         at = lanes(i)
         c = stack([g_ref[0, :, at], a_ref[0, :, at], second_grad[0, m0, :, at], second_grad[0, m1, :, at]]).astype(BF16)
@@ -131,9 +131,7 @@
         hidden[j] = jnp.concatenate(
             [zb0 * sb0, za0 * sa0, slope_a0 * ta0, slope_a1 * ta1, zb1 * sb1, za1 * sa1], 0).astype(BF16)
         keep[j] = jnp.concatenate([slope_of(zb1, sb1), slope_a1, curve_a1 * ga1 * ta1], 0)
-        returned[u] = returned[u] + times_transposed(e, w_up[0, j])
-    for b in range(blocks):
-        pack[:, lanes(b)] = returned[b].astype(BF16)
+        pushes[:, lanes(j)] = e
     for step, place, i in send_order(me, count, per):
         y = hidden[down_idx[0, i]]
         for group in range(3):
@@ -156,12 +154,17 @@
         pack[:, at] = moved.astype(BF16)
 
 
-def first_tick(count, per, up_idx, down_idx, order, w_up, w_down, g_ref, a_ref, back, second, second_tan, second_grad,
-               v_ref, t_ref, tan, near, far, keep, keep_tan, *refs):
-    sends, (packs, pulled, returned, hidden, hidden_fwd) = refs[:count], refs[count:]
-    back_first(count, per, up_idx, down_idx, order, w_up, w_down, g_ref, a_ref, back, second, second_tan,
-               second_grad, packs.at[1], keep, sends, pulled, returned, hidden)
-    forward_first(count * per, up_idx, down_idx, order, w_up, w_down, v_ref, t_ref, tan, packs.at[0], keep_tan, hidden_fwd)
+def first_streams(count, per, up_idx, down_idx, order, w_up, w_down, g_ref, a_ref, pushes, v_ref, t_ref, tan,
+                  near, far, keep_tan, packs, returned, hidden):
+    blocks = count * per
+    for b in range(blocks):
+        returned[b] = stack([g_ref[0, :, lanes(b)], a_ref[0, :, lanes(b)]])
+    for j in range(blocks):
+        u = up_idx[0, j]
+        returned[u] = returned[u] + times_transposed(pushes[:, lanes(j)], w_up[0, j])
+    for b in range(blocks):
+        packs[1, :, lanes(b)] = returned[b].astype(BF16)
+    forward_first(blocks, up_idx, down_idx, order, w_up, w_down, v_ref, t_ref, tan, packs.at[0], keep_tan, hidden)
     hand_out(packs, near, far)
 
 
@@ -196,12 +199,33 @@
         pack[:, at] = (rows[:, at].astype(F32) + times(hidden[down_idx[0, i]], w_down[0, i])).astype(BF16)
 
 
-def second_tick(count, per, up_idx, down_idx, w_up, w_down, near_in, far_in, keep, keep_tan, near, far, *refs):
-    sends, (came, packs, pulled, returned, hidden) = refs[:count], refs[count:]
-    take_in(near_in, far_in, came)
-    back_second(count, per, up_idx, down_idx, w_up, w_down, came.at[1], keep, packs.at[1], sends, pulled, returned)
-    forward_second(count * per, up_idx, down_idx, w_up, w_down, came.at[0], keep_tan, packs.at[0], hidden)
-    hand_out(packs, near, far)
+def near_phase(count, per, up_idx, down_idx, w_up, w_down, near_in, keep, keep_tan, far, *refs):
+    sends, (pulled, returned, hidden) = refs[:count], refs[count:]
+    odd = odd_section()
+
+    @pl.when(odd == 0)
+    def _():
+        back_second(count, per, up_idx, down_idx, w_up, w_down, near_in, keep, far, sends, pulled, returned)
+
+    @pl.when(odd == 1)
+    def _():
+        forward_second(count * per, up_idx, down_idx, w_up, w_down, near_in, keep_tan, far, hidden)
+
+
+def far_phase(count, per, up_idx, down_idx, w_up, w_down, far_in, keep, keep_tan, *refs):
+    done, near, refs = refs[:count], refs[count], refs[count + 1:]
+    sends, (pulled, returned, hidden) = refs[:count], refs[count:]
+    odd = odd_section()
+
+    @pl.when(odd == 0)
+    def _():
+        for source, target in zip(done, sends):
+            target[...] = source[...]
+        forward_second(count * per, up_idx, down_idx, w_up, w_down, far_in, keep_tan, near, hidden)
+
+    @pl.when(odd == 1)
+    def _():
+        back_second(count, per, up_idx, down_idx, w_up, w_down, far_in, keep, near, sends, pulled, returned)
 
 
 def early_grads(count, per, *refs):
@@ -214,7 +238,7 @@
             grads[out, place] = outer(xs, es)
 
 
-def finish(count, per, scale, near, far, grads, *rest):
+def finish(count, per, scale, far, near, grads, *rest):
     early, late = rest[:count], rest[count:2 * count]
     values, score, tangent, adjoint, grad_up, grad_down, came = rest[2 * count:]
     take_in(near, far, came)
@@ -249,12 +273,6 @@
     )(*operands, *after)
 
 
-def hand_on(*refs):
-    half = len(refs) // 2
-    for source, target in zip(refs[:half], refs[half:]):
-        target[...] = source[...]
-
-
 def on_device(w_up, up_index, w_down, down_index, tick_order, values_in, score_grad_in, tangent_in, state_adjoint_in,
               saved_back, saved_tan, saved_second, saved_second_tan, saved_second_grad):
     count = lax.axis_size("dp")
@@ -279,32 +297,36 @@
     rows = (score_grad_in, state_adjoint_in, saved_back, saved_second, saved_second_tan, saved_second_grad)
     ten = shape((10, 16, part), BF16)
     (token,) = call(open_launch, (), [], [shape((8, BLOCK), F32)], [], cost=WORK)
-    near, far, keep, keep_tan, *early = call(
-        body(first_tick, count, per),
-        (up_index, down_index, tick_order, w_up, w_down) + rows + (values_in, tangent_in, saved_tan),
-        [smem] * 3 + [vmem] * 11,
-        [pair, pair, shape((blocks, 24, BLOCK), F32), shape((blocks, 8, BLOCK), F32)] + [ten] * count,
-        [vmem((2, 16, width), BF16), vmem((blocks, 32, BLOCK), F32), vmem((blocks, 16, BLOCK), F32),
-         vmem((blocks, 48, BLOCK), BF16), vmem((blocks, 16, BLOCK), BF16)],
+    tables = (up_index, down_index, tick_order, w_up, w_down)
+    keep, pushes, *early = call(
+        body(first_rows, count, per), tables + rows, [smem] * 3 + [vmem] * 8,
+        [shape((blocks, 24, BLOCK), F32), pair] + [ten] * count,
+        [vmem((blocks, 32, BLOCK), F32), vmem((blocks, 48, BLOCK), BF16)],
         after=(token,), cost=WORK)
+    near, far, keep_tan = call(
+        body(first_streams, count, per),
+        tables + (score_grad_in, state_adjoint_in, pushes, values_in, tangent_in, saved_tan), [smem] * 3 + [vmem] * 8,
+        [pair, pair, shape((blocks, 8, BLOCK), F32)],
+        [vmem((2, 16, width), BF16), vmem((blocks, 16, BLOCK), F32), vmem((blocks, 16, BLOCK), BF16)], cost=STREAMS)
     near, far = swap_sections(near, far)
     early = to_replicas(early)
-    near, far, *late = call(
-        body(second_tick, count, per), (up_index, down_index, w_up, w_down, near, far, keep, keep_tan),
-        [smem] * 2 + [vmem] * 6,
-        [pair, pair] + [shape((2, 16, part), BF16)] * count,
-        [vmem((2, 16, width), BF16), vmem((2, 16, width), BF16), vmem((blocks, 16, BLOCK), F32),
-         vmem((blocks, 16, BLOCK), F32), vmem((blocks, 16, BLOCK), BF16)])
-    near, far = swap_sections(near, far)
-    two = shape((2, 16, part), BF16)
-    held = call(hand_on, tuple(late[1:]), [vmem] * (count - 1), [two] * (count - 1), [], after=(near,))
-    late = to_replicas(late[:1] + list(held))
+    tables = (up_index, down_index, w_up, w_down)
+    two = [shape((2, 16, part), BF16)] * count
+    scratch = [vmem((blocks, 16, BLOCK), F32), vmem((blocks, 16, BLOCK), F32), vmem((blocks, 16, BLOCK), BF16)]
+    far_out, *late = call(
+        body(near_phase, count, per), tables + (near, keep, keep_tan), [smem] * 2 + [vmem] * 5, [pair] + two, scratch)
+    near_out, *late = call(
+        body(far_phase, count, per), tables + (far, keep, keep_tan, *late), [smem] * 2 + [vmem] * (5 + count),
+        [pair] + two, scratch)
+    near, far = swap_sections(near_out, far_out)
+    late = to_replicas(late)
     (grads,) = call(
-        body(early_grads, count, per), tuple(early), [vmem] * count, [shape((2, per, BLOCK, BLOCK), F32)], [])
+        body(early_grads, count, per), tuple(early), [vmem] * count, [shape((2, per, BLOCK, BLOCK), F32)], [],
+        after=(far,))
     stream = shape((1,) + values_in.shape[1:], BF16)
     grad = shape((1, per, BLOCK, BLOCK), BF16)
     return tuple(call(
-        body(finish, count, per, scale), (near, far, grads, *early, *late), [vmem] * (3 + 2 * count),
+        body(finish, count, per, scale), (far, near, grads, *early, *late), [vmem] * (3 + 2 * count),
         [stream, stream, stream, stream, grad, grad], [vmem((2, 16, width), BF16)]))
 
 

time: 32.1 us -> 31.2 us (0.972)
  starting transfers between devices: 14.8 us -> 12.3 us
  waiting for transfers between devices: 6.22 us -> 8.02 us
    ppermute x2, starting transfers between devices: 6.64 us -> 4.01 us  [swap_sections(): lax.ppermute(far, 'section', [(i, (i + 2 * (i % 2) - 1) % count) for i in...]
    ppermute x2, waiting for transfers between devices: 3.58 us -> 4.58 us  [swap_sections(): lax.ppermute(far, 'section', [(i, (i + 2 * (i % 2) - 1) % count) for i in...]
    ppermute x6, waiting for transfers between devices: 2.64 us -> 3.43 us  [to_replicas(): lax.ppermute(parts[step], 'dp', swap_route(step, count))]
    pallas_call x6 -> x7, Pallas kernels: 8.5 us -> 8.32 us  [call(): pl.pallas_call(kernel, out_shape=outs, in_specs=[pl.BlockSpec(memory_spac...]
  transfers between devices with their start and end apart: 10 -> 10, of which waited for: 6 -> 5; matrix products, arithmetic and copies ran while one was open for 0% -> 0% of each run, Pallas kernels for 9% -> 18%
where the time goes in v9:
time: 31.2 us; the launch traced here: 31.1 us
  starting transfers between devices  12.3 us (39%)
  Pallas kernels  8.32 us (27%)
  waiting for transfers between devices  8.02 us (26%)
  local copies, waits for them, and re-layouts  1.66 us (5%)
  between operations  0.79 us (3%)
    pallas_call x7, Pallas kernels, call(): pl.pallas_call(kernel, out_shape=outs, in_specs=[pl.BlockSpec(memory_spac...  8.32 us
    ppermute x6, starting transfers between devices, to_replicas(): lax.ppermute(parts[step], 'dp', swap_route(step, count))  8.16 us
    ppermute x2, waiting for transfers between devices, swap_sections(): lax.ppermute(far, 'section', [(i, (i + 2 * (i % 2) - 1) % count) for i in...  4.58 us
    ppermute x2, starting transfers between devices, swap_sections(): lax.ppermute(far, 'section', [(i, (i + 2 * (i % 2) - 1) % count) for i in...  4.01 us
    ppermute x6, waiting for transfers between devices, to_replicas(): lax.ppermute(parts[step], 'dp', swap_route(step, count))  3.43 us
    unnamed x28, local copies, waits for them, and re-layouts  1.66 us
  transfers between devices with their start and end apart: 10, of which 5 were waited for; matrix products, arithmetic and copies ran while one was open for 0% of the time, Pallas kernels for 18%

profile of v9, /device:TPU:0, one launch (start us, length us, event | category | flops | bytes accessed | tf_op | source)
XLA Modules:
  0.0 31.1 jit_solution(15615281824133896320)
XLA Ops:
  0.8 0.5 %copy-done.8 = s32[1,32]{1,0:T(1,128)S(1)} copy-done((s32[1,32]{1,0:T(1,128)S(1)}, s32[1,32]{1,0:T(1,128)}, u32[]{:S(2)}) %copy-start.8) | copy-done | bytes 152
  1.3 0.6 %copy-done.1 = bf16[1,32,128,128]{3,2,1,0:T(8,128)(2,1)S(1)} copy-done((bf16[1,32,128,128]{3,2,1,0:T(8,128)(2,1)S(1)}, bf16[1,32,128,128]{3,2,1,0:T(8,128)(2,1)}, u32[]{:S(2)}) %copy-start.1) | copy-done | bytes 1048600
  1.9 0.3 %copy-done = bf16[1,32,128,128]{3,2,1,0:T(8,128)(2,1)S(1)} copy-done((bf16[1,32,128,128]{3,2,1,0:T(8,128)(2,1)S(1)}, bf16[1,32,128,128]{3,2,1,0:T(8,128)(2,1)}, u32[]{:S(2)}) %copy-start) | copy-done | bytes 1048600
  2.4 1.7 %shard_map.182 = (f32[32,24,128]{2,1,0:T(8,128)S(1)}, bf16[16,4096]{1,0:T(8,128)(2,1)S(1)}, bf16[10,16,1024]{2,1,0:T(8,128)(2,1)S(1)}, bf16[10,16,1024]{2,1,0:T(...) custom-call(s32[1,32]{1,0:T(1,128)S(1)} %copy-done.7, s32[1,32]{1,0:T(1,128)S(1)} %copy-done.8, ...), custom_call_target="tpu_custom_call" | custom-call | flops 10000000000 | bytes 100000000 | tf_op jit(solution)/shard_map/pallas_call | solution.py:265
  4.1 4.0 %collective-permute-start.4 = (bf16[10,16,1024]{2,1,0:T(8,128)(2,1)S(1)}, bf16[10,16,1024]{2,1,0:T(8,128)(2,1)S(1)}, u32[]{:S(2)}, u32[]{:S(2)}) collective-permute-start(bf16[10,16,1024]{2,1,0:T(8,128)(2,1)S(1)} %get-tuple-element.37), channel_id=1, source_target_pairs={{0,3},{1,2},{2,1},{3,0},{4,7},{5,6},{6,5},{7,4},{8,11},{9,10},{10,... | collective-permute-start | bytes 983048 | tf_op jit(solution)/shard_map/ppermute | solution.py:295
  8.0 0.5 %collective-permute-start.5 = (bf16[10,16,1024]{2,1,0:T(8,128)(2,1)S(1)}, bf16[10,16,1024]{2,1,0:T(8,128)(2,1)S(1)}, u32[]{:S(2)}, u32[]{:S(2)}) collective-permute-start(bf16[10,16,1024]{2,1,0:T(8,128)(2,1)S(1)} %get-tuple-element.38), channel_id=1, source_target_pairs={{0,1},{1,0},{2,3},{3,2},{4,5},{5,4},{6,7},{7,6},{8,9},{9,8},{10,11... | collective-permute-start | bytes 983048 | tf_op jit(solution)/shard_map/ppermute | solution.py:295
  8.6 1.9 %shard_map.183 = (bf16[16,4096]{1,0:T(8,128)(2,1)S(1)}, bf16[16,4096]{1,0:T(8,128)(2,1)S(1)}, f32[32,8,128]{2,1,0:T(8,128)S(1)}) custom-call(s32[1,32]{1,0:T(1,128)S(1)} %copy-done.7, s32[1,32]{1,0:T(1,128)S(1)} %copy-done.8, s32[1,2]{1,0:T(1,128)S(1)} %copy-done.9, bf16[1,32,128,128]{3,2,1,0:T(8,128)(2,1)S(1)} %copy-done, ...), custom_call_target="tpu_custom_call" | custom-call | flops 10000 | bytes 100 | tf_op jit(solution)/shard_map/pallas_call | solution.py:265
  10.5 0.1 collective-permute-start
  10.6 0.2 collective-permute-start.6
  10.7 3.8 %collective-permute-start.2 = (bf16[16,4096]{1,0:T(8,128)(2,1)S(1)}, bf16[16,4096]{1,0:T(8,128)(2,1)S(1)}, u32[]{:S(2)}, u32[]{:S(2)}) collective-permute-start(bf16[16,4096]{1,0:T(8,128)(2,1)S(1)} %get-tuple-element.30), channel_id=1, source_target_pairs={{0,28},{4,8},{8,4},{12,16},{16,12},{20,24},{24,20},{28,0},{1,29},{... | collective-permute-start | bytes 393224 | tf_op jit(solution)/shard_map/ppermute | solution.py:31
  14.5 1.9 %shard_map.184 = (bf16[16,4096]{1,0:T(8,128)(2,1)S(1)}, bf16[2,16,1024]{2,1,0:T(8,128)(2,1)S(1)}, bf16[2,16,1024]{2,1,0:T(8,128)(2,1)S(1)}, bf16[2,16,1024]{2,1,0:T(8,128)(2,1)S(1)}, bf16[2,16,1024]{2,1,0:T(8,128)(2,1)S(1)}) custom-call(s32[1,32]{1,0:T(1,128)S(1)} %copy-done.7, s32[1,32]{1,0:T(1,128)S(1)} %copy-done.8, ...), custom_call_target="tpu_custom_call" | custom-call | flops 10000 | bytes 100 | tf_op jit(solution)/shard_map/pallas_call | solution.py:265
  16.4 0.2 collective-permute-start.1
  16.7 1.5 %collective-permute-done.2.refs_4_ = bf16[16,4096]{1,0:T(8,128)(2,1)S(1)} collective-permute-done((bf16[16,4096]{1,0:T(8,128)(2,1)S(1)}, bf16[16,4096]{1,0:T(8,128)(2,1)S(1)}, u32[]{:S(2)}, u32[]{:S(2)}) %collective-permute-start.2) | collective-permute-done | bytes 131104 | tf_op jit(solution)/shard_map/ppermute | solution.py:31
  18.1 1.3 %shard_map.185 = (bf16[16,4096]{1,0:T(8,128)(2,1)S(1)}, bf16[2,16,1024]{2,1,0:T(8,128)(2,1)S(1)}, bf16[2,16,1024]{2,1,0:T(8,128)(2,1)S(1)}, bf16[2,16,1024]{2,1,0:T(8,128)(2,1)S(1)}, bf16[2,16,1024]{2,1,0:T(8,128)(2,1)S(1)}) custom-call(s32[1,32]{1,0:T(1,128)S(1)} %copy-done.7, s32[1,32]{1,0:T(1,128)S(1)} %copy-done.8, ...), custom_call_target="tpu_custom_call" | custom-call | flops 10000 | bytes 100 | tf_op jit(solution)/shard_map/pallas_call | solution.py:265
  19.5 0.1 collective-permute-start.3
  19.6 3.1 %collective-permute-done.1.refs_4_.refs_0_ = bf16[16,4096]{1,0:T(8,128)(2,1)S(1)} collective-permute-done((bf16[16,4096]{1,0:T(8,128)(2,1)S(1)}, bf16[16,4096]{1,0:T(8,128)(2,1)S(1)}, u32[]{:S(2)}, u32[]{:S(2)}) %collective-permute-start.1) | collective-permute-done | bytes 131104 | tf_op jit(solution)/shard_map/ppermute | solution.py:31
  22.7 2.4 %collective-permute-start.7 = (bf16[2,16,1024]{2,1,0:T(8,128)(2,1)S(1)}, bf16[2,16,1024]{2,1,0:T(8,128)(2,1)S(1)}, u32[]{:S(2)}, u32[]{:S(2)}) collective-permute-start(bf16[2,16,1024]{2,1,0:T(8,128)(2,1)S(1)} %get-tuple-element.41), channel_id=1, source_target_pairs={{0,3},{1,2},{2,1},{3,0},{4,7},{5,6},{6,5},{7,4},{8,11},{9,10},{10,... | collective-permute-start | bytes 196616 | tf_op jit(solution)/shard_map/ppermute | solution.py:295
  25.1 0.5 %collective-permute-start.8 = (bf16[2,16,1024]{2,1,0:T(8,128)(2,1)S(1)}, bf16[2,16,1024]{2,1,0:T(8,128)(2,1)S(1)}, u32[]{:S(2)}, u32[]{:S(2)}) collective-permute-start(bf16[2,16,1024]{2,1,0:T(8,128)(2,1)S(1)} %get-tuple-element.42), channel_id=1, source_target_pairs={{0,1},{1,0},{2,3},{3,2},{4,5},{5,4},{6,7},{7,6},{8,9},{9,8},{10,11... | collective-permute-start | bytes 196616 | tf_op jit(solution)/shard_map/ppermute | solution.py:295
  25.7 0.5 %collective-permute-start.9 = (bf16[2,16,1024]{2,1,0:T(8,128)(2,1)S(1)}, bf16[2,16,1024]{2,1,0:T(8,128)(2,1)S(1)}, u32[]{:S(2)}, u32[]{:S(2)}) collective-permute-start(bf16[2,16,1024]{2,1,0:T(8,128)(2,1)S(1)} %get-tuple-element.43), channel_id=1, source_target_pairs={{0,2},{1,3},{2,0},{3,1},{4,6},{5,7},{6,4},{7,5},{8,10},{9,11},{10,... | collective-permute-start | bytes 196616 | tf_op jit(solution)/shard_map/ppermute | solution.py:295
  26.2 0.3 %shard_map.186.refs_2_ = f32[2,8,128,128]{3,2,1,0:T(8,128)S(1)} custom-call(bf16[10,16,1024]{2,1,0:T(8,128)(2,1)S(1)} %get-tuple-element.36.refs_0_.refs_3_, bf16[10,16,1024]{2,1,0:T(8,128)(2,1)S(1)} %collective-permute-done.4.refs_1_.refs_4_, bf16[10,16,1024]{2,1,0:T(8,128)(2,1)S(1)} %collective-permute-done.5.refs_2_.refs_5_, ...), custom_call_target="tpu_custom_call" | custom-call | flops 10000 | bytes 100 | tf_op jit(solution)/shard_map/pallas_call | solution.py:265
  26.5 1.3 %collective-permute-done.7.refs_8_ = bf16[2,16,1024]{2,1,0:T(8,128)(2,1)S(1)} collective-permute-done((bf16[2,16,1024]{2,1,0:T(8,128)(2,1)S(1)}, bf16[2,16,1024]{2,1,0:T(8,128)(2,1)S(1)}, u32[]{:S(2)}, u32[]{:S(2)}) %collective-permute-start.7) | collective-permute-done | bytes 65568 | tf_op jit(solution)/shard_map/ppermute | solution.py:295
  27.8 1.5 %collective-permute-done.8.refs_9_ = bf16[2,16,1024]{2,1,0:T(8,128)(2,1)S(1)} collective-permute-done((bf16[2,16,1024]{2,1,0:T(8,128)(2,1)S(1)}, bf16[2,16,1024]{2,1,0:T(8,128)(2,1)S(1)}, u32[]{:S(2)}, u32[]{:S(2)}) %collective-permute-start.8) | collective-permute-done | bytes 65568 | tf_op jit(solution)/shard_map/ppermute | solution.py:295
  29.4 0.5 %collective-permute-done.9.refs_10_ = bf16[2,16,1024]{2,1,0:T(8,128)(2,1)S(1)} collective-permute-done((bf16[2,16,1024]{2,1,0:T(8,128)(2,1)S(1)}, bf16[2,16,1024]{2,1,0:T(8,128)(2,1)S(1)}, u32[]{:S(2)}, u32[]{:S(2)}) %collective-permute-start.9) | collective-permute-done | bytes 65568 | tf_op jit(solution)/shard_map/ppermute | solution.py:295
  29.9 1.2 %shard_map.187 = (bf16[1,8,4096]{2,1,0:T(8,128)(2,1)}, bf16[1,8,4096]{2,1,0:T(8,128)(2,1)}, bf16[1,8,4096]{2,1,0:T(8,128)(2,1)}, bf16[1,8,4096]{2,1,0:T(8,128)(2...) custom-call(bf16[16,4096]{1,0:T(8,128)(2,1)S(1)} %collective-permute-done.1.refs_4_.refs_0_, ...), custom_call_target="tpu_custom_call" | custom-call | flops 10000 | bytes 100 | tf_op jit(solution)/shard_map/pallas_call | solution.py:265
  (31 shorter events, 0.2 us)
Async XLA Ops:
  0.6 0.7 %copy-start.8 = (s32[1,32]{1,0:T(1,128)S(1)}, s32[1,32]{1,0:T(1,128)}, u32[]{:S(2)}) copy-start(s32[1,32]{1,0:T(1,128)} %refs_1_.7) | copy-start | bytes 388
  0.6 1.2 %copy-start.1 = (bf16[1,32,128,128]{3,2,1,0:T(8,128)(2,1)S(1)}, bf16[1,32,128,128]{3,2,1,0:T(8,128)(2,1)}, u32[]{:S(2)}) copy-start(bf16[1,32,128,128]{3,2,1,0:T(8,128)(2,1)} %refs_3_.7) | copy-start | bytes 3145732
  0.7 1.2 %copy-start.7 = (s32[1,32]{1,0:T(1,128)S(1)}, s32[1,32]{1,0:T(1,128)}, u32[]{:S(2)}) copy-start(s32[1,32]{1,0:T(1,128)} %refs_0_.7) | copy-start | bytes 388
  0.7 1.5 %copy-start = (bf16[1,32,128,128]{3,2,1,0:T(8,128)(2,1)S(1)}, bf16[1,32,128,128]{3,2,1,0:T(8,128)(2,1)}, u32[]{:S(2)}) copy-start(bf16[1,32,128,128]{3,2,1,0:T(8,128)(2,1)} %refs_2_.7) | copy-start | bytes 3145732
  0.7 1.5 %copy-start.4 = (bf16[1,8,4096]{2,1,0:T(8,128)(2,1)S(1)}, bf16[1,8,4096]{2,1,0:T(8,128)(2,1)}, u32[]{:S(2)}) copy-start(bf16[1,8,4096]{2,1,0:T(8,128)(2,1)} %refs_6_.3) | copy-start | bytes 196612
  0.7 1.5 %copy-start.3 = (bf16[1,8,4096]{2,1,0:T(8,128)(2,1)S(1)}, bf16[1,8,4096]{2,1,0:T(8,128)(2,1)}, u32[]{:S(2)}) copy-start(bf16[1,8,4096]{2,1,0:T(8,128)(2,1)} %refs_5_.3) | copy-start | bytes 196612
  0.7 1.5 %copy-start.9 = (s32[1,2]{1,0:T(1,128)S(1)}, s32[1,2]{1,0:T(1,128)}, u32[]{:S(2)}) copy-start(s32[1,2]{1,0:T(1,128)} %refs_2_.5) | copy-start | bytes 28
  0.7 1.6 %copy-start.13 = (bf16[1,2,8,4096]{3,2,1,0:T(8,128)(2,1)S(1)}, bf16[1,2,8,4096]{3,2,1,0:T(8,128)(2,1)}, u32[]{:S(2)}) copy-start(bf16[1,2,8,4096]{3,2,1,0:T(8,128)(2,1)} %refs_10_.2) | copy-start | bytes 393220
  0.7 1.6 %copy-start.12 = (bf16[1,2,8,4096]{3,2,1,0:T(8,128)(2,1)S(1)}, bf16[1,2,8,4096]{3,2,1,0:T(8,128)(2,1)}, u32[]{:S(2)}) copy-start(bf16[1,2,8,4096]{3,2,1,0:T(8,128)(2,1)} %refs_9_.2) | copy-start | bytes 393220
  0.7 1.6 %copy-start.11 = (bf16[1,2,8,4096]{3,2,1,0:T(8,128)(2,1)S(1)}, bf16[1,2,8,4096]{3,2,1,0:T(8,128)(2,1)}, u32[]{:S(2)}) copy-start(bf16[1,2,8,4096]{3,2,1,0:T(8,128)(2,1)} %refs_8_.2) | copy-start | bytes 393220
  0.7 1.6 %copy-start.10 = (bf16[1,2,8,4096]{3,2,1,0:T(8,128)(2,1)S(1)}, bf16[1,2,8,4096]{3,2,1,0:T(8,128)(2,1)}, u32[]{:S(2)}) copy-start(bf16[1,2,8,4096]{3,2,1,0:T(8,128)(2,1)} %refs_7_.1) | copy-start | bytes 393220
  2.4 6.2 %copy-start.2 = (bf16[1,2,8,4096]{3,2,1,0:T(8,128)(2,1)S(1)}, bf16[1,2,8,4096]{3,2,1,0:T(8,128)(2,1)}, u32[]{:S(2)}) copy-start(bf16[1,2,8,4096]{3,2,1,0:T(8,128)(2,1)} %refs_10_.3) | copy-start | bytes 393220
  2.4 6.2 %copy-start.5 = (bf16[1,8,4096]{2,1,0:T(8,128)(2,1)S(1)}, bf16[1,8,4096]{2,1,0:T(8,128)(2,1)}, u32[]{:S(2)}) copy-start(bf16[1,8,4096]{2,1,0:T(8,128)(2,1)} %refs_8_.3) | copy-start | bytes 196612
  2.4 6.2 %copy-start.6 = (bf16[1,8,4096]{2,1,0:T(8,128)(2,1)S(1)}, bf16[1,8,4096]{2,1,0:T(8,128)(2,1)}, u32[]{:S(2)}) copy-start(bf16[1,8,4096]{2,1,0:T(8,128)(2,1)} %refs_9_.3) | copy-start | bytes 196612
  4.1 21.0 %collective-permute-start.4 = (bf16[10,16,1024]{2,1,0:T(8,128)(2,1)S(1)}, bf16[10,16,1024]{2,1,0:T(8,128)(2,1)S(1)}, u32[]{:S(2)}, u32[]{:S(2)}) collective-permute-start(bf16[10,16,1024]{2,1,0:T(8,128)(2,1)S(1)} %get-tuple-element.37), channel_id=1, source_target_pairs={{0,3},{1,2},{2,1},{3,0},{4,7},{5,6},{6,5},{7,4},{8,11},{9,10},{10,... | collective-permute-start | bytes 983048 | tf_op jit(solution)/shard_map/ppermute | solution.py:295
  8.0 17.6 %collective-permute-start.5 = (bf16[10,16,1024]{2,1,0:T(8,128)(2,1)S(1)}, bf16[10,16,1024]{2,1,0:T(8,128)(2,1)S(1)}, u32[]{:S(2)}, u32[]{:S(2)}) collective-permute-start(bf16[10,16,1024]{2,1,0:T(8,128)(2,1)S(1)} %get-tuple-element.38), channel_id=1, source_target_pairs={{0,1},{1,0},{2,3},{3,2},{4,5},{5,4},{6,7},{7,6},{8,9},{9,8},{10,11... | collective-permute-start | bytes 983048 | tf_op jit(solution)/shard_map/ppermute | solution.py:295
  10.5 4.0 %collective-permute-start = (bf16[16,4096]{1,0:T(8,128)(2,1)S(1)}, bf16[16,4096]{1,0:T(8,128)(2,1)S(1)}, u32[]{:S(2)}, u32[]{:S(2)}) collective-permute-start(bf16[16,4096]{1,0:T(8,128)(2,1)S(1)} %get-tuple-element.26), channel_id=1, source_target_pairs={{0,4},{4,0},{8,12},{12,8},{16,20},{20,16},{24,28},{28,24},{1,5},{5... | collective-permute-start | bytes 393224 | tf_op jit(solution)/shard_map/ppermute | solution.py:32
  10.6 15.6 %collective-permute-start.6 = (bf16[10,16,1024]{2,1,0:T(8,128)(2,1)S(1)}, bf16[10,16,1024]{2,1,0:T(8,128)(2,1)S(1)}, u32[]{:S(2)}, u32[]{:S(2)}) collective-permute-start(bf16[10,16,1024]{2,1,0:T(8,128)(2,1)S(1)} %get-tuple-element.39), channel_id=1, source_target_pairs={{0,2},{1,3},{2,0},{3,1},{4,6},{5,7},{6,4},{7,5},{8,10},{9,11},{10,... | collective-permute-start | bytes 983048 | tf_op jit(solution)/shard_map/ppermute | solution.py:295
  10.7 7.4 %collective-permute-start.2 = (bf16[16,4096]{1,0:T(8,128)(2,1)S(1)}, bf16[16,4096]{1,0:T(8,128)(2,1)S(1)}, u32[]{:S(2)}, u32[]{:S(2)}) collective-permute-start(bf16[16,4096]{1,0:T(8,128)(2,1)S(1)} %get-tuple-element.30), channel_id=1, source_target_pairs={{0,28},{4,8},{8,4},{12,16},{16,12},{20,24},{24,20},{28,0},{1,29},{... | collective-permute-start | bytes 393224 | tf_op jit(solution)/shard_map/ppermute | solution.py:31
  16.4 6.3 %collective-permute-start.1 = (bf16[16,4096]{1,0:T(8,128)(2,1)S(1)}, bf16[16,4096]{1,0:T(8,128)(2,1)S(1)}, u32[]{:S(2)}, u32[]{:S(2)}) collective-permute-start(bf16[16,4096]{1,0:T(8,128)(2,1)S(1)} %get-tuple-element.29), channel_id=1, source_target_pairs={{0,28},{4,8},{8,4},{12,16},{16,12},{20,24},{24,20},{28,0},{1,29},{... | collective-permute-start | bytes 393224 | tf_op jit(solution)/shard_map/ppermute | solution.py:31
  19.5 10.4 %collective-permute-start.3 = (bf16[16,4096]{1,0:T(8,128)(2,1)S(1)}, bf16[16,4096]{1,0:T(8,128)(2,1)S(1)}, u32[]{:S(2)}, u32[]{:S(2)}) collective-permute-start(bf16[16,4096]{1,0:T(8,128)(2,1)S(1)} %get-tuple-element.35), channel_id=1, source_target_pairs={{0,4},{4,0},{8,12},{12,8},{16,20},{20,16},{24,28},{28,24},{1,5},{5... | collective-permute-start | bytes 393224 | tf_op jit(solution)/shard_map/ppermute | solution.py:32
  22.7 5.2 %collective-permute-start.7 = (bf16[2,16,1024]{2,1,0:T(8,128)(2,1)S(1)}, bf16[2,16,1024]{2,1,0:T(8,128)(2,1)S(1)}, u32[]{:S(2)}, u32[]{:S(2)}) collective-permute-start(bf16[2,16,1024]{2,1,0:T(8,128)(2,1)S(1)} %get-tuple-element.41), channel_id=1, source_target_pairs={{0,3},{1,2},{2,1},{3,0},{4,7},{5,6},{6,5},{7,4},{8,11},{9,10},{10,... | collective-permute-start | bytes 196616 | tf_op jit(solution)/shard_map/ppermute | solution.py:295
  25.1 4.3 %collective-permute-start.8 = (bf16[2,16,1024]{2,1,0:T(8,128)(2,1)S(1)}, bf16[2,16,1024]{2,1,0:T(8,128)(2,1)S(1)}, u32[]{:S(2)}, u32[]{:S(2)}) collective-permute-start(bf16[2,16,1024]{2,1,0:T(8,128)(2,1)S(1)} %get-tuple-element.42), channel_id=1, source_target_pairs={{0,1},{1,0},{2,3},{3,2},{4,5},{5,4},{6,7},{7,6},{8,9},{9,8},{10,11... | collective-permute-start | bytes 196616 | tf_op jit(solution)/shard_map/ppermute | solution.py:295
  25.7 4.3 %collective-permute-start.9 = (bf16[2,16,1024]{2,1,0:T(8,128)(2,1)S(1)}, bf16[2,16,1024]{2,1,0:T(8,128)(2,1)S(1)}, u32[]{:S(2)}, u32[]{:S(2)}) collective-permute-start(bf16[2,16,1024]{2,1,0:T(8,128)(2,1)S(1)} %get-tuple-element.43), channel_id=1, source_target_pairs={{0,2},{1,3},{2,0},{3,1},{4,6},{5,7},{6,4},{7,5},{8,10},{9,11},{10,... | collective-permute-start | bytes 196616 | tf_op jit(solution)/shard_map/ppermute | solution.py:295

commit v10 on v9

--- a/solution.py
+++ b/solution.py
@@ -11,7 +11,7 @@
 LIMIT = 40 * 1024 * 1024
 WORK = 10 ** 10
 LIGHT = 10 ** 4
-STREAMS = LIGHT
+PAD = BLOCK
 
 
 def partner(me, step, count):
@@ -75,16 +75,10 @@
     return lax.rem(lax.axis_index("section"), 2)
 
 
-def hand_out(packs, near, far):
-    odd = odd_section()
-    near[...] = packs[odd]
-    far[...] = packs[1 - odd]
-
-
 def take_in(near, far, packs):
     odd = odd_section()
     packs[1 - odd] = near[...]
-    packs[odd] = far[...]
+    packs[odd] = far[:, :packs.shape[2]]
 
 
 def open_launch(token):
@@ -154,18 +148,33 @@
         pack[:, at] = moved.astype(BF16)
 
 
-def first_streams(count, per, up_idx, down_idx, order, w_up, w_down, g_ref, a_ref, pushes, v_ref, t_ref, tan,
-                  near, far, keep_tan, packs, returned, hidden):
-    blocks = count * per
+def clear_pad(pack, blocks):
+    if pack.shape[1] > blocks * BLOCK:
+        pack[:, blocks * BLOCK:] = jnp.zeros((pack.shape[0], pack.shape[1] - blocks * BLOCK), BF16)
+
+
+def back_streams(blocks, up_idx, w_up, g_ref, a_ref, pushes, pack, returned):
     for b in range(blocks):
         returned[b] = stack([g_ref[0, :, lanes(b)], a_ref[0, :, lanes(b)]])
     for j in range(blocks):
         u = up_idx[0, j]
         returned[u] = returned[u] + times_transposed(pushes[:, lanes(j)], w_up[0, j])
     for b in range(blocks):
-        packs[1, :, lanes(b)] = returned[b].astype(BF16)
-    forward_first(blocks, up_idx, down_idx, order, w_up, w_down, v_ref, t_ref, tan, packs.at[0], keep_tan, hidden)
-    hand_out(packs, near, far)
+        pack[:, lanes(b)] = returned[b].astype(BF16)
+
+
+def first_streams(blocks, back_parity, up_idx, down_idx, order, w_up, w_down, g_ref, a_ref, pushes, v_ref, t_ref, tan,
+                  pack, keep, returned, hidden):
+    odd = odd_section()
+    clear_pad(pack, blocks)
+
+    @pl.when(odd == back_parity)
+    def _():
+        back_streams(blocks, up_idx, w_up, g_ref, a_ref, pushes, pack, returned)
+
+    @pl.when(odd != back_parity)
+    def _():
+        forward_first(blocks, up_idx, down_idx, order, w_up, w_down, v_ref, t_ref, tan, pack, keep, hidden)
 
 
 def back_second(count, per, up_idx, down_idx, w_up, w_down, rows, keep, pack, sends, pulled, returned):
@@ -202,6 +211,7 @@
 def near_phase(count, per, up_idx, down_idx, w_up, w_down, near_in, keep, keep_tan, far, *refs):
     sends, (pulled, returned, hidden) = refs[:count], refs[count:]
     odd = odd_section()
+    clear_pad(far, count * per)
 
     @pl.when(odd == 0)
     def _():
@@ -303,26 +313,27 @@
         [shape((blocks, 24, BLOCK), F32), pair] + [ten] * count,
         [vmem((blocks, 32, BLOCK), F32), vmem((blocks, 48, BLOCK), BF16)],
         after=(token,), cost=WORK)
-    near, far, keep_tan = call(
-        body(first_streams, count, per),
-        tables + (score_grad_in, state_adjoint_in, pushes, values_in, tangent_in, saved_tan), [smem] * 3 + [vmem] * 8,
-        [pair, pair, shape((blocks, 8, BLOCK), F32)],
-        [vmem((2, 16, width), BF16), vmem((blocks, 16, BLOCK), F32), vmem((blocks, 16, BLOCK), BF16)], cost=STREAMS)
+    taken = tables + (score_grad_in, state_adjoint_in, pushes, values_in, tangent_in, saved_tan)
+    made = [shape((blocks, 8, BLOCK), F32)]
+    long = shape((16, width + PAD), BF16)
+    scratch = [vmem((blocks, 16, BLOCK), F32), vmem((blocks, 16, BLOCK), BF16)]
+    far, far_keep = call(body(first_streams, blocks, 0), taken, [smem] * 3 + [vmem] * 8, [long] + made, scratch)
+    near, near_keep = call(body(first_streams, blocks, 1), taken, [smem] * 3 + [vmem] * 8, [pair] + made, scratch,
+                           after=(far,))
     near, far = swap_sections(near, far)
     early = to_replicas(early)
     tables = (up_index, down_index, w_up, w_down)
     two = [shape((2, 16, part), BF16)] * count
     scratch = [vmem((blocks, 16, BLOCK), F32), vmem((blocks, 16, BLOCK), F32), vmem((blocks, 16, BLOCK), BF16)]
     far_out, *late = call(
-        body(near_phase, count, per), tables + (near, keep, keep_tan), [smem] * 2 + [vmem] * 5, [pair] + two, scratch)
+        body(near_phase, count, per), tables + (near, keep, far_keep), [smem] * 2 + [vmem] * 5, [long] + two, scratch)
     near_out, *late = call(
-        body(far_phase, count, per), tables + (far, keep, keep_tan, *late), [smem] * 2 + [vmem] * (5 + count),
+        body(far_phase, count, per), tables + (far, keep, near_keep, *late), [smem] * 2 + [vmem] * (5 + count),
         [pair] + two, scratch)
     near, far = swap_sections(near_out, far_out)
     late = to_replicas(late)
     (grads,) = call(
-        body(early_grads, count, per), tuple(early), [vmem] * count, [shape((2, per, BLOCK, BLOCK), F32)], [],
-        after=(far,))
+        body(early_grads, count, per), tuple(early), [vmem] * count, [shape((2, per, BLOCK, BLOCK), F32)], [])
     stream = shape((1,) + values_in.shape[1:], BF16)
     grad = shape((1, per, BLOCK, BLOCK), BF16)
     return tuple(call(

time: 31.2 us -> 30.2 us (0.968)
  waiting for transfers between devices: 8.02 us -> 5.34 us
  starting transfers between devices: 12.3 us -> 13.2 us
  Pallas kernels: 8.32 us -> 9.04 us
    ppermute x2, waiting for transfers between devices: 4.58 us -> 0.01 us  [swap_sections(): lax.ppermute(far, 'section', [(i, (i + 2 * (i % 2) - 1) % count) for i in...]
    ppermute x2, waiting for transfers between devices: 0.01 us -> 1.34 us  [swap_sections(): near = lax.ppermute(near, 'section', [(i, i ^ 1) for i in range(count)])]
    ppermute x6, starting transfers between devices: 8.16 us -> 9.05 us  [to_replicas(): lax.ppermute(parts[step], 'dp', swap_route(step, count))]
    pallas_call x7 -> x8, Pallas kernels: 8.32 us -> 9.04 us  [call(): pl.pallas_call(kernel, out_shape=outs, in_specs=[pl.BlockSpec(memory_spac...]
    ppermute x2, starting transfers between devices: 4.01 us -> 3.34 us  [swap_sections(): lax.ppermute(far, 'section', [(i, (i + 2 * (i % 2) - 1) % count) for i in...]
    ppermute x2, starting transfers between devices: 0.14 us -> 0.78 us  [swap_sections(): near = lax.ppermute(near, 'section', [(i, i ^ 1) for i in range(count)])]
    ppermute x6, waiting for transfers between devices: 3.43 us -> 4 us  [to_replicas(): lax.ppermute(parts[step], 'dp', swap_route(step, count))]
  transfers between devices with their start and end apart: 10 -> 10, of which waited for: 5 -> 5; matrix products, arithmetic and copies ran while one was open for 0% -> 0% of each run, Pallas kernels for 18% -> 21%
where the time goes in v10:
time: 30.2 us; the launch traced here: 30 us
  starting transfers between devices  13.2 us (44%)
  Pallas kernels  9.04 us (30%)
  waiting for transfers between devices  5.34 us (18%)
  local copies, waits for them, and re-layouts  1.66 us (5%)
  between operations  0.79 us (3%)
    ppermute x6, starting transfers between devices, to_replicas(): lax.ppermute(parts[step], 'dp', swap_route(step, count))  9.05 us
    pallas_call x8, Pallas kernels, call(): pl.pallas_call(kernel, out_shape=outs, in_specs=[pl.BlockSpec(memory_spac...  9.04 us
    ppermute x6, waiting for transfers between devices, to_replicas(): lax.ppermute(parts[step], 'dp', swap_route(step, count))  4 us
    ppermute x2, starting transfers between devices, swap_sections(): lax.ppermute(far, 'section', [(i, (i + 2 * (i % 2) - 1) % count) for i in...  3.34 us
    unnamed x28, local copies, waits for them, and re-layouts  1.66 us
    ppermute x2, waiting for transfers between devices, swap_sections(): near = lax.ppermute(near, 'section', [(i, i ^ 1) for i in range(count)])  1.34 us
    ppermute x2, starting transfers between devices, swap_sections(): near = lax.ppermute(near, 'section', [(i, i ^ 1) for i in range(count)])  0.78 us
  transfers between devices with their start and end apart: 10, of which 5 were waited for; matrix products, arithmetic and copies ran while one was open for 0% of the time, Pallas kernels for 21%

profile of v10, /device:TPU:0, one launch (start us, length us, event | category | flops | bytes accessed | tf_op | source)
XLA Modules:
  0.0 30.0 jit_solution(8960394388892826795)
XLA Ops:
  0.8 0.5 %copy-done.8 = s32[1,32]{1,0:T(1,128)S(1)} copy-done((s32[1,32]{1,0:T(1,128)S(1)}, s32[1,32]{1,0:T(1,128)}, u32[]{:S(2)}) %copy-start.8) | copy-done | bytes 152
  1.3 0.6 %copy-done.1 = bf16[1,32,128,128]{3,2,1,0:T(8,128)(2,1)S(1)} copy-done((bf16[1,32,128,128]{3,2,1,0:T(8,128)(2,1)S(1)}, bf16[1,32,128,128]{3,2,1,0:T(8,128)(2,1)}, u32[]{:S(2)}) %copy-start.1) | copy-done | bytes 1048600
  1.9 0.3 %copy-done = bf16[1,32,128,128]{3,2,1,0:T(8,128)(2,1)S(1)} copy-done((bf16[1,32,128,128]{3,2,1,0:T(8,128)(2,1)S(1)}, bf16[1,32,128,128]{3,2,1,0:T(8,128)(2,1)}, u32[]{:S(2)}) %copy-start) | copy-done | bytes 1048600
  2.4 1.7 %shard_map.182 = (f32[32,24,128]{2,1,0:T(8,128)S(1)}, bf16[16,4096]{1,0:T(8,128)(2,1)S(1)}, bf16[10,16,1024]{2,1,0:T(8,128)(2,1)S(1)}, bf16[10,16,1024]{2,1,0:T(...) custom-call(s32[1,32]{1,0:T(1,128)S(1)} %copy-done.7, s32[1,32]{1,0:T(1,128)S(1)} %copy-done.8, ...), custom_call_target="tpu_custom_call" | custom-call | flops 10000000000 | bytes 100000000 | tf_op jit(solution)/shard_map/pallas_call | solution.py:275
  4.1 4.0 %collective-permute-start.4 = (bf16[10,16,1024]{2,1,0:T(8,128)(2,1)S(1)}, bf16[10,16,1024]{2,1,0:T(8,128)(2,1)S(1)}, u32[]{:S(2)}, u32[]{:S(2)}) collective-permute-start(bf16[10,16,1024]{2,1,0:T(8,128)(2,1)S(1)} %get-tuple-element.39), channel_id=1, source_target_pairs={{0,3},{1,2},{2,1},{3,0},{4,7},{5,6},{6,5},{7,4},{8,11},{9,10},{10,... | collective-permute-start | bytes 983048 | tf_op jit(solution)/shard_map/ppermute | solution.py:305
  8.0 0.5 %collective-permute-start.5 = (bf16[10,16,1024]{2,1,0:T(8,128)(2,1)S(1)}, bf16[10,16,1024]{2,1,0:T(8,128)(2,1)S(1)}, u32[]{:S(2)}, u32[]{:S(2)}) collective-permute-start(bf16[10,16,1024]{2,1,0:T(8,128)(2,1)S(1)} %get-tuple-element.40), channel_id=1, source_target_pairs={{0,1},{1,0},{2,3},{3,2},{4,5},{5,4},{6,7},{7,6},{8,9},{9,8},{10,11... | collective-permute-start | bytes 983048 | tf_op jit(solution)/shard_map/ppermute | solution.py:305
  8.6 0.1 collective-permute-start.6
  8.7 1.3 %shard_map.183 = (bf16[16,4224]{1,0:T(8,128)(2,1)S(1)}, f32[32,8,128]{2,1,0:T(8,128)S(1)}) custom-call(s32[1,32]{1,0:T(1,128)S(1)} %copy-done.7, s32[1,32]{1,0:T(1,128)S(1)} %copy-done.8, s32[1,2]{1,0:T(1,128)S(1)} %copy-done.9, bf16[1,32,128,128]{3,2,1,0:T(8,128)(2,1)S(1)} %copy-done, bf16[1,32,128,128]{3,2,1,0:T(8,128)(2,1)S(1)} %copy-done.1, ...), custom_call_target="tpu_custom_call" | custom-call | flops 10000 | bytes 100 | tf_op jit(solution)/shard_map/pallas_call | solution.py:275
  10.0 2.8 %collective-permute-start.2 = (bf16[16,4224]{1,0:T(8,128)(2,1)S(1)}, bf16[16,4224]{1,0:T(8,128)(2,1)S(1)}, u32[]{:S(2)}, u32[]{:S(2)}) collective-permute-start(bf16[16,4224]{1,0:T(8,128)(2,1)S(1)} %get-tuple-element.27.refs_11_), channel_id=1, source_target_pairs={{0,28},{4,8},{8,4},{12,16},{16,12},{20,24},{24,20},{28,0},{1,29},{... | collective-permute-start | bytes 405512 | tf_op jit(solution)/shard_map/ppermute | solution.py:31
  12.7 1.3 %shard_map.184 = (bf16[16,4096]{1,0:T(8,128)(2,1)S(1)}, f32[32,8,128]{2,1,0:T(8,128)S(1)}) custom-call(s32[1,32]{1,0:T(1,128)S(1)} %copy-done.7, s32[1,32]{1,0:T(1,128)S(1)} %copy-done.8, s32[1,2]{1,0:T(1,128)S(1)} %copy-done.9, bf16[1,32,128,128]{3,2,1,0:T(8,128)(2,1)S(1)} %copy-done, bf16[1,32,128,128]{3,2,1,0:T(8,128)(2,1)S(1)} %copy-done.1, ...), custom_call_target="tpu_custom_call" | custom-call | flops 10000 | bytes 100 | tf_op jit(solution)/shard_map/pallas_call | solution.py:275
  14.1 1.3 %collective-permute-done.refs_4_ = bf16[16,4096]{1,0:T(8,128)(2,1)S(1)} collective-permute-done((bf16[16,4096]{1,0:T(8,128)(2,1)S(1)}, bf16[16,4096]{1,0:T(8,128)(2,1)S(1)}, u32[]{:S(2)}, u32[]{:S(2)}) %collective-permute-start) | collective-permute-done | bytes 131104 | tf_op jit(solution)/shard_map/ppermute | solution.py:32
  15.5 1.9 %shard_map.185 = (bf16[16,4224]{1,0:T(8,128)(2,1)S(1)}, bf16[2,16,1024]{2,1,0:T(8,128)(2,1)S(1)}, bf16[2,16,1024]{2,1,0:T(8,128)(2,1)S(1)}, bf16[2,16,1024]{2,1,0:T(8,128)(2,1)S(1)}, bf16[2,16,1024]{2,1,0:T(8,128)(2,1)S(1)}) custom-call(s32[1,32]{1,0:T(1,128)S(1)} %copy-done.7, s32[1,32]{1,0:T(1,128)S(1)} %copy-done.8, ...), custom_call_target="tpu_custom_call" | custom-call | flops 10000 | bytes 100 | tf_op jit(solution)/shard_map/pallas_call | solution.py:275
  17.4 0.6 %collective-permute-start.1 = (bf16[16,4224]{1,0:T(8,128)(2,1)S(1)}, bf16[16,4224]{1,0:T(8,128)(2,1)S(1)}, u32[]{:S(2)}, u32[]{:S(2)}) collective-permute-start(bf16[16,4224]{1,0:T(8,128)(2,1)S(1)} %get-tuple-element.31), channel_id=1, source_target_pairs={{0,28},{4,8},{8,4},{12,16},{16,12},{20,24},{24,20},{28,0},{1,29},{... | collective-permute-start | bytes 405512 | tf_op jit(solution)/shard_map/ppermute | solution.py:31
  18.0 1.3 %shard_map.186 = (bf16[16,4096]{1,0:T(8,128)(2,1)S(1)}, bf16[2,16,1024]{2,1,0:T(8,128)(2,1)S(1)}, bf16[2,16,1024]{2,1,0:T(8,128)(2,1)S(1)}, bf16[2,16,1024]{2,1,0:T(8,128)(2,1)S(1)}, bf16[2,16,1024]{2,1,0:T(8,128)(2,1)S(1)}) custom-call(s32[1,32]{1,0:T(1,128)S(1)} %copy-done.7, s32[1,32]{1,0:T(1,128)S(1)} %copy-done.8, ...), custom_call_target="tpu_custom_call" | custom-call | flops 10000 | bytes 100 | tf_op jit(solution)/shard_map/pallas_call | solution.py:275
  19.3 0.7 %collective-permute-start.3 = (bf16[16,4096]{1,0:T(8,128)(2,1)S(1)}, bf16[16,4096]{1,0:T(8,128)(2,1)S(1)}, u32[]{:S(2)}, u32[]{:S(2)}) collective-permute-start(bf16[16,4096]{1,0:T(8,128)(2,1)S(1)} %get-tuple-element.37), channel_id=1, source_target_pairs={{0,4},{4,0},{8,12},{12,8},{16,20},{20,16},{24,28},{28,24},{1,5},{5... | collective-permute-start | bytes 393224 | tf_op jit(solution)/shard_map/ppermute | solution.py:32
  20.0 2.5 %collective-permute-start.7 = (bf16[2,16,1024]{2,1,0:T(8,128)(2,1)S(1)}, bf16[2,16,1024]{2,1,0:T(8,128)(2,1)S(1)}, u32[]{:S(2)}, u32[]{:S(2)}) collective-permute-start(bf16[2,16,1024]{2,1,0:T(8,128)(2,1)S(1)} %get-tuple-element.43), channel_id=1, source_target_pairs={{0,3},{1,2},{2,1},{3,0},{4,7},{5,6},{6,5},{7,4},{8,11},{9,10},{10,... | collective-permute-start | bytes 196616 | tf_op jit(solution)/shard_map/ppermute | solution.py:305
  22.5 0.6 %collective-permute-done.5.refs_2_.refs_5_ = bf16[10,16,1024]{2,1,0:T(8,128)(2,1)S(1)} collective-permute-done((bf16[10,16,1024]{2,1,0:T(8,128)(2,1)S(1)}, bf16[10,16,1024]{2,1,0:T(8,128)(2,1)S(1)}, u32[]{:S(2)}, u32[]{:S(2)}) %collective-permute-start.5) | collective-permute-done | bytes 327712 | tf_op jit(solution)/shard_map/ppermute | solution.py:305
  23.1 1.5 %collective-permute-start.8 = (bf16[2,16,1024]{2,1,0:T(8,128)(2,1)S(1)}, bf16[2,16,1024]{2,1,0:T(8,128)(2,1)S(1)}, u32[]{:S(2)}, u32[]{:S(2)}) collective-permute-start(bf16[2,16,1024]{2,1,0:T(8,128)(2,1)S(1)} %get-tuple-element.44), channel_id=1, source_target_pairs={{0,1},{1,0},{2,3},{3,2},{4,5},{5,4},{6,7},{7,6},{8,9},{9,8},{10,11... | collective-permute-start | bytes 196616 | tf_op jit(solution)/shard_map/ppermute | solution.py:305
  24.6 0.5 %collective-permute-start.9 = (bf16[2,16,1024]{2,1,0:T(8,128)(2,1)S(1)}, bf16[2,16,1024]{2,1,0:T(8,128)(2,1)S(1)}, u32[]{:S(2)}, u32[]{:S(2)}) collective-permute-start(bf16[2,16,1024]{2,1,0:T(8,128)(2,1)S(1)} %get-tuple-element.45), channel_id=1, source_target_pairs={{0,2},{1,3},{2,0},{3,1},{4,6},{5,7},{6,4},{7,5},{8,10},{9,11},{10,... | collective-permute-start | bytes 196616 | tf_op jit(solution)/shard_map/ppermute | solution.py:305
  25.1 0.3 %shard_map.187.refs_2_ = f32[2,8,128,128]{3,2,1,0:T(8,128)S(1)} custom-call(bf16[10,16,1024]{2,1,0:T(8,128)(2,1)S(1)} %get-tuple-element.38.refs_0_.refs_3_, bf16[10,16,1024]{2,1,0:T(8,128)(2,1)S(1)} %collective-permute-done.4.refs_1_.refs_4_, bf16[10,16,1024]{2,1,0:T(8,128)(2,1)S(1)} %collective-permute-done.5.refs_2_.refs_5_, ...), custom_call_target="tpu_custom_call" | custom-call | flops 10000 | bytes 100 | tf_op jit(solution)/shard_map/pallas_call | solution.py:275
  25.4 0.2 collective-permute-done.7.refs_8_
  25.6 1.8 %collective-permute-done.8.refs_9_ = bf16[2,16,1024]{2,1,0:T(8,128)(2,1)S(1)} collective-permute-done((bf16[2,16,1024]{2,1,0:T(8,128)(2,1)S(1)}, bf16[2,16,1024]{2,1,0:T(8,128)(2,1)S(1)}, u32[]{:S(2)}, u32[]{:S(2)}) %collective-permute-start.8) | collective-permute-done | bytes 65568 | tf_op jit(solution)/shard_map/ppermute | solution.py:305
  27.3 1.5 %collective-permute-done.9.refs_10_ = bf16[2,16,1024]{2,1,0:T(8,128)(2,1)S(1)} collective-permute-done((bf16[2,16,1024]{2,1,0:T(8,128)(2,1)S(1)}, bf16[2,16,1024]{2,1,0:T(8,128)(2,1)S(1)}, u32[]{:S(2)}, u32[]{:S(2)}) %collective-permute-start.9) | collective-permute-done | bytes 65568 | tf_op jit(solution)/shard_map/ppermute | solution.py:305
  28.8 1.2 %shard_map.188 = (bf16[1,8,4096]{2,1,0:T(8,128)(2,1)}, bf16[1,8,4096]{2,1,0:T(8,128)(2,1)}, bf16[1,8,4096]{2,1,0:T(8,128)(2,1)}, bf16[1,8,4096]{2,1,0:T(8,128)(2...) custom-call(bf16[16,4224]{1,0:T(8,128)(2,1)S(1)} %collective-permute-done.1.refs_0_, ...), custom_call_target="tpu_custom_call" | custom-call | flops 10000 | bytes 100 | tf_op jit(solution)/shard_map/pallas_call | solution.py:275
  (32 shorter events, 0.3 us)
Async XLA Ops:
  0.6 0.7 %copy-start.8 = (s32[1,32]{1,0:T(1,128)S(1)}, s32[1,32]{1,0:T(1,128)}, u32[]{:S(2)}) copy-start(s32[1,32]{1,0:T(1,128)} %refs_1_.9) | copy-start | bytes 388
  0.6 1.2 %copy-start.1 = (bf16[1,32,128,128]{3,2,1,0:T(8,128)(2,1)S(1)}, bf16[1,32,128,128]{3,2,1,0:T(8,128)(2,1)}, u32[]{:S(2)}) copy-start(bf16[1,32,128,128]{3,2,1,0:T(8,128)(2,1)} %refs_3_.9) | copy-start | bytes 3145732
  0.7 1.2 %copy-start.7 = (s32[1,32]{1,0:T(1,128)S(1)}, s32[1,32]{1,0:T(1,128)}, u32[]{:S(2)}) copy-start(s32[1,32]{1,0:T(1,128)} %refs_0_.9) | copy-start | bytes 388
  0.7 1.5 %copy-start = (bf16[1,32,128,128]{3,2,1,0:T(8,128)(2,1)S(1)}, bf16[1,32,128,128]{3,2,1,0:T(8,128)(2,1)}, u32[]{:S(2)}) copy-start(bf16[1,32,128,128]{3,2,1,0:T(8,128)(2,1)} %refs_2_.9) | copy-start | bytes 3145732
  0.7 1.5 %copy-start.4 = (bf16[1,8,4096]{2,1,0:T(8,128)(2,1)S(1)}, bf16[1,8,4096]{2,1,0:T(8,128)(2,1)}, u32[]{:S(2)}) copy-start(bf16[1,8,4096]{2,1,0:T(8,128)(2,1)} %refs_6_.5) | copy-start | bytes 196612
  0.7 1.5 %copy-start.3 = (bf16[1,8,4096]{2,1,0:T(8,128)(2,1)S(1)}, bf16[1,8,4096]{2,1,0:T(8,128)(2,1)}, u32[]{:S(2)}) copy-start(bf16[1,8,4096]{2,1,0:T(8,128)(2,1)} %refs_5_.5) | copy-start | bytes 196612
  0.7 1.5 %copy-start.9 = (s32[1,2]{1,0:T(1,128)S(1)}, s32[1,2]{1,0:T(1,128)}, u32[]{:S(2)}) copy-start(s32[1,2]{1,0:T(1,128)} %refs_2_.7) | copy-start | bytes 28
  0.7 1.6 %copy-start.13 = (bf16[1,2,8,4096]{3,2,1,0:T(8,128)(2,1)S(1)}, bf16[1,2,8,4096]{3,2,1,0:T(8,128)(2,1)}, u32[]{:S(2)}) copy-start(bf16[1,2,8,4096]{3,2,1,0:T(8,128)(2,1)} %refs_10_.3) | copy-start | bytes 393220
  0.7 1.6 %copy-start.12 = (bf16[1,2,8,4096]{3,2,1,0:T(8,128)(2,1)S(1)}, bf16[1,2,8,4096]{3,2,1,0:T(8,128)(2,1)}, u32[]{:S(2)}) copy-start(bf16[1,2,8,4096]{3,2,1,0:T(8,128)(2,1)} %refs_9_.3) | copy-start | bytes 393220
  0.7 1.6 %copy-start.11 = (bf16[1,2,8,4096]{3,2,1,0:T(8,128)(2,1)S(1)}, bf16[1,2,8,4096]{3,2,1,0:T(8,128)(2,1)}, u32[]{:S(2)}) copy-start(bf16[1,2,8,4096]{3,2,1,0:T(8,128)(2,1)} %refs_8_.3) | copy-start | bytes 393220
  0.7 1.6 %copy-start.10 = (bf16[1,2,8,4096]{3,2,1,0:T(8,128)(2,1)S(1)}, bf16[1,2,8,4096]{3,2,1,0:T(8,128)(2,1)}, u32[]{:S(2)}) copy-start(bf16[1,2,8,4096]{3,2,1,0:T(8,128)(2,1)} %refs_7_.1) | copy-start | bytes 393220
  2.4 6.3 %copy-start.2 = (bf16[1,2,8,4096]{3,2,1,0:T(8,128)(2,1)S(1)}, bf16[1,2,8,4096]{3,2,1,0:T(8,128)(2,1)}, u32[]{:S(2)}) copy-start(bf16[1,2,8,4096]{3,2,1,0:T(8,128)(2,1)} %refs_10_.5) | copy-start | bytes 393220
  2.4 6.3 %copy-start.5 = (bf16[1,8,4096]{2,1,0:T(8,128)(2,1)S(1)}, bf16[1,8,4096]{2,1,0:T(8,128)(2,1)}, u32[]{:S(2)}) copy-start(bf16[1,8,4096]{2,1,0:T(8,128)(2,1)} %refs_8_.5) | copy-start | bytes 196612
  2.4 6.3 %copy-start.6 = (bf16[1,8,4096]{2,1,0:T(8,128)(2,1)S(1)}, bf16[1,8,4096]{2,1,0:T(8,128)(2,1)}, u32[]{:S(2)}) copy-start(bf16[1,8,4096]{2,1,0:T(8,128)(2,1)} %refs_9_.5) | copy-start | bytes 196612
  4.1 15.9 %collective-permute-start.4 = (bf16[10,16,1024]{2,1,0:T(8,128)(2,1)S(1)}, bf16[10,16,1024]{2,1,0:T(8,128)(2,1)S(1)}, u32[]{:S(2)}, u32[]{:S(2)}) collective-permute-start(bf16[10,16,1024]{2,1,0:T(8,128)(2,1)S(1)} %get-tuple-element.39), channel_id=1, source_target_pairs={{0,3},{1,2},{2,1},{3,0},{4,7},{5,6},{6,5},{7,4},{8,11},{9,10},{10,... | collective-permute-start | bytes 983048 | tf_op jit(solution)/shard_map/ppermute | solution.py:305
  8.0 15.0 %collective-permute-start.5 = (bf16[10,16,1024]{2,1,0:T(8,128)(2,1)S(1)}, bf16[10,16,1024]{2,1,0:T(8,128)(2,1)S(1)}, u32[]{:S(2)}, u32[]{:S(2)}) collective-permute-start(bf16[10,16,1024]{2,1,0:T(8,128)(2,1)S(1)} %get-tuple-element.40), channel_id=1, source_target_pairs={{0,1},{1,0},{2,3},{3,2},{4,5},{5,4},{6,7},{7,6},{8,9},{9,8},{10,11... | collective-permute-start | bytes 983048 | tf_op jit(solution)/shard_map/ppermute | solution.py:305
  8.6 16.0 %collective-permute-start.6 = (bf16[10,16,1024]{2,1,0:T(8,128)(2,1)S(1)}, bf16[10,16,1024]{2,1,0:T(8,128)(2,1)S(1)}, u32[]{:S(2)}, u32[]{:S(2)}) collective-permute-start(bf16[10,16,1024]{2,1,0:T(8,128)(2,1)S(1)} %get-tuple-element.41), channel_id=1, source_target_pairs={{0,2},{1,3},{2,0},{3,1},{4,6},{5,7},{6,4},{7,5},{8,10},{9,11},{10,... | collective-permute-start | bytes 983048 | tf_op jit(solution)/shard_map/ppermute | solution.py:305
  10.0 8.0 %collective-permute-start.2 = (bf16[16,4224]{1,0:T(8,128)(2,1)S(1)}, bf16[16,4224]{1,0:T(8,128)(2,1)S(1)}, u32[]{:S(2)}, u32[]{:S(2)}) collective-permute-start(bf16[16,4224]{1,0:T(8,128)(2,1)S(1)} %get-tuple-element.27.refs_11_), channel_id=1, source_target_pairs={{0,28},{4,8},{8,4},{12,16},{16,12},{20,24},{24,20},{28,0},{1,29},{... | collective-permute-start | bytes 405512 | tf_op jit(solution)/shard_map/ppermute | solution.py:31
  14.1 1.4 %collective-permute-start = (bf16[16,4096]{1,0:T(8,128)(2,1)S(1)}, bf16[16,4096]{1,0:T(8,128)(2,1)S(1)}, u32[]{:S(2)}, u32[]{:S(2)}) collective-permute-start(bf16[16,4096]{1,0:T(8,128)(2,1)S(1)} %get-tuple-element.28), channel_id=1, source_target_pairs={{0,4},{4,0},{8,12},{12,8},{16,20},{20,16},{24,28},{28,24},{1,5},{5... | collective-permute-start | bytes 393224 | tf_op jit(solution)/shard_map/ppermute | solution.py:32
  17.4 11.5 %collective-permute-start.1 = (bf16[16,4224]{1,0:T(8,128)(2,1)S(1)}, bf16[16,4224]{1,0:T(8,128)(2,1)S(1)}, u32[]{:S(2)}, u32[]{:S(2)}) collective-permute-start(bf16[16,4224]{1,0:T(8,128)(2,1)S(1)} %get-tuple-element.31), channel_id=1, source_target_pairs={{0,28},{4,8},{8,4},{12,16},{16,12},{20,24},{24,20},{28,0},{1,29},{... | collective-permute-start | bytes 405512 | tf_op jit(solution)/shard_map/ppermute | solution.py:31
  19.3 9.5 %collective-permute-start.3 = (bf16[16,4096]{1,0:T(8,128)(2,1)S(1)}, bf16[16,4096]{1,0:T(8,128)(2,1)S(1)}, u32[]{:S(2)}, u32[]{:S(2)}) collective-permute-start(bf16[16,4096]{1,0:T(8,128)(2,1)S(1)} %get-tuple-element.37), channel_id=1, source_target_pairs={{0,4},{4,0},{8,12},{12,8},{16,20},{20,16},{24,28},{28,24},{1,5},{5... | collective-permute-start | bytes 393224 | tf_op jit(solution)/shard_map/ppermute | solution.py:32
  20.0 5.5 %collective-permute-start.7 = (bf16[2,16,1024]{2,1,0:T(8,128)(2,1)S(1)}, bf16[2,16,1024]{2,1,0:T(8,128)(2,1)S(1)}, u32[]{:S(2)}, u32[]{:S(2)}) collective-permute-start(bf16[2,16,1024]{2,1,0:T(8,128)(2,1)S(1)} %get-tuple-element.43), channel_id=1, source_target_pairs={{0,3},{1,2},{2,1},{3,0},{4,7},{5,6},{6,5},{7,4},{8,11},{9,10},{10,... | collective-permute-start | bytes 196616 | tf_op jit(solution)/shard_map/ppermute | solution.py:305
  23.1 4.3 %collective-permute-start.8 = (bf16[2,16,1024]{2,1,0:T(8,128)(2,1)S(1)}, bf16[2,16,1024]{2,1,0:T(8,128)(2,1)S(1)}, u32[]{:S(2)}, u32[]{:S(2)}) collective-permute-start(bf16[2,16,1024]{2,1,0:T(8,128)(2,1)S(1)} %get-tuple-element.44), channel_id=1, source_target_pairs={{0,1},{1,0},{2,3},{3,2},{4,5},{5,4},{6,7},{7,6},{8,9},{9,8},{10,11... | collective-permute-start | bytes 196616 | tf_op jit(solution)/shard_map/ppermute | solution.py:305
  24.6 4.3 %collective-permute-start.9 = (bf16[2,16,1024]{2,1,0:T(8,128)(2,1)S(1)}, bf16[2,16,1024]{2,1,0:T(8,128)(2,1)S(1)}, u32[]{:S(2)}, u32[]{:S(2)}) collective-permute-start(bf16[2,16,1024]{2,1,0:T(8,128)(2,1)S(1)} %get-tuple-element.45), channel_id=1, source_target_pairs={{0,2},{1,3},{2,0},{3,1},{4,6},{5,7},{6,4},{7,5},{8,10},{9,11},{10,... | collective-permute-start | bytes 196616 | tf_op jit(solution)/shard_map/ppermute | solution.py:305

commit v11 on v10

--- a/solution.py
+++ b/solution.py
@@ -87,7 +87,7 @@
 
 def first_rows(count, per, up_idx, down_idx, order, w_up, w_down, g_ref, a_ref, back, second, second_tan, second_grad,
                keep, pushes, *refs):
-    sends, (pulled, hidden) = refs[:count], refs[count:]
+    sends, (pulled, products, hidden) = refs[:count], refs[count:]
     blocks = count * per
     me = lax.axis_index("dp")
     for b in range(blocks):
@@ -99,8 +99,8 @@
         c = stack([g_ref[0, :, at], a_ref[0, :, at], second_grad[0, m0, :, at], second_grad[0, m1, :, at]]).astype(BF16)
         sends[step][8, :, lanes(place)] = c[0:16]
         sends[step][9, :, lanes(place)] = c[16:32]
-        target = down_idx[0, i]
-        pulled[target] = pulled[target] + times_transposed(c, w_down[0, i])
+        products[i] = times_transposed(c, w_down[0, i])
+    add_at(pulled, products, down_idx)
     for step, place, j in send_order(me, count, per):
         u = up_idx[0, j]
         at = lanes(u)
@@ -148,36 +148,42 @@
         pack[:, at] = moved.astype(BF16)
 
 
+def add_at(totals, products, table):
+    for k in range(products.shape[0]):
+        target = table[0, k]
+        totals[target] = totals[target] + products[k]
+
+
 def clear_pad(pack, blocks):
     if pack.shape[1] > blocks * BLOCK:
         pack[:, blocks * BLOCK:] = jnp.zeros((pack.shape[0], pack.shape[1] - blocks * BLOCK), BF16)
 
 
-def back_streams(blocks, up_idx, w_up, g_ref, a_ref, pushes, pack, returned):
+def back_streams(blocks, up_idx, w_up, g_ref, a_ref, pushes, pack, returned, products):
     for b in range(blocks):
         returned[b] = stack([g_ref[0, :, lanes(b)], a_ref[0, :, lanes(b)]])
     for j in range(blocks):
-        u = up_idx[0, j]
-        returned[u] = returned[u] + times_transposed(pushes[:, lanes(j)], w_up[0, j])
+        products[j] = times_transposed(pushes[:, lanes(j)], w_up[0, j])
+    add_at(returned, products, up_idx)
     for b in range(blocks):
         pack[:, lanes(b)] = returned[b].astype(BF16)
 
 
 def first_streams(blocks, back_parity, up_idx, down_idx, order, w_up, w_down, g_ref, a_ref, pushes, v_ref, t_ref, tan,
-                  pack, keep, returned, hidden):
+                  pack, keep, returned, products, hidden):
     odd = odd_section()
     clear_pad(pack, blocks)
 
     @pl.when(odd == back_parity)
     def _():
-        back_streams(blocks, up_idx, w_up, g_ref, a_ref, pushes, pack, returned)
+        back_streams(blocks, up_idx, w_up, g_ref, a_ref, pushes, pack, returned, products)
 
     @pl.when(odd != back_parity)
     def _():
         forward_first(blocks, up_idx, down_idx, order, w_up, w_down, v_ref, t_ref, tan, pack, keep, hidden)
 
 
-def back_second(count, per, up_idx, down_idx, w_up, w_down, rows, keep, pack, sends, pulled, returned):
+def back_second(count, per, up_idx, down_idx, w_up, w_down, rows, keep, pack, sends, pulled, returned, products):
     blocks = count * per
     me = lax.axis_index("dp")
     for b in range(blocks):
@@ -186,14 +192,14 @@
     for step, place, i in send_order(me, count, per):
         c = rows[:, lanes(i)]
         sends[step][1, :, lanes(place)] = c
-        target = down_idx[0, i]
-        pulled[target] = pulled[target] + times_transposed(c, w_down[0, i])
+        products[i] = times_transposed(c, w_down[0, i])
+    add_at(pulled, products, down_idx)
     for step, place, j in send_order(me, count, per):
-        u = up_idx[0, j]
         slope_b, slope_a, push = (keep[j, 8 * k:8 * k + 8] for k in range(3))
         e = jnp.concatenate([slope_b * pulled[j, 0:8], slope_a * pulled[j, 8:16] + push], 0).astype(BF16)
         sends[step][0, :, lanes(place)] = e
-        returned[u] = returned[u] + times_transposed(e, w_up[0, j])
+        products[j] = times_transposed(e, w_up[0, j])
+    add_at(returned, products, up_idx)
     for b in range(blocks):
         pack[:, lanes(b)] = returned[b].astype(BF16)
 
@@ -209,13 +215,13 @@
 
 
 def near_phase(count, per, up_idx, down_idx, w_up, w_down, near_in, keep, keep_tan, far, *refs):
-    sends, (pulled, returned, hidden) = refs[:count], refs[count:]
+    sends, (pulled, returned, products, hidden) = refs[:count], refs[count:]
     odd = odd_section()
     clear_pad(far, count * per)
 
     @pl.when(odd == 0)
     def _():
-        back_second(count, per, up_idx, down_idx, w_up, w_down, near_in, keep, far, sends, pulled, returned)
+        back_second(count, per, up_idx, down_idx, w_up, w_down, near_in, keep, far, sends, pulled, returned, products)
 
     @pl.when(odd == 1)
     def _():
@@ -224,7 +230,7 @@
 
 def far_phase(count, per, up_idx, down_idx, w_up, w_down, far_in, keep, keep_tan, *refs):
     done, near, refs = refs[:count], refs[count], refs[count + 1:]
-    sends, (pulled, returned, hidden) = refs[:count], refs[count:]
+    sends, (pulled, returned, products, hidden) = refs[:count], refs[count:]
     odd = odd_section()
 
     @pl.when(odd == 0)
@@ -235,7 +241,7 @@
 
     @pl.when(odd == 1)
     def _():
-        back_second(count, per, up_idx, down_idx, w_up, w_down, far_in, keep, near, sends, pulled, returned)
+        back_second(count, per, up_idx, down_idx, w_up, w_down, far_in, keep, near, sends, pulled, returned, products)
 
 
 def early_grads(count, per, *refs):
@@ -250,23 +256,31 @@
 
 def finish(count, per, scale, far, near, grads, *rest):
     early, late = rest[:count], rest[count:2 * count]
-    values, score, tangent, adjoint, grad_up, grad_down, came = rest[2 * count:]
+    outs, (came, streams, held, sems) = rest[2 * count:2 * count + 6], rest[2 * count + 6:]
+    copies = []
+
+    def leave(source, target):
+        copies.append(pltpu.make_async_copy(source, target, sems.at[len(copies)]))
+        copies[-1].start()
+
     take_in(near, far, came)
-    moved = came[0].astype(F32)
-    values[0] = moved[0:8].astype(BF16)
-    tangent[0] = moved[8:16].astype(BF16)
-    moved = came[1].astype(F32)
-    score[0] = moved[0:8].astype(BF16)
-    adjoint[0] = moved[8:16].astype(BF16)
+    forward = came[0].astype(F32)
+    backward = came[1].astype(F32)
+    for k, rows in enumerate((forward[0:8], backward[0:8], forward[8:16], backward[8:16])):
+        streams[k] = rows.astype(BF16)
+        leave(streams.at[k], outs[k].at[0])
     for place in range(per):
         at = lanes(place)
-        for k, (out, group) in enumerate(((grad_up, 2), (grad_down, 7))):
+        for k, group in enumerate((2, 7)):
             xs = [early[source][group, :, at] for source in range(count)]
             es = [late[source][k, :, at] for source in range(count)]
-            out[0, place] = ((grads[k, place] + outer(xs, es)) * scale).astype(BF16)
-
-
-def call(body, operands, spaces, outs, scratch, after=(), cost=LIGHT):
+            held[k, place] = ((grads[k, place] + outer(xs, es)) * scale).astype(BF16)
+            leave(held.at[k, place], outs[4 + k].at[0, place])
+    for copy in copies:
+        copy.wait()
+
+
+def call(body, operands, spaces, outs, scratch, after=(), cost=LIGHT, out_space=pltpu.VMEM):
     taken = len(operands)
 
     def kernel(*refs):
@@ -276,7 +290,7 @@
         kernel,
         out_shape=outs,
         in_specs=[pl.BlockSpec(memory_space=space) for space in spaces] + [pl.BlockSpec(memory_space=pl.ANY)] * len(after),
-        out_specs=[pl.BlockSpec(memory_space=pltpu.VMEM)] * len(outs),
+        out_specs=[pl.BlockSpec(memory_space=out_space)] * len(outs),
         scratch_shapes=scratch,
         compiler_params=pltpu.CompilerParams(vmem_limit_bytes=LIMIT),
         cost_estimate=pl.CostEstimate(flops=cost, bytes_accessed=cost // 100, transcendentals=0),
@@ -311,12 +325,12 @@
     keep, pushes, *early = call(
         body(first_rows, count, per), tables + rows, [smem] * 3 + [vmem] * 8,
         [shape((blocks, 24, BLOCK), F32), pair] + [ten] * count,
-        [vmem((blocks, 32, BLOCK), F32), vmem((blocks, 48, BLOCK), BF16)],
+        [vmem((blocks, 32, BLOCK), F32), vmem((blocks, 32, BLOCK), F32), vmem((blocks, 48, BLOCK), BF16)],
         after=(token,), cost=WORK)
     taken = tables + (score_grad_in, state_adjoint_in, pushes, values_in, tangent_in, saved_tan)
     made = [shape((blocks, 8, BLOCK), F32)]
     long = shape((16, width + PAD), BF16)
-    scratch = [vmem((blocks, 16, BLOCK), F32), vmem((blocks, 16, BLOCK), BF16)]
+    scratch = [vmem((blocks, 16, BLOCK), F32), vmem((blocks, 16, BLOCK), F32), vmem((blocks, 16, BLOCK), BF16)]
     far, far_keep = call(body(first_streams, blocks, 0), taken, [smem] * 3 + [vmem] * 8, [long] + made, scratch)
     near, near_keep = call(body(first_streams, blocks, 1), taken, [smem] * 3 + [vmem] * 8, [pair] + made, scratch,
                            after=(far,))
@@ -324,7 +338,7 @@
     early = to_replicas(early)
     tables = (up_index, down_index, w_up, w_down)
     two = [shape((2, 16, part), BF16)] * count
-    scratch = [vmem((blocks, 16, BLOCK), F32), vmem((blocks, 16, BLOCK), F32), vmem((blocks, 16, BLOCK), BF16)]
+    scratch = [vmem((blocks, 16, BLOCK), F32)] + scratch
     far_out, *late = call(
         body(near_phase, count, per), tables + (near, keep, far_keep), [smem] * 2 + [vmem] * 5, [long] + two, scratch)
     near_out, *late = call(
@@ -338,7 +352,9 @@
     grad = shape((1, per, BLOCK, BLOCK), BF16)
     return tuple(call(
         body(finish, count, per, scale), (far, near, grads, *early, *late), [vmem] * (3 + 2 * count),
-        [stream, stream, stream, stream, grad, grad], [vmem((2, 16, width), BF16)]))
+        [stream] * 4 + [grad] * 2,
+        [vmem((2, 16, width), BF16), vmem((4,) + values_in.shape[1:], BF16), vmem((2, per, BLOCK, BLOCK), BF16),
+         pltpu.SemaphoreType.DMA((4 + 2 * per,))], out_space=pl.ANY))
 
 
 def solution(mesh):

time: 30.2 us -> 30.3 us (level)
  waiting for transfers between devices: 5.34 us -> 5.02 us
    ppermute x2, starting transfers between devices: 0.78 us -> 1.11 us  [swap_sections(): near = lax.ppermute(near, 'section', [(i, i ^ 1) for i in range(count)])]
    ppermute x6, waiting for transfers between devices: 4 us -> 3.68 us  [to_replicas(): lax.ppermute(parts[step], 'dp', swap_route(step, count))]
where the time goes in v11:
time: 30.3 us; the launch traced here: 30.1 us
  starting transfers between devices  13.4 us (44%)
  Pallas kernels  9.32 us (31%)
  waiting for transfers between devices  5.02 us (17%)
  local copies, waits for them, and re-layouts  1.66 us (5%)
  between operations  0.79 us (3%)
    pallas_call x8, Pallas kernels, call(): pl.pallas_call(kernel, out_shape=outs, in_specs=[pl.BlockSpec(memory_spac...  9.32 us
    ppermute x6, starting transfers between devices, to_replicas(): lax.ppermute(parts[step], 'dp', swap_route(step, count))  9.05 us
    ppermute x6, waiting for transfers between devices, to_replicas(): lax.ppermute(parts[step], 'dp', swap_route(step, count))  3.68 us
    ppermute x2, starting transfers between devices, swap_sections(): lax.ppermute(far, 'section', [(i, (i + 2 * (i % 2) - 1) % count) for i in...  3.2 us
    unnamed x28, local copies, waits for them, and re-layouts  1.66 us
    ppermute x2, waiting for transfers between devices, swap_sections(): near = lax.ppermute(near, 'section', [(i, i ^ 1) for i in range(count)])  1.34 us
    ppermute x2, starting transfers between devices, swap_sections(): near = lax.ppermute(near, 'section', [(i, i ^ 1) for i in range(count)])  1.11 us
  transfers between devices with their start and end apart: 10, of which 5 were waited for; matrix products, arithmetic and copies ran while one was open for 0% of the time, Pallas kernels for 21%

profile of v11, /device:TPU:0, one launch (start us, length us, event | category | flops | bytes accessed | tf_op | source)
XLA Modules:
  0.0 30.1 jit_solution(3126995934709802829)
XLA Ops:
  0.8 0.5 %copy-done.8 = s32[1,32]{1,0:T(1,128)S(1)} copy-done((s32[1,32]{1,0:T(1,128)S(1)}, s32[1,32]{1,0:T(1,128)}, u32[]{:S(2)}) %copy-start.8) | copy-done | bytes 152
  1.3 0.6 %copy-done.1 = bf16[1,32,128,128]{3,2,1,0:T(8,128)(2,1)S(1)} copy-done((bf16[1,32,128,128]{3,2,1,0:T(8,128)(2,1)S(1)}, bf16[1,32,128,128]{3,2,1,0:T(8,128)(2,1)}, u32[]{:S(2)}) %copy-start.1) | copy-done | bytes 1048600
  1.9 0.3 %copy-done = bf16[1,32,128,128]{3,2,1,0:T(8,128)(2,1)S(1)} copy-done((bf16[1,32,128,128]{3,2,1,0:T(8,128)(2,1)S(1)}, bf16[1,32,128,128]{3,2,1,0:T(8,128)(2,1)}, u32[]{:S(2)}) %copy-start) | copy-done | bytes 1048600
  2.4 1.8 %shard_map.182 = (f32[32,24,128]{2,1,0:T(8,128)S(1)}, bf16[16,4096]{1,0:T(8,128)(2,1)S(1)}, bf16[10,16,1024]{2,1,0:T(8,128)(2,1)S(1)}, bf16[10,16,1024]{2,1,0:T(...) custom-call(s32[1,32]{1,0:T(1,128)S(1)} %copy-done.7, s32[1,32]{1,0:T(1,128)S(1)} %copy-done.8, ...), custom_call_target="tpu_custom_call" | custom-call | flops 10000000000 | bytes 100000000 | tf_op jit(solution)/shard_map/pallas_call | solution.py:289
  4.2 4.0 %collective-permute-start.4 = (bf16[10,16,1024]{2,1,0:T(8,128)(2,1)S(1)}, bf16[10,16,1024]{2,1,0:T(8,128)(2,1)S(1)}, u32[]{:S(2)}, u32[]{:S(2)}) collective-permute-start(bf16[10,16,1024]{2,1,0:T(8,128)(2,1)S(1)} %get-tuple-element.39), channel_id=1, source_target_pairs={{0,3},{1,2},{2,1},{3,0},{4,7},{5,6},{6,5},{7,4},{8,11},{9,10},{10,... | collective-permute-start | bytes 983048 | tf_op jit(solution)/shard_map/ppermute | solution.py:319
  8.1 0.5 %collective-permute-start.5 = (bf16[10,16,1024]{2,1,0:T(8,128)(2,1)S(1)}, bf16[10,16,1024]{2,1,0:T(8,128)(2,1)S(1)}, u32[]{:S(2)}, u32[]{:S(2)}) collective-permute-start(bf16[10,16,1024]{2,1,0:T(8,128)(2,1)S(1)} %get-tuple-element.40), channel_id=1, source_target_pairs={{0,1},{1,0},{2,3},{3,2},{4,5},{5,4},{6,7},{7,6},{8,9},{9,8},{10,11... | collective-permute-start | bytes 983048 | tf_op jit(solution)/shard_map/ppermute | solution.py:319
  8.7 0.1 collective-permute-start.6
  8.8 1.3 %shard_map.183 = (bf16[16,4224]{1,0:T(8,128)(2,1)S(1)}, f32[32,8,128]{2,1,0:T(8,128)S(1)}) custom-call(s32[1,32]{1,0:T(1,128)S(1)} %copy-done.7, s32[1,32]{1,0:T(1,128)S(1)} %copy-done.8, s32[1,2]{1,0:T(1,128)S(1)} %copy-done.9, bf16[1,32,128,128]{3,2,1,0:T(8,128)(2,1)S(1)} %copy-done, bf16[1,32,128,128]{3,2,1,0:T(8,128)(2,1)S(1)} %copy-done.1, ...), custom_call_target="tpu_custom_call" | custom-call | flops 10000 | bytes 100 | tf_op jit(solution)/shard_map/pallas_call | solution.py:289
  10.1 2.8 %collective-permute-start.2 = (bf16[16,4224]{1,0:T(8,128)(2,1)S(1)}, bf16[16,4224]{1,0:T(8,128)(2,1)S(1)}, u32[]{:S(2)}, u32[]{:S(2)}) collective-permute-start(bf16[16,4224]{1,0:T(8,128)(2,1)S(1)} %get-tuple-element.27.refs_11_), channel_id=1, source_target_pairs={{0,28},{4,8},{8,4},{12,16},{16,12},{20,24},{24,20},{28,0},{1,29},{... | collective-permute-start | bytes 405512 | tf_op jit(solution)/shard_map/ppermute | solution.py:31
  12.8 1.4 %shard_map.184 = (bf16[16,4096]{1,0:T(8,128)(2,1)S(1)}, f32[32,8,128]{2,1,0:T(8,128)S(1)}) custom-call(s32[1,32]{1,0:T(1,128)S(1)} %copy-done.7, s32[1,32]{1,0:T(1,128)S(1)} %copy-done.8, s32[1,2]{1,0:T(1,128)S(1)} %copy-done.9, bf16[1,32,128,128]{3,2,1,0:T(8,128)(2,1)S(1)} %copy-done, bf16[1,32,128,128]{3,2,1,0:T(8,128)(2,1)S(1)} %copy-done.1, ...), custom_call_target="tpu_custom_call" | custom-call | flops 10000 | bytes 100 | tf_op jit(solution)/shard_map/pallas_call | solution.py:289
  14.2 1.3 %collective-permute-done.refs_4_ = bf16[16,4096]{1,0:T(8,128)(2,1)S(1)} collective-permute-done((bf16[16,4096]{1,0:T(8,128)(2,1)S(1)}, bf16[16,4096]{1,0:T(8,128)(2,1)S(1)}, u32[]{:S(2)}, u32[]{:S(2)}) %collective-permute-start) | collective-permute-done | bytes 131104 | tf_op jit(solution)/shard_map/ppermute | solution.py:32
  15.6 2.0 %shard_map.185 = (bf16[16,4224]{1,0:T(8,128)(2,1)S(1)}, bf16[2,16,1024]{2,1,0:T(8,128)(2,1)S(1)}, bf16[2,16,1024]{2,1,0:T(8,128)(2,1)S(1)}, bf16[2,16,1024]{2,1,0:T(8,128)(2,1)S(1)}, bf16[2,16,1024]{2,1,0:T(8,128)(2,1)S(1)}) custom-call(s32[1,32]{1,0:T(1,128)S(1)} %copy-done.7, s32[1,32]{1,0:T(1,128)S(1)} %copy-done.8, ...), custom_call_target="tpu_custom_call" | custom-call | flops 10000 | bytes 100 | tf_op jit(solution)/shard_map/pallas_call | solution.py:289
  17.6 0.4 %collective-permute-start.1 = (bf16[16,4224]{1,0:T(8,128)(2,1)S(1)}, bf16[16,4224]{1,0:T(8,128)(2,1)S(1)}, u32[]{:S(2)}, u32[]{:S(2)}) collective-permute-start(bf16[16,4224]{1,0:T(8,128)(2,1)S(1)} %get-tuple-element.31), channel_id=1, source_target_pairs={{0,28},{4,8},{8,4},{12,16},{16,12},{20,24},{24,20},{28,0},{1,29},{... | collective-permute-start | bytes 405512 | tf_op jit(solution)/shard_map/ppermute | solution.py:31
  18.1 1.4 %shard_map.186 = (bf16[16,4096]{1,0:T(8,128)(2,1)S(1)}, bf16[2,16,1024]{2,1,0:T(8,128)(2,1)S(1)}, bf16[2,16,1024]{2,1,0:T(8,128)(2,1)S(1)}, bf16[2,16,1024]{2,1,0:T(8,128)(2,1)S(1)}, bf16[2,16,1024]{2,1,0:T(8,128)(2,1)S(1)}) custom-call(s32[1,32]{1,0:T(1,128)S(1)} %copy-done.7, s32[1,32]{1,0:T(1,128)S(1)} %copy-done.8, ...), custom_call_target="tpu_custom_call" | custom-call | flops 10000 | bytes 100 | tf_op jit(solution)/shard_map/pallas_call | solution.py:289
  19.4 1.0 %collective-permute-start.3 = (bf16[16,4096]{1,0:T(8,128)(2,1)S(1)}, bf16[16,4096]{1,0:T(8,128)(2,1)S(1)}, u32[]{:S(2)}, u32[]{:S(2)}) collective-permute-start(bf16[16,4096]{1,0:T(8,128)(2,1)S(1)} %get-tuple-element.37), channel_id=1, source_target_pairs={{0,4},{4,0},{8,12},{12,8},{16,20},{20,16},{24,28},{28,24},{1,5},{5... | collective-permute-start | bytes 393224 | tf_op jit(solution)/shard_map/ppermute | solution.py:32
  20.5 2.5 %collective-permute-start.7 = (bf16[2,16,1024]{2,1,0:T(8,128)(2,1)S(1)}, bf16[2,16,1024]{2,1,0:T(8,128)(2,1)S(1)}, u32[]{:S(2)}, u32[]{:S(2)}) collective-permute-start(bf16[2,16,1024]{2,1,0:T(8,128)(2,1)S(1)} %get-tuple-element.43), channel_id=1, source_target_pairs={{0,3},{1,2},{2,1},{3,0},{4,7},{5,6},{6,5},{7,4},{8,11},{9,10},{10,... | collective-permute-start | bytes 196616 | tf_op jit(solution)/shard_map/ppermute | solution.py:319
  22.9 0.3 collective-permute-done.5.refs_2_.refs_5_
  23.2 1.5 %collective-permute-start.8 = (bf16[2,16,1024]{2,1,0:T(8,128)(2,1)S(1)}, bf16[2,16,1024]{2,1,0:T(8,128)(2,1)S(1)}, u32[]{:S(2)}, u32[]{:S(2)}) collective-permute-start(bf16[2,16,1024]{2,1,0:T(8,128)(2,1)S(1)} %get-tuple-element.44), channel_id=1, source_target_pairs={{0,1},{1,0},{2,3},{3,2},{4,5},{5,4},{6,7},{7,6},{8,9},{9,8},{10,11... | collective-permute-start | bytes 196616 | tf_op jit(solution)/shard_map/ppermute | solution.py:319
  24.7 0.5 %collective-permute-start.9 = (bf16[2,16,1024]{2,1,0:T(8,128)(2,1)S(1)}, bf16[2,16,1024]{2,1,0:T(8,128)(2,1)S(1)}, u32[]{:S(2)}, u32[]{:S(2)}) collective-permute-start(bf16[2,16,1024]{2,1,0:T(8,128)(2,1)S(1)} %get-tuple-element.45), channel_id=1, source_target_pairs={{0,2},{1,3},{2,0},{3,1},{4,6},{5,7},{6,4},{7,5},{8,10},{9,11},{10,... | collective-permute-start | bytes 196616 | tf_op jit(solution)/shard_map/ppermute | solution.py:319
  25.2 0.3 %shard_map.187.refs_2_ = f32[2,8,128,128]{3,2,1,0:T(8,128)S(1)} custom-call(bf16[10,16,1024]{2,1,0:T(8,128)(2,1)S(1)} %get-tuple-element.38.refs_0_.refs_3_, bf16[10,16,1024]{2,1,0:T(8,128)(2,1)S(1)} %collective-permute-done.4.refs_1_.refs_4_, bf16[10,16,1024]{2,1,0:T(8,128)(2,1)S(1)} %collective-permute-done.5.refs_2_.refs_5_, ...), custom_call_target="tpu_custom_call" | custom-call | flops 10000 | bytes 100 | tf_op jit(solution)/shard_map/pallas_call | solution.py:289
  25.5 0.5 %collective-permute-done.7.refs_8_ = bf16[2,16,1024]{2,1,0:T(8,128)(2,1)S(1)} collective-permute-done((bf16[2,16,1024]{2,1,0:T(8,128)(2,1)S(1)}, bf16[2,16,1024]{2,1,0:T(8,128)(2,1)S(1)}, u32[]{:S(2)}, u32[]{:S(2)}) %collective-permute-start.7) | collective-permute-done | bytes 65568 | tf_op jit(solution)/shard_map/ppermute | solution.py:319
  26.0 1.4 %collective-permute-done.8.refs_9_ = bf16[2,16,1024]{2,1,0:T(8,128)(2,1)S(1)} collective-permute-done((bf16[2,16,1024]{2,1,0:T(8,128)(2,1)S(1)}, bf16[2,16,1024]{2,1,0:T(8,128)(2,1)S(1)}, u32[]{:S(2)}, u32[]{:S(2)}) %collective-permute-start.8) | collective-permute-done | bytes 65568 | tf_op jit(solution)/shard_map/ppermute | solution.py:319
  27.4 1.5 %collective-permute-done.9.refs_10_ = bf16[2,16,1024]{2,1,0:T(8,128)(2,1)S(1)} collective-permute-done((bf16[2,16,1024]{2,1,0:T(8,128)(2,1)S(1)}, bf16[2,16,1024]{2,1,0:T(8,128)(2,1)S(1)}, u32[]{:S(2)}, u32[]{:S(2)}) %collective-permute-start.9) | collective-permute-done | bytes 65568 | tf_op jit(solution)/shard_map/ppermute | solution.py:319
  28.9 1.2 %shard_map.188 = (bf16[1,8,4096]{2,1,0:T(8,128)(2,1)}, bf16[1,8,4096]{2,1,0:T(8,128)(2,1)}, bf16[1,8,4096]{2,1,0:T(8,128)(2,1)}, bf16[1,8,4096]{2,1,0:T(8,128)(2...) custom-call(bf16[16,4224]{1,0:T(8,128)(2,1)S(1)} %collective-permute-done.1.refs_0_, ...), custom_call_target="tpu_custom_call" | custom-call | flops 10000 | bytes 100 | tf_op jit(solution)/shard_map/pallas_call | solution.py:289
  (32 shorter events, 0.3 us)
Async XLA Ops:
  0.6 0.7 %copy-start.8 = (s32[1,32]{1,0:T(1,128)S(1)}, s32[1,32]{1,0:T(1,128)}, u32[]{:S(2)}) copy-start(s32[1,32]{1,0:T(1,128)} %refs_1_.9) | copy-start | bytes 388
  0.6 1.2 %copy-start.1 = (bf16[1,32,128,128]{3,2,1,0:T(8,128)(2,1)S(1)}, bf16[1,32,128,128]{3,2,1,0:T(8,128)(2,1)}, u32[]{:S(2)}) copy-start(bf16[1,32,128,128]{3,2,1,0:T(8,128)(2,1)} %refs_3_.9) | copy-start | bytes 3145732
  0.7 1.2 %copy-start.7 = (s32[1,32]{1,0:T(1,128)S(1)}, s32[1,32]{1,0:T(1,128)}, u32[]{:S(2)}) copy-start(s32[1,32]{1,0:T(1,128)} %refs_0_.9) | copy-start | bytes 388
  0.7 1.5 %copy-start = (bf16[1,32,128,128]{3,2,1,0:T(8,128)(2,1)S(1)}, bf16[1,32,128,128]{3,2,1,0:T(8,128)(2,1)}, u32[]{:S(2)}) copy-start(bf16[1,32,128,128]{3,2,1,0:T(8,128)(2,1)} %refs_2_.9) | copy-start | bytes 3145732
  0.7 1.5 %copy-start.4 = (bf16[1,8,4096]{2,1,0:T(8,128)(2,1)S(1)}, bf16[1,8,4096]{2,1,0:T(8,128)(2,1)}, u32[]{:S(2)}) copy-start(bf16[1,8,4096]{2,1,0:T(8,128)(2,1)} %refs_6_.5) | copy-start | bytes 196612
  0.7 1.5 %copy-start.3 = (bf16[1,8,4096]{2,1,0:T(8,128)(2,1)S(1)}, bf16[1,8,4096]{2,1,0:T(8,128)(2,1)}, u32[]{:S(2)}) copy-start(bf16[1,8,4096]{2,1,0:T(8,128)(2,1)} %refs_5_.5) | copy-start | bytes 196612
  0.7 1.5 %copy-start.9 = (s32[1,2]{1,0:T(1,128)S(1)}, s32[1,2]{1,0:T(1,128)}, u32[]{:S(2)}) copy-start(s32[1,2]{1,0:T(1,128)} %refs_2_.7) | copy-start | bytes 28
  0.7 1.6 %copy-start.13 = (bf16[1,2,8,4096]{3,2,1,0:T(8,128)(2,1)S(1)}, bf16[1,2,8,4096]{3,2,1,0:T(8,128)(2,1)}, u32[]{:S(2)}) copy-start(bf16[1,2,8,4096]{3,2,1,0:T(8,128)(2,1)} %refs_10_.3) | copy-start | bytes 393220
  0.7 1.6 %copy-start.12 = (bf16[1,2,8,4096]{3,2,1,0:T(8,128)(2,1)S(1)}, bf16[1,2,8,4096]{3,2,1,0:T(8,128)(2,1)}, u32[]{:S(2)}) copy-start(bf16[1,2,8,4096]{3,2,1,0:T(8,128)(2,1)} %refs_9_.3) | copy-start | bytes 393220
  0.7 1.6 %copy-start.11 = (bf16[1,2,8,4096]{3,2,1,0:T(8,128)(2,1)S(1)}, bf16[1,2,8,4096]{3,2,1,0:T(8,128)(2,1)}, u32[]{:S(2)}) copy-start(bf16[1,2,8,4096]{3,2,1,0:T(8,128)(2,1)} %refs_8_.3) | copy-start | bytes 393220
  0.7 1.6 %copy-start.10 = (bf16[1,2,8,4096]{3,2,1,0:T(8,128)(2,1)S(1)}, bf16[1,2,8,4096]{3,2,1,0:T(8,128)(2,1)}, u32[]{:S(2)}) copy-start(bf16[1,2,8,4096]{3,2,1,0:T(8,128)(2,1)} %refs_7_.1) | copy-start | bytes 393220
  2.4 6.4 %copy-start.2 = (bf16[1,2,8,4096]{3,2,1,0:T(8,128)(2,1)S(1)}, bf16[1,2,8,4096]{3,2,1,0:T(8,128)(2,1)}, u32[]{:S(2)}) copy-start(bf16[1,2,8,4096]{3,2,1,0:T(8,128)(2,1)} %refs_10_.5) | copy-start | bytes 393220
  2.4 6.4 %copy-start.5 = (bf16[1,8,4096]{2,1,0:T(8,128)(2,1)S(1)}, bf16[1,8,4096]{2,1,0:T(8,128)(2,1)}, u32[]{:S(2)}) copy-start(bf16[1,8,4096]{2,1,0:T(8,128)(2,1)} %refs_8_.5) | copy-start | bytes 196612
  2.4 6.4 %copy-start.6 = (bf16[1,8,4096]{2,1,0:T(8,128)(2,1)S(1)}, bf16[1,8,4096]{2,1,0:T(8,128)(2,1)}, u32[]{:S(2)}) copy-start(bf16[1,8,4096]{2,1,0:T(8,128)(2,1)} %refs_9_.5) | copy-start | bytes 196612
  4.2 16.3 %collective-permute-start.4 = (bf16[10,16,1024]{2,1,0:T(8,128)(2,1)S(1)}, bf16[10,16,1024]{2,1,0:T(8,128)(2,1)S(1)}, u32[]{:S(2)}, u32[]{:S(2)}) collective-permute-start(bf16[10,16,1024]{2,1,0:T(8,128)(2,1)S(1)} %get-tuple-element.39), channel_id=1, source_target_pairs={{0,3},{1,2},{2,1},{3,0},{4,7},{5,6},{6,5},{7,4},{8,11},{9,10},{10,... | collective-permute-start | bytes 983048 | tf_op jit(solution)/shard_map/ppermute | solution.py:319
  8.1 15.0 %collective-permute-start.5 = (bf16[10,16,1024]{2,1,0:T(8,128)(2,1)S(1)}, bf16[10,16,1024]{2,1,0:T(8,128)(2,1)S(1)}, u32[]{:S(2)}, u32[]{:S(2)}) collective-permute-start(bf16[10,16,1024]{2,1,0:T(8,128)(2,1)S(1)} %get-tuple-element.40), channel_id=1, source_target_pairs={{0,1},{1,0},{2,3},{3,2},{4,5},{5,4},{6,7},{7,6},{8,9},{9,8},{10,11... | collective-permute-start | bytes 983048 | tf_op jit(solution)/shard_map/ppermute | solution.py:319
  8.7 16.0 %collective-permute-start.6 = (bf16[10,16,1024]{2,1,0:T(8,128)(2,1)S(1)}, bf16[10,16,1024]{2,1,0:T(8,128)(2,1)S(1)}, u32[]{:S(2)}, u32[]{:S(2)}) collective-permute-start(bf16[10,16,1024]{2,1,0:T(8,128)(2,1)S(1)} %get-tuple-element.41), channel_id=1, source_target_pairs={{0,2},{1,3},{2,0},{3,1},{4,6},{5,7},{6,4},{7,5},{8,10},{9,11},{10,... | collective-permute-start | bytes 983048 | tf_op jit(solution)/shard_map/ppermute | solution.py:319
  10.1 8.0 %collective-permute-start.2 = (bf16[16,4224]{1,0:T(8,128)(2,1)S(1)}, bf16[16,4224]{1,0:T(8,128)(2,1)S(1)}, u32[]{:S(2)}, u32[]{:S(2)}) collective-permute-start(bf16[16,4224]{1,0:T(8,128)(2,1)S(1)} %get-tuple-element.27.refs_11_), channel_id=1, source_target_pairs={{0,28},{4,8},{8,4},{12,16},{16,12},{20,24},{24,20},{28,0},{1,29},{... | collective-permute-start | bytes 405512 | tf_op jit(solution)/shard_map/ppermute | solution.py:31
  14.2 1.4 %collective-permute-start = (bf16[16,4096]{1,0:T(8,128)(2,1)S(1)}, bf16[16,4096]{1,0:T(8,128)(2,1)S(1)}, u32[]{:S(2)}, u32[]{:S(2)}) collective-permute-start(bf16[16,4096]{1,0:T(8,128)(2,1)S(1)} %get-tuple-element.28), channel_id=1, source_target_pairs={{0,4},{4,0},{8,12},{12,8},{16,20},{20,16},{24,28},{28,24},{1,5},{5... | collective-permute-start | bytes 393224 | tf_op jit(solution)/shard_map/ppermute | solution.py:32
  17.6 11.3 %collective-permute-start.1 = (bf16[16,4224]{1,0:T(8,128)(2,1)S(1)}, bf16[16,4224]{1,0:T(8,128)(2,1)S(1)}, u32[]{:S(2)}, u32[]{:S(2)}) collective-permute-start(bf16[16,4224]{1,0:T(8,128)(2,1)S(1)} %get-tuple-element.31), channel_id=1, source_target_pairs={{0,28},{4,8},{8,4},{12,16},{16,12},{20,24},{24,20},{28,0},{1,29},{... | collective-permute-start | bytes 405512 | tf_op jit(solution)/shard_map/ppermute | solution.py:31
  19.4 9.5 %collective-permute-start.3 = (bf16[16,4096]{1,0:T(8,128)(2,1)S(1)}, bf16[16,4096]{1,0:T(8,128)(2,1)S(1)}, u32[]{:S(2)}, u32[]{:S(2)}) collective-permute-start(bf16[16,4096]{1,0:T(8,128)(2,1)S(1)} %get-tuple-element.37), channel_id=1, source_target_pairs={{0,4},{4,0},{8,12},{12,8},{16,20},{20,16},{24,28},{28,24},{1,5},{5... | collective-permute-start | bytes 393224 | tf_op jit(solution)/shard_map/ppermute | solution.py:32
  20.5 5.5 %collective-permute-start.7 = (bf16[2,16,1024]{2,1,0:T(8,128)(2,1)S(1)}, bf16[2,16,1024]{2,1,0:T(8,128)(2,1)S(1)}, u32[]{:S(2)}, u32[]{:S(2)}) collective-permute-start(bf16[2,16,1024]{2,1,0:T(8,128)(2,1)S(1)} %get-tuple-element.43), channel_id=1, source_target_pairs={{0,3},{1,2},{2,1},{3,0},{4,7},{5,6},{6,5},{7,4},{8,11},{9,10},{10,... | collective-permute-start | bytes 196616 | tf_op jit(solution)/shard_map/ppermute | solution.py:319
  23.2 4.3 %collective-permute-start.8 = (bf16[2,16,1024]{2,1,0:T(8,128)(2,1)S(1)}, bf16[2,16,1024]{2,1,0:T(8,128)(2,1)S(1)}, u32[]{:S(2)}, u32[]{:S(2)}) collective-permute-start(bf16[2,16,1024]{2,1,0:T(8,128)(2,1)S(1)} %get-tuple-element.44), channel_id=1, source_target_pairs={{0,1},{1,0},{2,3},{3,2},{4,5},{5,4},{6,7},{7,6},{8,9},{9,8},{10,11... | collective-permute-start | bytes 196616 | tf_op jit(solution)/shard_map/ppermute | solution.py:319
  24.7 4.3 %collective-permute-start.9 = (bf16[2,16,1024]{2,1,0:T(8,128)(2,1)S(1)}, bf16[2,16,1024]{2,1,0:T(8,128)(2,1)S(1)}, u32[]{:S(2)}, u32[]{:S(2)}) collective-permute-start(bf16[2,16,1024]{2,1,0:T(8,128)(2,1)S(1)} %get-tuple-element.45), channel_id=1, source_target_pairs={{0,2},{1,3},{2,0},{3,1},{4,6},{5,7},{6,4},{7,5},{8,10},{9,11},{10,... | collective-permute-start | bytes 196616 | tf_op jit(solution)/shard_map/ppermute | solution.py:319

commit v12 on v10

--- a/solution.py
+++ b/solution.py
@@ -12,6 +12,10 @@
 WORK = 10 ** 10
 LIGHT = 10 ** 4
 PAD = BLOCK
+C_FAR = LIGHT
+C_NEAR = LIGHT
+C_NEAR_PHASE = LIGHT
+C_FAR_PHASE = 147 * 10 ** 7
 
 
 def partner(me, step, count):
@@ -88,6 +92,7 @@
 def first_rows(count, per, up_idx, down_idx, order, w_up, w_down, g_ref, a_ref, back, second, second_tan, second_grad,
                keep, pushes, *refs):
     sends, (pulled, hidden) = refs[:count], refs[count:]
+    clear_pad(sends[-1], 10 * per)
     blocks = count * per
     me = lax.axis_index("dp")
     for b in range(blocks):
@@ -97,8 +102,8 @@
     for step, place, i in send_order(me, count, per):
         at = lanes(i)
         c = stack([g_ref[0, :, at], a_ref[0, :, at], second_grad[0, m0, :, at], second_grad[0, m1, :, at]]).astype(BF16)
-        sends[step][8, :, lanes(place)] = c[0:16]
-        sends[step][9, :, lanes(place)] = c[16:32]
+        sends[step][:, lanes(8 * per + place)] = c[0:16]
+        sends[step][:, lanes(9 * per + place)] = c[16:32]
         target = down_idx[0, i]
         pulled[target] = pulled[target] + times_transposed(c, w_down[0, i])
     for step, place, j in send_order(me, count, per):
@@ -107,9 +112,8 @@
         x = stack([back[0, m0, :, at], second[0, m0, :, at], second_tan[0, m0, :, at],
                    second_tan[0, m1, :, at], back[0, m1, :, at], second[0, m1, :, at]]).astype(BF16)
         out = sends[step]
-        here = lanes(place)
         for group in range(3):
-            out[group, :, here] = x[16 * group:16 * group + 16]
+            out[:, lanes(group * per + place)] = x[16 * group:16 * group + 16]
         z = times(x, w_up[0, j])
         zb0, za0, ta0, ta1, zb1, za1 = (z[8 * k:8 * k + 8] for k in range(6))
         pg, pa, ga0, ga1 = (pulled[j, 8 * k:8 * k + 8] for k in range(4))
@@ -120,8 +124,8 @@
         curve_a1 = sa1 * (1.0 - sa1) * (2.0 + za1 * (1.0 - 2.0 * sa1))
         push = slope_a0 * pa + curve_a0 * ga0 * ta0
         e = jnp.concatenate([slope_of(zb0, sb0) * pg, push], 0).astype(BF16)
-        out[3, :, here] = e
-        out[4, :, here] = jnp.concatenate([slope_a0 * ga0, slope_a1 * ga1], 0).astype(BF16)
+        out[:, lanes(3 * per + place)] = e
+        out[:, lanes(4 * per + place)] = jnp.concatenate([slope_a0 * ga0, slope_a1 * ga1], 0).astype(BF16)
         hidden[j] = jnp.concatenate(
             [zb0 * sb0, za0 * sa0, slope_a0 * ta0, slope_a1 * ta1, zb1 * sb1, za1 * sa1], 0).astype(BF16)
         keep[j] = jnp.concatenate([slope_of(zb1, sb1), slope_a1, curve_a1 * ga1 * ta1], 0)
@@ -129,7 +133,7 @@
     for step, place, i in send_order(me, count, per):
         y = hidden[down_idx[0, i]]
         for group in range(3):
-            sends[step][5 + group, :, lanes(place)] = y[16 * group:16 * group + 16]
+            sends[step][:, lanes((5 + group) * per + place)] = y[16 * group:16 * group + 16]
 
 
 def forward_first(blocks, up_idx, down_idx, order, w_up, w_down, v_ref, t_ref, tan, pack, keep, hidden):
@@ -163,8 +167,12 @@
         pack[:, lanes(b)] = returned[b].astype(BF16)
 
 
-def first_streams(blocks, back_parity, up_idx, down_idx, order, w_up, w_down, g_ref, a_ref, pushes, v_ref, t_ref, tan,
-                  pack, keep, returned, hidden):
+def first_streams(blocks, back_parity, held, up_idx, down_idx, order, w_up, w_down, g_ref, a_ref, pushes, v_ref, t_ref,
+                  tan, *refs):
+    pack, keep = refs[held:held + 2]
+    returned, hidden = refs[2 * held + 2:]
+    for source, target in zip(refs[:held], refs[held + 2:2 * held + 2]):
+        target[...] = source[...]
     odd = odd_section()
     clear_pad(pack, blocks)
 
@@ -185,14 +193,14 @@
         returned[b] = rows[:, lanes(b)].astype(F32)
     for step, place, i in send_order(me, count, per):
         c = rows[:, lanes(i)]
-        sends[step][1, :, lanes(place)] = c
+        sends[step][:, lanes(per + place)] = c
         target = down_idx[0, i]
         pulled[target] = pulled[target] + times_transposed(c, w_down[0, i])
     for step, place, j in send_order(me, count, per):
         u = up_idx[0, j]
         slope_b, slope_a, push = (keep[j, 8 * k:8 * k + 8] for k in range(3))
         e = jnp.concatenate([slope_b * pulled[j, 0:8], slope_a * pulled[j, 8:16] + push], 0).astype(BF16)
-        sends[step][0, :, lanes(place)] = e
+        sends[step][:, lanes(place)] = e
         returned[u] = returned[u] + times_transposed(e, w_up[0, j])
     for b in range(blocks):
         pack[:, lanes(b)] = returned[b].astype(BF16)
@@ -241,10 +249,9 @@
 def early_grads(count, per, *refs):
     early, grads = refs[:count], refs[count]
     for place in range(per):
-        at = lanes(place)
         for out, left, right in ((0, 0, 3), (1, 5, 8)):
-            xs = [early[source][left + k, :, at] for source in range(count) for k in range(2)]
-            es = [early[source][right + k, :, at] for source in range(count) for k in range(2)]
+            xs = [early[source][:, lanes((left + k) * per + place)] for source in range(count) for k in range(2)]
+            es = [early[source][:, lanes((right + k) * per + place)] for source in range(count) for k in range(2)]
             grads[out, place] = outer(xs, es)
 
 
@@ -259,10 +266,9 @@
     score[0] = moved[0:8].astype(BF16)
     adjoint[0] = moved[8:16].astype(BF16)
     for place in range(per):
-        at = lanes(place)
         for k, (out, group) in enumerate(((grad_up, 2), (grad_down, 7))):
-            xs = [early[source][group, :, at] for source in range(count)]
-            es = [late[source][k, :, at] for source in range(count)]
+            xs = [early[source][:, lanes(group * per + place)] for source in range(count)]
+            es = [late[source][:, lanes(k * per + place)] for source in range(count)]
             out[0, place] = ((grads[k, place] + outer(xs, es)) * scale).astype(BF16)
 
 
@@ -305,31 +311,37 @@
         return [parts[0]] + [lax.ppermute(parts[step], "dp", swap_route(step, count)) for step in steps]
 
     rows = (score_grad_in, state_adjoint_in, saved_back, saved_second, saved_second_tan, saved_second_grad)
-    ten = shape((10, 16, part), BF16)
+    ten = [shape((16, 10 * part), BF16)] * (count - 1) + [shape((16, 10 * part + 4 * PAD), BF16)]
     (token,) = call(open_launch, (), [], [shape((8, BLOCK), F32)], [], cost=WORK)
     tables = (up_index, down_index, tick_order, w_up, w_down)
     keep, pushes, *early = call(
         body(first_rows, count, per), tables + rows, [smem] * 3 + [vmem] * 8,
-        [shape((blocks, 24, BLOCK), F32), pair] + [ten] * count,
+        [shape((blocks, 24, BLOCK), F32), pair] + ten,
         [vmem((blocks, 32, BLOCK), F32), vmem((blocks, 48, BLOCK), BF16)],
         after=(token,), cost=WORK)
     taken = tables + (score_grad_in, state_adjoint_in, pushes, values_in, tangent_in, saved_tan)
     made = [shape((blocks, 8, BLOCK), F32)]
     long = shape((16, width + PAD), BF16)
     scratch = [vmem((blocks, 16, BLOCK), F32), vmem((blocks, 16, BLOCK), BF16)]
-    far, far_keep = call(body(first_streams, blocks, 0), taken, [smem] * 3 + [vmem] * 8, [long] + made, scratch)
-    near, near_keep = call(body(first_streams, blocks, 1), taken, [smem] * 3 + [vmem] * 8, [pair] + made, scratch,
-                           after=(far,))
+    far, far_keep = call(
+        body(first_streams, blocks, 0, 0), taken, [smem] * 3 + [vmem] * 8, [long] + made, scratch, cost=C_FAR)
+    neighbours = early[1:count - 1]
+    near, near_keep, *neighbours = call(
+        body(first_streams, blocks, 1, len(neighbours)), taken + tuple(neighbours),
+        [smem] * 3 + [vmem] * (8 + len(neighbours)), [pair] + made + ten[:len(neighbours)], scratch, after=(far,),
+        cost=C_NEAR)
+    early = [early[0], *neighbours, early[count - 1]]
     near, far = swap_sections(near, far)
     early = to_replicas(early)
     tables = (up_index, down_index, w_up, w_down)
-    two = [shape((2, 16, part), BF16)] * count
+    two = [shape((16, 2 * part), BF16)] * count
     scratch = [vmem((blocks, 16, BLOCK), F32), vmem((blocks, 16, BLOCK), F32), vmem((blocks, 16, BLOCK), BF16)]
     far_out, *late = call(
-        body(near_phase, count, per), tables + (near, keep, far_keep), [smem] * 2 + [vmem] * 5, [long] + two, scratch)
+        body(near_phase, count, per), tables + (near, keep, far_keep), [smem] * 2 + [vmem] * 5, [long] + two, scratch,
+        cost=C_NEAR_PHASE)
     near_out, *late = call(
         body(far_phase, count, per), tables + (far, keep, near_keep, *late), [smem] * 2 + [vmem] * (5 + count),
-        [pair] + two, scratch)
+        [pair] + two, scratch, cost=C_FAR_PHASE)
     near, far = swap_sections(near_out, far_out)
     late = to_replicas(late)
     (grads,) = call(

time: 30.2 us -> 31.4 us (1.040)
  waiting for transfers between devices: 5.34 us -> 7.37 us
  starting transfers between devices: 13.2 us -> 12.3 us
    ppermute x6, waiting for transfers between devices: 4 us -> 7.14 us  [to_replicas(): lax.ppermute(parts[step], 'dp', swap_route(step, count))]
    ppermute x2, waiting for transfers between devices: 1.34 us -> 0.23 us  [swap_sections(): near = lax.ppermute(near, 'section', [(i, i ^ 1) for i in range(count)])]
    ppermute x6, starting transfers between devices: 9.05 us -> 8.56 us  [to_replicas(): lax.ppermute(parts[step], 'dp', swap_route(step, count))]
    ppermute x2, starting transfers between devices: 3.34 us -> 3.02 us  [swap_sections(): lax.ppermute(far, 'section', [(i, (i + 2 * (i % 2) - 1) % count) for i in...]
  transfers between devices with their start and end apart: 10 -> 10, of which waited for: 5 -> 4; matrix products, arithmetic and copies ran while one was open for 0% -> 0% of each run, Pallas kernels for 21% -> 20%
where the time goes in v12:
time: 31.4 us; the launch traced here: 31.2 us
  starting transfers between devices  12.3 us (39%)
  Pallas kernels  9.06 us (29%)
  waiting for transfers between devices  7.37 us (23%)
  local copies, waits for them, and re-layouts  1.66 us (5%)
  between operations  0.79 us (3%)
    pallas_call x8, Pallas kernels, call(): pl.pallas_call(kernel, out_shape=outs, in_specs=[pl.BlockSpec(memory_spac...  9.06 us
    ppermute x6, starting transfers between devices, to_replicas(): lax.ppermute(parts[step], 'dp', swap_route(step, count))  8.56 us
    ppermute x6, waiting for transfers between devices, to_replicas(): lax.ppermute(parts[step], 'dp', swap_route(step, count))  7.14 us
    ppermute x2, starting transfers between devices, swap_sections(): lax.ppermute(far, 'section', [(i, (i + 2 * (i % 2) - 1) % count) for i in...  3.02 us
    unnamed x28, local copies, waits for them, and re-layouts  1.66 us
    ppermute x2, starting transfers between devices, swap_sections(): near = lax.ppermute(near, 'section', [(i, i ^ 1) for i in range(count)])  0.76 us
  transfers between devices with their start and end apart: 10, of which 4 were waited for; matrix products, arithmetic and copies ran while one was open for 0% of the time, Pallas kernels for 20%

profile of v12, /device:TPU:0, one launch (start us, length us, event | category | flops | bytes accessed | tf_op | source)
XLA Modules:
  0.0 31.2 jit_solution(5559400040830832851)
XLA Ops:
  0.8 0.5 %copy-done.8 = s32[1,32]{1,0:T(1,128)S(1)} copy-done((s32[1,32]{1,0:T(1,128)S(1)}, s32[1,32]{1,0:T(1,128)}, u32[]{:S(2)}) %copy-start.8) | copy-done | bytes 152
  1.3 0.6 %copy-done.1 = bf16[1,32,128,128]{3,2,1,0:T(8,128)(2,1)S(1)} copy-done((bf16[1,32,128,128]{3,2,1,0:T(8,128)(2,1)S(1)}, bf16[1,32,128,128]{3,2,1,0:T(8,128)(2,1)}, u32[]{:S(2)}) %copy-start.1) | copy-done | bytes 1048600
  1.9 0.3 %copy-done = bf16[1,32,128,128]{3,2,1,0:T(8,128)(2,1)S(1)} copy-done((bf16[1,32,128,128]{3,2,1,0:T(8,128)(2,1)S(1)}, bf16[1,32,128,128]{3,2,1,0:T(8,128)(2,1)}, u32[]{:S(2)}) %copy-start) | copy-done | bytes 1048600
  2.4 1.7 %shard_map.182 = (f32[32,24,128]{2,1,0:T(8,128)S(1)}, bf16[16,4096]{1,0:T(8,128)(2,1)S(1)}, bf16[16,10240]{1,0:T(8,128)(2,1)S(1)}, bf16[16,10240]{1,0:T(8,128)(2...) custom-call(s32[1,32]{1,0:T(1,128)S(1)} %copy-done.7, s32[1,32]{1,0:T(1,128)S(1)} %copy-done.8, ...), custom_call_target="tpu_custom_call" | custom-call | flops 10000000000 | bytes 100000000 | tf_op jit(solution)/shard_map/pallas_call | solution.py:281
  4.1 4.0 %collective-permute-start.4 = (bf16[16,10752]{1,0:T(8,128)(2,1)S(1)}, bf16[16,10752]{1,0:T(8,128)(2,1)S(1)}, u32[]{:S(2)}, u32[]{:S(2)}) collective-permute-start(bf16[16,10752]{1,0:T(8,128)(2,1)S(1)} %get-tuple-element.43), channel_id=1, source_target_pairs={{0,3},{1,2},{2,1},{3,0},{4,7},{5,6},{6,5},{7,4},{8,11},{9,10},{10,... | collective-permute-start | bytes 1032200 | tf_op jit(solution)/shard_map/ppermute | solution.py:311
  8.1 1.3 %shard_map.183 = (bf16[16,4224]{1,0:T(8,128)(2,1)S(1)}, f32[32,8,128]{2,1,0:T(8,128)S(1)}) custom-call(s32[1,32]{1,0:T(1,128)S(1)} %copy-done.7, s32[1,32]{1,0:T(1,128)S(1)} %copy-done.8, s32[1,2]{1,0:T(1,128)S(1)} %copy-done.9, bf16[1,32,128,128]{3,2,1,0:T(8,128)(2,1)S(1)} %copy-done, bf16[1,32,128,128]{3,2,1,0:T(8,128)(2,1)S(1)} %copy-done.1, ...), custom_call_target="tpu_custom_call" | custom-call | flops 10000 | bytes 100 | tf_op jit(solution)/shard_map/pallas_call | solution.py:281
  9.3 2.9 %collective-permute-start.2 = (bf16[16,4224]{1,0:T(8,128)(2,1)S(1)}, bf16[16,4224]{1,0:T(8,128)(2,1)S(1)}, u32[]{:S(2)}, u32[]{:S(2)}) collective-permute-start(bf16[16,4224]{1,0:T(8,128)(2,1)S(1)} %get-tuple-element.31.refs_13_), channel_id=1, source_target_pairs={{0,28},{4,8},{8,4},{12,16},{16,12},{20,24},{24,20},{28,0},{1,29},{... | collective-permute-start | bytes 405512 | tf_op jit(solution)/shard_map/ppermute | solution.py:35
  12.2 1.4 %shard_map.184 = (bf16[16,4096]{1,0:T(8,128)(2,1)S(1)}, f32[32,8,128]{2,1,0:T(8,128)S(1)}, bf16[16,10240]{1,0:T(8,128)(2,1)S(1)}, bf16[16,10240]{1,0:T(8,128)(2,1)S(1)}) custom-call(s32[1,32]{1,0:T(1,128)S(1)} %copy-done.7, s32[1,32]{1,0:T(1,128)S(1)} %copy-done.8, s32[1,2]{1,0:T(1,128)S(1)} %copy-done.9, bf16[1,32,128,128]{3,2,1,0:T(8,128)(2,1)S(1)} %copy-done, ...), custom_call_target="tpu_custom_call" | custom-call | flops 10000 | bytes 100 | tf_op jit(solution)/shard_map/pallas_call | solution.py:281
  13.6 0.1 collective-permute-start
  13.7 0.6 %collective-permute-start.5 = (bf16[16,10240]{1,0:T(8,128)(2,1)S(1)}, bf16[16,10240]{1,0:T(8,128)(2,1)S(1)}, u32[]{:S(2)}, u32[]{:S(2)}) collective-permute-start(bf16[16,10240]{1,0:T(8,128)(2,1)S(1)} %get-tuple-element.44), channel_id=1, source_target_pairs={{0,1},{1,0},{2,3},{3,2},{4,5},{5,4},{6,7},{7,6},{8,9},{9,8},{10,11... | collective-permute-start | bytes 983048 | tf_op jit(solution)/shard_map/ppermute | solution.py:311
  14.3 0.5 %collective-permute-start.6 = (bf16[16,10240]{1,0:T(8,128)(2,1)S(1)}, bf16[16,10240]{1,0:T(8,128)(2,1)S(1)}, u32[]{:S(2)}, u32[]{:S(2)}) collective-permute-start(bf16[16,10240]{1,0:T(8,128)(2,1)S(1)} %get-tuple-element.45), channel_id=1, source_target_pairs={{0,2},{1,3},{2,0},{3,1},{4,6},{5,7},{6,4},{7,5},{8,10},{9,11},{10,... | collective-permute-start | bytes 983048 | tf_op jit(solution)/shard_map/ppermute | solution.py:311
  14.8 0.2 collective-permute-done.refs_4_
  15.0 1.9 %shard_map.185 = (bf16[16,4224]{1,0:T(8,128)(2,1)S(1)}, bf16[16,2048]{1,0:T(8,128)(2,1)S(1)}, bf16[16,2048]{1,0:T(8,128)(2,1)S(1)}, bf16[16,2048]{1,0:T(8,128)(2,1)S(1)}, bf16[16,2048]{1,0:T(8,128)(2,1)S(1)}) custom-call(s32[1,32]{1,0:T(1,128)S(1)} %copy-done.7, s32[1,32]{1,0:T(1,128)S(1)} %copy-done.8, bf16[1,32,128,128]{3,2,1,0:T(8,128)(2,1)S(1)} %copy-done, ...), custom_call_target="tpu_custom_call" | custom-call | flops 10000 | bytes 100 | tf_op jit(solution)/shard_map/pallas_call | solution.py:281
  16.9 0.1 collective-permute-start.1
  17.0 1.4 %shard_map.186 = (bf16[16,4096]{1,0:T(8,128)(2,1)S(1)}, bf16[16,2048]{1,0:T(8,128)(2,1)S(1)}, bf16[16,2048]{1,0:T(8,128)(2,1)S(1)}, bf16[16,2048]{1,0:T(8,128)(2,1)S(1)}, bf16[16,2048]{1,0:T(8,128)(2,1)S(1)}) custom-call(s32[1,32]{1,0:T(1,128)S(1)} %copy-done.7, s32[1,32]{1,0:T(1,128)S(1)} %copy-done.8, bf16[1,32,128,128]{3,2,1,0:T(8,128)(2,1)S(1)} %copy-done, ...), custom_call_target="tpu_custom_call" | custom-call | flops 1470000000 | bytes 14700000 | tf_op jit(solution)/shard_map/pallas_call | solution.py:281
  18.4 0.7 %collective-permute-start.3 = (bf16[16,4096]{1,0:T(8,128)(2,1)S(1)}, bf16[16,4096]{1,0:T(8,128)(2,1)S(1)}, u32[]{:S(2)}, u32[]{:S(2)}) collective-permute-start(bf16[16,4096]{1,0:T(8,128)(2,1)S(1)} %get-tuple-element.41), channel_id=1, source_target_pairs={{0,4},{4,0},{8,12},{12,8},{16,20},{20,16},{24,28},{28,24},{1,5},{5... | collective-permute-start | bytes 393224 | tf_op jit(solution)/shard_map/ppermute | solution.py:36
  19.1 4.7 %collective-permute-done.5.refs_2_.refs_5_ = bf16[16,10240]{1,0:T(8,128)(2,1)S(1)} collective-permute-done((bf16[16,10240]{1,0:T(8,128)(2,1)S(1)}, bf16[16,10240]{1,0:T(8,128)(2,1)S(1)}, u32[]{:S(2)}, u32[]{:S(2)}) %collective-permute-start.5) | collective-permute-done | bytes 327712 | tf_op jit(solution)/shard_map/ppermute | solution.py:311
  23.8 1.0 %collective-permute-start.7 = (bf16[16,2048]{1,0:T(8,128)(2,1)S(1)}, bf16[16,2048]{1,0:T(8,128)(2,1)S(1)}, u32[]{:S(2)}, u32[]{:S(2)}) collective-permute-start(bf16[16,2048]{1,0:T(8,128)(2,1)S(1)} %get-tuple-element.47), channel_id=1, source_target_pairs={{0,3},{1,2},{2,1},{3,0},{4,7},{5,6},{6,5},{7,4},{8,11},{9,10},{10,... | collective-permute-start | bytes 196616 | tf_op jit(solution)/shard_map/ppermute | solution.py:311
  24.8 1.0 %collective-permute-start.8 = (bf16[16,2048]{1,0:T(8,128)(2,1)S(1)}, bf16[16,2048]{1,0:T(8,128)(2,1)S(1)}, u32[]{:S(2)}, u32[]{:S(2)}) collective-permute-start(bf16[16,2048]{1,0:T(8,128)(2,1)S(1)} %get-tuple-element.48), channel_id=1, source_target_pairs={{0,1},{1,0},{2,3},{3,2},{4,5},{5,4},{6,7},{7,6},{8,9},{9,8},{10,11... | collective-permute-start | bytes 196616 | tf_op jit(solution)/shard_map/ppermute | solution.py:311
  25.8 1.5 %collective-permute-start.9 = (bf16[16,2048]{1,0:T(8,128)(2,1)S(1)}, bf16[16,2048]{1,0:T(8,128)(2,1)S(1)}, u32[]{:S(2)}, u32[]{:S(2)}) collective-permute-start(bf16[16,2048]{1,0:T(8,128)(2,1)S(1)} %get-tuple-element.49), channel_id=1, source_target_pairs={{0,2},{1,3},{2,0},{3,1},{4,6},{5,7},{6,4},{7,5},{8,10},{9,11},{10,... | collective-permute-start | bytes 196616 | tf_op jit(solution)/shard_map/ppermute | solution.py:311
  27.3 0.3 %shard_map.187.refs_2_ = f32[2,8,128,128]{3,2,1,0:T(8,128)S(1)} custom-call(bf16[16,10240]{1,0:T(8,128)(2,1)S(1)} %get-tuple-element.42.refs_0_.refs_3_, bf16[16,10752]{1,0:T(8,128)(2,1)S(1)} %collective-permute-done.4.refs_1_.refs_4_, bf16[16,10240]{1,0:T(8,128)(2,1)S(1)} %collective-permute-done.5.refs_2_.refs_5_, ...), custom_call_target="tpu_custom_call" | custom-call | flops 10000 | bytes 100 | tf_op jit(solution)/shard_map/pallas_call | solution.py:281
  27.6 1.5 %collective-permute-done.7.refs_8_ = bf16[16,2048]{1,0:T(8,128)(2,1)S(1)} collective-permute-done((bf16[16,2048]{1,0:T(8,128)(2,1)S(1)}, bf16[16,2048]{1,0:T(8,128)(2,1)S(1)}, u32[]{:S(2)}, u32[]{:S(2)}) %collective-permute-start.7) | collective-permute-done | bytes 65568 | tf_op jit(solution)/shard_map/ppermute | solution.py:311
  29.2 0.9 %collective-permute-done.9.refs_10_ = bf16[16,2048]{1,0:T(8,128)(2,1)S(1)} collective-permute-done((bf16[16,2048]{1,0:T(8,128)(2,1)S(1)}, bf16[16,2048]{1,0:T(8,128)(2,1)S(1)}, u32[]{:S(2)}, u32[]{:S(2)}) %collective-permute-start.9) | collective-permute-done | bytes 65568 | tf_op jit(solution)/shard_map/ppermute | solution.py:311
  30.1 1.2 %shard_map.188 = (bf16[1,8,4096]{2,1,0:T(8,128)(2,1)}, bf16[1,8,4096]{2,1,0:T(8,128)(2,1)}, bf16[1,8,4096]{2,1,0:T(8,128)(2,1)}, bf16[1,8,4096]{2,1,0:T(8,128)(2...) custom-call(bf16[16,4224]{1,0:T(8,128)(2,1)S(1)} %collective-permute-done.1.refs_0_, ...), custom_call_target="tpu_custom_call" | custom-call | flops 10000 | bytes 100 | tf_op jit(solution)/shard_map/pallas_call | solution.py:281
  (32 shorter events, 0.2 us)
Async XLA Ops:
  0.6 0.7 %copy-start.8 = (s32[1,32]{1,0:T(1,128)S(1)}, s32[1,32]{1,0:T(1,128)}, u32[]{:S(2)}) copy-start(s32[1,32]{1,0:T(1,128)} %refs_1_.9) | copy-start | bytes 388
  0.6 1.2 %copy-start.1 = (bf16[1,32,128,128]{3,2,1,0:T(8,128)(2,1)S(1)}, bf16[1,32,128,128]{3,2,1,0:T(8,128)(2,1)}, u32[]{:S(2)}) copy-start(bf16[1,32,128,128]{3,2,1,0:T(8,128)(2,1)} %refs_3_.9) | copy-start | bytes 3145732
  0.7 1.2 %copy-start.7 = (s32[1,32]{1,0:T(1,128)S(1)}, s32[1,32]{1,0:T(1,128)}, u32[]{:S(2)}) copy-start(s32[1,32]{1,0:T(1,128)} %refs_0_.9) | copy-start | bytes 388
  0.7 1.5 %copy-start = (bf16[1,32,128,128]{3,2,1,0:T(8,128)(2,1)S(1)}, bf16[1,32,128,128]{3,2,1,0:T(8,128)(2,1)}, u32[]{:S(2)}) copy-start(bf16[1,32,128,128]{3,2,1,0:T(8,128)(2,1)} %refs_2_.9) | copy-start | bytes 3145732
  0.7 1.5 %copy-start.4 = (bf16[1,8,4096]{2,1,0:T(8,128)(2,1)S(1)}, bf16[1,8,4096]{2,1,0:T(8,128)(2,1)}, u32[]{:S(2)}) copy-start(bf16[1,8,4096]{2,1,0:T(8,128)(2,1)} %refs_6_.5) | copy-start | bytes 196612
  0.7 1.5 %copy-start.3 = (bf16[1,8,4096]{2,1,0:T(8,128)(2,1)S(1)}, bf16[1,8,4096]{2,1,0:T(8,128)(2,1)}, u32[]{:S(2)}) copy-start(bf16[1,8,4096]{2,1,0:T(8,128)(2,1)} %refs_5_.5) | copy-start | bytes 196612
  0.7 1.5 %copy-start.9 = (s32[1,2]{1,0:T(1,128)S(1)}, s32[1,2]{1,0:T(1,128)}, u32[]{:S(2)}) copy-start(s32[1,2]{1,0:T(1,128)} %refs_2_.7) | copy-start | bytes 28
  0.7 1.6 %copy-start.13 = (bf16[1,2,8,4096]{3,2,1,0:T(8,128)(2,1)S(1)}, bf16[1,2,8,4096]{3,2,1,0:T(8,128)(2,1)}, u32[]{:S(2)}) copy-start(bf16[1,2,8,4096]{3,2,1,0:T(8,128)(2,1)} %refs_10_.3) | copy-start | bytes 393220
  0.7 1.6 %copy-start.12 = (bf16[1,2,8,4096]{3,2,1,0:T(8,128)(2,1)S(1)}, bf16[1,2,8,4096]{3,2,1,0:T(8,128)(2,1)}, u32[]{:S(2)}) copy-start(bf16[1,2,8,4096]{3,2,1,0:T(8,128)(2,1)} %refs_9_.3) | copy-start | bytes 393220
  0.7 1.6 %copy-start.11 = (bf16[1,2,8,4096]{3,2,1,0:T(8,128)(2,1)S(1)}, bf16[1,2,8,4096]{3,2,1,0:T(8,128)(2,1)}, u32[]{:S(2)}) copy-start(bf16[1,2,8,4096]{3,2,1,0:T(8,128)(2,1)} %refs_8_.3) | copy-start | bytes 393220
  0.7 1.6 %copy-start.10 = (bf16[1,2,8,4096]{3,2,1,0:T(8,128)(2,1)S(1)}, bf16[1,2,8,4096]{3,2,1,0:T(8,128)(2,1)}, u32[]{:S(2)}) copy-start(bf16[1,2,8,4096]{3,2,1,0:T(8,128)(2,1)} %refs_7_.1) | copy-start | bytes 393220
  2.4 5.7 %copy-start.2 = (bf16[1,2,8,4096]{3,2,1,0:T(8,128)(2,1)S(1)}, bf16[1,2,8,4096]{3,2,1,0:T(8,128)(2,1)}, u32[]{:S(2)}) copy-start(bf16[1,2,8,4096]{3,2,1,0:T(8,128)(2,1)} %refs_10_.5) | copy-start | bytes 393220
  2.4 5.7 %copy-start.5 = (bf16[1,8,4096]{2,1,0:T(8,128)(2,1)S(1)}, bf16[1,8,4096]{2,1,0:T(8,128)(2,1)}, u32[]{:S(2)}) copy-start(bf16[1,8,4096]{2,1,0:T(8,128)(2,1)} %refs_8_.5) | copy-start | bytes 196612
  2.4 5.7 %copy-start.6 = (bf16[1,8,4096]{2,1,0:T(8,128)(2,1)S(1)}, bf16[1,8,4096]{2,1,0:T(8,128)(2,1)}, u32[]{:S(2)}) copy-start(bf16[1,8,4096]{2,1,0:T(8,128)(2,1)} %refs_9_.5) | copy-start | bytes 196612
  4.1 21.7 %collective-permute-start.4 = (bf16[16,10752]{1,0:T(8,128)(2,1)S(1)}, bf16[16,10752]{1,0:T(8,128)(2,1)S(1)}, u32[]{:S(2)}, u32[]{:S(2)}) collective-permute-start(bf16[16,10752]{1,0:T(8,128)(2,1)S(1)} %get-tuple-element.43), channel_id=1, source_target_pairs={{0,3},{1,2},{2,1},{3,0},{4,7},{5,6},{6,5},{7,4},{8,11},{9,10},{10,... | collective-permute-start | bytes 1032200 | tf_op jit(solution)/shard_map/ppermute | solution.py:311
  9.3 7.7 %collective-permute-start.2 = (bf16[16,4224]{1,0:T(8,128)(2,1)S(1)}, bf16[16,4224]{1,0:T(8,128)(2,1)S(1)}, u32[]{:S(2)}, u32[]{:S(2)}) collective-permute-start(bf16[16,4224]{1,0:T(8,128)(2,1)S(1)} %get-tuple-element.31.refs_13_), channel_id=1, source_target_pairs={{0,28},{4,8},{8,4},{12,16},{16,12},{20,24},{24,20},{28,0},{1,29},{... | collective-permute-start | bytes 405512 | tf_op jit(solution)/shard_map/ppermute | solution.py:35
  13.6 1.4 %collective-permute-start = (bf16[16,4096]{1,0:T(8,128)(2,1)S(1)}, bf16[16,4096]{1,0:T(8,128)(2,1)S(1)}, u32[]{:S(2)}, u32[]{:S(2)}) collective-permute-start(bf16[16,4096]{1,0:T(8,128)(2,1)S(1)} %get-tuple-element.32), channel_id=1, source_target_pairs={{0,4},{4,0},{8,12},{12,8},{16,20},{20,16},{24,28},{28,24},{1,5},{5... | collective-permute-start | bytes 393224 | tf_op jit(solution)/shard_map/ppermute | solution.py:36
  13.7 10.1 %collective-permute-start.5 = (bf16[16,10240]{1,0:T(8,128)(2,1)S(1)}, bf16[16,10240]{1,0:T(8,128)(2,1)S(1)}, u32[]{:S(2)}, u32[]{:S(2)}) collective-permute-start(bf16[16,10240]{1,0:T(8,128)(2,1)S(1)} %get-tuple-element.44), channel_id=1, source_target_pairs={{0,1},{1,0},{2,3},{3,2},{4,5},{5,4},{6,7},{7,6},{8,9},{9,8},{10,11... | collective-permute-start | bytes 983048 | tf_op jit(solution)/shard_map/ppermute | solution.py:311
  14.3 10.5 %collective-permute-start.6 = (bf16[16,10240]{1,0:T(8,128)(2,1)S(1)}, bf16[16,10240]{1,0:T(8,128)(2,1)S(1)}, u32[]{:S(2)}, u32[]{:S(2)}) collective-permute-start(bf16[16,10240]{1,0:T(8,128)(2,1)S(1)} %get-tuple-element.45), channel_id=1, source_target_pairs={{0,2},{1,3},{2,0},{3,1},{4,6},{5,7},{6,4},{7,5},{8,10},{9,11},{10,... | collective-permute-start | bytes 983048 | tf_op jit(solution)/shard_map/ppermute | solution.py:311
  16.9 13.1 %collective-permute-start.1 = (bf16[16,4224]{1,0:T(8,128)(2,1)S(1)}, bf16[16,4224]{1,0:T(8,128)(2,1)S(1)}, u32[]{:S(2)}, u32[]{:S(2)}) collective-permute-start(bf16[16,4224]{1,0:T(8,128)(2,1)S(1)} %get-tuple-element.35), channel_id=1, source_target_pairs={{0,28},{4,8},{8,4},{12,16},{16,12},{20,24},{24,20},{28,0},{1,29},{... | collective-permute-start | bytes 405512 | tf_op jit(solution)/shard_map/ppermute | solution.py:35
  18.4 11.7 %collective-permute-start.3 = (bf16[16,4096]{1,0:T(8,128)(2,1)S(1)}, bf16[16,4096]{1,0:T(8,128)(2,1)S(1)}, u32[]{:S(2)}, u32[]{:S(2)}) collective-permute-start(bf16[16,4096]{1,0:T(8,128)(2,1)S(1)} %get-tuple-element.41), channel_id=1, source_target_pairs={{0,4},{4,0},{8,12},{12,8},{16,20},{20,16},{24,28},{28,24},{1,5},{5... | collective-permute-start | bytes 393224 | tf_op jit(solution)/shard_map/ppermute | solution.py:36
  23.8 5.3 %collective-permute-start.7 = (bf16[16,2048]{1,0:T(8,128)(2,1)S(1)}, bf16[16,2048]{1,0:T(8,128)(2,1)S(1)}, u32[]{:S(2)}, u32[]{:S(2)}) collective-permute-start(bf16[16,2048]{1,0:T(8,128)(2,1)S(1)} %get-tuple-element.47), channel_id=1, source_target_pairs={{0,3},{1,2},{2,1},{3,0},{4,7},{5,6},{6,5},{7,4},{8,11},{9,10},{10,... | collective-permute-start | bytes 196616 | tf_op jit(solution)/shard_map/ppermute | solution.py:311
  24.8 4.3 %collective-permute-start.8 = (bf16[16,2048]{1,0:T(8,128)(2,1)S(1)}, bf16[16,2048]{1,0:T(8,128)(2,1)S(1)}, u32[]{:S(2)}, u32[]{:S(2)}) collective-permute-start(bf16[16,2048]{1,0:T(8,128)(2,1)S(1)} %get-tuple-element.48), channel_id=1, source_target_pairs={{0,1},{1,0},{2,3},{3,2},{4,5},{5,4},{6,7},{7,6},{8,9},{9,8},{10,11... | collective-permute-start | bytes 196616 | tf_op jit(solution)/shard_map/ppermute | solution.py:311
  25.8 4.3 %collective-permute-start.9 = (bf16[16,2048]{1,0:T(8,128)(2,1)S(1)}, bf16[16,2048]{1,0:T(8,128)(2,1)S(1)}, u32[]{:S(2)}, u32[]{:S(2)}) collective-permute-start(bf16[16,2048]{1,0:T(8,128)(2,1)S(1)} %get-tuple-element.49), channel_id=1, source_target_pairs={{0,2},{1,3},{2,0},{3,1},{4,6},{5,7},{6,4},{7,5},{8,10},{9,11},{10,... | collective-permute-start | bytes 196616 | tf_op jit(solution)/shard_map/ppermute | solution.py:311

commit v13 on v12

--- a/solution.py
+++ b/solution.py
@@ -15,7 +15,7 @@
 C_FAR = LIGHT
 C_NEAR = LIGHT
 C_NEAR_PHASE = LIGHT
-C_FAR_PHASE = 147 * 10 ** 7
+C_FAR_PHASE = 200 * 10 ** 7
 
 
 def partner(me, step, count):
@@ -92,7 +92,6 @@
 def first_rows(count, per, up_idx, down_idx, order, w_up, w_down, g_ref, a_ref, back, second, second_tan, second_grad,
                keep, pushes, *refs):
     sends, (pulled, hidden) = refs[:count], refs[count:]
-    clear_pad(sends[-1], 10 * per)
     blocks = count * per
     me = lax.axis_index("dp")
     for b in range(blocks):
@@ -311,7 +310,7 @@
         return [parts[0]] + [lax.ppermute(parts[step], "dp", swap_route(step, count)) for step in steps]
 
     rows = (score_grad_in, state_adjoint_in, saved_back, saved_second, saved_second_tan, saved_second_grad)
-    ten = [shape((16, 10 * part), BF16)] * (count - 1) + [shape((16, 10 * part + 4 * PAD), BF16)]
+    ten = [shape((16, 10 * part), BF16)] * (count - 1) + [shape((16, 10 * part), BF16)]
     (token,) = call(open_launch, (), [], [shape((8, BLOCK), F32)], [], cost=WORK)
     tables = (up_index, down_index, tick_order, w_up, w_down)
     keep, pushes, *early = call(
@@ -341,7 +340,7 @@
         cost=C_NEAR_PHASE)
     near_out, *late = call(
         body(far_phase, count, per), tables + (far, keep, near_keep, *late), [smem] * 2 + [vmem] * (5 + count),
-        [pair] + two, scratch, cost=C_FAR_PHASE)
+        [pair] + two, scratch, cost=C_FAR_PHASE, after=(early[1],))
     near, far = swap_sections(near_out, far_out)
     late = to_replicas(late)
     (grads,) = call(

time: 31.4 us -> 31.1 us (level)
  starting transfers between devices: 12.3 us -> 11.9 us
    ppermute x6, starting transfers between devices: 8.56 us -> 8.06 us  [to_replicas(): lax.ppermute(parts[step], 'dp', swap_route(step, count))]
  transfers between devices with their start and end apart: 10 -> 10, of which waited for: 4 -> 5; matrix products, arithmetic and copies ran while one was open for 0% -> 0% of each run, Pallas kernels for 20% -> 20%
where the time goes in v13:
time: 31.1 us; the launch traced here: 30.9 us
  starting transfers between devices  11.9 us (38%)
  Pallas kernels  9.06 us (29%)
  waiting for transfers between devices  7.51 us (24%)
  local copies, waits for them, and re-layouts  1.66 us (5%)
  between operations  0.8 us (3%)
    pallas_call x8, Pallas kernels, call(): pl.pallas_call(kernel, out_shape=outs, in_specs=[pl.BlockSpec(memory_spac...  9.06 us
    ppermute x6, starting transfers between devices, to_replicas(): lax.ppermute(parts[step], 'dp', swap_route(step, count))  8.06 us
    ppermute x6, waiting for transfers between devices, to_replicas(): lax.ppermute(parts[step], 'dp', swap_route(step, count))  7.28 us
    ppermute x2, starting transfers between devices, swap_sections(): lax.ppermute(far, 'section', [(i, (i + 2 * (i % 2) - 1) % count) for i in...  3.03 us
    unnamed x28, local copies, waits for them, and re-layouts  1.66 us
    ppermute x2, starting transfers between devices, swap_sections(): near = lax.ppermute(near, 'section', [(i, i ^ 1) for i in range(count)])  0.79 us
  transfers between devices with their start and end apart: 10, of which 5 were waited for; matrix products, arithmetic and copies ran while one was open for 0% of the time, Pallas kernels for 20%

profile of v13, /device:TPU:0, one launch (start us, length us, event | category | flops | bytes accessed | tf_op | source)
XLA Modules:
  0.0 30.9 jit_solution(14965500666226989623)
XLA Ops:
  0.8 0.5 %copy-done.8 = s32[1,32]{1,0:T(1,128)S(1)} copy-done((s32[1,32]{1,0:T(1,128)S(1)}, s32[1,32]{1,0:T(1,128)}, u32[]{:S(2)}) %copy-start.8) | copy-done | bytes 152
  1.3 0.6 %copy-done.1 = bf16[1,32,128,128]{3,2,1,0:T(8,128)(2,1)S(1)} copy-done((bf16[1,32,128,128]{3,2,1,0:T(8,128)(2,1)S(1)}, bf16[1,32,128,128]{3,2,1,0:T(8,128)(2,1)}, u32[]{:S(2)}) %copy-start.1) | copy-done | bytes 1048600
  1.9 0.3 %copy-done = bf16[1,32,128,128]{3,2,1,0:T(8,128)(2,1)S(1)} copy-done((bf16[1,32,128,128]{3,2,1,0:T(8,128)(2,1)S(1)}, bf16[1,32,128,128]{3,2,1,0:T(8,128)(2,1)}, u32[]{:S(2)}) %copy-start) | copy-done | bytes 1048600
  2.4 1.7 %shard_map.182 = (f32[32,24,128]{2,1,0:T(8,128)S(1)}, bf16[16,4096]{1,0:T(8,128)(2,1)S(1)}, bf16[16,10240]{1,0:T(8,128)(2,1)S(1)}, bf16[16,10240]{1,0:T(8,128)(2...) custom-call(s32[1,32]{1,0:T(1,128)S(1)} %copy-done.7, s32[1,32]{1,0:T(1,128)S(1)} %copy-done.8, ...), custom_call_target="tpu_custom_call" | custom-call | flops 10000000000 | bytes 100000000 | tf_op jit(solution)/shard_map/pallas_call | solution.py:280
  4.1 4.0 %collective-permute-start.3 = (bf16[16,10240]{1,0:T(8,128)(2,1)S(1)}, bf16[16,10240]{1,0:T(8,128)(2,1)S(1)}, u32[]{:S(2)}, u32[]{:S(2)}) collective-permute-start(bf16[16,10240]{1,0:T(8,128)(2,1)S(1)} %get-tuple-element.41), channel_id=1, source_target_pairs={{0,3},{1,2},{2,1},{3,0},{4,7},{5,6},{6,5},{7,4},{8,11},{9,10},{10,... | collective-permute-start | bytes 983048 | tf_op jit(solution)/shard_map/ppermute | solution.py:310
  8.1 1.2 %shard_map.183 = (bf16[16,4224]{1,0:T(8,128)(2,1)S(1)}, f32[32,8,128]{2,1,0:T(8,128)S(1)}) custom-call(s32[1,32]{1,0:T(1,128)S(1)} %copy-done.7, s32[1,32]{1,0:T(1,128)S(1)} %copy-done.8, s32[1,2]{1,0:T(1,128)S(1)} %copy-done.9, bf16[1,32,128,128]{3,2,1,0:T(8,128)(2,1)S(1)} %copy-done, bf16[1,32,128,128]{3,2,1,0:T(8,128)(2,1)S(1)} %copy-done.1, ...), custom_call_target="tpu_custom_call" | custom-call | flops 10000 | bytes 100 | tf_op jit(solution)/shard_map/pallas_call | solution.py:280
  9.3 2.9 %collective-permute-start.2 = (bf16[16,4224]{1,0:T(8,128)(2,1)S(1)}, bf16[16,4224]{1,0:T(8,128)(2,1)S(1)}, u32[]{:S(2)}, u32[]{:S(2)}) collective-permute-start(bf16[16,4224]{1,0:T(8,128)(2,1)S(1)} %get-tuple-element.31.refs_13_), channel_id=1, source_target_pairs={{0,28},{4,8},{8,4},{12,16},{16,12},{20,24},{24,20},{28,0},{1,29},{... | collective-permute-start | bytes 405512 | tf_op jit(solution)/shard_map/ppermute | solution.py:35
  12.2 1.4 %shard_map.184 = (bf16[16,4096]{1,0:T(8,128)(2,1)S(1)}, f32[32,8,128]{2,1,0:T(8,128)S(1)}, bf16[16,10240]{1,0:T(8,128)(2,1)S(1)}, bf16[16,10240]{1,0:T(8,128)(2,1)S(1)}) custom-call(s32[1,32]{1,0:T(1,128)S(1)} %copy-done.7, s32[1,32]{1,0:T(1,128)S(1)} %copy-done.8, s32[1,2]{1,0:T(1,128)S(1)} %copy-done.9, bf16[1,32,128,128]{3,2,1,0:T(8,128)(2,1)S(1)} %copy-done, ...), custom_call_target="tpu_custom_call" | custom-call | flops 10000 | bytes 100 | tf_op jit(solution)/shard_map/pallas_call | solution.py:280
  13.6 0.1 collective-permute-start
  13.7 0.6 %collective-permute-start.5 = (bf16[16,10240]{1,0:T(8,128)(2,1)S(1)}, bf16[16,10240]{1,0:T(8,128)(2,1)S(1)}, u32[]{:S(2)}, u32[]{:S(2)}) collective-permute-start(bf16[16,10240]{1,0:T(8,128)(2,1)S(1)} %get-tuple-element.44), channel_id=1, source_target_pairs={{0,1},{1,0},{2,3},{3,2},{4,5},{5,4},{6,7},{7,6},{8,9},{9,8},{10,11... | collective-permute-start | bytes 983048 | tf_op jit(solution)/shard_map/ppermute | solution.py:310
  14.3 0.5 %collective-permute-start.6 = (bf16[16,10240]{1,0:T(8,128)(2,1)S(1)}, bf16[16,10240]{1,0:T(8,128)(2,1)S(1)}, u32[]{:S(2)}, u32[]{:S(2)}) collective-permute-start(bf16[16,10240]{1,0:T(8,128)(2,1)S(1)} %get-tuple-element.45), channel_id=1, source_target_pairs={{0,2},{1,3},{2,0},{3,1},{4,6},{5,7},{6,4},{7,5},{8,10},{9,11},{10,... | collective-permute-start | bytes 983048 | tf_op jit(solution)/shard_map/ppermute | solution.py:310
  14.8 0.2 collective-permute-done.refs_4_
  15.0 1.9 %shard_map.185 = (bf16[16,4224]{1,0:T(8,128)(2,1)S(1)}, bf16[16,2048]{1,0:T(8,128)(2,1)S(1)}, bf16[16,2048]{1,0:T(8,128)(2,1)S(1)}, bf16[16,2048]{1,0:T(8,128)(2,1)S(1)}, bf16[16,2048]{1,0:T(8,128)(2,1)S(1)}) custom-call(s32[1,32]{1,0:T(1,128)S(1)} %copy-done.7, s32[1,32]{1,0:T(1,128)S(1)} %copy-done.8, bf16[1,32,128,128]{3,2,1,0:T(8,128)(2,1)S(1)} %copy-done, ...), custom_call_target="tpu_custom_call" | custom-call | flops 10000 | bytes 100 | tf_op jit(solution)/shard_map/pallas_call | solution.py:280
  16.9 0.1 collective-permute-start.1
  17.0 1.4 %shard_map.186 = (bf16[16,4096]{1,0:T(8,128)(2,1)S(1)}, bf16[16,2048]{1,0:T(8,128)(2,1)S(1)}, bf16[16,2048]{1,0:T(8,128)(2,1)S(1)}, bf16[16,2048]{1,0:T(8,128)(2,1)S(1)}, bf16[16,2048]{1,0:T(8,128)(2,1)S(1)}) custom-call(s32[1,32]{1,0:T(1,128)S(1)} %copy-done.7, s32[1,32]{1,0:T(1,128)S(1)} %copy-done.8, bf16[1,32,128,128]{3,2,1,0:T(8,128)(2,1)S(1)} %copy-done, ...), custom_call_target="tpu_custom_call" | custom-call | flops 2000000000 | bytes 20000000 | tf_op jit(solution)/shard_map/pallas_call | solution.py:280
  18.4 0.7 %collective-permute-start.4 = (bf16[16,4096]{1,0:T(8,128)(2,1)S(1)}, bf16[16,4096]{1,0:T(8,128)(2,1)S(1)}, u32[]{:S(2)}, u32[]{:S(2)}) collective-permute-start(bf16[16,4096]{1,0:T(8,128)(2,1)S(1)} %get-tuple-element.42), channel_id=1, source_target_pairs={{0,4},{4,0},{8,12},{12,8},{16,20},{20,16},{24,28},{28,24},{1,5},{5... | collective-permute-start | bytes 393224 | tf_op jit(solution)/shard_map/ppermute | solution.py:36
  19.1 2.5 %collective-permute-start.7 = (bf16[16,2048]{1,0:T(8,128)(2,1)S(1)}, bf16[16,2048]{1,0:T(8,128)(2,1)S(1)}, u32[]{:S(2)}, u32[]{:S(2)}) collective-permute-start(bf16[16,2048]{1,0:T(8,128)(2,1)S(1)} %get-tuple-element.47), channel_id=1, source_target_pairs={{0,3},{1,2},{2,1},{3,0},{4,7},{5,6},{6,5},{7,4},{8,11},{9,10},{10,... | collective-permute-start | bytes 196616 | tf_op jit(solution)/shard_map/ppermute | solution.py:310
  21.6 2.7 %collective-permute-done.5.refs_2_.refs_5_ = bf16[16,10240]{1,0:T(8,128)(2,1)S(1)} collective-permute-done((bf16[16,10240]{1,0:T(8,128)(2,1)S(1)}, bf16[16,10240]{1,0:T(8,128)(2,1)S(1)}, u32[]{:S(2)}, u32[]{:S(2)}) %collective-permute-start.5) | collective-permute-done | bytes 327712 | tf_op jit(solution)/shard_map/ppermute | solution.py:310
  24.3 0.5 %collective-permute-start.8 = (bf16[16,2048]{1,0:T(8,128)(2,1)S(1)}, bf16[16,2048]{1,0:T(8,128)(2,1)S(1)}, u32[]{:S(2)}, u32[]{:S(2)}) collective-permute-start(bf16[16,2048]{1,0:T(8,128)(2,1)S(1)} %get-tuple-element.48), channel_id=1, source_target_pairs={{0,1},{1,0},{2,3},{3,2},{4,5},{5,4},{6,7},{7,6},{8,9},{9,8},{10,11... | collective-permute-start | bytes 196616 | tf_op jit(solution)/shard_map/ppermute | solution.py:310
  24.8 0.7 %collective-permute-done.6.refs_3_.refs_6_ = bf16[16,10240]{1,0:T(8,128)(2,1)S(1)} collective-permute-done((bf16[16,10240]{1,0:T(8,128)(2,1)S(1)}, bf16[16,10240]{1,0:T(8,128)(2,1)S(1)}, u32[]{:S(2)}, u32[]{:S(2)}) %collective-permute-start.6) | collective-permute-done | bytes 327712 | tf_op jit(solution)/shard_map/ppermute | solution.py:310
  25.5 0.3 %shard_map.187.refs_2_ = f32[2,8,128,128]{3,2,1,0:T(8,128)S(1)} custom-call(bf16[16,10240]{1,0:T(8,128)(2,1)S(1)} %get-tuple-element.43.refs_0_.refs_3_, bf16[16,10240]{1,0:T(8,128)(2,1)S(1)} %collective-permute-done.3.refs_11_.refs_1_.refs_4_, bf16[16,10240]{1,0:T(8,128)(2,1)S(1)} %collective-permute-done.5.refs_2_.refs_5_, ...), custom_call_target="tpu_custom_call" | custom-call | flops 10000 | bytes 100 | tf_op jit(solution)/shard_map/pallas_call | solution.py:280
  25.8 2.7 %collective-permute-done.8.refs_9_ = bf16[16,2048]{1,0:T(8,128)(2,1)S(1)} collective-permute-done((bf16[16,2048]{1,0:T(8,128)(2,1)S(1)}, bf16[16,2048]{1,0:T(8,128)(2,1)S(1)}, u32[]{:S(2)}, u32[]{:S(2)}) %collective-permute-start.8) | collective-permute-done | bytes 65568 | tf_op jit(solution)/shard_map/ppermute | solution.py:310
  28.5 1.2 %collective-permute-done.9.refs_10_ = bf16[16,2048]{1,0:T(8,128)(2,1)S(1)} collective-permute-done((bf16[16,2048]{1,0:T(8,128)(2,1)S(1)}, bf16[16,2048]{1,0:T(8,128)(2,1)S(1)}, u32[]{:S(2)}, u32[]{:S(2)}) %collective-permute-start.9) | collective-permute-done | bytes 65568 | tf_op jit(solution)/shard_map/ppermute | solution.py:310
  29.7 1.2 %shard_map.188 = (bf16[1,8,4096]{2,1,0:T(8,128)(2,1)}, bf16[1,8,4096]{2,1,0:T(8,128)(2,1)}, bf16[1,8,4096]{2,1,0:T(8,128)(2,1)}, bf16[1,8,4096]{2,1,0:T(8,128)(2...) custom-call(bf16[16,4224]{1,0:T(8,128)(2,1)S(1)} %collective-permute-done.1.refs_0_, ...), custom_call_target="tpu_custom_call" | custom-call | flops 10000 | bytes 100 | tf_op jit(solution)/shard_map/pallas_call | solution.py:280
  (32 shorter events, 0.2 us)
Async XLA Ops:
  0.6 0.7 %copy-start.8 = (s32[1,32]{1,0:T(1,128)S(1)}, s32[1,32]{1,0:T(1,128)}, u32[]{:S(2)}) copy-start(s32[1,32]{1,0:T(1,128)} %refs_1_.9) | copy-start | bytes 388
  0.6 1.2 %copy-start.1 = (bf16[1,32,128,128]{3,2,1,0:T(8,128)(2,1)S(1)}, bf16[1,32,128,128]{3,2,1,0:T(8,128)(2,1)}, u32[]{:S(2)}) copy-start(bf16[1,32,128,128]{3,2,1,0:T(8,128)(2,1)} %refs_3_.9) | copy-start | bytes 3145732
  0.7 1.2 %copy-start.7 = (s32[1,32]{1,0:T(1,128)S(1)}, s32[1,32]{1,0:T(1,128)}, u32[]{:S(2)}) copy-start(s32[1,32]{1,0:T(1,128)} %refs_0_.9) | copy-start | bytes 388
  0.7 1.5 %copy-start = (bf16[1,32,128,128]{3,2,1,0:T(8,128)(2,1)S(1)}, bf16[1,32,128,128]{3,2,1,0:T(8,128)(2,1)}, u32[]{:S(2)}) copy-start(bf16[1,32,128,128]{3,2,1,0:T(8,128)(2,1)} %refs_2_.9) | copy-start | bytes 3145732
  0.7 1.5 %copy-start.4 = (bf16[1,8,4096]{2,1,0:T(8,128)(2,1)S(1)}, bf16[1,8,4096]{2,1,0:T(8,128)(2,1)}, u32[]{:S(2)}) copy-start(bf16[1,8,4096]{2,1,0:T(8,128)(2,1)} %refs_6_.5) | copy-start | bytes 196612
  0.7 1.5 %copy-start.3 = (bf16[1,8,4096]{2,1,0:T(8,128)(2,1)S(1)}, bf16[1,8,4096]{2,1,0:T(8,128)(2,1)}, u32[]{:S(2)}) copy-start(bf16[1,8,4096]{2,1,0:T(8,128)(2,1)} %refs_5_.5) | copy-start | bytes 196612
  0.7 1.5 %copy-start.9 = (s32[1,2]{1,0:T(1,128)S(1)}, s32[1,2]{1,0:T(1,128)}, u32[]{:S(2)}) copy-start(s32[1,2]{1,0:T(1,128)} %refs_2_.7) | copy-start | bytes 28
  0.7 1.6 %copy-start.13 = (bf16[1,2,8,4096]{3,2,1,0:T(8,128)(2,1)S(1)}, bf16[1,2,8,4096]{3,2,1,0:T(8,128)(2,1)}, u32[]{:S(2)}) copy-start(bf16[1,2,8,4096]{3,2,1,0:T(8,128)(2,1)} %refs_10_.3) | copy-start | bytes 393220
  0.7 1.6 %copy-start.12 = (bf16[1,2,8,4096]{3,2,1,0:T(8,128)(2,1)S(1)}, bf16[1,2,8,4096]{3,2,1,0:T(8,128)(2,1)}, u32[]{:S(2)}) copy-start(bf16[1,2,8,4096]{3,2,1,0:T(8,128)(2,1)} %refs_9_.3) | copy-start | bytes 393220
  0.7 1.6 %copy-start.11 = (bf16[1,2,8,4096]{3,2,1,0:T(8,128)(2,1)S(1)}, bf16[1,2,8,4096]{3,2,1,0:T(8,128)(2,1)}, u32[]{:S(2)}) copy-start(bf16[1,2,8,4096]{3,2,1,0:T(8,128)(2,1)} %refs_8_.3) | copy-start | bytes 393220
  0.7 1.6 %copy-start.10 = (bf16[1,2,8,4096]{3,2,1,0:T(8,128)(2,1)S(1)}, bf16[1,2,8,4096]{3,2,1,0:T(8,128)(2,1)}, u32[]{:S(2)}) copy-start(bf16[1,2,8,4096]{3,2,1,0:T(8,128)(2,1)} %refs_7_.1) | copy-start | bytes 393220
  2.4 5.7 %copy-start.2 = (bf16[1,2,8,4096]{3,2,1,0:T(8,128)(2,1)S(1)}, bf16[1,2,8,4096]{3,2,1,0:T(8,128)(2,1)}, u32[]{:S(2)}) copy-start(bf16[1,2,8,4096]{3,2,1,0:T(8,128)(2,1)} %refs_10_.5) | copy-start | bytes 393220
  2.4 5.7 %copy-start.5 = (bf16[1,8,4096]{2,1,0:T(8,128)(2,1)S(1)}, bf16[1,8,4096]{2,1,0:T(8,128)(2,1)}, u32[]{:S(2)}) copy-start(bf16[1,8,4096]{2,1,0:T(8,128)(2,1)} %refs_8_.5) | copy-start | bytes 196612
  2.4 5.7 %copy-start.6 = (bf16[1,8,4096]{2,1,0:T(8,128)(2,1)S(1)}, bf16[1,8,4096]{2,1,0:T(8,128)(2,1)}, u32[]{:S(2)}) copy-start(bf16[1,8,4096]{2,1,0:T(8,128)(2,1)} %refs_9_.5) | copy-start | bytes 196612
  4.1 12.9 %collective-permute-start.3 = (bf16[16,10240]{1,0:T(8,128)(2,1)S(1)}, bf16[16,10240]{1,0:T(8,128)(2,1)S(1)}, u32[]{:S(2)}, u32[]{:S(2)}) collective-permute-start(bf16[16,10240]{1,0:T(8,128)(2,1)S(1)} %get-tuple-element.41), channel_id=1, source_target_pairs={{0,3},{1,2},{2,1},{3,0},{4,7},{5,6},{6,5},{7,4},{8,11},{9,10},{10,... | collective-permute-start | bytes 983048 | tf_op jit(solution)/shard_map/ppermute | solution.py:310
  9.3 7.7 %collective-permute-start.2 = (bf16[16,4224]{1,0:T(8,128)(2,1)S(1)}, bf16[16,4224]{1,0:T(8,128)(2,1)S(1)}, u32[]{:S(2)}, u32[]{:S(2)}) collective-permute-start(bf16[16,4224]{1,0:T(8,128)(2,1)S(1)} %get-tuple-element.31.refs_13_), channel_id=1, source_target_pairs={{0,28},{4,8},{8,4},{12,16},{16,12},{20,24},{24,20},{28,0},{1,29},{... | collective-permute-start | bytes 405512 | tf_op jit(solution)/shard_map/ppermute | solution.py:35
  13.6 1.4 %collective-permute-start = (bf16[16,4096]{1,0:T(8,128)(2,1)S(1)}, bf16[16,4096]{1,0:T(8,128)(2,1)S(1)}, u32[]{:S(2)}, u32[]{:S(2)}) collective-permute-start(bf16[16,4096]{1,0:T(8,128)(2,1)S(1)} %get-tuple-element.32), channel_id=1, source_target_pairs={{0,4},{4,0},{8,12},{12,8},{16,20},{20,16},{24,28},{28,24},{1,5},{5... | collective-permute-start | bytes 393224 | tf_op jit(solution)/shard_map/ppermute | solution.py:36
  13.7 10.6 %collective-permute-start.5 = (bf16[16,10240]{1,0:T(8,128)(2,1)S(1)}, bf16[16,10240]{1,0:T(8,128)(2,1)S(1)}, u32[]{:S(2)}, u32[]{:S(2)}) collective-permute-start(bf16[16,10240]{1,0:T(8,128)(2,1)S(1)} %get-tuple-element.44), channel_id=1, source_target_pairs={{0,1},{1,0},{2,3},{3,2},{4,5},{5,4},{6,7},{7,6},{8,9},{9,8},{10,11... | collective-permute-start | bytes 983048 | tf_op jit(solution)/shard_map/ppermute | solution.py:310
  14.3 11.2 %collective-permute-start.6 = (bf16[16,10240]{1,0:T(8,128)(2,1)S(1)}, bf16[16,10240]{1,0:T(8,128)(2,1)S(1)}, u32[]{:S(2)}, u32[]{:S(2)}) collective-permute-start(bf16[16,10240]{1,0:T(8,128)(2,1)S(1)} %get-tuple-element.45), channel_id=1, source_target_pairs={{0,2},{1,3},{2,0},{3,1},{4,6},{5,7},{6,4},{7,5},{8,10},{9,11},{10,... | collective-permute-start | bytes 983048 | tf_op jit(solution)/shard_map/ppermute | solution.py:310
  16.9 8.9 %collective-permute-start.1 = (bf16[16,4224]{1,0:T(8,128)(2,1)S(1)}, bf16[16,4224]{1,0:T(8,128)(2,1)S(1)}, u32[]{:S(2)}, u32[]{:S(2)}) collective-permute-start(bf16[16,4224]{1,0:T(8,128)(2,1)S(1)} %get-tuple-element.35), channel_id=1, source_target_pairs={{0,28},{4,8},{8,4},{12,16},{16,12},{20,24},{24,20},{28,0},{1,29},{... | collective-permute-start | bytes 405512 | tf_op jit(solution)/shard_map/ppermute | solution.py:35
  18.4 11.4 %collective-permute-start.4 = (bf16[16,4096]{1,0:T(8,128)(2,1)S(1)}, bf16[16,4096]{1,0:T(8,128)(2,1)S(1)}, u32[]{:S(2)}, u32[]{:S(2)}) collective-permute-start(bf16[16,4096]{1,0:T(8,128)(2,1)S(1)} %get-tuple-element.42), channel_id=1, source_target_pairs={{0,4},{4,0},{8,12},{12,8},{16,20},{20,16},{24,28},{28,24},{1,5},{5... | collective-permute-start | bytes 393224 | tf_op jit(solution)/shard_map/ppermute | solution.py:36
  19.1 6.7 %collective-permute-start.7 = (bf16[16,2048]{1,0:T(8,128)(2,1)S(1)}, bf16[16,2048]{1,0:T(8,128)(2,1)S(1)}, u32[]{:S(2)}, u32[]{:S(2)}) collective-permute-start(bf16[16,2048]{1,0:T(8,128)(2,1)S(1)} %get-tuple-element.47), channel_id=1, source_target_pairs={{0,3},{1,2},{2,1},{3,0},{4,7},{5,6},{6,5},{7,4},{8,11},{9,10},{10,... | collective-permute-start | bytes 196616 | tf_op jit(solution)/shard_map/ppermute | solution.py:310
  24.3 4.3 %collective-permute-start.8 = (bf16[16,2048]{1,0:T(8,128)(2,1)S(1)}, bf16[16,2048]{1,0:T(8,128)(2,1)S(1)}, u32[]{:S(2)}, u32[]{:S(2)}) collective-permute-start(bf16[16,2048]{1,0:T(8,128)(2,1)S(1)} %get-tuple-element.48), channel_id=1, source_target_pairs={{0,1},{1,0},{2,3},{3,2},{4,5},{5,4},{6,7},{7,6},{8,9},{9,8},{10,11... | collective-permute-start | bytes 196616 | tf_op jit(solution)/shard_map/ppermute | solution.py:310
  25.5 4.3 %collective-permute-start.9 = (bf16[16,2048]{1,0:T(8,128)(2,1)S(1)}, bf16[16,2048]{1,0:T(8,128)(2,1)S(1)}, u32[]{:S(2)}, u32[]{:S(2)}) collective-permute-start(bf16[16,2048]{1,0:T(8,128)(2,1)S(1)} %get-tuple-element.49), channel_id=1, source_target_pairs={{0,2},{1,3},{2,0},{3,1},{4,6},{5,7},{6,4},{7,5},{8,10},{9,11},{10,... | collective-permute-start | bytes 196616 | tf_op jit(solution)/shard_map/ppermute | solution.py:310

commit v14 on v13

--- a/solution.py
+++ b/solution.py
@@ -15,7 +15,7 @@
 C_FAR = LIGHT
 C_NEAR = LIGHT
 C_NEAR_PHASE = LIGHT
-C_FAR_PHASE = 200 * 10 ** 7
+C_FAR_PHASE = 144 * 10 ** 7
 
 
 def partner(me, step, count):
@@ -92,6 +92,7 @@
 def first_rows(count, per, up_idx, down_idx, order, w_up, w_down, g_ref, a_ref, back, second, second_tan, second_grad,
                keep, pushes, *refs):
     sends, (pulled, hidden) = refs[:count], refs[count:]
+    clear_pad(sends[1], 10 * per)
     blocks = count * per
     me = lax.axis_index("dp")
     for b in range(blocks):
@@ -310,7 +311,7 @@
         return [parts[0]] + [lax.ppermute(parts[step], "dp", swap_route(step, count)) for step in steps]
 
     rows = (score_grad_in, state_adjoint_in, saved_back, saved_second, saved_second_tan, saved_second_grad)
-    ten = [shape((16, 10 * part), BF16)] * (count - 1) + [shape((16, 10 * part), BF16)]
+    ten = [shape((16, 10 * part + (4 * PAD if step == 1 else 0)), BF16) for step in range(count)]
     (token,) = call(open_launch, (), [], [shape((8, BLOCK), F32)], [], cost=WORK)
     tables = (up_index, down_index, tick_order, w_up, w_down)
     keep, pushes, *early = call(
@@ -324,12 +325,12 @@
     scratch = [vmem((blocks, 16, BLOCK), F32), vmem((blocks, 16, BLOCK), BF16)]
     far, far_keep = call(
         body(first_streams, blocks, 0, 0), taken, [smem] * 3 + [vmem] * 8, [long] + made, scratch, cost=C_FAR)
-    neighbours = early[1:count - 1]
+    neighbours = early[2:count - 1]
     near, near_keep, *neighbours = call(
         body(first_streams, blocks, 1, len(neighbours)), taken + tuple(neighbours),
-        [smem] * 3 + [vmem] * (8 + len(neighbours)), [pair] + made + ten[:len(neighbours)], scratch, after=(far,),
+        [smem] * 3 + [vmem] * (8 + len(neighbours)), [pair] + made + [ten[0]] * len(neighbours), scratch, after=(far,),
         cost=C_NEAR)
-    early = [early[0], *neighbours, early[count - 1]]
+    early = [*early[:2], *neighbours, early[count - 1]]
     near, far = swap_sections(near, far)
     early = to_replicas(early)
     tables = (up_index, down_index, w_up, w_down)

time: 31.1 us -> 32.6 us (1.048)
  starting transfers between devices: 11.9 us -> 13.3 us
    ppermute x6, starting transfers between devices: 8.06 us -> 9.58 us  [to_replicas(): lax.ppermute(parts[step], 'dp', swap_route(step, count))]
    ppermute x2, waiting for transfers between devices: 0.23 us -> 0.77 us  [swap_sections(): near = lax.ppermute(near, 'section', [(i, i ^ 1) for i in range(count)])]
    ppermute x6, waiting for transfers between devices: 7.28 us -> 6.82 us  [to_replicas(): lax.ppermute(parts[step], 'dp', swap_route(step, count))]
  transfers between devices with their start and end apart: 10 -> 10, of which waited for: 5 -> 4; matrix products, arithmetic and copies ran while one was open for 0% -> 0% of each run, Pallas kernels for 20% -> 19%
where the time goes in v14:
time: 32.6 us; the launch traced here: 32.4 us
  starting transfers between devices  13.3 us (41%)
  Pallas kernels  9.05 us (28%)
  waiting for transfers between devices  7.59 us (23%)
  local copies, waits for them, and re-layouts  1.66 us (5%)
  between operations  0.8 us (2%)
    ppermute x6, starting transfers between devices, to_replicas(): lax.ppermute(parts[step], 'dp', swap_route(step, count))  9.58 us
    pallas_call x8, Pallas kernels, call(): pl.pallas_call(kernel, out_shape=outs, in_specs=[pl.BlockSpec(memory_spac...  9.05 us
    ppermute x6, waiting for transfers between devices, to_replicas(): lax.ppermute(parts[step], 'dp', swap_route(step, count))  6.82 us
    ppermute x2, starting transfers between devices, swap_sections(): lax.ppermute(far, 'section', [(i, (i + 2 * (i % 2) - 1) % count) for i in...  3.02 us
    unnamed x28, local copies, waits for them, and re-layouts  1.66 us
    ppermute x2, waiting for transfers between devices, swap_sections(): near = lax.ppermute(near, 'section', [(i, i ^ 1) for i in range(count)])  0.77 us
    ppermute x2, starting transfers between devices, swap_sections(): near = lax.ppermute(near, 'section', [(i, i ^ 1) for i in range(count)])  0.73 us
  transfers between devices with their start and end apart: 10, of which 4 were waited for; matrix products, arithmetic and copies ran while one was open for 0% of the time, Pallas kernels for 19%

profile of v14, /device:TPU:0, one launch (start us, length us, event | category | flops | bytes accessed | tf_op | source)
XLA Modules:
  0.0 32.4 jit_solution(10523376730141594855)
XLA Ops:
  0.8 0.5 %copy-done.8 = s32[1,32]{1,0:T(1,128)S(1)} copy-done((s32[1,32]{1,0:T(1,128)S(1)}, s32[1,32]{1,0:T(1,128)}, u32[]{:S(2)}) %copy-start.8) | copy-done | bytes 152
  1.3 0.6 %copy-done.1 = bf16[1,32,128,128]{3,2,1,0:T(8,128)(2,1)S(1)} copy-done((bf16[1,32,128,128]{3,2,1,0:T(8,128)(2,1)S(1)}, bf16[1,32,128,128]{3,2,1,0:T(8,128)(2,1)}, u32[]{:S(2)}) %copy-start.1) | copy-done | bytes 1048600
  1.9 0.3 %copy-done = bf16[1,32,128,128]{3,2,1,0:T(8,128)(2,1)S(1)} copy-done((bf16[1,32,128,128]{3,2,1,0:T(8,128)(2,1)S(1)}, bf16[1,32,128,128]{3,2,1,0:T(8,128)(2,1)}, u32[]{:S(2)}) %copy-start) | copy-done | bytes 1048600
  2.4 1.7 %shard_map.182 = (f32[32,24,128]{2,1,0:T(8,128)S(1)}, bf16[16,4096]{1,0:T(8,128)(2,1)S(1)}, bf16[16,10240]{1,0:T(8,128)(2,1)S(1)}, bf16[16,10752]{1,0:T(8,128)(2...) custom-call(s32[1,32]{1,0:T(1,128)S(1)} %copy-done.7, s32[1,32]{1,0:T(1,128)S(1)} %copy-done.8, ...), custom_call_target="tpu_custom_call" | custom-call | flops 10000000000 | bytes 100000000 | tf_op jit(solution)/shard_map/pallas_call | solution.py:281
  4.1 4.0 %collective-permute-start.3 = (bf16[16,10240]{1,0:T(8,128)(2,1)S(1)}, bf16[16,10240]{1,0:T(8,128)(2,1)S(1)}, u32[]{:S(2)}, u32[]{:S(2)}) collective-permute-start(bf16[16,10240]{1,0:T(8,128)(2,1)S(1)} %get-tuple-element.39), channel_id=1, source_target_pairs={{0,3},{1,2},{2,1},{3,0},{4,7},{5,6},{6,5},{7,4},{8,11},{9,10},{10,... | collective-permute-start | bytes 983048 | tf_op jit(solution)/shard_map/ppermute | solution.py:311
  8.1 0.5 %collective-permute-start.5 = (bf16[16,10752]{1,0:T(8,128)(2,1)S(1)}, bf16[16,10752]{1,0:T(8,128)(2,1)S(1)}, u32[]{:S(2)}, u32[]{:S(2)}) collective-permute-start(bf16[16,10752]{1,0:T(8,128)(2,1)S(1)} %get-tuple-element.42), channel_id=1, source_target_pairs={{0,1},{1,0},{2,3},{3,2},{4,5},{5,4},{6,7},{7,6},{8,9},{9,8},{10,11... | collective-permute-start | bytes 1032200 | tf_op jit(solution)/shard_map/ppermute | solution.py:311
  8.6 1.2 %shard_map.183 = (bf16[16,4224]{1,0:T(8,128)(2,1)S(1)}, f32[32,8,128]{2,1,0:T(8,128)S(1)}) custom-call(s32[1,32]{1,0:T(1,128)S(1)} %copy-done.7, s32[1,32]{1,0:T(1,128)S(1)} %copy-done.8, s32[1,2]{1,0:T(1,128)S(1)} %copy-done.9, bf16[1,32,128,128]{3,2,1,0:T(8,128)(2,1)S(1)} %copy-done, bf16[1,32,128,128]{3,2,1,0:T(8,128)(2,1)S(1)} %copy-done.1, ...), custom_call_target="tpu_custom_call" | custom-call | flops 10000 | bytes 100 | tf_op jit(solution)/shard_map/pallas_call | solution.py:281
  9.8 2.6 %collective-permute-start.2 = (bf16[16,4224]{1,0:T(8,128)(2,1)S(1)}, bf16[16,4224]{1,0:T(8,128)(2,1)S(1)}, u32[]{:S(2)}, u32[]{:S(2)}) collective-permute-start(bf16[16,4224]{1,0:T(8,128)(2,1)S(1)} %get-tuple-element.29.refs_12_), channel_id=1, source_target_pairs={{0,28},{4,8},{8,4},{12,16},{16,12},{20,24},{24,20},{28,0},{1,29},{... | collective-permute-start | bytes 405512 | tf_op jit(solution)/shard_map/ppermute | solution.py:35
  12.5 1.4 %shard_map.184 = (bf16[16,4096]{1,0:T(8,128)(2,1)S(1)}, f32[32,8,128]{2,1,0:T(8,128)S(1)}, bf16[16,10240]{1,0:T(8,128)(2,1)S(1)}) custom-call(s32[1,32]{1,0:T(1,128)S(1)} %copy-done.7, s32[1,32]{1,0:T(1,128)S(1)} %copy-done.8, s32[1,2]{1,0:T(1,128)S(1)} %copy-done.9, bf16[1,32,128,128]{3,2,1,0:T(8,128)(2,1)S(1)} %copy-done, ...), custom_call_target="tpu_custom_call" | custom-call | flops 10000 | bytes 100 | tf_op jit(solution)/shard_map/pallas_call | solution.py:281
  13.8 0.1 collective-permute-start
  13.9 0.6 %collective-permute-start.6 = (bf16[16,10240]{1,0:T(8,128)(2,1)S(1)}, bf16[16,10240]{1,0:T(8,128)(2,1)S(1)}, u32[]{:S(2)}, u32[]{:S(2)}) collective-permute-start(bf16[16,10240]{1,0:T(8,128)(2,1)S(1)} %get-tuple-element.43), channel_id=1, source_target_pairs={{0,2},{1,3},{2,0},{3,1},{4,6},{5,7},{6,4},{7,5},{8,10},{9,11},{10,... | collective-permute-start | bytes 983048 | tf_op jit(solution)/shard_map/ppermute | solution.py:311
  14.5 0.8 %collective-permute-done.refs_4_ = bf16[16,4096]{1,0:T(8,128)(2,1)S(1)} collective-permute-done((bf16[16,4096]{1,0:T(8,128)(2,1)S(1)}, bf16[16,4096]{1,0:T(8,128)(2,1)S(1)}, u32[]{:S(2)}, u32[]{:S(2)}) %collective-permute-start) | collective-permute-done | bytes 131104 | tf_op jit(solution)/shard_map/ppermute | solution.py:36
  15.3 1.9 %shard_map.185 = (bf16[16,4224]{1,0:T(8,128)(2,1)S(1)}, bf16[16,2048]{1,0:T(8,128)(2,1)S(1)}, bf16[16,2048]{1,0:T(8,128)(2,1)S(1)}, bf16[16,2048]{1,0:T(8,128)(2,1)S(1)}, bf16[16,2048]{1,0:T(8,128)(2,1)S(1)}) custom-call(s32[1,32]{1,0:T(1,128)S(1)} %copy-done.7, s32[1,32]{1,0:T(1,128)S(1)} %copy-done.8, bf16[1,32,128,128]{3,2,1,0:T(8,128)(2,1)S(1)} %copy-done, ...), custom_call_target="tpu_custom_call" | custom-call | flops 10000 | bytes 100 | tf_op jit(solution)/shard_map/pallas_call | solution.py:281
  17.2 0.4 %collective-permute-start.1 = (bf16[16,4224]{1,0:T(8,128)(2,1)S(1)}, bf16[16,4224]{1,0:T(8,128)(2,1)S(1)}, u32[]{:S(2)}, u32[]{:S(2)}) collective-permute-start(bf16[16,4224]{1,0:T(8,128)(2,1)S(1)} %get-tuple-element.33), channel_id=1, source_target_pairs={{0,28},{4,8},{8,4},{12,16},{16,12},{20,24},{24,20},{28,0},{1,29},{... | collective-permute-start | bytes 405512 | tf_op jit(solution)/shard_map/ppermute | solution.py:35
  17.5 1.4 %shard_map.186 = (bf16[16,4096]{1,0:T(8,128)(2,1)S(1)}, bf16[16,2048]{1,0:T(8,128)(2,1)S(1)}, bf16[16,2048]{1,0:T(8,128)(2,1)S(1)}, bf16[16,2048]{1,0:T(8,128)(2,1)S(1)}, bf16[16,2048]{1,0:T(8,128)(2,1)S(1)}) custom-call(s32[1,32]{1,0:T(1,128)S(1)} %copy-done.7, s32[1,32]{1,0:T(1,128)S(1)} %copy-done.8, bf16[1,32,128,128]{3,2,1,0:T(8,128)(2,1)S(1)} %copy-done, ...), custom_call_target="tpu_custom_call" | custom-call | flops 1440000000 | bytes 14400000 | tf_op jit(solution)/shard_map/pallas_call | solution.py:281
  18.9 0.7 %collective-permute-start.4 = (bf16[16,4096]{1,0:T(8,128)(2,1)S(1)}, bf16[16,4096]{1,0:T(8,128)(2,1)S(1)}, u32[]{:S(2)}, u32[]{:S(2)}) collective-permute-start(bf16[16,4096]{1,0:T(8,128)(2,1)S(1)} %get-tuple-element.40), channel_id=1, source_target_pairs={{0,4},{4,0},{8,12},{12,8},{16,20},{20,16},{24,28},{28,24},{1,5},{5... | collective-permute-start | bytes 393224 | tf_op jit(solution)/shard_map/ppermute | solution.py:36
  19.6 2.0 %collective-permute-start.7 = (bf16[16,2048]{1,0:T(8,128)(2,1)S(1)}, bf16[16,2048]{1,0:T(8,128)(2,1)S(1)}, u32[]{:S(2)}, u32[]{:S(2)}) collective-permute-start(bf16[16,2048]{1,0:T(8,128)(2,1)S(1)} %get-tuple-element.45), channel_id=1, source_target_pairs={{0,3},{1,2},{2,1},{3,0},{4,7},{5,6},{6,5},{7,4},{8,11},{9,10},{10,... | collective-permute-start | bytes 196616 | tf_op jit(solution)/shard_map/ppermute | solution.py:311
  21.5 3.9 %collective-permute-done.6.refs_3_.refs_6_ = bf16[16,10240]{1,0:T(8,128)(2,1)S(1)} collective-permute-done((bf16[16,10240]{1,0:T(8,128)(2,1)S(1)}, bf16[16,10240]{1,0:T(8,128)(2,1)S(1)}, u32[]{:S(2)}, u32[]{:S(2)}) %collective-permute-start.6) | collective-permute-done | bytes 327712 | tf_op jit(solution)/shard_map/ppermute | solution.py:311
  25.5 1.5 %collective-permute-start.8 = (bf16[16,2048]{1,0:T(8,128)(2,1)S(1)}, bf16[16,2048]{1,0:T(8,128)(2,1)S(1)}, u32[]{:S(2)}, u32[]{:S(2)}) collective-permute-start(bf16[16,2048]{1,0:T(8,128)(2,1)S(1)} %get-tuple-element.46), channel_id=1, source_target_pairs={{0,1},{1,0},{2,3},{3,2},{4,5},{5,4},{6,7},{7,6},{8,9},{9,8},{10,11... | collective-permute-start | bytes 196616 | tf_op jit(solution)/shard_map/ppermute | solution.py:311
  27.0 1.0 %collective-permute-start.9 = (bf16[16,2048]{1,0:T(8,128)(2,1)S(1)}, bf16[16,2048]{1,0:T(8,128)(2,1)S(1)}, u32[]{:S(2)}, u32[]{:S(2)}) collective-permute-start(bf16[16,2048]{1,0:T(8,128)(2,1)S(1)} %get-tuple-element.47), channel_id=1, source_target_pairs={{0,2},{1,3},{2,0},{3,1},{4,6},{5,7},{6,4},{7,5},{8,10},{9,11},{10,... | collective-permute-start | bytes 196616 | tf_op jit(solution)/shard_map/ppermute | solution.py:311
  28.0 0.3 %shard_map.187.refs_2_ = f32[2,8,128,128]{3,2,1,0:T(8,128)S(1)} custom-call(bf16[16,10240]{1,0:T(8,128)(2,1)S(1)} %get-tuple-element.41.refs_0_.refs_3_, bf16[16,10240]{1,0:T(8,128)(2,1)S(1)} %collective-permute-done.3.refs_11_.refs_1_.refs_4_, bf16[16,10752]{1,0:T(8,128)(2,1)S(1)} %collective-permute-done.5.refs_2_.refs_5_, ...), custom_call_target="tpu_custom_call" | custom-call | flops 10000 | bytes 100 | tf_op jit(solution)/shard_map/pallas_call | solution.py:281
  28.4 1.4 %collective-permute-done.8.refs_9_ = bf16[16,2048]{1,0:T(8,128)(2,1)S(1)} collective-permute-done((bf16[16,2048]{1,0:T(8,128)(2,1)S(1)}, bf16[16,2048]{1,0:T(8,128)(2,1)S(1)}, u32[]{:S(2)}, u32[]{:S(2)}) %collective-permute-start.8) | collective-permute-done | bytes 65568 | tf_op jit(solution)/shard_map/ppermute | solution.py:311
  29.7 1.5 %collective-permute-done.9.refs_10_ = bf16[16,2048]{1,0:T(8,128)(2,1)S(1)} collective-permute-done((bf16[16,2048]{1,0:T(8,128)(2,1)S(1)}, bf16[16,2048]{1,0:T(8,128)(2,1)S(1)}, u32[]{:S(2)}, u32[]{:S(2)}) %collective-permute-start.9) | collective-permute-done | bytes 65568 | tf_op jit(solution)/shard_map/ppermute | solution.py:311
  31.3 1.2 %shard_map.188 = (bf16[1,8,4096]{2,1,0:T(8,128)(2,1)}, bf16[1,8,4096]{2,1,0:T(8,128)(2,1)}, bf16[1,8,4096]{2,1,0:T(8,128)(2,1)}, bf16[1,8,4096]{2,1,0:T(8,128)(2...) custom-call(bf16[16,4224]{1,0:T(8,128)(2,1)S(1)} %collective-permute-done.1.refs_0_, ...), custom_call_target="tpu_custom_call" | custom-call | flops 10000 | bytes 100 | tf_op jit(solution)/shard_map/pallas_call | solution.py:281
  (32 shorter events, 0.2 us)
Async XLA Ops:
  0.6 0.7 %copy-start.8 = (s32[1,32]{1,0:T(1,128)S(1)}, s32[1,32]{1,0:T(1,128)}, u32[]{:S(2)}) copy-start(s32[1,32]{1,0:T(1,128)} %refs_1_.9) | copy-start | bytes 388
  0.6 1.2 %copy-start.1 = (bf16[1,32,128,128]{3,2,1,0:T(8,128)(2,1)S(1)}, bf16[1,32,128,128]{3,2,1,0:T(8,128)(2,1)}, u32[]{:S(2)}) copy-start(bf16[1,32,128,128]{3,2,1,0:T(8,128)(2,1)} %refs_3_.9) | copy-start | bytes 3145732
  0.7 1.2 %copy-start.7 = (s32[1,32]{1,0:T(1,128)S(1)}, s32[1,32]{1,0:T(1,128)}, u32[]{:S(2)}) copy-start(s32[1,32]{1,0:T(1,128)} %refs_0_.9) | copy-start | bytes 388
  0.7 1.5 %copy-start = (bf16[1,32,128,128]{3,2,1,0:T(8,128)(2,1)S(1)}, bf16[1,32,128,128]{3,2,1,0:T(8,128)(2,1)}, u32[]{:S(2)}) copy-start(bf16[1,32,128,128]{3,2,1,0:T(8,128)(2,1)} %refs_2_.9) | copy-start | bytes 3145732
  0.7 1.5 %copy-start.4 = (bf16[1,8,4096]{2,1,0:T(8,128)(2,1)S(1)}, bf16[1,8,4096]{2,1,0:T(8,128)(2,1)}, u32[]{:S(2)}) copy-start(bf16[1,8,4096]{2,1,0:T(8,128)(2,1)} %refs_6_.5) | copy-start | bytes 196612
  0.7 1.5 %copy-start.3 = (bf16[1,8,4096]{2,1,0:T(8,128)(2,1)S(1)}, bf16[1,8,4096]{2,1,0:T(8,128)(2,1)}, u32[]{:S(2)}) copy-start(bf16[1,8,4096]{2,1,0:T(8,128)(2,1)} %refs_5_.5) | copy-start | bytes 196612
  0.7 1.5 %copy-start.9 = (s32[1,2]{1,0:T(1,128)S(1)}, s32[1,2]{1,0:T(1,128)}, u32[]{:S(2)}) copy-start(s32[1,2]{1,0:T(1,128)} %refs_2_.7) | copy-start | bytes 28
  0.7 1.6 %copy-start.13 = (bf16[1,2,8,4096]{3,2,1,0:T(8,128)(2,1)S(1)}, bf16[1,2,8,4096]{3,2,1,0:T(8,128)(2,1)}, u32[]{:S(2)}) copy-start(bf16[1,2,8,4096]{3,2,1,0:T(8,128)(2,1)} %refs_10_.3) | copy-start | bytes 393220
  0.7 1.6 %copy-start.12 = (bf16[1,2,8,4096]{3,2,1,0:T(8,128)(2,1)S(1)}, bf16[1,2,8,4096]{3,2,1,0:T(8,128)(2,1)}, u32[]{:S(2)}) copy-start(bf16[1,2,8,4096]{3,2,1,0:T(8,128)(2,1)} %refs_9_.3) | copy-start | bytes 393220
  0.7 1.6 %copy-start.11 = (bf16[1,2,8,4096]{3,2,1,0:T(8,128)(2,1)S(1)}, bf16[1,2,8,4096]{3,2,1,0:T(8,128)(2,1)}, u32[]{:S(2)}) copy-start(bf16[1,2,8,4096]{3,2,1,0:T(8,128)(2,1)} %refs_8_.3) | copy-start | bytes 393220
  0.7 1.6 %copy-start.10 = (bf16[1,2,8,4096]{3,2,1,0:T(8,128)(2,1)S(1)}, bf16[1,2,8,4096]{3,2,1,0:T(8,128)(2,1)}, u32[]{:S(2)}) copy-start(bf16[1,2,8,4096]{3,2,1,0:T(8,128)(2,1)} %refs_7_.1) | copy-start | bytes 393220
  2.4 6.2 %copy-start.2 = (bf16[1,2,8,4096]{3,2,1,0:T(8,128)(2,1)S(1)}, bf16[1,2,8,4096]{3,2,1,0:T(8,128)(2,1)}, u32[]{:S(2)}) copy-start(bf16[1,2,8,4096]{3,2,1,0:T(8,128)(2,1)} %refs_10_.5) | copy-start | bytes 393220
  2.4 6.2 %copy-start.5 = (bf16[1,8,4096]{2,1,0:T(8,128)(2,1)S(1)}, bf16[1,8,4096]{2,1,0:T(8,128)(2,1)}, u32[]{:S(2)}) copy-start(bf16[1,8,4096]{2,1,0:T(8,128)(2,1)} %refs_8_.5) | copy-start | bytes 196612
  2.4 6.2 %copy-start.6 = (bf16[1,8,4096]{2,1,0:T(8,128)(2,1)S(1)}, bf16[1,8,4096]{2,1,0:T(8,128)(2,1)}, u32[]{:S(2)}) copy-start(bf16[1,8,4096]{2,1,0:T(8,128)(2,1)} %refs_9_.5) | copy-start | bytes 196612
  4.1 13.5 %collective-permute-start.3 = (bf16[16,10240]{1,0:T(8,128)(2,1)S(1)}, bf16[16,10240]{1,0:T(8,128)(2,1)S(1)}, u32[]{:S(2)}, u32[]{:S(2)}) collective-permute-start(bf16[16,10240]{1,0:T(8,128)(2,1)S(1)} %get-tuple-element.39), channel_id=1, source_target_pairs={{0,3},{1,2},{2,1},{3,0},{4,7},{5,6},{6,5},{7,4},{8,11},{9,10},{10,... | collective-permute-start | bytes 983048 | tf_op jit(solution)/shard_map/ppermute | solution.py:311
  8.1 18.9 %collective-permute-start.5 = (bf16[16,10752]{1,0:T(8,128)(2,1)S(1)}, bf16[16,10752]{1,0:T(8,128)(2,1)S(1)}, u32[]{:S(2)}, u32[]{:S(2)}) collective-permute-start(bf16[16,10752]{1,0:T(8,128)(2,1)S(1)} %get-tuple-element.42), channel_id=1, source_target_pairs={{0,1},{1,0},{2,3},{3,2},{4,5},{5,4},{6,7},{7,6},{8,9},{9,8},{10,11... | collective-permute-start | bytes 1032200 | tf_op jit(solution)/shard_map/ppermute | solution.py:311
  9.8 7.7 %collective-permute-start.2 = (bf16[16,4224]{1,0:T(8,128)(2,1)S(1)}, bf16[16,4224]{1,0:T(8,128)(2,1)S(1)}, u32[]{:S(2)}, u32[]{:S(2)}) collective-permute-start(bf16[16,4224]{1,0:T(8,128)(2,1)S(1)} %get-tuple-element.29.refs_12_), channel_id=1, source_target_pairs={{0,28},{4,8},{8,4},{12,16},{16,12},{20,24},{24,20},{28,0},{1,29},{... | collective-permute-start | bytes 405512 | tf_op jit(solution)/shard_map/ppermute | solution.py:35
  13.8 1.4 %collective-permute-start = (bf16[16,4096]{1,0:T(8,128)(2,1)S(1)}, bf16[16,4096]{1,0:T(8,128)(2,1)S(1)}, u32[]{:S(2)}, u32[]{:S(2)}) collective-permute-start(bf16[16,4096]{1,0:T(8,128)(2,1)S(1)} %get-tuple-element.30), channel_id=1, source_target_pairs={{0,4},{4,0},{8,12},{12,8},{16,20},{20,16},{24,28},{28,24},{1,5},{5... | collective-permute-start | bytes 393224 | tf_op jit(solution)/shard_map/ppermute | solution.py:36
  13.9 11.5 %collective-permute-start.6 = (bf16[16,10240]{1,0:T(8,128)(2,1)S(1)}, bf16[16,10240]{1,0:T(8,128)(2,1)S(1)}, u32[]{:S(2)}, u32[]{:S(2)}) collective-permute-start(bf16[16,10240]{1,0:T(8,128)(2,1)S(1)} %get-tuple-element.43), channel_id=1, source_target_pairs={{0,2},{1,3},{2,0},{3,1},{4,6},{5,7},{6,4},{7,5},{8,10},{9,11},{10,... | collective-permute-start | bytes 983048 | tf_op jit(solution)/shard_map/ppermute | solution.py:311
  17.2 11.2 %collective-permute-start.1 = (bf16[16,4224]{1,0:T(8,128)(2,1)S(1)}, bf16[16,4224]{1,0:T(8,128)(2,1)S(1)}, u32[]{:S(2)}, u32[]{:S(2)}) collective-permute-start(bf16[16,4224]{1,0:T(8,128)(2,1)S(1)} %get-tuple-element.33), channel_id=1, source_target_pairs={{0,28},{4,8},{8,4},{12,16},{16,12},{20,24},{24,20},{28,0},{1,29},{... | collective-permute-start | bytes 405512 | tf_op jit(solution)/shard_map/ppermute | solution.py:35
  18.9 12.4 %collective-permute-start.4 = (bf16[16,4096]{1,0:T(8,128)(2,1)S(1)}, bf16[16,4096]{1,0:T(8,128)(2,1)S(1)}, u32[]{:S(2)}, u32[]{:S(2)}) collective-permute-start(bf16[16,4096]{1,0:T(8,128)(2,1)S(1)} %get-tuple-element.40), channel_id=1, source_target_pairs={{0,4},{4,0},{8,12},{12,8},{16,20},{20,16},{24,28},{28,24},{1,5},{5... | collective-permute-start | bytes 393224 | tf_op jit(solution)/shard_map/ppermute | solution.py:36
  19.6 8.8 %collective-permute-start.7 = (bf16[16,2048]{1,0:T(8,128)(2,1)S(1)}, bf16[16,2048]{1,0:T(8,128)(2,1)S(1)}, u32[]{:S(2)}, u32[]{:S(2)}) collective-permute-start(bf16[16,2048]{1,0:T(8,128)(2,1)S(1)} %get-tuple-element.45), channel_id=1, source_target_pairs={{0,3},{1,2},{2,1},{3,0},{4,7},{5,6},{6,5},{7,4},{8,11},{9,10},{10,... | collective-permute-start | bytes 196616 | tf_op jit(solution)/shard_map/ppermute | solution.py:311
  25.5 4.3 %collective-permute-start.8 = (bf16[16,2048]{1,0:T(8,128)(2,1)S(1)}, bf16[16,2048]{1,0:T(8,128)(2,1)S(1)}, u32[]{:S(2)}, u32[]{:S(2)}) collective-permute-start(bf16[16,2048]{1,0:T(8,128)(2,1)S(1)} %get-tuple-element.46), channel_id=1, source_target_pairs={{0,1},{1,0},{2,3},{3,2},{4,5},{5,4},{6,7},{7,6},{8,9},{9,8},{10,11... | collective-permute-start | bytes 196616 | tf_op jit(solution)/shard_map/ppermute | solution.py:311
  27.0 4.3 %collective-permute-start.9 = (bf16[16,2048]{1,0:T(8,128)(2,1)S(1)}, bf16[16,2048]{1,0:T(8,128)(2,1)S(1)}, u32[]{:S(2)}, u32[]{:S(2)}) collective-permute-start(bf16[16,2048]{1,0:T(8,128)(2,1)S(1)} %get-tuple-element.47), channel_id=1, source_target_pairs={{0,2},{1,3},{2,0},{3,1},{4,6},{5,7},{6,4},{7,5},{8,10},{9,11},{10,... | collective-permute-start | bytes 196616 | tf_op jit(solution)/shard_map/ppermute | solution.py:311

commit v15 on v10

--- a/solution.py
+++ b/solution.py
@@ -12,6 +12,9 @@
 WORK = 10 ** 10
 LIGHT = 10 ** 4
 PAD = BLOCK
+C_STREAMS = LIGHT
+C_NEAR_PHASE = 5 * 10 ** 8
+C_FAR_PHASE = LIGHT
 
 
 def partner(me, step, count):
@@ -163,18 +166,14 @@
         pack[:, lanes(b)] = returned[b].astype(BF16)
 
 
-def first_streams(blocks, back_parity, up_idx, down_idx, order, w_up, w_down, g_ref, a_ref, pushes, v_ref, t_ref, tan,
-                  pack, keep, returned, hidden):
+def first_streams(blocks, up_idx, down_idx, order, w_up, w_down, g_ref, a_ref, pushes, v_ref, t_ref, tan,
+                  near, far, keep, packs, returned, hidden):
     odd = odd_section()
-    clear_pad(pack, blocks)
-
-    @pl.when(odd == back_parity)
-    def _():
-        back_streams(blocks, up_idx, w_up, g_ref, a_ref, pushes, pack, returned)
-
-    @pl.when(odd != back_parity)
-    def _():
-        forward_first(blocks, up_idx, down_idx, order, w_up, w_down, v_ref, t_ref, tan, pack, keep, hidden)
+    clear_pad(far, blocks)
+    back_streams(blocks, up_idx, w_up, g_ref, a_ref, pushes, packs.at[1], returned)
+    forward_first(blocks, up_idx, down_idx, order, w_up, w_down, v_ref, t_ref, tan, packs.at[0], keep, hidden)
+    near[...] = packs[odd]
+    far[:, :packs.shape[2]] = packs[1 - odd]
 
 
 def back_second(count, per, up_idx, down_idx, w_up, w_down, rows, keep, pack, sends, pulled, returned):
@@ -314,22 +313,21 @@
         [vmem((blocks, 32, BLOCK), F32), vmem((blocks, 48, BLOCK), BF16)],
         after=(token,), cost=WORK)
     taken = tables + (score_grad_in, state_adjoint_in, pushes, values_in, tangent_in, saved_tan)
-    made = [shape((blocks, 8, BLOCK), F32)]
     long = shape((16, width + PAD), BF16)
-    scratch = [vmem((blocks, 16, BLOCK), F32), vmem((blocks, 16, BLOCK), BF16)]
-    far, far_keep = call(body(first_streams, blocks, 0), taken, [smem] * 3 + [vmem] * 8, [long] + made, scratch)
-    near, near_keep = call(body(first_streams, blocks, 1), taken, [smem] * 3 + [vmem] * 8, [pair] + made, scratch,
-                           after=(far,))
+    near, far, keep_tan = call(
+        body(first_streams, blocks), taken, [smem] * 3 + [vmem] * 8, [pair, long, shape((blocks, 8, BLOCK), F32)],
+        [vmem((2, 16, width), BF16), vmem((blocks, 16, BLOCK), F32), vmem((blocks, 16, BLOCK), BF16)], cost=C_STREAMS)
     near, far = swap_sections(near, far)
     early = to_replicas(early)
     tables = (up_index, down_index, w_up, w_down)
     two = [shape((2, 16, part), BF16)] * count
     scratch = [vmem((blocks, 16, BLOCK), F32), vmem((blocks, 16, BLOCK), F32), vmem((blocks, 16, BLOCK), BF16)]
     far_out, *late = call(
-        body(near_phase, count, per), tables + (near, keep, far_keep), [smem] * 2 + [vmem] * 5, [long] + two, scratch)
+        body(near_phase, count, per), tables + (near, keep, keep_tan), [smem] * 2 + [vmem] * 5, [long] + two, scratch,
+        cost=C_NEAR_PHASE)
     near_out, *late = call(
-        body(far_phase, count, per), tables + (far, keep, near_keep, *late), [smem] * 2 + [vmem] * (5 + count),
-        [pair] + two, scratch)
+        body(far_phase, count, per), tables + (far, keep, keep_tan, *late), [smem] * 2 + [vmem] * (5 + count),
+        [pair] + two, scratch, cost=C_FAR_PHASE)
     near, far = swap_sections(near_out, far_out)
     late = to_replicas(late)
     (grads,) = call(

time: 30.2 us -> 30.2 us (level)
  Pallas kernels: 9.04 us -> 8.33 us
  starting transfers between devices: 13.2 us -> 13.9 us
    ppermute x2, waiting for transfers between devices: 1.34 us -> 0.01 us  [swap_sections(): near = lax.ppermute(near, 'section', [(i, i ^ 1) for i in range(count)])]
    ppermute x2, starting transfers between devices: 3.34 us -> 4.61 us  [swap_sections(): lax.ppermute(far, 'section', [(i, (i + 2 * (i % 2) - 1) % count) for i in...]
    ppermute x2, waiting for transfers between devices: 0.01 us -> 1.06 us  [swap_sections(): lax.ppermute(far, 'section', [(i, (i + 2 * (i % 2) - 1) % count) for i in...]
    pallas_call x8 -> x7, Pallas kernels: 9.04 us -> 8.33 us  [call(): pl.pallas_call(kernel, out_shape=outs, in_specs=[pl.BlockSpec(memory_spac...]
    ppermute x2, starting transfers between devices: 0.78 us -> 0.14 us  [swap_sections(): near = lax.ppermute(near, 'section', [(i, i ^ 1) for i in range(count)])]
  transfers between devices with their start and end apart: 10 -> 10, of which waited for: 5 -> 4; matrix products, arithmetic and copies ran while one was open for 0% -> 0% of each run, Pallas kernels for 21% -> 18%
where the time goes in v15:
time: 30.2 us; the launch traced here: 30 us
  starting transfers between devices  13.9 us (46%)
  Pallas kernels  8.33 us (28%)
  waiting for transfers between devices  5.36 us (18%)
  local copies, waits for them, and re-layouts  1.66 us (5%)
  between operations  0.8 us (3%)
    ppermute x6, starting transfers between devices, to_replicas(): lax.ppermute(parts[step], 'dp', swap_route(step, count))  9.11 us
    pallas_call x7, Pallas kernels, call(): pl.pallas_call(kernel, out_shape=outs, in_specs=[pl.BlockSpec(memory_spac...  8.33 us
    ppermute x2, starting transfers between devices, swap_sections(): lax.ppermute(far, 'section', [(i, (i + 2 * (i % 2) - 1) % count) for i in...  4.61 us
    ppermute x6, waiting for transfers between devices, to_replicas(): lax.ppermute(parts[step], 'dp', swap_route(step, count))  4.3 us
    unnamed x28, local copies, waits for them, and re-layouts  1.66 us
    ppermute x2, waiting for transfers between devices, swap_sections(): lax.ppermute(far, 'section', [(i, (i + 2 * (i % 2) - 1) % count) for i in...  1.06 us
  transfers between devices with their start and end apart: 10, of which 4 were waited for; matrix products, arithmetic and copies ran while one was open for 0% of the time, Pallas kernels for 18%

profile of v15, /device:TPU:0, one launch (start us, length us, event | category | flops | bytes accessed | tf_op | source)
XLA Modules:
  0.0 30.0 jit_solution(14681174450054129178)
XLA Ops:
  0.8 0.5 %copy-done.8 = s32[1,32]{1,0:T(1,128)S(1)} copy-done((s32[1,32]{1,0:T(1,128)S(1)}, s32[1,32]{1,0:T(1,128)}, u32[]{:S(2)}) %copy-start.8) | copy-done | bytes 152
  1.3 0.6 %copy-done.1 = bf16[1,32,128,128]{3,2,1,0:T(8,128)(2,1)S(1)} copy-done((bf16[1,32,128,128]{3,2,1,0:T(8,128)(2,1)S(1)}, bf16[1,32,128,128]{3,2,1,0:T(8,128)(2,1)}, u32[]{:S(2)}) %copy-start.1) | copy-done | bytes 1048600
  1.9 0.3 %copy-done = bf16[1,32,128,128]{3,2,1,0:T(8,128)(2,1)S(1)} copy-done((bf16[1,32,128,128]{3,2,1,0:T(8,128)(2,1)S(1)}, bf16[1,32,128,128]{3,2,1,0:T(8,128)(2,1)}, u32[]{:S(2)}) %copy-start) | copy-done | bytes 1048600
  2.3 0.0 copy-done.12
  2.4 1.7 %shard_map.182 = (f32[32,24,128]{2,1,0:T(8,128)S(1)}, bf16[16,4096]{1,0:T(8,128)(2,1)S(1)}, bf16[10,16,1024]{2,1,0:T(8,128)(2,1)S(1)}, bf16[10,16,1024]{2,1,0:T(...) custom-call(s32[1,32]{1,0:T(1,128)S(1)} %copy-done.7, s32[1,32]{1,0:T(1,128)S(1)} %copy-done.8, ...), custom_call_target="tpu_custom_call" | custom-call | flops 10000000000 | bytes 100000000 | tf_op jit(solution)/shard_map/pallas_call | solution.py:274
  4.1 4.0 %collective-permute-start.4 = (bf16[10,16,1024]{2,1,0:T(8,128)(2,1)S(1)}, bf16[10,16,1024]{2,1,0:T(8,128)(2,1)S(1)}, u32[]{:S(2)}, u32[]{:S(2)}) collective-permute-start(bf16[10,16,1024]{2,1,0:T(8,128)(2,1)S(1)} %get-tuple-element.37), channel_id=1, source_target_pairs={{0,3},{1,2},{2,1},{3,0},{4,7},{5,6},{6,5},{7,4},{8,11},{9,10},{10,... | collective-permute-start | bytes 983048 | tf_op jit(solution)/shard_map/ppermute | solution.py:304
  8.0 0.5 %collective-permute-start.5 = (bf16[10,16,1024]{2,1,0:T(8,128)(2,1)S(1)}, bf16[10,16,1024]{2,1,0:T(8,128)(2,1)S(1)}, u32[]{:S(2)}, u32[]{:S(2)}) collective-permute-start(bf16[10,16,1024]{2,1,0:T(8,128)(2,1)S(1)} %get-tuple-element.38), channel_id=1, source_target_pairs={{0,1},{1,0},{2,3},{3,2},{4,5},{5,4},{6,7},{7,6},{8,9},{9,8},{10,11... | collective-permute-start | bytes 983048 | tf_op jit(solution)/shard_map/ppermute | solution.py:304
  8.6 0.1 collective-permute-start.6
  8.7 1.9 %shard_map.183 = (bf16[16,4096]{1,0:T(8,128)(2,1)S(1)}, bf16[16,4224]{1,0:T(8,128)(2,1)S(1)}, f32[32,8,128]{2,1,0:T(8,128)S(1)}) custom-call(s32[1,32]{1,0:T(1,128)S(1)} %copy-done.7, s32[1,32]{1,0:T(1,128)S(1)} %copy-done.8, s32[1,2]{1,0:T(1,128)S(1)} %copy-done.9, bf16[1,32,128,128]{3,2,1,0:T(8,128)(2,1)S(1)} %copy-done, ...), custom_call_target="tpu_custom_call" | custom-call | flops 10000 | bytes 100 | tf_op jit(solution)/shard_map/pallas_call | solution.py:274
  10.6 0.1 collective-permute-start
  10.7 4.1 %collective-permute-start.2 = (bf16[16,4224]{1,0:T(8,128)(2,1)S(1)}, bf16[16,4224]{1,0:T(8,128)(2,1)S(1)}, u32[]{:S(2)}, u32[]{:S(2)}) collective-permute-start(bf16[16,4224]{1,0:T(8,128)(2,1)S(1)} %get-tuple-element.30), channel_id=1, source_target_pairs={{0,28},{4,8},{8,4},{12,16},{16,12},{20,24},{24,20},{28,0},{1,29},{... | collective-permute-start | bytes 405512 | tf_op jit(solution)/shard_map/ppermute | solution.py:34
  14.8 1.9 %shard_map.184 = (bf16[16,4224]{1,0:T(8,128)(2,1)S(1)}, bf16[2,16,1024]{2,1,0:T(8,128)(2,1)S(1)}, bf16[2,16,1024]{2,1,0:T(8,128)(2,1)S(1)}, bf16[2,16,1024]{2,1,0:T(8,128)(2,1)S(1)}, bf16[2,16,1024]{2,1,0:T(8,128)(2,1)S(1)}) custom-call(s32[1,32]{1,0:T(1,128)S(1)} %copy-done.7, s32[1,32]{1,0:T(1,128)S(1)} %copy-done.8, ...), custom_call_target="tpu_custom_call" | custom-call | flops 500000000 | bytes 5000000 | tf_op jit(solution)/shard_map/pallas_call | solution.py:274
  16.7 0.5 %collective-permute-start.1 = (bf16[16,4224]{1,0:T(8,128)(2,1)S(1)}, bf16[16,4224]{1,0:T(8,128)(2,1)S(1)}, u32[]{:S(2)}, u32[]{:S(2)}) collective-permute-start(bf16[16,4224]{1,0:T(8,128)(2,1)S(1)} %get-tuple-element.29), channel_id=1, source_target_pairs={{0,28},{4,8},{8,4},{12,16},{16,12},{20,24},{24,20},{28,0},{1,29},{... | collective-permute-start | bytes 405512 | tf_op jit(solution)/shard_map/ppermute | solution.py:34
  17.2 1.1 %collective-permute-done.2.refs_4_ = bf16[16,4224]{1,0:T(8,128)(2,1)S(1)} collective-permute-done((bf16[16,4224]{1,0:T(8,128)(2,1)S(1)}, bf16[16,4224]{1,0:T(8,128)(2,1)S(1)}, u32[]{:S(2)}, u32[]{:S(2)}) %collective-permute-start.2) | collective-permute-done | bytes 135200 | tf_op jit(solution)/shard_map/ppermute | solution.py:34
  18.2 1.4 %shard_map.185 = (bf16[16,4096]{1,0:T(8,128)(2,1)S(1)}, bf16[2,16,1024]{2,1,0:T(8,128)(2,1)S(1)}, bf16[2,16,1024]{2,1,0:T(8,128)(2,1)S(1)}, bf16[2,16,1024]{2,1,0:T(8,128)(2,1)S(1)}, bf16[2,16,1024]{2,1,0:T(8,128)(2,1)S(1)}) custom-call(s32[1,32]{1,0:T(1,128)S(1)} %copy-done.7, s32[1,32]{1,0:T(1,128)S(1)} %copy-done.8, ...), custom_call_target="tpu_custom_call" | custom-call | flops 10000 | bytes 100 | tf_op jit(solution)/shard_map/pallas_call | solution.py:274
  19.6 0.1 collective-permute-start.3
  19.7 2.5 %collective-permute-start.7 = (bf16[2,16,1024]{2,1,0:T(8,128)(2,1)S(1)}, bf16[2,16,1024]{2,1,0:T(8,128)(2,1)S(1)}, u32[]{:S(2)}, u32[]{:S(2)}) collective-permute-start(bf16[2,16,1024]{2,1,0:T(8,128)(2,1)S(1)} %get-tuple-element.41), channel_id=1, source_target_pairs={{0,3},{1,2},{2,1},{3,0},{4,7},{5,6},{6,5},{7,4},{8,11},{9,10},{10,... | collective-permute-start | bytes 196616 | tf_op jit(solution)/shard_map/ppermute | solution.py:304
  22.2 0.9 %collective-permute-done.5.refs_2_.refs_5_ = bf16[10,16,1024]{2,1,0:T(8,128)(2,1)S(1)} collective-permute-done((bf16[10,16,1024]{2,1,0:T(8,128)(2,1)S(1)}, bf16[10,16,1024]{2,1,0:T(8,128)(2,1)S(1)}, u32[]{:S(2)}, u32[]{:S(2)}) %collective-permute-start.5) | collective-permute-done | bytes 327712 | tf_op jit(solution)/shard_map/ppermute | solution.py:304
  23.1 1.5 %collective-permute-start.8 = (bf16[2,16,1024]{2,1,0:T(8,128)(2,1)S(1)}, bf16[2,16,1024]{2,1,0:T(8,128)(2,1)S(1)}, u32[]{:S(2)}, u32[]{:S(2)}) collective-permute-start(bf16[2,16,1024]{2,1,0:T(8,128)(2,1)S(1)} %get-tuple-element.42), channel_id=1, source_target_pairs={{0,1},{1,0},{2,3},{3,2},{4,5},{5,4},{6,7},{7,6},{8,9},{9,8},{10,11... | collective-permute-start | bytes 196616 | tf_op jit(solution)/shard_map/ppermute | solution.py:304
  24.6 0.5 %collective-permute-start.9 = (bf16[2,16,1024]{2,1,0:T(8,128)(2,1)S(1)}, bf16[2,16,1024]{2,1,0:T(8,128)(2,1)S(1)}, u32[]{:S(2)}, u32[]{:S(2)}) collective-permute-start(bf16[2,16,1024]{2,1,0:T(8,128)(2,1)S(1)} %get-tuple-element.43), channel_id=1, source_target_pairs={{0,2},{1,3},{2,0},{3,1},{4,6},{5,7},{6,4},{7,5},{8,10},{9,11},{10,... | collective-permute-start | bytes 196616 | tf_op jit(solution)/shard_map/ppermute | solution.py:304
  25.1 0.3 %shard_map.186.refs_2_ = f32[2,8,128,128]{3,2,1,0:T(8,128)S(1)} custom-call(bf16[10,16,1024]{2,1,0:T(8,128)(2,1)S(1)} %get-tuple-element.36.refs_0_.refs_3_, bf16[10,16,1024]{2,1,0:T(8,128)(2,1)S(1)} %collective-permute-done.4.refs_1_.refs_4_, bf16[10,16,1024]{2,1,0:T(8,128)(2,1)S(1)} %collective-permute-done.5.refs_2_.refs_5_, ...), custom_call_target="tpu_custom_call" | custom-call | flops 10000 | bytes 100 | tf_op jit(solution)/shard_map/pallas_call | solution.py:274
  25.4 1.9 %collective-permute-done.8.refs_9_ = bf16[2,16,1024]{2,1,0:T(8,128)(2,1)S(1)} collective-permute-done((bf16[2,16,1024]{2,1,0:T(8,128)(2,1)S(1)}, bf16[2,16,1024]{2,1,0:T(8,128)(2,1)S(1)}, u32[]{:S(2)}, u32[]{:S(2)}) %collective-permute-start.8) | collective-permute-done | bytes 65568 | tf_op jit(solution)/shard_map/ppermute | solution.py:304
  27.3 1.5 %collective-permute-done.9.refs_10_ = bf16[2,16,1024]{2,1,0:T(8,128)(2,1)S(1)} collective-permute-done((bf16[2,16,1024]{2,1,0:T(8,128)(2,1)S(1)}, bf16[2,16,1024]{2,1,0:T(8,128)(2,1)S(1)}, u32[]{:S(2)}, u32[]{:S(2)}) %collective-permute-start.9) | collective-permute-done | bytes 65568 | tf_op jit(solution)/shard_map/ppermute | solution.py:304
  28.8 1.2 %shard_map.187 = (bf16[1,8,4096]{2,1,0:T(8,128)(2,1)}, bf16[1,8,4096]{2,1,0:T(8,128)(2,1)}, bf16[1,8,4096]{2,1,0:T(8,128)(2,1)}, bf16[1,8,4096]{2,1,0:T(8,128)(2...) custom-call(bf16[16,4224]{1,0:T(8,128)(2,1)S(1)} %collective-permute-done.1.refs_0_, ...), custom_call_target="tpu_custom_call" | custom-call | flops 10000 | bytes 100 | tf_op jit(solution)/shard_map/pallas_call | solution.py:274
  (31 shorter events, 0.2 us)
Async XLA Ops:
  0.6 0.7 %copy-start.8 = (s32[1,32]{1,0:T(1,128)S(1)}, s32[1,32]{1,0:T(1,128)}, u32[]{:S(2)}) copy-start(s32[1,32]{1,0:T(1,128)} %refs_1_.7) | copy-start | bytes 388
  0.6 1.2 %copy-start.1 = (bf16[1,32,128,128]{3,2,1,0:T(8,128)(2,1)S(1)}, bf16[1,32,128,128]{3,2,1,0:T(8,128)(2,1)}, u32[]{:S(2)}) copy-start(bf16[1,32,128,128]{3,2,1,0:T(8,128)(2,1)} %refs_3_.7) | copy-start | bytes 3145732
  0.7 1.2 %copy-start.7 = (s32[1,32]{1,0:T(1,128)S(1)}, s32[1,32]{1,0:T(1,128)}, u32[]{:S(2)}) copy-start(s32[1,32]{1,0:T(1,128)} %refs_0_.7) | copy-start | bytes 388
  0.7 1.5 %copy-start = (bf16[1,32,128,128]{3,2,1,0:T(8,128)(2,1)S(1)}, bf16[1,32,128,128]{3,2,1,0:T(8,128)(2,1)}, u32[]{:S(2)}) copy-start(bf16[1,32,128,128]{3,2,1,0:T(8,128)(2,1)} %refs_2_.7) | copy-start | bytes 3145732
  0.7 1.5 %copy-start.4 = (bf16[1,8,4096]{2,1,0:T(8,128)(2,1)S(1)}, bf16[1,8,4096]{2,1,0:T(8,128)(2,1)}, u32[]{:S(2)}) copy-start(bf16[1,8,4096]{2,1,0:T(8,128)(2,1)} %refs_6_.3) | copy-start | bytes 196612
  0.7 1.5 %copy-start.3 = (bf16[1,8,4096]{2,1,0:T(8,128)(2,1)S(1)}, bf16[1,8,4096]{2,1,0:T(8,128)(2,1)}, u32[]{:S(2)}) copy-start(bf16[1,8,4096]{2,1,0:T(8,128)(2,1)} %refs_5_.3) | copy-start | bytes 196612
  0.7 1.5 %copy-start.9 = (s32[1,2]{1,0:T(1,128)S(1)}, s32[1,2]{1,0:T(1,128)}, u32[]{:S(2)}) copy-start(s32[1,2]{1,0:T(1,128)} %refs_2_.5) | copy-start | bytes 28
  0.7 1.6 %copy-start.13 = (bf16[1,2,8,4096]{3,2,1,0:T(8,128)(2,1)S(1)}, bf16[1,2,8,4096]{3,2,1,0:T(8,128)(2,1)}, u32[]{:S(2)}) copy-start(bf16[1,2,8,4096]{3,2,1,0:T(8,128)(2,1)} %refs_10_.2) | copy-start | bytes 393220
  0.7 1.6 %copy-start.12 = (bf16[1,2,8,4096]{3,2,1,0:T(8,128)(2,1)S(1)}, bf16[1,2,8,4096]{3,2,1,0:T(8,128)(2,1)}, u32[]{:S(2)}) copy-start(bf16[1,2,8,4096]{3,2,1,0:T(8,128)(2,1)} %refs_9_.2) | copy-start | bytes 393220
  0.7 1.6 %copy-start.11 = (bf16[1,2,8,4096]{3,2,1,0:T(8,128)(2,1)S(1)}, bf16[1,2,8,4096]{3,2,1,0:T(8,128)(2,1)}, u32[]{:S(2)}) copy-start(bf16[1,2,8,4096]{3,2,1,0:T(8,128)(2,1)} %refs_8_.2) | copy-start | bytes 393220
  0.7 1.6 %copy-start.10 = (bf16[1,2,8,4096]{3,2,1,0:T(8,128)(2,1)S(1)}, bf16[1,2,8,4096]{3,2,1,0:T(8,128)(2,1)}, u32[]{:S(2)}) copy-start(bf16[1,2,8,4096]{3,2,1,0:T(8,128)(2,1)} %refs_7_.1) | copy-start | bytes 393220
  2.4 6.3 %copy-start.2 = (bf16[1,2,8,4096]{3,2,1,0:T(8,128)(2,1)S(1)}, bf16[1,2,8,4096]{3,2,1,0:T(8,128)(2,1)}, u32[]{:S(2)}) copy-start(bf16[1,2,8,4096]{3,2,1,0:T(8,128)(2,1)} %refs_10_.3) | copy-start | bytes 393220
  2.4 6.3 %copy-start.5 = (bf16[1,8,4096]{2,1,0:T(8,128)(2,1)S(1)}, bf16[1,8,4096]{2,1,0:T(8,128)(2,1)}, u32[]{:S(2)}) copy-start(bf16[1,8,4096]{2,1,0:T(8,128)(2,1)} %refs_8_.3) | copy-start | bytes 196612
  2.4 6.3 %copy-start.6 = (bf16[1,8,4096]{2,1,0:T(8,128)(2,1)S(1)}, bf16[1,8,4096]{2,1,0:T(8,128)(2,1)}, u32[]{:S(2)}) copy-start(bf16[1,8,4096]{2,1,0:T(8,128)(2,1)} %refs_9_.3) | copy-start | bytes 196612
  4.1 15.6 %collective-permute-start.4 = (bf16[10,16,1024]{2,1,0:T(8,128)(2,1)S(1)}, bf16[10,16,1024]{2,1,0:T(8,128)(2,1)S(1)}, u32[]{:S(2)}, u32[]{:S(2)}) collective-permute-start(bf16[10,16,1024]{2,1,0:T(8,128)(2,1)S(1)} %get-tuple-element.37), channel_id=1, source_target_pairs={{0,3},{1,2},{2,1},{3,0},{4,7},{5,6},{6,5},{7,4},{8,11},{9,10},{10,... | collective-permute-start | bytes 983048 | tf_op jit(solution)/shard_map/ppermute | solution.py:304
  8.0 15.0 %collective-permute-start.5 = (bf16[10,16,1024]{2,1,0:T(8,128)(2,1)S(1)}, bf16[10,16,1024]{2,1,0:T(8,128)(2,1)S(1)}, u32[]{:S(2)}, u32[]{:S(2)}) collective-permute-start(bf16[10,16,1024]{2,1,0:T(8,128)(2,1)S(1)} %get-tuple-element.38), channel_id=1, source_target_pairs={{0,1},{1,0},{2,3},{3,2},{4,5},{5,4},{6,7},{7,6},{8,9},{9,8},{10,11... | collective-permute-start | bytes 983048 | tf_op jit(solution)/shard_map/ppermute | solution.py:304
  8.6 16.0 %collective-permute-start.6 = (bf16[10,16,1024]{2,1,0:T(8,128)(2,1)S(1)}, bf16[10,16,1024]{2,1,0:T(8,128)(2,1)S(1)}, u32[]{:S(2)}, u32[]{:S(2)}) collective-permute-start(bf16[10,16,1024]{2,1,0:T(8,128)(2,1)S(1)} %get-tuple-element.39), channel_id=1, source_target_pairs={{0,2},{1,3},{2,0},{3,1},{4,6},{5,7},{6,4},{7,5},{8,10},{9,11},{10,... | collective-permute-start | bytes 983048 | tf_op jit(solution)/shard_map/ppermute | solution.py:304
  10.6 4.2 %collective-permute-start = (bf16[16,4096]{1,0:T(8,128)(2,1)S(1)}, bf16[16,4096]{1,0:T(8,128)(2,1)S(1)}, u32[]{:S(2)}, u32[]{:S(2)}) collective-permute-start(bf16[16,4096]{1,0:T(8,128)(2,1)S(1)} %get-tuple-element.26), channel_id=1, source_target_pairs={{0,4},{4,0},{8,12},{12,8},{16,20},{20,16},{24,28},{28,24},{1,5},{5... | collective-permute-start | bytes 393224 | tf_op jit(solution)/shard_map/ppermute | solution.py:35
  10.7 7.6 %collective-permute-start.2 = (bf16[16,4224]{1,0:T(8,128)(2,1)S(1)}, bf16[16,4224]{1,0:T(8,128)(2,1)S(1)}, u32[]{:S(2)}, u32[]{:S(2)}) collective-permute-start(bf16[16,4224]{1,0:T(8,128)(2,1)S(1)} %get-tuple-element.30), channel_id=1, source_target_pairs={{0,28},{4,8},{8,4},{12,16},{16,12},{20,24},{24,20},{28,0},{1,29},{... | collective-permute-start | bytes 405512 | tf_op jit(solution)/shard_map/ppermute | solution.py:34
  16.7 12.2 %collective-permute-start.1 = (bf16[16,4224]{1,0:T(8,128)(2,1)S(1)}, bf16[16,4224]{1,0:T(8,128)(2,1)S(1)}, u32[]{:S(2)}, u32[]{:S(2)}) collective-permute-start(bf16[16,4224]{1,0:T(8,128)(2,1)S(1)} %get-tuple-element.29), channel_id=1, source_target_pairs={{0,28},{4,8},{8,4},{12,16},{16,12},{20,24},{24,20},{28,0},{1,29},{... | collective-permute-start | bytes 405512 | tf_op jit(solution)/shard_map/ppermute | solution.py:34
  19.6 9.2 %collective-permute-start.3 = (bf16[16,4096]{1,0:T(8,128)(2,1)S(1)}, bf16[16,4096]{1,0:T(8,128)(2,1)S(1)}, u32[]{:S(2)}, u32[]{:S(2)}) collective-permute-start(bf16[16,4096]{1,0:T(8,128)(2,1)S(1)} %get-tuple-element.35), channel_id=1, source_target_pairs={{0,4},{4,0},{8,12},{12,8},{16,20},{20,16},{24,28},{28,24},{1,5},{5... | collective-permute-start | bytes 393224 | tf_op jit(solution)/shard_map/ppermute | solution.py:35
  19.7 5.7 %collective-permute-start.7 = (bf16[2,16,1024]{2,1,0:T(8,128)(2,1)S(1)}, bf16[2,16,1024]{2,1,0:T(8,128)(2,1)S(1)}, u32[]{:S(2)}, u32[]{:S(2)}) collective-permute-start(bf16[2,16,1024]{2,1,0:T(8,128)(2,1)S(1)} %get-tuple-element.41), channel_id=1, source_target_pairs={{0,3},{1,2},{2,1},{3,0},{4,7},{5,6},{6,5},{7,4},{8,11},{9,10},{10,... | collective-permute-start | bytes 196616 | tf_op jit(solution)/shard_map/ppermute | solution.py:304
  23.1 4.3 %collective-permute-start.8 = (bf16[2,16,1024]{2,1,0:T(8,128)(2,1)S(1)}, bf16[2,16,1024]{2,1,0:T(8,128)(2,1)S(1)}, u32[]{:S(2)}, u32[]{:S(2)}) collective-permute-start(bf16[2,16,1024]{2,1,0:T(8,128)(2,1)S(1)} %get-tuple-element.42), channel_id=1, source_target_pairs={{0,1},{1,0},{2,3},{3,2},{4,5},{5,4},{6,7},{7,6},{8,9},{9,8},{10,11... | collective-permute-start | bytes 196616 | tf_op jit(solution)/shard_map/ppermute | solution.py:304
  24.6 4.3 %collective-permute-start.9 = (bf16[2,16,1024]{2,1,0:T(8,128)(2,1)S(1)}, bf16[2,16,1024]{2,1,0:T(8,128)(2,1)S(1)}, u32[]{:S(2)}, u32[]{:S(2)}) collective-permute-start(bf16[2,16,1024]{2,1,0:T(8,128)(2,1)S(1)} %get-tuple-element.43), channel_id=1, source_target_pairs={{0,2},{1,3},{2,0},{3,1},{4,6},{5,7},{6,4},{7,5},{8,10},{9,11},{10,... | collective-permute-start | bytes 196616 | tf_op jit(solution)/shard_map/ppermute | solution.py:304

commit v16 on v15

--- a/solution.py
+++ b/solution.py
@@ -13,7 +13,7 @@
 LIGHT = 10 ** 4
 PAD = BLOCK
 C_STREAMS = LIGHT
-C_NEAR_PHASE = 5 * 10 ** 8
+C_NEAR_PHASE = LIGHT
 C_FAR_PHASE = LIGHT
 
 

time: 30.2 us -> 30.2 us (level)
  waiting for transfers between devices: 5.36 us -> 5.77 us
  starting transfers between devices: 13.9 us -> 13.5 us
    ppermute x2, waiting for transfers between devices: 0.01 us -> 1.35 us  [swap_sections(): near = lax.ppermute(near, 'section', [(i, i ^ 1) for i in range(count)])]
    ppermute x2, starting transfers between devices: 4.61 us -> 3.41 us  [swap_sections(): lax.ppermute(far, 'section', [(i, (i + 2 * (i % 2) - 1) % count) for i in...]
    ppermute x2, waiting for transfers between devices: 1.06 us -> 0.37 us  [swap_sections(): lax.ppermute(far, 'section', [(i, (i + 2 * (i % 2) - 1) % count) for i in...]
    ppermute x6, starting transfers between devices: 9.11 us -> 9.67 us  [to_replicas(): lax.ppermute(parts[step], 'dp', swap_route(step, count))]
  transfers between devices with their start and end apart: 10 -> 10, of which waited for: 4 -> 5; matrix products, arithmetic and copies ran while one was open for 0% -> 0% of each run, Pallas kernels for 18% -> 18%
where the time goes in v16:
time: 30.2 us; the launch traced here: 30 us
  starting transfers between devices  13.5 us (45%)
  Pallas kernels  8.34 us (28%)
  waiting for transfers between devices  5.77 us (19%)
  local copies, waits for them, and re-layouts  1.66 us (5%)
  between operations  0.78 us (3%)
    ppermute x6, starting transfers between devices, to_replicas(): lax.ppermute(parts[step], 'dp', swap_route(step, count))  9.67 us
    pallas_call x7, Pallas kernels, call(): pl.pallas_call(kernel, out_shape=outs, in_specs=[pl.BlockSpec(memory_spac...  8.34 us
    ppermute x6, waiting for transfers between devices, to_replicas(): lax.ppermute(parts[step], 'dp', swap_route(step, count))  4.05 us
    ppermute x2, starting transfers between devices, swap_sections(): lax.ppermute(far, 'section', [(i, (i + 2 * (i % 2) - 1) % count) for i in...  3.41 us
    unnamed x28, local copies, waits for them, and re-layouts  1.66 us
    ppermute x2, waiting for transfers between devices, swap_sections(): near = lax.ppermute(near, 'section', [(i, i ^ 1) for i in range(count)])  1.35 us
  transfers between devices with their start and end apart: 10, of which 5 were waited for; matrix products, arithmetic and copies ran while one was open for 0% of the time, Pallas kernels for 18%

profile of v16, /device:TPU:0, one launch (start us, length us, event | category | flops | bytes accessed | tf_op | source)
XLA Modules:
  0.0 30.0 jit_solution(4479637937625091379)
XLA Ops:
  0.8 0.5 %copy-done.8 = s32[1,32]{1,0:T(1,128)S(1)} copy-done((s32[1,32]{1,0:T(1,128)S(1)}, s32[1,32]{1,0:T(1,128)}, u32[]{:S(2)}) %copy-start.8) | copy-done | bytes 152
  1.3 0.6 %copy-done.1 = bf16[1,32,128,128]{3,2,1,0:T(8,128)(2,1)S(1)} copy-done((bf16[1,32,128,128]{3,2,1,0:T(8,128)(2,1)S(1)}, bf16[1,32,128,128]{3,2,1,0:T(8,128)(2,1)}, u32[]{:S(2)}) %copy-start.1) | copy-done | bytes 1048600
  1.9 0.3 %copy-done = bf16[1,32,128,128]{3,2,1,0:T(8,128)(2,1)S(1)} copy-done((bf16[1,32,128,128]{3,2,1,0:T(8,128)(2,1)S(1)}, bf16[1,32,128,128]{3,2,1,0:T(8,128)(2,1)}, u32[]{:S(2)}) %copy-start) | copy-done | bytes 1048600
  2.3 0.0 copy-done.12
  2.4 1.7 %shard_map.182 = (f32[32,24,128]{2,1,0:T(8,128)S(1)}, bf16[16,4096]{1,0:T(8,128)(2,1)S(1)}, bf16[10,16,1024]{2,1,0:T(8,128)(2,1)S(1)}, bf16[10,16,1024]{2,1,0:T(...) custom-call(s32[1,32]{1,0:T(1,128)S(1)} %copy-done.7, s32[1,32]{1,0:T(1,128)S(1)} %copy-done.8, ...), custom_call_target="tpu_custom_call" | custom-call | flops 10000000000 | bytes 100000000 | tf_op jit(solution)/shard_map/pallas_call | solution.py:274
  4.1 4.0 %collective-permute-start.4 = (bf16[10,16,1024]{2,1,0:T(8,128)(2,1)S(1)}, bf16[10,16,1024]{2,1,0:T(8,128)(2,1)S(1)}, u32[]{:S(2)}, u32[]{:S(2)}) collective-permute-start(bf16[10,16,1024]{2,1,0:T(8,128)(2,1)S(1)} %get-tuple-element.37), channel_id=1, source_target_pairs={{0,3},{1,2},{2,1},{3,0},{4,7},{5,6},{6,5},{7,4},{8,11},{9,10},{10,... | collective-permute-start | bytes 983048 | tf_op jit(solution)/shard_map/ppermute | solution.py:304
  8.0 0.5 %collective-permute-start.5 = (bf16[10,16,1024]{2,1,0:T(8,128)(2,1)S(1)}, bf16[10,16,1024]{2,1,0:T(8,128)(2,1)S(1)}, u32[]{:S(2)}, u32[]{:S(2)}) collective-permute-start(bf16[10,16,1024]{2,1,0:T(8,128)(2,1)S(1)} %get-tuple-element.38), channel_id=1, source_target_pairs={{0,1},{1,0},{2,3},{3,2},{4,5},{5,4},{6,7},{7,6},{8,9},{9,8},{10,11... | collective-permute-start | bytes 983048 | tf_op jit(solution)/shard_map/ppermute | solution.py:304
  8.6 0.1 collective-permute-start.6
  8.7 1.9 %shard_map.183 = (bf16[16,4096]{1,0:T(8,128)(2,1)S(1)}, bf16[16,4224]{1,0:T(8,128)(2,1)S(1)}, f32[32,8,128]{2,1,0:T(8,128)S(1)}) custom-call(s32[1,32]{1,0:T(1,128)S(1)} %copy-done.7, s32[1,32]{1,0:T(1,128)S(1)} %copy-done.8, s32[1,2]{1,0:T(1,128)S(1)} %copy-done.9, bf16[1,32,128,128]{3,2,1,0:T(8,128)(2,1)S(1)} %copy-done, ...), custom_call_target="tpu_custom_call" | custom-call | flops 10000 | bytes 100 | tf_op jit(solution)/shard_map/pallas_call | solution.py:274
  10.6 2.7 %collective-permute-start.2 = (bf16[16,4224]{1,0:T(8,128)(2,1)S(1)}, bf16[16,4224]{1,0:T(8,128)(2,1)S(1)}, u32[]{:S(2)}, u32[]{:S(2)}) collective-permute-start(bf16[16,4224]{1,0:T(8,128)(2,1)S(1)} %get-tuple-element.30), channel_id=1, source_target_pairs={{0,28},{4,8},{8,4},{12,16},{16,12},{20,24},{24,20},{28,0},{1,29},{... | collective-permute-start | bytes 405512 | tf_op jit(solution)/shard_map/ppermute | solution.py:34
  13.3 1.3 %collective-permute-done.refs_4_ = bf16[16,4096]{1,0:T(8,128)(2,1)S(1)} collective-permute-done((bf16[16,4096]{1,0:T(8,128)(2,1)S(1)}, bf16[16,4096]{1,0:T(8,128)(2,1)S(1)}, u32[]{:S(2)}, u32[]{:S(2)}) %collective-permute-start) | collective-permute-done | bytes 131104 | tf_op jit(solution)/shard_map/ppermute | solution.py:35
  14.6 1.9 %shard_map.184 = (bf16[16,4224]{1,0:T(8,128)(2,1)S(1)}, bf16[2,16,1024]{2,1,0:T(8,128)(2,1)S(1)}, bf16[2,16,1024]{2,1,0:T(8,128)(2,1)S(1)}, bf16[2,16,1024]{2,1,0:T(8,128)(2,1)S(1)}, bf16[2,16,1024]{2,1,0:T(8,128)(2,1)S(1)}) custom-call(s32[1,32]{1,0:T(1,128)S(1)} %copy-done.7, s32[1,32]{1,0:T(1,128)S(1)} %copy-done.8, ...), custom_call_target="tpu_custom_call" | custom-call | flops 10000 | bytes 100 | tf_op jit(solution)/shard_map/pallas_call | solution.py:274
  16.5 0.7 %collective-permute-start.1 = (bf16[16,4224]{1,0:T(8,128)(2,1)S(1)}, bf16[16,4224]{1,0:T(8,128)(2,1)S(1)}, u32[]{:S(2)}, u32[]{:S(2)}) collective-permute-start(bf16[16,4224]{1,0:T(8,128)(2,1)S(1)} %get-tuple-element.29), channel_id=1, source_target_pairs={{0,28},{4,8},{8,4},{12,16},{16,12},{20,24},{24,20},{28,0},{1,29},{... | collective-permute-start | bytes 405512 | tf_op jit(solution)/shard_map/ppermute | solution.py:34
  17.2 0.4 %collective-permute-done.2.refs_4_ = bf16[16,4224]{1,0:T(8,128)(2,1)S(1)} collective-permute-done((bf16[16,4224]{1,0:T(8,128)(2,1)S(1)}, bf16[16,4224]{1,0:T(8,128)(2,1)S(1)}, u32[]{:S(2)}, u32[]{:S(2)}) %collective-permute-start.2) | collective-permute-done | bytes 135200 | tf_op jit(solution)/shard_map/ppermute | solution.py:34
  17.6 1.4 %shard_map.185 = (bf16[16,4096]{1,0:T(8,128)(2,1)S(1)}, bf16[2,16,1024]{2,1,0:T(8,128)(2,1)S(1)}, bf16[2,16,1024]{2,1,0:T(8,128)(2,1)S(1)}, bf16[2,16,1024]{2,1,0:T(8,128)(2,1)S(1)}, bf16[2,16,1024]{2,1,0:T(8,128)(2,1)S(1)}) custom-call(s32[1,32]{1,0:T(1,128)S(1)} %copy-done.7, s32[1,32]{1,0:T(1,128)S(1)} %copy-done.8, ...), custom_call_target="tpu_custom_call" | custom-call | flops 10000 | bytes 100 | tf_op jit(solution)/shard_map/pallas_call | solution.py:274
  19.0 0.4 %collective-permute-start.3 = (bf16[16,4096]{1,0:T(8,128)(2,1)S(1)}, bf16[16,4096]{1,0:T(8,128)(2,1)S(1)}, u32[]{:S(2)}, u32[]{:S(2)}) collective-permute-start(bf16[16,4096]{1,0:T(8,128)(2,1)S(1)} %get-tuple-element.35), channel_id=1, source_target_pairs={{0,4},{4,0},{8,12},{12,8},{16,20},{20,16},{24,28},{28,24},{1,5},{5... | collective-permute-start | bytes 393224 | tf_op jit(solution)/shard_map/ppermute | solution.py:35
  19.4 3.1 %collective-permute-start.7 = (bf16[2,16,1024]{2,1,0:T(8,128)(2,1)S(1)}, bf16[2,16,1024]{2,1,0:T(8,128)(2,1)S(1)}, u32[]{:S(2)}, u32[]{:S(2)}) collective-permute-start(bf16[2,16,1024]{2,1,0:T(8,128)(2,1)S(1)} %get-tuple-element.41), channel_id=1, source_target_pairs={{0,3},{1,2},{2,1},{3,0},{4,7},{5,6},{6,5},{7,4},{8,11},{9,10},{10,... | collective-permute-start | bytes 196616 | tf_op jit(solution)/shard_map/ppermute | solution.py:304
  22.4 0.6 %collective-permute-done.5.refs_2_.refs_5_ = bf16[10,16,1024]{2,1,0:T(8,128)(2,1)S(1)} collective-permute-done((bf16[10,16,1024]{2,1,0:T(8,128)(2,1)S(1)}, bf16[10,16,1024]{2,1,0:T(8,128)(2,1)S(1)}, u32[]{:S(2)}, u32[]{:S(2)}) %collective-permute-start.5) | collective-permute-done | bytes 327712 | tf_op jit(solution)/shard_map/ppermute | solution.py:304
  23.1 1.5 %collective-permute-start.8 = (bf16[2,16,1024]{2,1,0:T(8,128)(2,1)S(1)}, bf16[2,16,1024]{2,1,0:T(8,128)(2,1)S(1)}, u32[]{:S(2)}, u32[]{:S(2)}) collective-permute-start(bf16[2,16,1024]{2,1,0:T(8,128)(2,1)S(1)} %get-tuple-element.42), channel_id=1, source_target_pairs={{0,1},{1,0},{2,3},{3,2},{4,5},{5,4},{6,7},{7,6},{8,9},{9,8},{10,11... | collective-permute-start | bytes 196616 | tf_op jit(solution)/shard_map/ppermute | solution.py:304
  24.6 0.5 %collective-permute-start.9 = (bf16[2,16,1024]{2,1,0:T(8,128)(2,1)S(1)}, bf16[2,16,1024]{2,1,0:T(8,128)(2,1)S(1)}, u32[]{:S(2)}, u32[]{:S(2)}) collective-permute-start(bf16[2,16,1024]{2,1,0:T(8,128)(2,1)S(1)} %get-tuple-element.43), channel_id=1, source_target_pairs={{0,2},{1,3},{2,0},{3,1},{4,6},{5,7},{6,4},{7,5},{8,10},{9,11},{10,... | collective-permute-start | bytes 196616 | tf_op jit(solution)/shard_map/ppermute | solution.py:304
  25.1 0.3 %shard_map.186.refs_2_ = f32[2,8,128,128]{3,2,1,0:T(8,128)S(1)} custom-call(bf16[10,16,1024]{2,1,0:T(8,128)(2,1)S(1)} %get-tuple-element.36.refs_0_.refs_3_, bf16[10,16,1024]{2,1,0:T(8,128)(2,1)S(1)} %collective-permute-done.4.refs_1_.refs_4_, bf16[10,16,1024]{2,1,0:T(8,128)(2,1)S(1)} %collective-permute-done.5.refs_2_.refs_5_, ...), custom_call_target="tpu_custom_call" | custom-call | flops 10000 | bytes 100 | tf_op jit(solution)/shard_map/pallas_call | solution.py:274
  25.4 1.9 %collective-permute-done.8.refs_9_ = bf16[2,16,1024]{2,1,0:T(8,128)(2,1)S(1)} collective-permute-done((bf16[2,16,1024]{2,1,0:T(8,128)(2,1)S(1)}, bf16[2,16,1024]{2,1,0:T(8,128)(2,1)S(1)}, u32[]{:S(2)}, u32[]{:S(2)}) %collective-permute-start.8) | collective-permute-done | bytes 65568 | tf_op jit(solution)/shard_map/ppermute | solution.py:304
  27.3 1.5 %collective-permute-done.9.refs_10_ = bf16[2,16,1024]{2,1,0:T(8,128)(2,1)S(1)} collective-permute-done((bf16[2,16,1024]{2,1,0:T(8,128)(2,1)S(1)}, bf16[2,16,1024]{2,1,0:T(8,128)(2,1)S(1)}, u32[]{:S(2)}, u32[]{:S(2)}) %collective-permute-start.9) | collective-permute-done | bytes 65568 | tf_op jit(solution)/shard_map/ppermute | solution.py:304
  28.8 1.2 %shard_map.187 = (bf16[1,8,4096]{2,1,0:T(8,128)(2,1)}, bf16[1,8,4096]{2,1,0:T(8,128)(2,1)}, bf16[1,8,4096]{2,1,0:T(8,128)(2,1)}, bf16[1,8,4096]{2,1,0:T(8,128)(2...) custom-call(bf16[16,4224]{1,0:T(8,128)(2,1)S(1)} %collective-permute-done.1.refs_0_, ...), custom_call_target="tpu_custom_call" | custom-call | flops 10000 | bytes 100 | tf_op jit(solution)/shard_map/pallas_call | solution.py:274
  (31 shorter events, 0.2 us)
Async XLA Ops:
  0.6 0.7 %copy-start.8 = (s32[1,32]{1,0:T(1,128)S(1)}, s32[1,32]{1,0:T(1,128)}, u32[]{:S(2)}) copy-start(s32[1,32]{1,0:T(1,128)} %refs_1_.7) | copy-start | bytes 388
  0.6 1.2 %copy-start.1 = (bf16[1,32,128,128]{3,2,1,0:T(8,128)(2,1)S(1)}, bf16[1,32,128,128]{3,2,1,0:T(8,128)(2,1)}, u32[]{:S(2)}) copy-start(bf16[1,32,128,128]{3,2,1,0:T(8,128)(2,1)} %refs_3_.7) | copy-start | bytes 3145732
  0.7 1.2 %copy-start.7 = (s32[1,32]{1,0:T(1,128)S(1)}, s32[1,32]{1,0:T(1,128)}, u32[]{:S(2)}) copy-start(s32[1,32]{1,0:T(1,128)} %refs_0_.7) | copy-start | bytes 388
  0.7 1.5 %copy-start = (bf16[1,32,128,128]{3,2,1,0:T(8,128)(2,1)S(1)}, bf16[1,32,128,128]{3,2,1,0:T(8,128)(2,1)}, u32[]{:S(2)}) copy-start(bf16[1,32,128,128]{3,2,1,0:T(8,128)(2,1)} %refs_2_.7) | copy-start | bytes 3145732
  0.7 1.5 %copy-start.4 = (bf16[1,8,4096]{2,1,0:T(8,128)(2,1)S(1)}, bf16[1,8,4096]{2,1,0:T(8,128)(2,1)}, u32[]{:S(2)}) copy-start(bf16[1,8,4096]{2,1,0:T(8,128)(2,1)} %refs_6_.3) | copy-start | bytes 196612
  0.7 1.5 %copy-start.3 = (bf16[1,8,4096]{2,1,0:T(8,128)(2,1)S(1)}, bf16[1,8,4096]{2,1,0:T(8,128)(2,1)}, u32[]{:S(2)}) copy-start(bf16[1,8,4096]{2,1,0:T(8,128)(2,1)} %refs_5_.3) | copy-start | bytes 196612
  0.7 1.5 %copy-start.9 = (s32[1,2]{1,0:T(1,128)S(1)}, s32[1,2]{1,0:T(1,128)}, u32[]{:S(2)}) copy-start(s32[1,2]{1,0:T(1,128)} %refs_2_.5) | copy-start | bytes 28
  0.7 1.6 %copy-start.13 = (bf16[1,2,8,4096]{3,2,1,0:T(8,128)(2,1)S(1)}, bf16[1,2,8,4096]{3,2,1,0:T(8,128)(2,1)}, u32[]{:S(2)}) copy-start(bf16[1,2,8,4096]{3,2,1,0:T(8,128)(2,1)} %refs_10_.2) | copy-start | bytes 393220
  0.7 1.6 %copy-start.12 = (bf16[1,2,8,4096]{3,2,1,0:T(8,128)(2,1)S(1)}, bf16[1,2,8,4096]{3,2,1,0:T(8,128)(2,1)}, u32[]{:S(2)}) copy-start(bf16[1,2,8,4096]{3,2,1,0:T(8,128)(2,1)} %refs_9_.2) | copy-start | bytes 393220
  0.7 1.6 %copy-start.11 = (bf16[1,2,8,4096]{3,2,1,0:T(8,128)(2,1)S(1)}, bf16[1,2,8,4096]{3,2,1,0:T(8,128)(2,1)}, u32[]{:S(2)}) copy-start(bf16[1,2,8,4096]{3,2,1,0:T(8,128)(2,1)} %refs_8_.2) | copy-start | bytes 393220
  0.7 1.6 %copy-start.10 = (bf16[1,2,8,4096]{3,2,1,0:T(8,128)(2,1)S(1)}, bf16[1,2,8,4096]{3,2,1,0:T(8,128)(2,1)}, u32[]{:S(2)}) copy-start(bf16[1,2,8,4096]{3,2,1,0:T(8,128)(2,1)} %refs_7_.1) | copy-start | bytes 393220
  2.4 6.3 %copy-start.2 = (bf16[1,2,8,4096]{3,2,1,0:T(8,128)(2,1)S(1)}, bf16[1,2,8,4096]{3,2,1,0:T(8,128)(2,1)}, u32[]{:S(2)}) copy-start(bf16[1,2,8,4096]{3,2,1,0:T(8,128)(2,1)} %refs_10_.3) | copy-start | bytes 393220
  2.4 6.3 %copy-start.5 = (bf16[1,8,4096]{2,1,0:T(8,128)(2,1)S(1)}, bf16[1,8,4096]{2,1,0:T(8,128)(2,1)}, u32[]{:S(2)}) copy-start(bf16[1,8,4096]{2,1,0:T(8,128)(2,1)} %refs_8_.3) | copy-start | bytes 196612
  2.4 6.3 %copy-start.6 = (bf16[1,8,4096]{2,1,0:T(8,128)(2,1)S(1)}, bf16[1,8,4096]{2,1,0:T(8,128)(2,1)}, u32[]{:S(2)}) copy-start(bf16[1,8,4096]{2,1,0:T(8,128)(2,1)} %refs_9_.3) | copy-start | bytes 196612
  4.1 15.3 %collective-permute-start.4 = (bf16[10,16,1024]{2,1,0:T(8,128)(2,1)S(1)}, bf16[10,16,1024]{2,1,0:T(8,128)(2,1)S(1)}, u32[]{:S(2)}, u32[]{:S(2)}) collective-permute-start(bf16[10,16,1024]{2,1,0:T(8,128)(2,1)S(1)} %get-tuple-element.37), channel_id=1, source_target_pairs={{0,3},{1,2},{2,1},{3,0},{4,7},{5,6},{6,5},{7,4},{8,11},{9,10},{10,... | collective-permute-start | bytes 983048 | tf_op jit(solution)/shard_map/ppermute | solution.py:304
  8.0 15.0 %collective-permute-start.5 = (bf16[10,16,1024]{2,1,0:T(8,128)(2,1)S(1)}, bf16[10,16,1024]{2,1,0:T(8,128)(2,1)S(1)}, u32[]{:S(2)}, u32[]{:S(2)}) collective-permute-start(bf16[10,16,1024]{2,1,0:T(8,128)(2,1)S(1)} %get-tuple-element.38), channel_id=1, source_target_pairs={{0,1},{1,0},{2,3},{3,2},{4,5},{5,4},{6,7},{7,6},{8,9},{9,8},{10,11... | collective-permute-start | bytes 983048 | tf_op jit(solution)/shard_map/ppermute | solution.py:304
  8.6 16.0 %collective-permute-start.6 = (bf16[10,16,1024]{2,1,0:T(8,128)(2,1)S(1)}, bf16[10,16,1024]{2,1,0:T(8,128)(2,1)S(1)}, u32[]{:S(2)}, u32[]{:S(2)}) collective-permute-start(bf16[10,16,1024]{2,1,0:T(8,128)(2,1)S(1)} %get-tuple-element.39), channel_id=1, source_target_pairs={{0,2},{1,3},{2,0},{3,1},{4,6},{5,7},{6,4},{7,5},{8,10},{9,11},{10,... | collective-permute-start | bytes 983048 | tf_op jit(solution)/shard_map/ppermute | solution.py:304
  10.6 7.0 %collective-permute-start.2 = (bf16[16,4224]{1,0:T(8,128)(2,1)S(1)}, bf16[16,4224]{1,0:T(8,128)(2,1)S(1)}, u32[]{:S(2)}, u32[]{:S(2)}) collective-permute-start(bf16[16,4224]{1,0:T(8,128)(2,1)S(1)} %get-tuple-element.30), channel_id=1, source_target_pairs={{0,28},{4,8},{8,4},{12,16},{16,12},{20,24},{24,20},{28,0},{1,29},{... | collective-permute-start | bytes 405512 | tf_op jit(solution)/shard_map/ppermute | solution.py:34
  13.3 1.3 %collective-permute-start = (bf16[16,4096]{1,0:T(8,128)(2,1)S(1)}, bf16[16,4096]{1,0:T(8,128)(2,1)S(1)}, u32[]{:S(2)}, u32[]{:S(2)}) collective-permute-start(bf16[16,4096]{1,0:T(8,128)(2,1)S(1)} %get-tuple-element.26), channel_id=1, source_target_pairs={{0,4},{4,0},{8,12},{12,8},{16,20},{20,16},{24,28},{28,24},{1,5},{5... | collective-permute-start | bytes 393224 | tf_op jit(solution)/shard_map/ppermute | solution.py:35
  16.5 12.3 %collective-permute-start.1 = (bf16[16,4224]{1,0:T(8,128)(2,1)S(1)}, bf16[16,4224]{1,0:T(8,128)(2,1)S(1)}, u32[]{:S(2)}, u32[]{:S(2)}) collective-permute-start(bf16[16,4224]{1,0:T(8,128)(2,1)S(1)} %get-tuple-element.29), channel_id=1, source_target_pairs={{0,28},{4,8},{8,4},{12,16},{16,12},{20,24},{24,20},{28,0},{1,29},{... | collective-permute-start | bytes 405512 | tf_op jit(solution)/shard_map/ppermute | solution.py:34
  19.0 9.9 %collective-permute-start.3 = (bf16[16,4096]{1,0:T(8,128)(2,1)S(1)}, bf16[16,4096]{1,0:T(8,128)(2,1)S(1)}, u32[]{:S(2)}, u32[]{:S(2)}) collective-permute-start(bf16[16,4096]{1,0:T(8,128)(2,1)S(1)} %get-tuple-element.35), channel_id=1, source_target_pairs={{0,4},{4,0},{8,12},{12,8},{16,20},{20,16},{24,28},{28,24},{1,5},{5... | collective-permute-start | bytes 393224 | tf_op jit(solution)/shard_map/ppermute | solution.py:35
  19.4 6.1 %collective-permute-start.7 = (bf16[2,16,1024]{2,1,0:T(8,128)(2,1)S(1)}, bf16[2,16,1024]{2,1,0:T(8,128)(2,1)S(1)}, u32[]{:S(2)}, u32[]{:S(2)}) collective-permute-start(bf16[2,16,1024]{2,1,0:T(8,128)(2,1)S(1)} %get-tuple-element.41), channel_id=1, source_target_pairs={{0,3},{1,2},{2,1},{3,0},{4,7},{5,6},{6,5},{7,4},{8,11},{9,10},{10,... | collective-permute-start | bytes 196616 | tf_op jit(solution)/shard_map/ppermute | solution.py:304
  23.1 4.3 %collective-permute-start.8 = (bf16[2,16,1024]{2,1,0:T(8,128)(2,1)S(1)}, bf16[2,16,1024]{2,1,0:T(8,128)(2,1)S(1)}, u32[]{:S(2)}, u32[]{:S(2)}) collective-permute-start(bf16[2,16,1024]{2,1,0:T(8,128)(2,1)S(1)} %get-tuple-element.42), channel_id=1, source_target_pairs={{0,1},{1,0},{2,3},{3,2},{4,5},{5,4},{6,7},{7,6},{8,9},{9,8},{10,11... | collective-permute-start | bytes 196616 | tf_op jit(solution)/shard_map/ppermute | solution.py:304
  24.6 4.3 %collective-permute-start.9 = (bf16[2,16,1024]{2,1,0:T(8,128)(2,1)S(1)}, bf16[2,16,1024]{2,1,0:T(8,128)(2,1)S(1)}, u32[]{:S(2)}, u32[]{:S(2)}) collective-permute-start(bf16[2,16,1024]{2,1,0:T(8,128)(2,1)S(1)} %get-tuple-element.43), channel_id=1, source_target_pairs={{0,2},{1,3},{2,0},{3,1},{4,6},{5,7},{6,4},{7,5},{8,10},{9,11},{10,... | collective-permute-start | bytes 196616 | tf_op jit(solution)/shard_map/ppermute | solution.py:304

commit v17 on v16

--- a/solution.py
+++ b/solution.py
@@ -282,6 +282,17 @@
     )(*operands, *after)
 
 
+def hand_on(*refs):
+    half = len(refs) // 2
+    for source, target in zip(refs[:half], refs[half:]):
+        target[...] = source[...]
+
+
+def held_until(there, arrays):
+    shapes = [jax.ShapeDtypeStruct(x.shape, x.dtype) for x in arrays]
+    return call(hand_on, tuple(arrays), [pltpu.VMEM] * len(arrays), shapes, [], after=(there,))
+
+
 def on_device(w_up, up_index, w_down, down_index, tick_order, values_in, score_grad_in, tangent_in, state_adjoint_in,
               saved_back, saved_tan, saved_second, saved_second_tan, saved_second_grad):
     count = lax.axis_size("dp")
@@ -329,9 +340,10 @@
         body(far_phase, count, per), tables + (far, keep, keep_tan, *late), [smem] * 2 + [vmem] * (5 + count),
         [pair] + two, scratch, cost=C_FAR_PHASE)
     near, far = swap_sections(near_out, far_out)
-    late = to_replicas(late)
+    late = to_replicas([late[0], *held_until(near, late[1:2]), *late[2:]])
     (grads,) = call(
-        body(early_grads, count, per), tuple(early), [vmem] * count, [shape((2, per, BLOCK, BLOCK), F32)], [])
+        body(early_grads, count, per), tuple(early), [vmem] * count, [shape((2, per, BLOCK, BLOCK), F32)], [],
+        after=(far,))
     stream = shape((1,) + values_in.shape[1:], BF16)
     grad = shape((1, per, BLOCK, BLOCK), BF16)
     return tuple(call(

time: 30.2 us -> 29.1 us (0.964)
  starting transfers between devices: 13.5 us -> 12.3 us
    ppermute x6, waiting for transfers between devices: 4.05 us -> 2.43 us  [to_replicas(): lax.ppermute(parts[step], 'dp', swap_route(step, count))]
    ppermute x2, waiting for transfers between devices: 0.37 us -> 1.84 us  [swap_sections(): lax.ppermute(far, 'section', [(i, (i + 2 * (i % 2) - 1) % count) for i in...]
    ppermute x6, starting transfers between devices: 9.67 us -> 9.13 us  [to_replicas(): lax.ppermute(parts[step], 'dp', swap_route(step, count))]
    ppermute x2, starting transfers between devices: 0.38 us -> 0.07 us  [swap_sections(): near = lax.ppermute(near, 'section', [(i, i ^ 1) for i in range(count)])]
    pallas_call x7 -> x8, Pallas kernels: 8.34 us -> 8.32 us  [call(): pl.pallas_call(kernel, out_shape=outs, in_specs=[pl.BlockSpec(memory_spac...]
  transfers between devices with their start and end apart: 10 -> 10, of which waited for: 5 -> 7; matrix products, arithmetic and copies ran while one was open for 0% -> 0% of each run, Pallas kernels for 18% -> 19%
where the time goes in v17:
time: 29.1 us; the launch traced here: 29 us
  starting transfers between devices  12.3 us (42%)
  Pallas kernels  8.32 us (29%)
  waiting for transfers between devices  5.9 us (20%)
  local copies, waits for them, and re-layouts  1.66 us (6%)
  between operations  0.78 us (3%)
    ppermute x6, starting transfers between devices, to_replicas(): lax.ppermute(parts[step], 'dp', swap_route(step, count))  9.13 us
    pallas_call x8, Pallas kernels, call(): pl.pallas_call(kernel, out_shape=outs, in_specs=[pl.BlockSpec(memory_spac...  8.32 us
    ppermute x2, starting transfers between devices, swap_sections(): lax.ppermute(far, 'section', [(i, (i + 2 * (i % 2) - 1) % count) for i in...  3.12 us
    ppermute x6, waiting for transfers between devices, to_replicas(): lax.ppermute(parts[step], 'dp', swap_route(step, count))  2.43 us
    ppermute x2, waiting for transfers between devices, swap_sections(): lax.ppermute(far, 'section', [(i, (i + 2 * (i % 2) - 1) % count) for i in...  1.84 us
    unnamed x28, local copies, waits for them, and re-layouts  1.66 us
    ppermute x2, waiting for transfers between devices, swap_sections(): near = lax.ppermute(near, 'section', [(i, i ^ 1) for i in range(count)])  1.64 us
  transfers between devices with their start and end apart: 10, of which 7 were waited for; matrix products, arithmetic and copies ran while one was open for 0% of the time, Pallas kernels for 19%

profile of v17, /device:TPU:0, one launch (start us, length us, event | category | flops | bytes accessed | tf_op | source)
XLA Modules:
  0.0 29.0 jit_solution(1231350287686378432)
XLA Ops:
  0.8 0.5 %copy-done.8 = s32[1,32]{1,0:T(1,128)S(1)} copy-done((s32[1,32]{1,0:T(1,128)S(1)}, s32[1,32]{1,0:T(1,128)}, u32[]{:S(2)}) %copy-start.8) | copy-done | bytes 152
  1.3 0.6 %copy-done.1 = bf16[1,32,128,128]{3,2,1,0:T(8,128)(2,1)S(1)} copy-done((bf16[1,32,128,128]{3,2,1,0:T(8,128)(2,1)S(1)}, bf16[1,32,128,128]{3,2,1,0:T(8,128)(2,1)}, u32[]{:S(2)}) %copy-start.1) | copy-done | bytes 1048600
  1.9 0.3 %copy-done = bf16[1,32,128,128]{3,2,1,0:T(8,128)(2,1)S(1)} copy-done((bf16[1,32,128,128]{3,2,1,0:T(8,128)(2,1)S(1)}, bf16[1,32,128,128]{3,2,1,0:T(8,128)(2,1)}, u32[]{:S(2)}) %copy-start) | copy-done | bytes 1048600
  2.4 1.7 %shard_map.182 = (f32[32,24,128]{2,1,0:T(8,128)S(1)}, bf16[16,4096]{1,0:T(8,128)(2,1)S(1)}, bf16[10,16,1024]{2,1,0:T(8,128)(2,1)S(1)}, bf16[10,16,1024]{2,1,0:T(...) custom-call(s32[1,32]{1,0:T(1,128)S(1)} %copy-done.7, s32[1,32]{1,0:T(1,128)S(1)} %copy-done.8, ...), custom_call_target="tpu_custom_call" | custom-call | flops 10000000000 | bytes 100000000 | tf_op jit(solution)/shard_map/pallas_call | solution.py:274
  4.1 4.0 %collective-permute-start.4 = (bf16[10,16,1024]{2,1,0:T(8,128)(2,1)S(1)}, bf16[10,16,1024]{2,1,0:T(8,128)(2,1)S(1)}, u32[]{:S(2)}, u32[]{:S(2)}) collective-permute-start(bf16[10,16,1024]{2,1,0:T(8,128)(2,1)S(1)} %get-tuple-element.37), channel_id=1, source_target_pairs={{0,3},{1,2},{2,1},{3,0},{4,7},{5,6},{6,5},{7,4},{8,11},{9,10},{10,... | collective-permute-start | bytes 983048 | tf_op jit(solution)/shard_map/ppermute | solution.py:315
  8.1 1.9 %shard_map.183 = (bf16[16,4096]{1,0:T(8,128)(2,1)S(1)}, bf16[16,4224]{1,0:T(8,128)(2,1)S(1)}, f32[32,8,128]{2,1,0:T(8,128)S(1)}) custom-call(s32[1,32]{1,0:T(1,128)S(1)} %copy-done.7, s32[1,32]{1,0:T(1,128)S(1)} %copy-done.8, s32[1,2]{1,0:T(1,128)S(1)} %copy-done.9, bf16[1,32,128,128]{3,2,1,0:T(8,128)(2,1)S(1)} %copy-done, ...), custom_call_target="tpu_custom_call" | custom-call | flops 10000 | bytes 100 | tf_op jit(solution)/shard_map/pallas_call | solution.py:274
  9.9 2.8 %collective-permute-start.2 = (bf16[16,4224]{1,0:T(8,128)(2,1)S(1)}, bf16[16,4224]{1,0:T(8,128)(2,1)S(1)}, u32[]{:S(2)}, u32[]{:S(2)}) collective-permute-start(bf16[16,4224]{1,0:T(8,128)(2,1)S(1)} %get-tuple-element.30), channel_id=1, source_target_pairs={{0,28},{4,8},{8,4},{12,16},{16,12},{20,24},{24,20},{28,0},{1,29},{... | collective-permute-start | bytes 405512 | tf_op jit(solution)/shard_map/ppermute | solution.py:34
  12.8 0.5 %collective-permute-start.5 = (bf16[10,16,1024]{2,1,0:T(8,128)(2,1)S(1)}, bf16[10,16,1024]{2,1,0:T(8,128)(2,1)S(1)}, u32[]{:S(2)}, u32[]{:S(2)}) collective-permute-start(bf16[10,16,1024]{2,1,0:T(8,128)(2,1)S(1)} %get-tuple-element.38), channel_id=1, source_target_pairs={{0,1},{1,0},{2,3},{3,2},{4,5},{5,4},{6,7},{7,6},{8,9},{9,8},{10,11... | collective-permute-start | bytes 983048 | tf_op jit(solution)/shard_map/ppermute | solution.py:315
  13.3 0.5 %collective-permute-start.6 = (bf16[10,16,1024]{2,1,0:T(8,128)(2,1)S(1)}, bf16[10,16,1024]{2,1,0:T(8,128)(2,1)S(1)}, u32[]{:S(2)}, u32[]{:S(2)}) collective-permute-start(bf16[10,16,1024]{2,1,0:T(8,128)(2,1)S(1)} %get-tuple-element.39), channel_id=1, source_target_pairs={{0,2},{1,3},{2,0},{3,1},{4,6},{5,7},{6,4},{7,5},{8,10},{9,11},{10,... | collective-permute-start | bytes 983048 | tf_op jit(solution)/shard_map/ppermute | solution.py:315
  13.8 0.3 %collective-permute-done.refs_4_ = bf16[16,4096]{1,0:T(8,128)(2,1)S(1)} collective-permute-done((bf16[16,4096]{1,0:T(8,128)(2,1)S(1)}, bf16[16,4096]{1,0:T(8,128)(2,1)S(1)}, u32[]{:S(2)}, u32[]{:S(2)}) %collective-permute-start) | collective-permute-done | bytes 131104 | tf_op jit(solution)/shard_map/ppermute | solution.py:35
  14.1 1.9 %shard_map.184 = (bf16[16,4224]{1,0:T(8,128)(2,1)S(1)}, bf16[2,16,1024]{2,1,0:T(8,128)(2,1)S(1)}, bf16[2,16,1024]{2,1,0:T(8,128)(2,1)S(1)}, bf16[2,16,1024]{2,1,0:T(8,128)(2,1)S(1)}, bf16[2,16,1024]{2,1,0:T(8,128)(2,1)S(1)}) custom-call(s32[1,32]{1,0:T(1,128)S(1)} %copy-done.7, s32[1,32]{1,0:T(1,128)S(1)} %copy-done.8, ...), custom_call_target="tpu_custom_call" | custom-call | flops 10000 | bytes 100 | tf_op jit(solution)/shard_map/pallas_call | solution.py:274
  16.0 0.3 collective-permute-start.1
  16.3 1.1 %collective-permute-done.2.refs_4_ = bf16[16,4224]{1,0:T(8,128)(2,1)S(1)} collective-permute-done((bf16[16,4224]{1,0:T(8,128)(2,1)S(1)}, bf16[16,4224]{1,0:T(8,128)(2,1)S(1)}, u32[]{:S(2)}, u32[]{:S(2)}) %collective-permute-start.2) | collective-permute-done | bytes 135200 | tf_op jit(solution)/shard_map/ppermute | solution.py:34
  17.4 1.3 %shard_map.185 = (bf16[16,4096]{1,0:T(8,128)(2,1)S(1)}, bf16[2,16,1024]{2,1,0:T(8,128)(2,1)S(1)}, bf16[2,16,1024]{2,1,0:T(8,128)(2,1)S(1)}, bf16[2,16,1024]{2,1,0:T(8,128)(2,1)S(1)}, bf16[2,16,1024]{2,1,0:T(8,128)(2,1)S(1)}) custom-call(s32[1,32]{1,0:T(1,128)S(1)} %copy-done.7, s32[1,32]{1,0:T(1,128)S(1)} %copy-done.8, ...), custom_call_target="tpu_custom_call" | custom-call | flops 10000 | bytes 100 | tf_op jit(solution)/shard_map/pallas_call | solution.py:274
  18.9 1.3 %collective-permute-done.3.refs_1_ = bf16[16,4096]{1,0:T(8,128)(2,1)S(1)} collective-permute-done((bf16[16,4096]{1,0:T(8,128)(2,1)S(1)}, bf16[16,4096]{1,0:T(8,128)(2,1)S(1)}, u32[]{:S(2)}, u32[]{:S(2)}) %collective-permute-start.3) | collective-permute-done | bytes 131104 | tf_op jit(solution)/shard_map/ppermute | solution.py:35
  20.2 1.6 %collective-permute-start.7 = (bf16[2,16,1024]{2,1,0:T(8,128)(2,1)S(1)}, bf16[2,16,1024]{2,1,0:T(8,128)(2,1)S(1)}, u32[]{:S(2)}, u32[]{:S(2)}) collective-permute-start(bf16[2,16,1024]{2,1,0:T(8,128)(2,1)S(1)} %get-tuple-element.41), channel_id=1, source_target_pairs={{0,3},{1,2},{2,1},{3,0},{4,7},{5,6},{6,5},{7,4},{8,11},{9,10},{10,... | collective-permute-start | bytes 196616 | tf_op jit(solution)/shard_map/ppermute | solution.py:315
  21.8 0.7 %collective-permute-done.1.refs_4_.refs_0_ = bf16[16,4224]{1,0:T(8,128)(2,1)S(1)} collective-permute-done((bf16[16,4224]{1,0:T(8,128)(2,1)S(1)}, bf16[16,4224]{1,0:T(8,128)(2,1)S(1)}, u32[]{:S(2)}, u32[]{:S(2)}) %collective-permute-start.1) | collective-permute-done | bytes 135200 | tf_op jit(solution)/shard_map/ppermute | solution.py:34
  22.5 1.0 %collective-permute-start.9 = (bf16[2,16,1024]{2,1,0:T(8,128)(2,1)S(1)}, bf16[2,16,1024]{2,1,0:T(8,128)(2,1)S(1)}, u32[]{:S(2)}, u32[]{:S(2)}) collective-permute-start(bf16[2,16,1024]{2,1,0:T(8,128)(2,1)S(1)} %get-tuple-element.43), channel_id=1, source_target_pairs={{0,2},{1,3},{2,0},{3,1},{4,6},{5,7},{6,4},{7,5},{8,10},{9,11},{10,... | collective-permute-start | bytes 196616 | tf_op jit(solution)/shard_map/ppermute | solution.py:315
  23.5 1.5 %collective-permute-start.8 = (bf16[2,16,1024]{2,1,0:T(8,128)(2,1)S(1)}, bf16[2,16,1024]{2,1,0:T(8,128)(2,1)S(1)}, u32[]{:S(2)}, u32[]{:S(2)}) collective-permute-start(bf16[2,16,1024]{2,1,0:T(8,128)(2,1)S(1)} %shard_map.187), channel_id=1, source_target_pairs={{0,1},{1,0},{2,3},{3,2},{4,5},{5,4},{6,7},{7,6},{8,9},{9,8},{10,11... | collective-permute-start | bytes 196616 | tf_op jit(solution)/shard_map/ppermute | solution.py:315
  25.0 0.3 %shard_map.186.refs_2_ = f32[2,8,128,128]{3,2,1,0:T(8,128)S(1)} custom-call(bf16[10,16,1024]{2,1,0:T(8,128)(2,1)S(1)} %get-tuple-element.36.refs_0_.refs_3_, bf16[10,16,1024]{2,1,0:T(8,128)(2,1)S(1)} %collective-permute-done.4.refs_1_.refs_4_, bf16[10,16,1024]{2,1,0:T(8,128)(2,1)S(1)} %collective-permute-done.5.refs_2_.refs_5_, ...), custom_call_target="tpu_custom_call" | custom-call | flops 10000 | bytes 100 | tf_op jit(solution)/shard_map/pallas_call | solution.py:274
  25.4 0.1 collective-permute-done.7.refs_8_
  25.5 1.3 %collective-permute-done.9.refs_10_ = bf16[2,16,1024]{2,1,0:T(8,128)(2,1)S(1)} collective-permute-done((bf16[2,16,1024]{2,1,0:T(8,128)(2,1)S(1)}, bf16[2,16,1024]{2,1,0:T(8,128)(2,1)S(1)}, u32[]{:S(2)}, u32[]{:S(2)}) %collective-permute-start.9) | collective-permute-done | bytes 65568 | tf_op jit(solution)/shard_map/ppermute | solution.py:315
  26.8 1.0 %collective-permute-done.8.refs_9_ = bf16[2,16,1024]{2,1,0:T(8,128)(2,1)S(1)} collective-permute-done((bf16[2,16,1024]{2,1,0:T(8,128)(2,1)S(1)}, bf16[2,16,1024]{2,1,0:T(8,128)(2,1)S(1)}, u32[]{:S(2)}, u32[]{:S(2)}) %collective-permute-start.8) | collective-permute-done | bytes 65568 | tf_op jit(solution)/shard_map/ppermute | solution.py:315
  27.8 1.2 %shard_map.188 = (bf16[1,8,4096]{2,1,0:T(8,128)(2,1)}, bf16[1,8,4096]{2,1,0:T(8,128)(2,1)}, bf16[1,8,4096]{2,1,0:T(8,128)(2,1)}, bf16[1,8,4096]{2,1,0:T(8,128)(2...) custom-call(bf16[16,4224]{1,0:T(8,128)(2,1)S(1)} %collective-permute-done.1.refs_4_.refs_0_, ...), custom_call_target="tpu_custom_call" | custom-call | flops 10000 | bytes 100 | tf_op jit(solution)/shard_map/pallas_call | solution.py:274
  (32 shorter events, 0.3 us)
Async XLA Ops:
  0.6 0.7 %copy-start.8 = (s32[1,32]{1,0:T(1,128)S(1)}, s32[1,32]{1,0:T(1,128)}, u32[]{:S(2)}) copy-start(s32[1,32]{1,0:T(1,128)} %refs_1_.7) | copy-start | bytes 388
  0.6 1.2 %copy-start.1 = (bf16[1,32,128,128]{3,2,1,0:T(8,128)(2,1)S(1)}, bf16[1,32,128,128]{3,2,1,0:T(8,128)(2,1)}, u32[]{:S(2)}) copy-start(bf16[1,32,128,128]{3,2,1,0:T(8,128)(2,1)} %refs_3_.7) | copy-start | bytes 3145732
  0.7 1.2 %copy-start.7 = (s32[1,32]{1,0:T(1,128)S(1)}, s32[1,32]{1,0:T(1,128)}, u32[]{:S(2)}) copy-start(s32[1,32]{1,0:T(1,128)} %refs_0_.7) | copy-start | bytes 388
  0.7 1.5 %copy-start = (bf16[1,32,128,128]{3,2,1,0:T(8,128)(2,1)S(1)}, bf16[1,32,128,128]{3,2,1,0:T(8,128)(2,1)}, u32[]{:S(2)}) copy-start(bf16[1,32,128,128]{3,2,1,0:T(8,128)(2,1)} %refs_2_.7) | copy-start | bytes 3145732
  0.7 1.5 %copy-start.4 = (bf16[1,8,4096]{2,1,0:T(8,128)(2,1)S(1)}, bf16[1,8,4096]{2,1,0:T(8,128)(2,1)}, u32[]{:S(2)}) copy-start(bf16[1,8,4096]{2,1,0:T(8,128)(2,1)} %refs_6_.3) | copy-start | bytes 196612
  0.7 1.5 %copy-start.3 = (bf16[1,8,4096]{2,1,0:T(8,128)(2,1)S(1)}, bf16[1,8,4096]{2,1,0:T(8,128)(2,1)}, u32[]{:S(2)}) copy-start(bf16[1,8,4096]{2,1,0:T(8,128)(2,1)} %refs_5_.3) | copy-start | bytes 196612
  0.7 1.5 %copy-start.9 = (s32[1,2]{1,0:T(1,128)S(1)}, s32[1,2]{1,0:T(1,128)}, u32[]{:S(2)}) copy-start(s32[1,2]{1,0:T(1,128)} %refs_2_.5) | copy-start | bytes 28
  0.7 1.6 %copy-start.13 = (bf16[1,2,8,4096]{3,2,1,0:T(8,128)(2,1)S(1)}, bf16[1,2,8,4096]{3,2,1,0:T(8,128)(2,1)}, u32[]{:S(2)}) copy-start(bf16[1,2,8,4096]{3,2,1,0:T(8,128)(2,1)} %refs_10_.2) | copy-start | bytes 393220
  0.7 1.6 %copy-start.12 = (bf16[1,2,8,4096]{3,2,1,0:T(8,128)(2,1)S(1)}, bf16[1,2,8,4096]{3,2,1,0:T(8,128)(2,1)}, u32[]{:S(2)}) copy-start(bf16[1,2,8,4096]{3,2,1,0:T(8,128)(2,1)} %refs_9_.2) | copy-start | bytes 393220
  0.7 1.6 %copy-start.11 = (bf16[1,2,8,4096]{3,2,1,0:T(8,128)(2,1)S(1)}, bf16[1,2,8,4096]{3,2,1,0:T(8,128)(2,1)}, u32[]{:S(2)}) copy-start(bf16[1,2,8,4096]{3,2,1,0:T(8,128)(2,1)} %refs_8_.2) | copy-start | bytes 393220
  0.7 1.6 %copy-start.10 = (bf16[1,2,8,4096]{3,2,1,0:T(8,128)(2,1)S(1)}, bf16[1,2,8,4096]{3,2,1,0:T(8,128)(2,1)}, u32[]{:S(2)}) copy-start(bf16[1,2,8,4096]{3,2,1,0:T(8,128)(2,1)} %refs_7_.1) | copy-start | bytes 393220
  2.4 5.7 %copy-start.2 = (bf16[1,2,8,4096]{3,2,1,0:T(8,128)(2,1)S(1)}, bf16[1,2,8,4096]{3,2,1,0:T(8,128)(2,1)}, u32[]{:S(2)}) copy-start(bf16[1,2,8,4096]{3,2,1,0:T(8,128)(2,1)} %refs_10_.3) | copy-start | bytes 393220
  2.4 5.7 %copy-start.5 = (bf16[1,8,4096]{2,1,0:T(8,128)(2,1)S(1)}, bf16[1,8,4096]{2,1,0:T(8,128)(2,1)}, u32[]{:S(2)}) copy-start(bf16[1,8,4096]{2,1,0:T(8,128)(2,1)} %refs_8_.3) | copy-start | bytes 196612
  2.4 5.7 %copy-start.6 = (bf16[1,8,4096]{2,1,0:T(8,128)(2,1)S(1)}, bf16[1,8,4096]{2,1,0:T(8,128)(2,1)}, u32[]{:S(2)}) copy-start(bf16[1,8,4096]{2,1,0:T(8,128)(2,1)} %refs_9_.3) | copy-start | bytes 196612
  4.1 19.5 %collective-permute-start.4 = (bf16[10,16,1024]{2,1,0:T(8,128)(2,1)S(1)}, bf16[10,16,1024]{2,1,0:T(8,128)(2,1)S(1)}, u32[]{:S(2)}, u32[]{:S(2)}) collective-permute-start(bf16[10,16,1024]{2,1,0:T(8,128)(2,1)S(1)} %get-tuple-element.37), channel_id=1, source_target_pairs={{0,3},{1,2},{2,1},{3,0},{4,7},{5,6},{6,5},{7,4},{8,11},{9,10},{10,... | collective-permute-start | bytes 983048 | tf_op jit(solution)/shard_map/ppermute | solution.py:315
  9.9 7.5 %collective-permute-start.2 = (bf16[16,4224]{1,0:T(8,128)(2,1)S(1)}, bf16[16,4224]{1,0:T(8,128)(2,1)S(1)}, u32[]{:S(2)}, u32[]{:S(2)}) collective-permute-start(bf16[16,4224]{1,0:T(8,128)(2,1)S(1)} %get-tuple-element.30), channel_id=1, source_target_pairs={{0,28},{4,8},{8,4},{12,16},{16,12},{20,24},{24,20},{28,0},{1,29},{... | collective-permute-start | bytes 405512 | tf_op jit(solution)/shard_map/ppermute | solution.py:34
  12.8 1.3 %collective-permute-start = (bf16[16,4096]{1,0:T(8,128)(2,1)S(1)}, bf16[16,4096]{1,0:T(8,128)(2,1)S(1)}, u32[]{:S(2)}, u32[]{:S(2)}) collective-permute-start(bf16[16,4096]{1,0:T(8,128)(2,1)S(1)} %get-tuple-element.26), channel_id=1, source_target_pairs={{0,4},{4,0},{8,12},{12,8},{16,20},{20,16},{24,28},{28,24},{1,5},{5... | collective-permute-start | bytes 393224 | tf_op jit(solution)/shard_map/ppermute | solution.py:35
  12.8 12.3 %collective-permute-start.5 = (bf16[10,16,1024]{2,1,0:T(8,128)(2,1)S(1)}, bf16[10,16,1024]{2,1,0:T(8,128)(2,1)S(1)}, u32[]{:S(2)}, u32[]{:S(2)}) collective-permute-start(bf16[10,16,1024]{2,1,0:T(8,128)(2,1)S(1)} %get-tuple-element.38), channel_id=1, source_target_pairs={{0,1},{1,0},{2,3},{3,2},{4,5},{5,4},{6,7},{7,6},{8,9},{9,8},{10,11... | collective-permute-start | bytes 983048 | tf_op jit(solution)/shard_map/ppermute | solution.py:315
  13.3 11.7 %collective-permute-start.6 = (bf16[10,16,1024]{2,1,0:T(8,128)(2,1)S(1)}, bf16[10,16,1024]{2,1,0:T(8,128)(2,1)S(1)}, u32[]{:S(2)}, u32[]{:S(2)}) collective-permute-start(bf16[10,16,1024]{2,1,0:T(8,128)(2,1)S(1)} %get-tuple-element.39), channel_id=1, source_target_pairs={{0,2},{1,3},{2,0},{3,1},{4,6},{5,7},{6,4},{7,5},{8,10},{9,11},{10,... | collective-permute-start | bytes 983048 | tf_op jit(solution)/shard_map/ppermute | solution.py:315
  16.0 6.5 %collective-permute-start.1 = (bf16[16,4224]{1,0:T(8,128)(2,1)S(1)}, bf16[16,4224]{1,0:T(8,128)(2,1)S(1)}, u32[]{:S(2)}, u32[]{:S(2)}) collective-permute-start(bf16[16,4224]{1,0:T(8,128)(2,1)S(1)} %get-tuple-element.29), channel_id=1, source_target_pairs={{0,28},{4,8},{8,4},{12,16},{16,12},{20,24},{24,20},{28,0},{1,29},{... | collective-permute-start | bytes 405512 | tf_op jit(solution)/shard_map/ppermute | solution.py:34
  18.8 1.4 %collective-permute-start.3 = (bf16[16,4096]{1,0:T(8,128)(2,1)S(1)}, bf16[16,4096]{1,0:T(8,128)(2,1)S(1)}, u32[]{:S(2)}, u32[]{:S(2)}) collective-permute-start(bf16[16,4096]{1,0:T(8,128)(2,1)S(1)} %get-tuple-element.35), channel_id=1, source_target_pairs={{0,4},{4,0},{8,12},{12,8},{16,20},{20,16},{24,28},{28,24},{1,5},{5... | collective-permute-start | bytes 393224 | tf_op jit(solution)/shard_map/ppermute | solution.py:35
  20.2 5.3 %collective-permute-start.7 = (bf16[2,16,1024]{2,1,0:T(8,128)(2,1)S(1)}, bf16[2,16,1024]{2,1,0:T(8,128)(2,1)S(1)}, u32[]{:S(2)}, u32[]{:S(2)}) collective-permute-start(bf16[2,16,1024]{2,1,0:T(8,128)(2,1)S(1)} %get-tuple-element.41), channel_id=1, source_target_pairs={{0,3},{1,2},{2,1},{3,0},{4,7},{5,6},{6,5},{7,4},{8,11},{9,10},{10,... | collective-permute-start | bytes 196616 | tf_op jit(solution)/shard_map/ppermute | solution.py:315
  22.5 4.3 %collective-permute-start.9 = (bf16[2,16,1024]{2,1,0:T(8,128)(2,1)S(1)}, bf16[2,16,1024]{2,1,0:T(8,128)(2,1)S(1)}, u32[]{:S(2)}, u32[]{:S(2)}) collective-permute-start(bf16[2,16,1024]{2,1,0:T(8,128)(2,1)S(1)} %get-tuple-element.43), channel_id=1, source_target_pairs={{0,2},{1,3},{2,0},{3,1},{4,6},{5,7},{6,4},{7,5},{8,10},{9,11},{10,... | collective-permute-start | bytes 196616 | tf_op jit(solution)/shard_map/ppermute | solution.py:315
  23.5 4.3 %collective-permute-start.8 = (bf16[2,16,1024]{2,1,0:T(8,128)(2,1)S(1)}, bf16[2,16,1024]{2,1,0:T(8,128)(2,1)S(1)}, u32[]{:S(2)}, u32[]{:S(2)}) collective-permute-start(bf16[2,16,1024]{2,1,0:T(8,128)(2,1)S(1)} %shard_map.187), channel_id=1, source_target_pairs={{0,1},{1,0},{2,3},{3,2},{4,5},{5,4},{6,7},{7,6},{8,9},{9,8},{10,11... | collective-permute-start | bytes 196616 | tf_op jit(solution)/shard_map/ppermute | solution.py:315

commit v18 on v17

--- a/solution.py
+++ b/solution.py
@@ -338,7 +338,7 @@
         cost=C_NEAR_PHASE)
     near_out, *late = call(
         body(far_phase, count, per), tables + (far, keep, keep_tan, *late), [smem] * 2 + [vmem] * (5 + count),
-        [pair] + two, scratch, cost=C_FAR_PHASE)
+        [pair] + two, scratch, cost=C_FAR_PHASE, after=(early[1],))
     near, far = swap_sections(near_out, far_out)
     late = to_replicas([late[0], *held_until(near, late[1:2]), *late[2:]])
     (grads,) = call(

time: 29.1 us -> 28.1 us (0.966)
  starting transfers between devices: 12.3 us -> 11.7 us
  waiting for transfers between devices: 5.9 us -> 5.53 us
    ppermute x2, waiting for transfers between devices: 1.64 us -> 0.3 us  [swap_sections(): near = lax.ppermute(near, 'section', [(i, i ^ 1) for i in range(count)])]
    ppermute x6, starting transfers between devices: 9.13 us -> 8.49 us  [to_replicas(): lax.ppermute(parts[step], 'dp', swap_route(step, count))]
    ppermute x6, waiting for transfers between devices: 2.43 us -> 2.95 us  [to_replicas(): lax.ppermute(parts[step], 'dp', swap_route(step, count))]
    ppermute x2, waiting for transfers between devices: 1.84 us -> 2.27 us  [swap_sections(): lax.ppermute(far, 'section', [(i, (i + 2 * (i % 2) - 1) % count) for i in...]
  transfers between devices with their start and end apart: 10 -> 10, of which waited for: 7 -> 6; matrix products, arithmetic and copies ran while one was open for 0% -> 0% of each run, Pallas kernels for 19% -> 20%
where the time goes in v18:
time: 28.1 us; the launch traced here: 28 us
  starting transfers between devices  11.7 us (42%)
  Pallas kernels  8.34 us (30%)
  waiting for transfers between devices  5.53 us (20%)
  local copies, waits for them, and re-layouts  1.66 us (6%)
  between operations  0.79 us (3%)
    ppermute x6, starting transfers between devices, to_replicas(): lax.ppermute(parts[step], 'dp', swap_route(step, count))  8.49 us
    pallas_call x8, Pallas kernels, call(): pl.pallas_call(kernel, out_shape=outs, in_specs=[pl.BlockSpec(memory_spac...  8.34 us
    ppermute x2, starting transfers between devices, swap_sections(): lax.ppermute(far, 'section', [(i, (i + 2 * (i % 2) - 1) % count) for i in...  3.12 us
    ppermute x6, waiting for transfers between devices, to_replicas(): lax.ppermute(parts[step], 'dp', swap_route(step, count))  2.95 us
    ppermute x2, waiting for transfers between devices, swap_sections(): lax.ppermute(far, 'section', [(i, (i + 2 * (i % 2) - 1) % count) for i in...  2.27 us
    unnamed x28, local copies, waits for them, and re-layouts  1.66 us
  transfers between devices with their start and end apart: 10, of which 6 were waited for; matrix products, arithmetic and copies ran while one was open for 0% of the time, Pallas kernels for 20%

profile of v18, /device:TPU:0, one launch (start us, length us, event | category | flops | bytes accessed | tf_op | source)
XLA Modules:
  0.0 28.0 jit_solution(10361525657645012529)
XLA Ops:
  0.8 0.5 %copy-done.8 = s32[1,32]{1,0:T(1,128)S(1)} copy-done((s32[1,32]{1,0:T(1,128)S(1)}, s32[1,32]{1,0:T(1,128)}, u32[]{:S(2)}) %copy-start.8) | copy-done | bytes 152
  1.3 0.6 %copy-done.1 = bf16[1,32,128,128]{3,2,1,0:T(8,128)(2,1)S(1)} copy-done((bf16[1,32,128,128]{3,2,1,0:T(8,128)(2,1)S(1)}, bf16[1,32,128,128]{3,2,1,0:T(8,128)(2,1)}, u32[]{:S(2)}) %copy-start.1) | copy-done | bytes 1048600
  1.9 0.3 %copy-done = bf16[1,32,128,128]{3,2,1,0:T(8,128)(2,1)S(1)} copy-done((bf16[1,32,128,128]{3,2,1,0:T(8,128)(2,1)S(1)}, bf16[1,32,128,128]{3,2,1,0:T(8,128)(2,1)}, u32[]{:S(2)}) %copy-start) | copy-done | bytes 1048600
  2.4 1.7 %shard_map.182 = (f32[32,24,128]{2,1,0:T(8,128)S(1)}, bf16[16,4096]{1,0:T(8,128)(2,1)S(1)}, bf16[10,16,1024]{2,1,0:T(8,128)(2,1)S(1)}, bf16[10,16,1024]{2,1,0:T(...) custom-call(s32[1,32]{1,0:T(1,128)S(1)} %copy-done.7, s32[1,32]{1,0:T(1,128)S(1)} %copy-done.8, ...), custom_call_target="tpu_custom_call" | custom-call | flops 10000000000 | bytes 100000000 | tf_op jit(solution)/shard_map/pallas_call | solution.py:274
  4.1 4.0 %collective-permute-start.3 = (bf16[10,16,1024]{2,1,0:T(8,128)(2,1)S(1)}, bf16[10,16,1024]{2,1,0:T(8,128)(2,1)S(1)}, u32[]{:S(2)}, u32[]{:S(2)}) collective-permute-start(bf16[10,16,1024]{2,1,0:T(8,128)(2,1)S(1)} %get-tuple-element.35), channel_id=1, source_target_pairs={{0,3},{1,2},{2,1},{3,0},{4,7},{5,6},{6,5},{7,4},{8,11},{9,10},{10,... | collective-permute-start | bytes 983048 | tf_op jit(solution)/shard_map/ppermute | solution.py:315
  8.1 1.9 %shard_map.183 = (bf16[16,4096]{1,0:T(8,128)(2,1)S(1)}, bf16[16,4224]{1,0:T(8,128)(2,1)S(1)}, f32[32,8,128]{2,1,0:T(8,128)S(1)}) custom-call(s32[1,32]{1,0:T(1,128)S(1)} %copy-done.7, s32[1,32]{1,0:T(1,128)S(1)} %copy-done.8, s32[1,2]{1,0:T(1,128)S(1)} %copy-done.9, bf16[1,32,128,128]{3,2,1,0:T(8,128)(2,1)S(1)} %copy-done, ...), custom_call_target="tpu_custom_call" | custom-call | flops 10000 | bytes 100 | tf_op jit(solution)/shard_map/pallas_call | solution.py:274
  10.0 2.8 %collective-permute-start.2 = (bf16[16,4224]{1,0:T(8,128)(2,1)S(1)}, bf16[16,4224]{1,0:T(8,128)(2,1)S(1)}, u32[]{:S(2)}, u32[]{:S(2)}) collective-permute-start(bf16[16,4224]{1,0:T(8,128)(2,1)S(1)} %get-tuple-element.30), channel_id=1, source_target_pairs={{0,28},{4,8},{8,4},{12,16},{16,12},{20,24},{24,20},{28,0},{1,29},{... | collective-permute-start | bytes 405512 | tf_op jit(solution)/shard_map/ppermute | solution.py:34
  12.8 0.5 %collective-permute-start.5 = (bf16[10,16,1024]{2,1,0:T(8,128)(2,1)S(1)}, bf16[10,16,1024]{2,1,0:T(8,128)(2,1)S(1)}, u32[]{:S(2)}, u32[]{:S(2)}) collective-permute-start(bf16[10,16,1024]{2,1,0:T(8,128)(2,1)S(1)} %get-tuple-element.38), channel_id=1, source_target_pairs={{0,1},{1,0},{2,3},{3,2},{4,5},{5,4},{6,7},{7,6},{8,9},{9,8},{10,11... | collective-permute-start | bytes 983048 | tf_op jit(solution)/shard_map/ppermute | solution.py:315
  13.3 0.5 %collective-permute-start.6 = (bf16[10,16,1024]{2,1,0:T(8,128)(2,1)S(1)}, bf16[10,16,1024]{2,1,0:T(8,128)(2,1)S(1)}, u32[]{:S(2)}, u32[]{:S(2)}) collective-permute-start(bf16[10,16,1024]{2,1,0:T(8,128)(2,1)S(1)} %get-tuple-element.39), channel_id=1, source_target_pairs={{0,2},{1,3},{2,0},{3,1},{4,6},{5,7},{6,4},{7,5},{8,10},{9,11},{10,... | collective-permute-start | bytes 983048 | tf_op jit(solution)/shard_map/ppermute | solution.py:315
  13.8 0.3 %collective-permute-done.refs_4_ = bf16[16,4096]{1,0:T(8,128)(2,1)S(1)} collective-permute-done((bf16[16,4096]{1,0:T(8,128)(2,1)S(1)}, bf16[16,4096]{1,0:T(8,128)(2,1)S(1)}, u32[]{:S(2)}, u32[]{:S(2)}) %collective-permute-start) | collective-permute-done | bytes 131104 | tf_op jit(solution)/shard_map/ppermute | solution.py:35
  14.1 1.9 %shard_map.184 = (bf16[16,4224]{1,0:T(8,128)(2,1)S(1)}, bf16[2,16,1024]{2,1,0:T(8,128)(2,1)S(1)}, bf16[2,16,1024]{2,1,0:T(8,128)(2,1)S(1)}, bf16[2,16,1024]{2,1,0:T(8,128)(2,1)S(1)}, bf16[2,16,1024]{2,1,0:T(8,128)(2,1)S(1)}) custom-call(s32[1,32]{1,0:T(1,128)S(1)} %copy-done.7, s32[1,32]{1,0:T(1,128)S(1)} %copy-done.8, ...), custom_call_target="tpu_custom_call" | custom-call | flops 10000 | bytes 100 | tf_op jit(solution)/shard_map/pallas_call | solution.py:274
  16.0 0.3 %collective-permute-start.1 = (bf16[16,4224]{1,0:T(8,128)(2,1)S(1)}, bf16[16,4224]{1,0:T(8,128)(2,1)S(1)}, u32[]{:S(2)}, u32[]{:S(2)}) collective-permute-start(bf16[16,4224]{1,0:T(8,128)(2,1)S(1)} %get-tuple-element.29), channel_id=1, source_target_pairs={{0,28},{4,8},{8,4},{12,16},{16,12},{20,24},{24,20},{28,0},{1,29},{... | collective-permute-start | bytes 405512 | tf_op jit(solution)/shard_map/ppermute | solution.py:34
  16.3 1.1 %collective-permute-done.2.refs_4_ = bf16[16,4224]{1,0:T(8,128)(2,1)S(1)} collective-permute-done((bf16[16,4224]{1,0:T(8,128)(2,1)S(1)}, bf16[16,4224]{1,0:T(8,128)(2,1)S(1)}, u32[]{:S(2)}, u32[]{:S(2)}) %collective-permute-start.2) | collective-permute-done | bytes 135200 | tf_op jit(solution)/shard_map/ppermute | solution.py:34
  17.4 1.4 %shard_map.185 = (bf16[16,4096]{1,0:T(8,128)(2,1)S(1)}, bf16[2,16,1024]{2,1,0:T(8,128)(2,1)S(1)}, bf16[2,16,1024]{2,1,0:T(8,128)(2,1)S(1)}, bf16[2,16,1024]{2,1,0:T(8,128)(2,1)S(1)}, bf16[2,16,1024]{2,1,0:T(8,128)(2,1)S(1)}) custom-call(s32[1,32]{1,0:T(1,128)S(1)} %copy-done.7, s32[1,32]{1,0:T(1,128)S(1)} %copy-done.8, ...), custom_call_target="tpu_custom_call" | custom-call | flops 10000 | bytes 100 | tf_op jit(solution)/shard_map/pallas_call | solution.py:274
  18.8 0.1 collective-permute-start.4
  18.9 2.0 %collective-permute-start.7 = (bf16[2,16,1024]{2,1,0:T(8,128)(2,1)S(1)}, bf16[2,16,1024]{2,1,0:T(8,128)(2,1)S(1)}, u32[]{:S(2)}, u32[]{:S(2)}) collective-permute-start(bf16[2,16,1024]{2,1,0:T(8,128)(2,1)S(1)} %get-tuple-element.41), channel_id=1, source_target_pairs={{0,3},{1,2},{2,1},{3,0},{4,7},{5,6},{6,5},{7,4},{8,11},{9,10},{10,... | collective-permute-start | bytes 196616 | tf_op jit(solution)/shard_map/ppermute | solution.py:315
  20.9 0.5 %collective-permute-start.9 = (bf16[2,16,1024]{2,1,0:T(8,128)(2,1)S(1)}, bf16[2,16,1024]{2,1,0:T(8,128)(2,1)S(1)}, u32[]{:S(2)}, u32[]{:S(2)}) collective-permute-start(bf16[2,16,1024]{2,1,0:T(8,128)(2,1)S(1)} %get-tuple-element.43), channel_id=1, source_target_pairs={{0,2},{1,3},{2,0},{3,1},{4,6},{5,7},{6,4},{7,5},{8,10},{9,11},{10,... | collective-permute-start | bytes 196616 | tf_op jit(solution)/shard_map/ppermute | solution.py:315
  21.4 1.2 %collective-permute-done.1.refs_4_.refs_0_ = bf16[16,4224]{1,0:T(8,128)(2,1)S(1)} collective-permute-done((bf16[16,4224]{1,0:T(8,128)(2,1)S(1)}, bf16[16,4224]{1,0:T(8,128)(2,1)S(1)}, u32[]{:S(2)}, u32[]{:S(2)}) %collective-permute-start.1) | collective-permute-done | bytes 135200 | tf_op jit(solution)/shard_map/ppermute | solution.py:34
  22.6 1.0 %collective-permute-start.8 = (bf16[2,16,1024]{2,1,0:T(8,128)(2,1)S(1)}, bf16[2,16,1024]{2,1,0:T(8,128)(2,1)S(1)}, u32[]{:S(2)}, u32[]{:S(2)}) collective-permute-start(bf16[2,16,1024]{2,1,0:T(8,128)(2,1)S(1)} %shard_map.187), channel_id=1, source_target_pairs={{0,1},{1,0},{2,3},{3,2},{4,5},{5,4},{6,7},{7,6},{8,9},{9,8},{10,11... | collective-permute-start | bytes 196616 | tf_op jit(solution)/shard_map/ppermute | solution.py:315
  23.5 1.2 %collective-permute-done.6.refs_3_.refs_6_ = bf16[10,16,1024]{2,1,0:T(8,128)(2,1)S(1)} collective-permute-done((bf16[10,16,1024]{2,1,0:T(8,128)(2,1)S(1)}, bf16[10,16,1024]{2,1,0:T(8,128)(2,1)S(1)}, u32[]{:S(2)}, u32[]{:S(2)}) %collective-permute-start.6) | collective-permute-done | bytes 327712 | tf_op jit(solution)/shard_map/ppermute | solution.py:315
  24.7 0.3 %shard_map.186.refs_2_ = f32[2,8,128,128]{3,2,1,0:T(8,128)S(1)} custom-call(bf16[10,16,1024]{2,1,0:T(8,128)(2,1)S(1)} %get-tuple-element.37.refs_0_.refs_3_, bf16[10,16,1024]{2,1,0:T(8,128)(2,1)S(1)} %collective-permute-done.3.refs_11_.refs_1_.refs_4_, bf16[10,16,1024]{2,1,0:T(8,128)(2,1)S(1)} %collective-permute-done.5.refs_2_.refs_5_, ...), custom_call_target="tpu_custom_call" | custom-call | flops 10000 | bytes 100 | tf_op jit(solution)/shard_map/pallas_call | solution.py:274
  25.1 0.9 %collective-permute-done.9.refs_10_ = bf16[2,16,1024]{2,1,0:T(8,128)(2,1)S(1)} collective-permute-done((bf16[2,16,1024]{2,1,0:T(8,128)(2,1)S(1)}, bf16[2,16,1024]{2,1,0:T(8,128)(2,1)S(1)}, u32[]{:S(2)}, u32[]{:S(2)}) %collective-permute-start.9) | collective-permute-done | bytes 65568 | tf_op jit(solution)/shard_map/ppermute | solution.py:315
  26.0 0.9 %collective-permute-done.8.refs_9_ = bf16[2,16,1024]{2,1,0:T(8,128)(2,1)S(1)} collective-permute-done((bf16[2,16,1024]{2,1,0:T(8,128)(2,1)S(1)}, bf16[2,16,1024]{2,1,0:T(8,128)(2,1)S(1)}, u32[]{:S(2)}, u32[]{:S(2)}) %collective-permute-start.8) | collective-permute-done | bytes 65568 | tf_op jit(solution)/shard_map/ppermute | solution.py:315
  26.8 1.2 %shard_map.188 = (bf16[1,8,4096]{2,1,0:T(8,128)(2,1)}, bf16[1,8,4096]{2,1,0:T(8,128)(2,1)}, bf16[1,8,4096]{2,1,0:T(8,128)(2,1)}, bf16[1,8,4096]{2,1,0:T(8,128)(2...) custom-call(bf16[16,4224]{1,0:T(8,128)(2,1)S(1)} %collective-permute-done.1.refs_4_.refs_0_, ...), custom_call_target="tpu_custom_call" | custom-call | flops 10000 | bytes 100 | tf_op jit(solution)/shard_map/pallas_call | solution.py:274
  (32 shorter events, 0.2 us)
Async XLA Ops:
  0.6 0.7 %copy-start.8 = (s32[1,32]{1,0:T(1,128)S(1)}, s32[1,32]{1,0:T(1,128)}, u32[]{:S(2)}) copy-start(s32[1,32]{1,0:T(1,128)} %refs_1_.7) | copy-start | bytes 388
  0.6 1.2 %copy-start.1 = (bf16[1,32,128,128]{3,2,1,0:T(8,128)(2,1)S(1)}, bf16[1,32,128,128]{3,2,1,0:T(8,128)(2,1)}, u32[]{:S(2)}) copy-start(bf16[1,32,128,128]{3,2,1,0:T(8,128)(2,1)} %refs_3_.7) | copy-start | bytes 3145732
  0.7 1.2 %copy-start.7 = (s32[1,32]{1,0:T(1,128)S(1)}, s32[1,32]{1,0:T(1,128)}, u32[]{:S(2)}) copy-start(s32[1,32]{1,0:T(1,128)} %refs_0_.7) | copy-start | bytes 388
  0.7 1.5 %copy-start = (bf16[1,32,128,128]{3,2,1,0:T(8,128)(2,1)S(1)}, bf16[1,32,128,128]{3,2,1,0:T(8,128)(2,1)}, u32[]{:S(2)}) copy-start(bf16[1,32,128,128]{3,2,1,0:T(8,128)(2,1)} %refs_2_.7) | copy-start | bytes 3145732
  0.7 1.5 %copy-start.4 = (bf16[1,8,4096]{2,1,0:T(8,128)(2,1)S(1)}, bf16[1,8,4096]{2,1,0:T(8,128)(2,1)}, u32[]{:S(2)}) copy-start(bf16[1,8,4096]{2,1,0:T(8,128)(2,1)} %refs_6_.3) | copy-start | bytes 196612
  0.7 1.5 %copy-start.3 = (bf16[1,8,4096]{2,1,0:T(8,128)(2,1)S(1)}, bf16[1,8,4096]{2,1,0:T(8,128)(2,1)}, u32[]{:S(2)}) copy-start(bf16[1,8,4096]{2,1,0:T(8,128)(2,1)} %refs_5_.3) | copy-start | bytes 196612
  0.7 1.5 %copy-start.9 = (s32[1,2]{1,0:T(1,128)S(1)}, s32[1,2]{1,0:T(1,128)}, u32[]{:S(2)}) copy-start(s32[1,2]{1,0:T(1,128)} %refs_2_.5) | copy-start | bytes 28
  0.7 1.6 %copy-start.13 = (bf16[1,2,8,4096]{3,2,1,0:T(8,128)(2,1)S(1)}, bf16[1,2,8,4096]{3,2,1,0:T(8,128)(2,1)}, u32[]{:S(2)}) copy-start(bf16[1,2,8,4096]{3,2,1,0:T(8,128)(2,1)} %refs_10_.2) | copy-start | bytes 393220
  0.7 1.6 %copy-start.12 = (bf16[1,2,8,4096]{3,2,1,0:T(8,128)(2,1)S(1)}, bf16[1,2,8,4096]{3,2,1,0:T(8,128)(2,1)}, u32[]{:S(2)}) copy-start(bf16[1,2,8,4096]{3,2,1,0:T(8,128)(2,1)} %refs_9_.2) | copy-start | bytes 393220
  0.7 1.6 %copy-start.11 = (bf16[1,2,8,4096]{3,2,1,0:T(8,128)(2,1)S(1)}, bf16[1,2,8,4096]{3,2,1,0:T(8,128)(2,1)}, u32[]{:S(2)}) copy-start(bf16[1,2,8,4096]{3,2,1,0:T(8,128)(2,1)} %refs_8_.2) | copy-start | bytes 393220
  0.7 1.6 %copy-start.10 = (bf16[1,2,8,4096]{3,2,1,0:T(8,128)(2,1)S(1)}, bf16[1,2,8,4096]{3,2,1,0:T(8,128)(2,1)}, u32[]{:S(2)}) copy-start(bf16[1,2,8,4096]{3,2,1,0:T(8,128)(2,1)} %refs_7_.1) | copy-start | bytes 393220
  2.4 5.7 %copy-start.2 = (bf16[1,2,8,4096]{3,2,1,0:T(8,128)(2,1)S(1)}, bf16[1,2,8,4096]{3,2,1,0:T(8,128)(2,1)}, u32[]{:S(2)}) copy-start(bf16[1,2,8,4096]{3,2,1,0:T(8,128)(2,1)} %refs_10_.3) | copy-start | bytes 393220
  2.4 5.7 %copy-start.5 = (bf16[1,8,4096]{2,1,0:T(8,128)(2,1)S(1)}, bf16[1,8,4096]{2,1,0:T(8,128)(2,1)}, u32[]{:S(2)}) copy-start(bf16[1,8,4096]{2,1,0:T(8,128)(2,1)} %refs_8_.3) | copy-start | bytes 196612
  2.4 5.7 %copy-start.6 = (bf16[1,8,4096]{2,1,0:T(8,128)(2,1)S(1)}, bf16[1,8,4096]{2,1,0:T(8,128)(2,1)}, u32[]{:S(2)}) copy-start(bf16[1,8,4096]{2,1,0:T(8,128)(2,1)} %refs_9_.3) | copy-start | bytes 196612
  4.1 13.3 %collective-permute-start.3 = (bf16[10,16,1024]{2,1,0:T(8,128)(2,1)S(1)}, bf16[10,16,1024]{2,1,0:T(8,128)(2,1)S(1)}, u32[]{:S(2)}, u32[]{:S(2)}) collective-permute-start(bf16[10,16,1024]{2,1,0:T(8,128)(2,1)S(1)} %get-tuple-element.35), channel_id=1, source_target_pairs={{0,3},{1,2},{2,1},{3,0},{4,7},{5,6},{6,5},{7,4},{8,11},{9,10},{10,... | collective-permute-start | bytes 983048 | tf_op jit(solution)/shard_map/ppermute | solution.py:315
  10.0 7.5 %collective-permute-start.2 = (bf16[16,4224]{1,0:T(8,128)(2,1)S(1)}, bf16[16,4224]{1,0:T(8,128)(2,1)S(1)}, u32[]{:S(2)}, u32[]{:S(2)}) collective-permute-start(bf16[16,4224]{1,0:T(8,128)(2,1)S(1)} %get-tuple-element.30), channel_id=1, source_target_pairs={{0,28},{4,8},{8,4},{12,16},{16,12},{20,24},{24,20},{28,0},{1,29},{... | collective-permute-start | bytes 405512 | tf_op jit(solution)/shard_map/ppermute | solution.py:34
  12.8 1.3 %collective-permute-start = (bf16[16,4096]{1,0:T(8,128)(2,1)S(1)}, bf16[16,4096]{1,0:T(8,128)(2,1)S(1)}, u32[]{:S(2)}, u32[]{:S(2)}) collective-permute-start(bf16[16,4096]{1,0:T(8,128)(2,1)S(1)} %get-tuple-element.26), channel_id=1, source_target_pairs={{0,4},{4,0},{8,12},{12,8},{16,20},{20,16},{24,28},{28,24},{1,5},{5... | collective-permute-start | bytes 393224 | tf_op jit(solution)/shard_map/ppermute | solution.py:35
  12.8 10.7 %collective-permute-start.5 = (bf16[10,16,1024]{2,1,0:T(8,128)(2,1)S(1)}, bf16[10,16,1024]{2,1,0:T(8,128)(2,1)S(1)}, u32[]{:S(2)}, u32[]{:S(2)}) collective-permute-start(bf16[10,16,1024]{2,1,0:T(8,128)(2,1)S(1)} %get-tuple-element.38), channel_id=1, source_target_pairs={{0,1},{1,0},{2,3},{3,2},{4,5},{5,4},{6,7},{7,6},{8,9},{9,8},{10,11... | collective-permute-start | bytes 983048 | tf_op jit(solution)/shard_map/ppermute | solution.py:315
  13.3 11.4 %collective-permute-start.6 = (bf16[10,16,1024]{2,1,0:T(8,128)(2,1)S(1)}, bf16[10,16,1024]{2,1,0:T(8,128)(2,1)S(1)}, u32[]{:S(2)}, u32[]{:S(2)}) collective-permute-start(bf16[10,16,1024]{2,1,0:T(8,128)(2,1)S(1)} %get-tuple-element.39), channel_id=1, source_target_pairs={{0,2},{1,3},{2,0},{3,1},{4,6},{5,7},{6,4},{7,5},{8,10},{9,11},{10,... | collective-permute-start | bytes 983048 | tf_op jit(solution)/shard_map/ppermute | solution.py:315
  16.0 6.5 %collective-permute-start.1 = (bf16[16,4224]{1,0:T(8,128)(2,1)S(1)}, bf16[16,4224]{1,0:T(8,128)(2,1)S(1)}, u32[]{:S(2)}, u32[]{:S(2)}) collective-permute-start(bf16[16,4224]{1,0:T(8,128)(2,1)S(1)} %get-tuple-element.29), channel_id=1, source_target_pairs={{0,28},{4,8},{8,4},{12,16},{16,12},{20,24},{24,20},{28,0},{1,29},{... | collective-permute-start | bytes 405512 | tf_op jit(solution)/shard_map/ppermute | solution.py:34
  18.8 2.1 %collective-permute-start.4 = (bf16[16,4096]{1,0:T(8,128)(2,1)S(1)}, bf16[16,4096]{1,0:T(8,128)(2,1)S(1)}, u32[]{:S(2)}, u32[]{:S(2)}) collective-permute-start(bf16[16,4096]{1,0:T(8,128)(2,1)S(1)} %get-tuple-element.36), channel_id=1, source_target_pairs={{0,4},{4,0},{8,12},{12,8},{16,20},{20,16},{24,28},{28,24},{1,5},{5... | collective-permute-start | bytes 393224 | tf_op jit(solution)/shard_map/ppermute | solution.py:35
  18.9 6.2 %collective-permute-start.7 = (bf16[2,16,1024]{2,1,0:T(8,128)(2,1)S(1)}, bf16[2,16,1024]{2,1,0:T(8,128)(2,1)S(1)}, u32[]{:S(2)}, u32[]{:S(2)}) collective-permute-start(bf16[2,16,1024]{2,1,0:T(8,128)(2,1)S(1)} %get-tuple-element.41), channel_id=1, source_target_pairs={{0,3},{1,2},{2,1},{3,0},{4,7},{5,6},{6,5},{7,4},{8,11},{9,10},{10,... | collective-permute-start | bytes 196616 | tf_op jit(solution)/shard_map/ppermute | solution.py:315
  20.9 5.1 %collective-permute-start.9 = (bf16[2,16,1024]{2,1,0:T(8,128)(2,1)S(1)}, bf16[2,16,1024]{2,1,0:T(8,128)(2,1)S(1)}, u32[]{:S(2)}, u32[]{:S(2)}) collective-permute-start(bf16[2,16,1024]{2,1,0:T(8,128)(2,1)S(1)} %get-tuple-element.43), channel_id=1, source_target_pairs={{0,2},{1,3},{2,0},{3,1},{4,6},{5,7},{6,4},{7,5},{8,10},{9,11},{10,... | collective-permute-start | bytes 196616 | tf_op jit(solution)/shard_map/ppermute | solution.py:315
  22.6 4.3 %collective-permute-start.8 = (bf16[2,16,1024]{2,1,0:T(8,128)(2,1)S(1)}, bf16[2,16,1024]{2,1,0:T(8,128)(2,1)S(1)}, u32[]{:S(2)}, u32[]{:S(2)}) collective-permute-start(bf16[2,16,1024]{2,1,0:T(8,128)(2,1)S(1)} %shard_map.187), channel_id=1, source_target_pairs={{0,1},{1,0},{2,3},{3,2},{4,5},{5,4},{6,7},{7,6},{8,9},{9,8},{10,11... | collective-permute-start | bytes 196616 | tf_op jit(solution)/shard_map/ppermute | solution.py:315

commit v19 on v18

--- a/solution.py
+++ b/solution.py
@@ -238,18 +238,7 @@
 
 
 def early_grads(count, per, *refs):
-    early, grads = refs[:count], refs[count]
-    for place in range(per):
-        at = lanes(place)
-        for out, left, right in ((0, 0, 3), (1, 5, 8)):
-            xs = [early[source][left + k, :, at] for source in range(count) for k in range(2)]
-            es = [early[source][right + k, :, at] for source in range(count) for k in range(2)]
-            grads[out, place] = outer(xs, es)
-
-
-def finish(count, per, scale, far, near, grads, *rest):
-    early, late = rest[:count], rest[count:2 * count]
-    values, score, tangent, adjoint, grad_up, grad_down, came = rest[2 * count:]
+    early, (far, near, grads, values, score, tangent, adjoint, came) = refs[:count], refs[count:]
     take_in(near, far, came)
     moved = came[0].astype(F32)
     values[0] = moved[0:8].astype(BF16)
@@ -257,6 +246,17 @@
     moved = came[1].astype(F32)
     score[0] = moved[0:8].astype(BF16)
     adjoint[0] = moved[8:16].astype(BF16)
+    for place in range(per):
+        at = lanes(place)
+        for out, left, right in ((0, 0, 3), (1, 5, 8)):
+            xs = [early[source][left + k, :, at] for source in range(count) for k in range(2)]
+            es = [early[source][right + k, :, at] for source in range(count) for k in range(2)]
+            grads[out, place] = outer(xs, es)
+
+
+def finish(count, per, scale, grads, *rest):
+    early, late = rest[:count], rest[count:2 * count]
+    grad_up, grad_down = rest[2 * count:]
     for place in range(per):
         at = lanes(place)
         for k, (out, group) in enumerate(((grad_up, 2), (grad_down, 7))):
@@ -341,14 +341,14 @@
         [pair] + two, scratch, cost=C_FAR_PHASE, after=(early[1],))
     near, far = swap_sections(near_out, far_out)
     late = to_replicas([late[0], *held_until(near, late[1:2]), *late[2:]])
-    (grads,) = call(
-        body(early_grads, count, per), tuple(early), [vmem] * count, [shape((2, per, BLOCK, BLOCK), F32)], [],
-        after=(far,))
     stream = shape((1,) + values_in.shape[1:], BF16)
     grad = shape((1, per, BLOCK, BLOCK), BF16)
-    return tuple(call(
-        body(finish, count, per, scale), (far, near, grads, *early, *late), [vmem] * (3 + 2 * count),
-        [stream, stream, stream, stream, grad, grad], [vmem((2, 16, width), BF16)]))
+    grads, *streams = call(
+        body(early_grads, count, per), (*early, far, near), [vmem] * (count + 2),
+        [shape((2, per, BLOCK, BLOCK), F32)] + [stream] * 4, [vmem((2, 16, width), BF16)])
+    grads = call(
+        body(finish, count, per, scale), (grads, *early, *late), [vmem] * (1 + 2 * count), [grad] * 2, [])
+    return (*streams, *grads)
 
 
 def solution(mesh):

time: 28.1 us -> 28.1 us (level)
  waiting for transfers between devices: 5.53 us -> 4.9 us
  Pallas kernels: 8.34 us -> 8.94 us
    ppermute x6, waiting for transfers between devices: 2.95 us -> 2.33 us  [to_replicas(): lax.ppermute(parts[step], 'dp', swap_route(step, count))]
    pallas_call x8, Pallas kernels: 8.34 us -> 8.94 us  [call(): pl.pallas_call(kernel, out_shape=outs, in_specs=[pl.BlockSpec(memory_spac...]
  transfers between devices with their start and end apart: 10 -> 10, of which waited for: 6 -> 6; matrix products, arithmetic and copies ran while one was open for 0% -> 0% of each run, Pallas kernels for 20% -> 22%
where the time goes in v19:
time: 28.1 us; the launch traced here: 27.9 us
  starting transfers between devices  11.7 us (42%)
  Pallas kernels  8.94 us (32%)
  waiting for transfers between devices  4.9 us (17%)
  local copies, waits for them, and re-layouts  1.65 us (6%)
  between operations  0.78 us (3%)
    pallas_call x8, Pallas kernels, call(): pl.pallas_call(kernel, out_shape=outs, in_specs=[pl.BlockSpec(memory_spac...  8.94 us
    ppermute x6, starting transfers between devices, to_replicas(): lax.ppermute(parts[step], 'dp', swap_route(step, count))  8.5 us
    ppermute x2, starting transfers between devices, swap_sections(): lax.ppermute(far, 'section', [(i, (i + 2 * (i % 2) - 1) % count) for i in...  3.12 us
    ppermute x6, waiting for transfers between devices, to_replicas(): lax.ppermute(parts[step], 'dp', swap_route(step, count))  2.33 us
    ppermute x2, waiting for transfers between devices, swap_sections(): lax.ppermute(far, 'section', [(i, (i + 2 * (i % 2) - 1) % count) for i in...  2.27 us
    unnamed x28, local copies, waits for them, and re-layouts  1.65 us
  transfers between devices with their start and end apart: 10, of which 6 were waited for; matrix products, arithmetic and copies ran while one was open for 0% of the time, Pallas kernels for 22%

profile of v19, /device:TPU:0, one launch (start us, length us, event | category | flops | bytes accessed | tf_op | source)
XLA Modules:
  0.0 27.9 jit_solution(17455599857176192800)
XLA Ops:
  0.8 0.5 %copy-done.7 = s32[1,32]{1,0:T(1,128)S(1)} copy-done((s32[1,32]{1,0:T(1,128)S(1)}, s32[1,32]{1,0:T(1,128)}, u32[]{:S(2)}) %copy-start.7) | copy-done | bytes 152
  1.3 0.6 %copy-done = bf16[1,32,128,128]{3,2,1,0:T(8,128)(2,1)S(1)} copy-done((bf16[1,32,128,128]{3,2,1,0:T(8,128)(2,1)S(1)}, bf16[1,32,128,128]{3,2,1,0:T(8,128)(2,1)}, u32[]{:S(2)}) %copy-start) | copy-done | bytes 1048600
  1.9 0.3 %copy-done.1 = bf16[1,32,128,128]{3,2,1,0:T(8,128)(2,1)S(1)} copy-done((bf16[1,32,128,128]{3,2,1,0:T(8,128)(2,1)S(1)}, bf16[1,32,128,128]{3,2,1,0:T(8,128)(2,1)}, u32[]{:S(2)}) %copy-start.1) | copy-done | bytes 1048600
  2.4 1.7 %shard_map.182 = (f32[32,24,128]{2,1,0:T(8,128)S(1)}, bf16[16,4096]{1,0:T(8,128)(2,1)S(1)}, bf16[10,16,1024]{2,1,0:T(8,128)(2,1)S(1)}, bf16[10,16,1024]{2,1,0:T(...) custom-call(s32[1,32]{1,0:T(1,128)S(1)} %copy-done.7, s32[1,32]{1,0:T(1,128)S(1)} %copy-done.8, ...), custom_call_target="tpu_custom_call" | custom-call | flops 10000000000 | bytes 100000000 | tf_op jit(solution)/shard_map/pallas_call | solution.py:274
  4.1 4.0 %collective-permute-start = (bf16[10,16,1024]{2,1,0:T(8,128)(2,1)S(1)}, bf16[10,16,1024]{2,1,0:T(8,128)(2,1)S(1)}, u32[]{:S(2)}, u32[]{:S(2)}) collective-permute-start(bf16[10,16,1024]{2,1,0:T(8,128)(2,1)S(1)} %get-tuple-element.33), channel_id=1, source_target_pairs={{0,3},{1,2},{2,1},{3,0},{4,7},{5,6},{6,5},{7,4},{8,11},{9,10},{10,... | collective-permute-start | bytes 983048 | tf_op jit(solution)/shard_map/ppermute | solution.py:315
  8.0 1.9 %shard_map.183 = (bf16[16,4096]{1,0:T(8,128)(2,1)S(1)}, bf16[16,4224]{1,0:T(8,128)(2,1)S(1)}, f32[32,8,128]{2,1,0:T(8,128)S(1)}) custom-call(s32[1,32]{1,0:T(1,128)S(1)} %copy-done.7, s32[1,32]{1,0:T(1,128)S(1)} %copy-done.8, s32[1,2]{1,0:T(1,128)S(1)} %copy-done.9, bf16[1,32,128,128]{3,2,1,0:T(8,128)(2,1)S(1)} %copy-done, ...), custom_call_target="tpu_custom_call" | custom-call | flops 10000 | bytes 100 | tf_op jit(solution)/shard_map/pallas_call | solution.py:274
  9.9 2.8 %collective-permute-start.5 = (bf16[16,4224]{1,0:T(8,128)(2,1)S(1)}, bf16[16,4224]{1,0:T(8,128)(2,1)S(1)}, u32[]{:S(2)}, u32[]{:S(2)}) collective-permute-start(bf16[16,4224]{1,0:T(8,128)(2,1)S(1)} %get-tuple-element.41), channel_id=1, source_target_pairs={{0,28},{4,8},{8,4},{12,16},{16,12},{20,24},{24,20},{28,0},{1,29},{... | collective-permute-start | bytes 405512 | tf_op jit(solution)/shard_map/ppermute | solution.py:34
  12.8 0.5 %collective-permute-start.1 = (bf16[10,16,1024]{2,1,0:T(8,128)(2,1)S(1)}, bf16[10,16,1024]{2,1,0:T(8,128)(2,1)S(1)}, u32[]{:S(2)}, u32[]{:S(2)}) collective-permute-start(bf16[10,16,1024]{2,1,0:T(8,128)(2,1)S(1)} %get-tuple-element.34), channel_id=1, source_target_pairs={{0,1},{1,0},{2,3},{3,2},{4,5},{5,4},{6,7},{7,6},{8,9},{9,8},{10,11... | collective-permute-start | bytes 983048 | tf_op jit(solution)/shard_map/ppermute | solution.py:315
  13.3 0.5 %collective-permute-start.2 = (bf16[10,16,1024]{2,1,0:T(8,128)(2,1)S(1)}, bf16[10,16,1024]{2,1,0:T(8,128)(2,1)S(1)}, u32[]{:S(2)}, u32[]{:S(2)}) collective-permute-start(bf16[10,16,1024]{2,1,0:T(8,128)(2,1)S(1)} %get-tuple-element.35), channel_id=1, source_target_pairs={{0,2},{1,3},{2,0},{3,1},{4,6},{5,7},{6,4},{7,5},{8,10},{9,11},{10,... | collective-permute-start | bytes 983048 | tf_op jit(solution)/shard_map/ppermute | solution.py:315
  13.8 0.3 %collective-permute-done.3.refs_4_ = bf16[16,4096]{1,0:T(8,128)(2,1)S(1)} collective-permute-done((bf16[16,4096]{1,0:T(8,128)(2,1)S(1)}, bf16[16,4096]{1,0:T(8,128)(2,1)S(1)}, u32[]{:S(2)}, u32[]{:S(2)}) %collective-permute-start.3) | collective-permute-done | bytes 131104 | tf_op jit(solution)/shard_map/ppermute | solution.py:35
  14.1 1.9 %shard_map.184 = (bf16[16,4224]{1,0:T(8,128)(2,1)S(1)}, bf16[2,16,1024]{2,1,0:T(8,128)(2,1)S(1)}, bf16[2,16,1024]{2,1,0:T(8,128)(2,1)S(1)}, bf16[2,16,1024]{2,1,0:T(8,128)(2,1)S(1)}, bf16[2,16,1024]{2,1,0:T(8,128)(2,1)S(1)}) custom-call(s32[1,32]{1,0:T(1,128)S(1)} %copy-done.7, s32[1,32]{1,0:T(1,128)S(1)} %copy-done.8, ...), custom_call_target="tpu_custom_call" | custom-call | flops 10000 | bytes 100 | tf_op jit(solution)/shard_map/pallas_call | solution.py:274
  16.0 0.3 %collective-permute-start.4 = (bf16[16,4224]{1,0:T(8,128)(2,1)S(1)}, bf16[16,4224]{1,0:T(8,128)(2,1)S(1)}, u32[]{:S(2)}, u32[]{:S(2)}) collective-permute-start(bf16[16,4224]{1,0:T(8,128)(2,1)S(1)} %get-tuple-element.40), channel_id=1, source_target_pairs={{0,28},{4,8},{8,4},{12,16},{16,12},{20,24},{24,20},{28,0},{1,29},{... | collective-permute-start | bytes 405512 | tf_op jit(solution)/shard_map/ppermute | solution.py:34
  16.3 1.1 %collective-permute-done.5.refs_4_ = bf16[16,4224]{1,0:T(8,128)(2,1)S(1)} collective-permute-done((bf16[16,4224]{1,0:T(8,128)(2,1)S(1)}, bf16[16,4224]{1,0:T(8,128)(2,1)S(1)}, u32[]{:S(2)}, u32[]{:S(2)}) %collective-permute-start.5) | collective-permute-done | bytes 135200 | tf_op jit(solution)/shard_map/ppermute | solution.py:34
  17.4 1.4 %shard_map.185 = (bf16[16,4096]{1,0:T(8,128)(2,1)S(1)}, bf16[2,16,1024]{2,1,0:T(8,128)(2,1)S(1)}, bf16[2,16,1024]{2,1,0:T(8,128)(2,1)S(1)}, bf16[2,16,1024]{2,1,0:T(8,128)(2,1)S(1)}, bf16[2,16,1024]{2,1,0:T(8,128)(2,1)S(1)}) custom-call(s32[1,32]{1,0:T(1,128)S(1)} %copy-done.7, s32[1,32]{1,0:T(1,128)S(1)} %copy-done.8, ...), custom_call_target="tpu_custom_call" | custom-call | flops 10000 | bytes 100 | tf_op jit(solution)/shard_map/pallas_call | solution.py:274
  18.8 0.1 collective-permute-start.6
  18.9 2.0 %collective-permute-start.7 = (bf16[2,16,1024]{2,1,0:T(8,128)(2,1)S(1)}, bf16[2,16,1024]{2,1,0:T(8,128)(2,1)S(1)}, u32[]{:S(2)}, u32[]{:S(2)}) collective-permute-start(bf16[2,16,1024]{2,1,0:T(8,128)(2,1)S(1)} %get-tuple-element.53), channel_id=1, source_target_pairs={{0,3},{1,2},{2,1},{3,0},{4,7},{5,6},{6,5},{7,4},{8,11},{9,10},{10,... | collective-permute-start | bytes 196616 | tf_op jit(solution)/shard_map/ppermute | solution.py:315
  20.9 0.5 %collective-permute-start.9 = (bf16[2,16,1024]{2,1,0:T(8,128)(2,1)S(1)}, bf16[2,16,1024]{2,1,0:T(8,128)(2,1)S(1)}, u32[]{:S(2)}, u32[]{:S(2)}) collective-permute-start(bf16[2,16,1024]{2,1,0:T(8,128)(2,1)S(1)} %get-tuple-element.55), channel_id=1, source_target_pairs={{0,2},{1,3},{2,0},{3,1},{4,6},{5,7},{6,4},{7,5},{8,10},{9,11},{10,... | collective-permute-start | bytes 196616 | tf_op jit(solution)/shard_map/ppermute | solution.py:315
  21.4 1.2 %collective-permute-done.4.refs_4_ = bf16[16,4224]{1,0:T(8,128)(2,1)S(1)} collective-permute-done((bf16[16,4224]{1,0:T(8,128)(2,1)S(1)}, bf16[16,4224]{1,0:T(8,128)(2,1)S(1)}, u32[]{:S(2)}, u32[]{:S(2)}) %collective-permute-start.4) | collective-permute-done | bytes 135200 | tf_op jit(solution)/shard_map/ppermute | solution.py:34
  22.5 1.0 %collective-permute-start.8 = (bf16[2,16,1024]{2,1,0:T(8,128)(2,1)S(1)}, bf16[2,16,1024]{2,1,0:T(8,128)(2,1)S(1)}, u32[]{:S(2)}, u32[]{:S(2)}) collective-permute-start(bf16[2,16,1024]{2,1,0:T(8,128)(2,1)S(1)} %shard_map.187), channel_id=1, source_target_pairs={{0,1},{1,0},{2,3},{3,2},{4,5},{5,4},{6,7},{7,6},{8,9},{9,8},{10,11... | collective-permute-start | bytes 196616 | tf_op jit(solution)/shard_map/ppermute | solution.py:315
  23.5 1.2 %collective-permute-done.2.refs_3_.refs_4_ = bf16[10,16,1024]{2,1,0:T(8,128)(2,1)S(1)} collective-permute-done((bf16[10,16,1024]{2,1,0:T(8,128)(2,1)S(1)}, bf16[10,16,1024]{2,1,0:T(8,128)(2,1)S(1)}, u32[]{:S(2)}, u32[]{:S(2)}) %collective-permute-start.2) | collective-permute-done | bytes 327712 | tf_op jit(solution)/shard_map/ppermute | solution.py:315
  24.7 1.0 %shard_map.186 = (f32[2,8,128,128]{3,2,1,0:T(8,128)S(1)}, bf16[1,8,4096]{2,1,0:T(8,128)(2,1)}, bf16[1,8,4096]{2,1,0:T(8,128)(2,1)}, bf16[1,8,4096]{2,1,0:T(8,128)(2,1)}, bf16[1,8,4096]{2,1,0:T(8,128)(2,1)}) custom-call(bf16[10,16,1024]{2,1,0:T(8,128)(2,1)S(1)} %get-tuple-element.32.refs_0_.refs_1_, ...), custom_call_target="tpu_custom_call" | custom-call | flops 10000 | bytes 100 | tf_op jit(solution)/shard_map/pallas_call | solution.py:274
  25.7 0.3 %collective-permute-done.9.refs_8_ = bf16[2,16,1024]{2,1,0:T(8,128)(2,1)S(1)} collective-permute-done((bf16[2,16,1024]{2,1,0:T(8,128)(2,1)S(1)}, bf16[2,16,1024]{2,1,0:T(8,128)(2,1)S(1)}, u32[]{:S(2)}, u32[]{:S(2)}) %collective-permute-start.9) | collective-permute-done | bytes 65568 | tf_op jit(solution)/shard_map/ppermute | solution.py:315
  26.0 0.8 %collective-permute-done.8.refs_7_ = bf16[2,16,1024]{2,1,0:T(8,128)(2,1)S(1)} collective-permute-done((bf16[2,16,1024]{2,1,0:T(8,128)(2,1)S(1)}, bf16[2,16,1024]{2,1,0:T(8,128)(2,1)S(1)}, u32[]{:S(2)}, u32[]{:S(2)}) %collective-permute-start.8) | collective-permute-done | bytes 65568 | tf_op jit(solution)/shard_map/ppermute | solution.py:315
  26.8 1.1 %shard_map.188 = (bf16[1,8,128,128]{3,2,1,0:T(8,128)(2,1)}, bf16[1,8,128,128]{3,2,1,0:T(8,128)(2,1)}) custom-call(f32[2,8,128,128]{3,2,1,0:T(8,128)S(1)} %get-tuple-element.51.refs_0_, bf16[10,16,1024]{2,1,0:T(8,128)(2,1)S(1)} %get-tuple-element.32.refs_0_.refs_1_, bf16[10,16,1024]{2,1,0:T(8,128)(2,1)S(1)} %collective-permute-done.refs_11_.refs_1_.refs_2_, ...), custom_call_target="tpu_custom_call" | custom-call | flops 10000 | bytes 100 | tf_op jit(solution)/shard_map/pallas_call | solution.py:274
  (32 shorter events, 0.2 us)
Async XLA Ops:
  0.6 0.7 %copy-start.7 = (s32[1,32]{1,0:T(1,128)S(1)}, s32[1,32]{1,0:T(1,128)}, u32[]{:S(2)}) copy-start(s32[1,32]{1,0:T(1,128)} %refs_0_.7) | copy-start | bytes 388
  0.6 0.7 %copy-start.8 = (s32[1,32]{1,0:T(1,128)S(1)}, s32[1,32]{1,0:T(1,128)}, u32[]{:S(2)}) copy-start(s32[1,32]{1,0:T(1,128)} %refs_1_.7) | copy-start | bytes 388
  0.7 0.7 %copy-start.9 = (s32[1,2]{1,0:T(1,128)S(1)}, s32[1,2]{1,0:T(1,128)}, u32[]{:S(2)}) copy-start(s32[1,2]{1,0:T(1,128)} %refs_2_.5) | copy-start | bytes 28
  0.7 1.2 %copy-start = (bf16[1,32,128,128]{3,2,1,0:T(8,128)(2,1)S(1)}, bf16[1,32,128,128]{3,2,1,0:T(8,128)(2,1)}, u32[]{:S(2)}) copy-start(bf16[1,32,128,128]{3,2,1,0:T(8,128)(2,1)} %refs_2_.7) | copy-start | bytes 3145732
  0.7 1.5 %copy-start.1 = (bf16[1,32,128,128]{3,2,1,0:T(8,128)(2,1)S(1)}, bf16[1,32,128,128]{3,2,1,0:T(8,128)(2,1)}, u32[]{:S(2)}) copy-start(bf16[1,32,128,128]{3,2,1,0:T(8,128)(2,1)} %refs_3_.7) | copy-start | bytes 3145732
  0.7 1.5 %copy-start.3 = (bf16[1,8,4096]{2,1,0:T(8,128)(2,1)S(1)}, bf16[1,8,4096]{2,1,0:T(8,128)(2,1)}, u32[]{:S(2)}) copy-start(bf16[1,8,4096]{2,1,0:T(8,128)(2,1)} %refs_5_.3) | copy-start | bytes 196612
  0.7 1.5 %copy-start.4 = (bf16[1,8,4096]{2,1,0:T(8,128)(2,1)S(1)}, bf16[1,8,4096]{2,1,0:T(8,128)(2,1)}, u32[]{:S(2)}) copy-start(bf16[1,8,4096]{2,1,0:T(8,128)(2,1)} %refs_6_.3) | copy-start | bytes 196612
  0.7 1.6 %copy-start.10 = (bf16[1,2,8,4096]{3,2,1,0:T(8,128)(2,1)S(1)}, bf16[1,2,8,4096]{3,2,1,0:T(8,128)(2,1)}, u32[]{:S(2)}) copy-start(bf16[1,2,8,4096]{3,2,1,0:T(8,128)(2,1)} %refs_7_.1) | copy-start | bytes 393220
  0.7 1.6 %copy-start.11 = (bf16[1,2,8,4096]{3,2,1,0:T(8,128)(2,1)S(1)}, bf16[1,2,8,4096]{3,2,1,0:T(8,128)(2,1)}, u32[]{:S(2)}) copy-start(bf16[1,2,8,4096]{3,2,1,0:T(8,128)(2,1)} %refs_8_.2) | copy-start | bytes 393220
  0.7 1.6 %copy-start.12 = (bf16[1,2,8,4096]{3,2,1,0:T(8,128)(2,1)S(1)}, bf16[1,2,8,4096]{3,2,1,0:T(8,128)(2,1)}, u32[]{:S(2)}) copy-start(bf16[1,2,8,4096]{3,2,1,0:T(8,128)(2,1)} %refs_9_.2) | copy-start | bytes 393220
  0.7 1.6 %copy-start.13 = (bf16[1,2,8,4096]{3,2,1,0:T(8,128)(2,1)S(1)}, bf16[1,2,8,4096]{3,2,1,0:T(8,128)(2,1)}, u32[]{:S(2)}) copy-start(bf16[1,2,8,4096]{3,2,1,0:T(8,128)(2,1)} %refs_10_.2) | copy-start | bytes 393220
  2.4 5.7 %copy-start.2 = (bf16[1,2,8,4096]{3,2,1,0:T(8,128)(2,1)S(1)}, bf16[1,2,8,4096]{3,2,1,0:T(8,128)(2,1)}, u32[]{:S(2)}) copy-start(bf16[1,2,8,4096]{3,2,1,0:T(8,128)(2,1)} %refs_10_.3) | copy-start | bytes 393220
  2.4 5.7 %copy-start.5 = (bf16[1,8,4096]{2,1,0:T(8,128)(2,1)S(1)}, bf16[1,8,4096]{2,1,0:T(8,128)(2,1)}, u32[]{:S(2)}) copy-start(bf16[1,8,4096]{2,1,0:T(8,128)(2,1)} %refs_8_.3) | copy-start | bytes 196612
  2.4 5.7 %copy-start.6 = (bf16[1,8,4096]{2,1,0:T(8,128)(2,1)S(1)}, bf16[1,8,4096]{2,1,0:T(8,128)(2,1)}, u32[]{:S(2)}) copy-start(bf16[1,8,4096]{2,1,0:T(8,128)(2,1)} %refs_9_.3) | copy-start | bytes 196612
  4.1 13.4 %collective-permute-start = (bf16[10,16,1024]{2,1,0:T(8,128)(2,1)S(1)}, bf16[10,16,1024]{2,1,0:T(8,128)(2,1)S(1)}, u32[]{:S(2)}, u32[]{:S(2)}) collective-permute-start(bf16[10,16,1024]{2,1,0:T(8,128)(2,1)S(1)} %get-tuple-element.33), channel_id=1, source_target_pairs={{0,3},{1,2},{2,1},{3,0},{4,7},{5,6},{6,5},{7,4},{8,11},{9,10},{10,... | collective-permute-start | bytes 983048 | tf_op jit(solution)/shard_map/ppermute | solution.py:315
  9.9 7.5 %collective-permute-start.5 = (bf16[16,4224]{1,0:T(8,128)(2,1)S(1)}, bf16[16,4224]{1,0:T(8,128)(2,1)S(1)}, u32[]{:S(2)}, u32[]{:S(2)}) collective-permute-start(bf16[16,4224]{1,0:T(8,128)(2,1)S(1)} %get-tuple-element.41), channel_id=1, source_target_pairs={{0,28},{4,8},{8,4},{12,16},{16,12},{20,24},{24,20},{28,0},{1,29},{... | collective-permute-start | bytes 405512 | tf_op jit(solution)/shard_map/ppermute | solution.py:34
  12.8 1.3 %collective-permute-start.3 = (bf16[16,4096]{1,0:T(8,128)(2,1)S(1)}, bf16[16,4096]{1,0:T(8,128)(2,1)S(1)}, u32[]{:S(2)}, u32[]{:S(2)}) collective-permute-start(bf16[16,4096]{1,0:T(8,128)(2,1)S(1)} %get-tuple-element.37), channel_id=1, source_target_pairs={{0,4},{4,0},{8,12},{12,8},{16,20},{20,16},{24,28},{28,24},{1,5},{5... | collective-permute-start | bytes 393224 | tf_op jit(solution)/shard_map/ppermute | solution.py:35
  12.8 10.7 %collective-permute-start.1 = (bf16[10,16,1024]{2,1,0:T(8,128)(2,1)S(1)}, bf16[10,16,1024]{2,1,0:T(8,128)(2,1)S(1)}, u32[]{:S(2)}, u32[]{:S(2)}) collective-permute-start(bf16[10,16,1024]{2,1,0:T(8,128)(2,1)S(1)} %get-tuple-element.34), channel_id=1, source_target_pairs={{0,1},{1,0},{2,3},{3,2},{4,5},{5,4},{6,7},{7,6},{8,9},{9,8},{10,11... | collective-permute-start | bytes 983048 | tf_op jit(solution)/shard_map/ppermute | solution.py:315
  13.3 11.4 %collective-permute-start.2 = (bf16[10,16,1024]{2,1,0:T(8,128)(2,1)S(1)}, bf16[10,16,1024]{2,1,0:T(8,128)(2,1)S(1)}, u32[]{:S(2)}, u32[]{:S(2)}) collective-permute-start(bf16[10,16,1024]{2,1,0:T(8,128)(2,1)S(1)} %get-tuple-element.35), channel_id=1, source_target_pairs={{0,2},{1,3},{2,0},{3,1},{4,6},{5,7},{6,4},{7,5},{8,10},{9,11},{10,... | collective-permute-start | bytes 983048 | tf_op jit(solution)/shard_map/ppermute | solution.py:315
  16.0 6.5 %collective-permute-start.4 = (bf16[16,4224]{1,0:T(8,128)(2,1)S(1)}, bf16[16,4224]{1,0:T(8,128)(2,1)S(1)}, u32[]{:S(2)}, u32[]{:S(2)}) collective-permute-start(bf16[16,4224]{1,0:T(8,128)(2,1)S(1)} %get-tuple-element.40), channel_id=1, source_target_pairs={{0,28},{4,8},{8,4},{12,16},{16,12},{20,24},{24,20},{28,0},{1,29},{... | collective-permute-start | bytes 405512 | tf_op jit(solution)/shard_map/ppermute | solution.py:34
  18.8 2.1 %collective-permute-start.6 = (bf16[16,4096]{1,0:T(8,128)(2,1)S(1)}, bf16[16,4096]{1,0:T(8,128)(2,1)S(1)}, u32[]{:S(2)}, u32[]{:S(2)}) collective-permute-start(bf16[16,4096]{1,0:T(8,128)(2,1)S(1)} %get-tuple-element.46), channel_id=1, source_target_pairs={{0,4},{4,0},{8,12},{12,8},{16,20},{20,16},{24,28},{28,24},{1,5},{5... | collective-permute-start | bytes 393224 | tf_op jit(solution)/shard_map/ppermute | solution.py:35
  18.9 6.8 %collective-permute-start.7 = (bf16[2,16,1024]{2,1,0:T(8,128)(2,1)S(1)}, bf16[2,16,1024]{2,1,0:T(8,128)(2,1)S(1)}, u32[]{:S(2)}, u32[]{:S(2)}) collective-permute-start(bf16[2,16,1024]{2,1,0:T(8,128)(2,1)S(1)} %get-tuple-element.53), channel_id=1, source_target_pairs={{0,3},{1,2},{2,1},{3,0},{4,7},{5,6},{6,5},{7,4},{8,11},{9,10},{10,... | collective-permute-start | bytes 196616 | tf_op jit(solution)/shard_map/ppermute | solution.py:315
  20.9 5.1 %collective-permute-start.9 = (bf16[2,16,1024]{2,1,0:T(8,128)(2,1)S(1)}, bf16[2,16,1024]{2,1,0:T(8,128)(2,1)S(1)}, u32[]{:S(2)}, u32[]{:S(2)}) collective-permute-start(bf16[2,16,1024]{2,1,0:T(8,128)(2,1)S(1)} %get-tuple-element.55), channel_id=1, source_target_pairs={{0,2},{1,3},{2,0},{3,1},{4,6},{5,7},{6,4},{7,5},{8,10},{9,11},{10,... | collective-permute-start | bytes 196616 | tf_op jit(solution)/shard_map/ppermute | solution.py:315
  22.5 4.3 %collective-permute-start.8 = (bf16[2,16,1024]{2,1,0:T(8,128)(2,1)S(1)}, bf16[2,16,1024]{2,1,0:T(8,128)(2,1)S(1)}, u32[]{:S(2)}, u32[]{:S(2)}) collective-permute-start(bf16[2,16,1024]{2,1,0:T(8,128)(2,1)S(1)} %shard_map.187), channel_id=1, source_target_pairs={{0,1},{1,0},{2,3},{3,2},{4,5},{5,4},{6,7},{7,6},{8,9},{9,8},{10,11... | collective-permute-start | bytes 196616 | tf_op jit(solution)/shard_map/ppermute | solution.py:315
